TPU v7x, 512 devices: a whole 4x4x16 slice. The times are simulated.
512 devices in a mesh: dp: 32 (over y_hi, z), expert: 16 (over y_lo, x, core).
Axes of the slice: x: 4, y: 4 (y_hi: 2, y_lo: 2; y = y_hi * 2 + y_lo), z: 16, core: 2. Of those that a mesh axis runs over, the one named last changes fastest.
Arguments:
- tokens: bfloat16 [65536, 1024], P(('dp', 'expert')), may hold values from -6 to 6
- cotangent: bfloat16 [65536, 1024], P(('dp', 'expert')), may hold values from -6 to 6
- route_experts: int32 [65536, 8], P(('dp', 'expert')), may hold values from 0 to 15, as said below
- route_weights: float32 [65536, 8], P(('dp', 'expert')), may hold values from 0.05 to 0.4
- gate_up: bfloat16 [16, 1024, 768], P('expert', 'dp'), may hold values from -0.1875 to 0.1875
- down: bfloat16 [16, 1024, 384], P('expert', 'dp'), may hold values from -0.3125 to 0.3125
Outputs:
- token_grad: bfloat16 [65536, 1024], P(('dp', 'expert'))
- grad_gate_up: float32 [16, 1024, 768], P('expert', 'dp')
Inputs may be any that keep to these rules, and one draw needn't show every extreme that they name: `route_experts`: each token names 8 different experts. Among the rows of one device no expert is named by more than 80 rows, and one expert is named by exactly 80 rows of every device.
All inputs are finite; a program needn't handle non-finite values.
Results may differ from a plain program's by a relative error of at most 0.02.
Values may be sent and summed in bfloat16 or wider, within the bound.
No kernel may reach another device: no remote copies, remote signals or barrier semaphores. Data moves between devices by JAX's collectives and lax.ppermute only.
A program may use at most 64 MiB of HBM per device.

v0:
```python
import math

import jax
import jax.numpy as jnp
from jax import lax
from jax.sharding import PartitionSpec as P

EXPERTS = 16
CAP = 80


def slot_pairs(route_rows):
    pair_total = route_rows.shape[0] * route_rows.shape[1]
    flat_experts = route_rows.reshape(pair_total)
    onehot = (flat_experts[:, None] == jnp.arange(EXPERTS, dtype=jnp.int32)[None, :]).astype(
        jnp.int32
    )
    running = jnp.cumsum(onehot, axis=0)
    within = jnp.sum(running * onehot, axis=1) - 1
    position = flat_experts * CAP + within
    owner_pair = (
        jnp.full((EXPERTS * CAP,), pair_total, jnp.int32)
        .at[position]
        .set(jnp.arange(pair_total, dtype=jnp.int32))
    )
    return (position, owner_pair)


def shards(tokens, cotangent, route_experts, route_weights, gate_up, down):
    tok_rows, features = tokens.shape
    choose_count = route_experts.shape[1]
    hidden_units = down.shape[2]
    owner_count = lax.axis_size("expert")
    local_count = gate_up.shape[0]
    slot_total = EXPERTS * CAP
    pair_total = tok_rows * choose_count
    slot_shape = (owner_count, local_count, CAP, features)
    position, owner_pair = slot_pairs(route_experts)
    filled = owner_pair < pair_total
    source_pair = jnp.minimum(owner_pair, pair_total - 1)
    source_token = source_pair // choose_count
    send_inputs = jnp.where(filled[:, None], tokens[source_token], jnp.zeros((), tokens.dtype))
    row_weights = jnp.where(filled, route_weights.reshape(pair_total)[source_pair], 0.0)
    send_cot = (row_weights[:, None] * cotangent[source_token].astype(jnp.float32)).astype(
        jnp.bfloat16
    )
    send_inputs = send_inputs.reshape(slot_shape)
    send_cot = send_cot.reshape(slot_shape)
    got_inputs, got_cot = (
        lax.all_to_all(send_inputs, "expert", split_axis=0, concat_axis=0, tiled=True),
        lax.all_to_all(send_cot, "expert", split_axis=0, concat_axis=0, tiled=True),
    )
    full_gate_up, full_down = (
        lax.all_gather(gate_up, "dp", axis=1, tiled=True),
        lax.all_gather(down, "dp", axis=1, tiled=True),
    )
    projected = jnp.einsum(
        "secd,edf->secf", got_inputs, full_gate_up, preferred_element_type=jnp.float32
    )
    hidden_grad = jnp.einsum(
        "secd,edf->secf", got_cot, full_down, preferred_element_type=jnp.float32
    )
    gate_part = projected[..., :hidden_units]
    up_part = projected[..., hidden_units:]
    sigmoid_gate = jax.nn.sigmoid(gate_part)
    grad_gate = hidden_grad * up_part * sigmoid_gate * (1.0 + gate_part * (1.0 - sigmoid_gate))
    grad_up = hidden_grad * gate_part * sigmoid_gate
    pre_grad = jnp.concatenate([grad_gate, grad_up], axis=3).astype(jnp.bfloat16)
    row_grads = jnp.einsum(
        "secf,edf->secd", pre_grad, full_gate_up, preferred_element_type=jnp.float32
    ).astype(jnp.bfloat16)
    returned = lax.all_to_all(row_grads, "expert", split_axis=0, concat_axis=0, tiled=True)
    back_rows = returned.reshape(slot_total, features)[position].reshape(
        tok_rows, choose_count, features
    )
    token_grad = jnp.sum(back_rows, axis=1, dtype=jnp.float32).astype(jnp.bfloat16)
    summed = lax.psum_scatter(
        jnp.einsum("secd,secf->def", got_inputs, pre_grad, preferred_element_type=jnp.float32),
        "dp",
        scatter_dimension=0,
        tiled=True,
    )
    grad_scale = 1.0 / math.sqrt(tok_rows * lax.axis_size("dp") * owner_count)
    grad_gate_up = jnp.transpose(summed, (1, 0, 2)) * grad_scale
    return (token_grad, grad_gate_up)


def solution(mesh):
    in_specs = (
        P(("dp", "expert"), None),
        P(("dp", "expert"), None),
        P(("dp", "expert"), None),
        P(("dp", "expert"), None),
        P("expert", "dp", None),
        P("expert", "dp", None),
    )
    out_specs = (P(("dp", "expert"), None), P("expert", "dp", None))
    return jax.shard_map(shards, mesh=mesh, in_specs=in_specs, out_specs=out_specs, check_vma=False)
```

profile of v0, /device:TPU:6, one launch (start us, length us, event | category | flops | bytes accessed | tf_op | source)
XLA Modules:
  0.0 535.6 jit_solution(6515707506157420587)
XLA Ops:
  8.9 4.5 reduce-window.6
  14.1 4.3 scatter_custom_fusion
  19.3 5.0 gather_fusion
  24.4 4.3 gather_fusion.2
  28.7 1.8 broadcast_select_fusion
  30.5 9.5 %all-to-all-start.1 = ((bf16[16,1,80,1024]{3,2,1,0:T(8,128)(2,1)}), bf16[16,1,80,1024]{3,2,1,0:T(8,128)(2,1)S(1)}, u32[]{:S(2)}, u32[]{:S(2)}) async-start(bf16[16,1,80,1024]{3,2,1,0:T(8,128)(2,1)} %broadcast_select_fusion), calls=%async_computation.1 | async-start | bytes 5242880 | tf_op jit(solution)/shard_map/all_to_all | solution.py:50
  40.9 5.1 gather_fusion.1
  45.9 3.8 fusion
  49.7 23.2 %all-to-all-done.1 = bf16[16,1,80,1024]{3,2,1,0:T(8,128)(2,1)S(1)} async-done(((bf16[16,1,80,1024]{3,2,1,0:T(8,128)(2,1)}), bf16[16,1,80,1024]{3,2,1,0:T(8,128)(2,1)S(1)}, u32[]{:S(2)}, u32[]{:S(2)}) %all-to-all-start.1) | async-done | bytes 2621472 | tf_op jit(solution)/shard_map/all_to_all | solution.py:50
  72.9 7.0 %all-to-all-start = ((bf16[16,1,80,1024]{3,2,1,0:T(8,128)(2,1)}), bf16[16,1,80,1024]{3,2,1,0:T(8,128)(2,1)}, u32[]{:S(2)}, u32[]{:S(2)}) async-start(bf16[16,1,80,1024]{3,2,1,0:T(8,128)(2,1)} %fusion), calls=%async_computation | async-start | bytes 5242880 | tf_op jit(solution)/shard_map/all_to_all | solution.py:51
  80.0 90.5 %all_gather.6 = bf16[1,1024,384]{2,1,0:T(8,128)(2,1)} all-gather(bf16[1,32,384]{2,1,0:T(8,128)(2,1)S(1)} %copy-done.8), channel_id=1, replica_groups=mesh['dp'=32,'expert'=16] {'dp'}, dimensions={1}, use_global_device_ids=true | all-gather | bytes 811008 | tf_op jit(solution)/shard_map/all_gather | solution.py:55
  170.5 26.5 %all-gather.2.cloned.1.call-done = bf16[1,1024,768]{2,1,0:T(8,128)(2,1)} async-done(((bf16[1,32,768]{2,1,0:T(8,128)(2,1)}), bf16[1,1024,768]{2,1,0:T(8,128)(2,1)}) %all-gather.2.cloned.1.call-update) | async-done | bytes 1572880 | tf_op jit(solution)/shard_map/all_gather | solution.py:54
  197.0 5.5 %fusion.7 = f32[16,1,80,768]{3,2,0,1:T(8,128)} fusion(bf16[16,1,80,1024]{3,2,1,0:T(8,128)(2,1)S(1)} %all-to-all-done.1, bf16[1,1024,768]{2,1,0:T(8,128)(2,1)} %all-gather.2.cloned.1.call-done), kind=kOutput, calls=%fused_computation.16 | convolution fusion | flops 2013265920 | bytes 8126464 | tf_op jit(solution)/shard_map/secd,edf->secf/dot_general | solution.py:57
  202.5 5.4 %fusion.21 = (bf16[16,80,384]{2,1,0:T(8,128)(2,1)S(1)}, bf16[16,80,384]{2,1,0:T(8,128)(2,1)S(1)}) fusion(f32[16,1,80,768]{3,2,0,1:T(8,128)} %fusion.7, bf16[1,1024,384]{2,1,0:T(8,128)(2,1)} %all_gather.6, bf16[16,1,80,1024]{3,2,1,0:T(8,128)(2,1)} %all-to-all-done), kind=kOutput, calls=%fused_computation.30 | convolution fusion | flops 1013022720 | bytes 9306112 | tf_op jit(solution)/shard_map/secd,edf->secf/dot_general | solution.py:60
  209.2 2.3 fusion.15
  211.5 5.5 %copy.27 = f32[1024,1,768]{2,1,0:T(1,128)} copy(f32[1024,1,768]{0,2,1:T(8,128)S(1)} %fusion.15) | data formatting | bytes 6291456 | tf_op jit(solution)/shard_map/secd,secf->def/transpose | solution.py:78
  217.0 1.2 copy-done.5
  218.5 5.2 convert_bitcast_fusion
  223.7 4.9 all-to-all-start.2
  228.6 1.3 dynamic-slice
  230.5 36.1 %all-to-all-done.2 = bf16[16,1,80,1024]{3,2,1,0:T(8,128)(2,1)S(1)} async-done(((bf16[16,1,80,1024]{3,2,1,0:T(8,128)(2,1)}), bf16[16,1,80,1024]{3,2,1,0:T(8,128)(2,1)S(1)}, u32[]{:S(2)}, u32[]{:S(2)}) %all-to-all-start.2) | async-done | bytes 2621472 | tf_op jit(solution)/shard_map/all_to_all | solution.py:72
  266.6 5.4 %gather_fusion.3 = bf16[1024,1024]{1,0:T(8,128)(2,1)} fusion(bf16[1280,1024]{1,0:T(8,128)(2,1)S(1)} %bitcast.94, s32[1024]{0:T(1024)S(1)} %broadcast_clamp_fusion), kind=kCustom, calls=%fused_computation.3 | custom fusion | bytes 4198400 | tf_op jit(solution)/shard_map/gather | solution.py:73
  272.0 3.7 bitcast_reduce_fusion
  275.8 251.4 %all-reduce.3.cloned.1.call-done = f32[1024,1,768]{2,1,0:T(1,128)} async-done(((f32[1024,1,768]{2,1,0:T(1,128)}), f32[1024,1,768]{2,1,0:T(1,128)}) %all-reduce.3.cloned.1.call-update) | async-done | bytes 3145744
  (49 shorter events, 7.4 us)
Async XLA Ops:
  7.2 17.3 %copy-start = (bf16[128,1024]{1,0:T(8,128)(2,1)S(1)}, bf16[128,1024]{1,0:T(8,128)(2,1)}, u32[]{:S(2)}) copy-start(bf16[128,1024]{1,0:T(8,128)(2,1)} %param.6) | copy-start | bytes 786436
  30.5 10.3 %copy-start.1 = (bf16[128,1024]{1,0:T(8,128)(2,1)S(1)}, bf16[128,1024]{1,0:T(8,128)(2,1)}, u32[]{:S(2)}) copy-start(bf16[128,1024]{1,0:T(8,128)(2,1)} %param.7) | copy-start | bytes 786436
  30.5 42.4 %all-to-all-start.1 = ((bf16[16,1,80,1024]{3,2,1,0:T(8,128)(2,1)}), bf16[16,1,80,1024]{3,2,1,0:T(8,128)(2,1)S(1)}, u32[]{:S(2)}, u32[]{:S(2)}) async-start(bf16[16,1,80,1024]{3,2,1,0:T(8,128)(2,1)} %broadcast_select_fusion), calls=%async_computation.1 | async-start | bytes 5242880 | tf_op jit(solution)/shard_map/all_to_all | solution.py:50
  40.1 157.0 %all-gather.2.cloned.1.call-start = ((), (), s32[]{:S(2)}) async-start(), calls=%async_computation.3 | async-start | bytes 1622016 | tf_op jit(solution)/shard_map/all_gather | solution.py:54
  49.7 30.2 %copy-start.8 = (bf16[1,32,384]{2,1,0:T(8,128)(2,1)S(1)}, bf16[1,32,384]{2,1,0:T(8,128)(2,1)}, u32[]{:S(2)}) copy-start(bf16[1,32,384]{2,1,0:T(8,128)(2,1)} %param.11) | copy-start | bytes 73732
  72.9 124.1 %copy-start.2 = (bf16[16,1,80,1024]{3,2,1,0:T(8,128)(2,1)}, bf16[16,1,80,1024]{3,2,1,0:T(8,128)(2,1)S(1)}, u32[]{:S(2)}) copy-start(bf16[16,1,80,1024]{3,2,1,0:T(8,128)(2,1)S(1)} %all-to-all-done.1) | copy-start | bytes 7864324
  72.9 129.6 %all-to-all-start = ((bf16[16,1,80,1024]{3,2,1,0:T(8,128)(2,1)}), bf16[16,1,80,1024]{3,2,1,0:T(8,128)(2,1)}, u32[]{:S(2)}, u32[]{:S(2)}) async-start(bf16[16,1,80,1024]{3,2,1,0:T(8,128)(2,1)} %fusion), calls=%async_computation | async-start | bytes 5242880 | tf_op jit(solution)/shard_map/all_to_all | solution.py:51
  79.9 447.2 %all-reduce.3.cloned.1.call-start = ((), (), s32[]{:S(2)}) async-start(), calls=%async_computation.4 | async-start | bytes 6291456
  202.5 6.7 %copy-start.3 = (bf16[16,1,80,1024]{3,2,1,0:T(8,128)(2,1)S(1)}, bf16[16,1,80,1024]{3,2,1,0:T(8,128)(2,1)}, u32[]{:S(2)}) copy-start(bf16[16,1,80,1024]{3,2,1,0:T(8,128)(2,1)} %copy-done.2) | copy-start | bytes 7864324
  207.9 1.0 copy-start.4
  207.9 1.3 copy-start.6
  217.0 1.2 copy-start.5
  217.0 1.5 copy-start.7
  223.7 42.9 %all-to-all-start.2 = ((bf16[16,1,80,1024]{3,2,1,0:T(8,128)(2,1)}), bf16[16,1,80,1024]{3,2,1,0:T(8,128)(2,1)S(1)}, u32[]{:S(2)}, u32[]{:S(2)}) async-start(bf16[16,1,80,1024]{3,2,1,0:T(8,128)(2,1)} %convert_bitcast_fusion), calls=%async_computation.2 | async-start | bytes 5242880 | tf_op jit(solution)/shard_map/all_to_all | solution.py:72
Sparse Core Ops, SparseCore 0:
  44.0 152.9 all-gather.1
  217.1 309.9 all-reduce.2
where the time goes:
time: 536 us
  waiting for transfers between devices  338 us (63%)
  blocking collectives  90.5 us (17%)
  local copies, waits for them, and re-layouts  36.8 us (7%)
  starting transfers between devices  21.5 us (4%)
  matrix products  18.3 us (3%)
  other arithmetic  15.7 us (3%)
  between operations  14.9 us (3%)
    unnamed x3, waiting for transfers between devices  252 us
    all_gather x1, blocking collectives, shards(): lax.all_gather(down, 'dp', axis=1, tiled=True)  90.5 us
    all_to_all x1, waiting for transfers between devices, shards(): lax.all_to_all(row_grads, 'expert', split_axis=0, concat_axis=0, tiled=True)  36.1 us
    all_gather x1, waiting for transfers between devices, shards(): lax.all_gather(gate_up, 'dp', axis=1, tiled=True)  26.5 us
    all_to_all x1, waiting for transfers between devices, shards(): lax.all_to_all(send_inputs, 'expert', split_axis=0, concat_axis=0, tiled=...  23.2 us
  transfers between devices with their start and end apart: 5, of which 4 were waited for; matrix products, arithmetic and copies ran while one was open for 6% of the time, Pallas kernels for 0%

commit v1 on v0

v1 whole, which is shorter than its diff:
```python
import functools
import math

import jax
import jax.numpy as jnp
from jax import lax
from jax.experimental import pallas as pl
from jax.experimental.pallas import tpu as pltpu
from jax.sharding import PartitionSpec as P

EXPERTS = 16
CAP = 80
LANES = 128
RING = 16
NEAR = 4
GROUP = 4
BF16 = jnp.bfloat16
F32 = jnp.float32


def iota(shape, dim):
    return lax.broadcasted_iota(jnp.int32, shape, dim)


def strict_lower(rows):
    return (iota((rows, rows), 0) > iota((rows, rows), 1)).astype(F32).astype(BF16)


def pack_kernel(tok_ref, cot_ref, experts_ref, weights_ref, packed_ref, rank_ref):
    rows, features = tok_ref.shape
    packed_ref[:, :features] = tok_ref[...]
    packed_ref[:, features : 2 * features] = cot_ref[...]
    choices = experts_ref.shape[0]
    label = iota((2 * EXPERTS, rows), 0) % EXPERTS
    dense = jnp.zeros((2 * EXPERTS, rows), F32)
    for k in range(choices):
        dense += jnp.where(experts_ref[k : k + 1, :] == label, weights_ref[k : k + 1, :], 0.0)
    dense = jnp.concatenate([dense, jnp.zeros((LANES - 2 * EXPERTS, rows), F32)], axis=0).T
    high = dense.astype(BF16).astype(F32)
    lane = iota((rows, LANES), 1)
    packed_ref[:, 2 * features :] = jnp.where(lane < EXPERTS, high, dense - high).astype(BF16)
    routed = dense > 0.0
    rank = jnp.dot(
        strict_lower(rows), routed.astype(F32).astype(BF16), preferred_element_type=F32
    )
    rank_ref[...] = jnp.where(routed, rank, 200.0).astype(BF16)


def pack(tokens, cotangent, route_experts, route_weights):
    rows, features = tokens.shape
    return pl.pallas_call(
        pack_kernel,
        out_shape=(
            jax.ShapeDtypeStruct((rows, 2 * features + LANES), BF16),
            jax.ShapeDtypeStruct((rows, LANES), BF16),
        ),
        name="pack_rows",
    )(tokens, cotangent, route_experts.T, route_weights.T)


def expert_kernel(
    my_expert, my_dp, features, hidden, piece_total, g_ref, *refs
):
    pieces = refs[:piece_total]
    row_ref, mine_ref, theirs_ref, weights, inputs, cots, total, sems = refs[piece_total:]
    step = pl.program_id(0)
    expert = my_expert()
    half = features // 2
    dp = my_dp()
    upper = dp // RING
    place = dp % RING
    shard = features // (2 * RING)

    def copies():
        out = []
        for index, (ref, offset, part, source) in enumerate(piece_plan(pieces, shard)):
            spot = (place + offset + RING) % RING
            owner = upper if part == 0 else 1 - upper
            start = pl.multiple_of(owner * half + spot * shard, shard)
            out.append(
                pltpu.make_async_copy(
                    ref.at[pl.ds(source, shard), :], weights.at[pl.ds(start, shard), :], sems.at[index]
                )
            )
        return out

    @pl.when(step == 0)
    def _():
        for copy in copies():
            copy.start()

    rows = g_ref.shape[0] // GROUP
    lane = iota((rows, LANES), 1)
    lower = strict_lower(rows)
    slot_lane = iota((CAP, LANES), 1)
    for s in range(GROUP):
        block = g_ref[s * rows : (s + 1) * rows, :]
        dense = block[:, 2 * features :].astype(F32)
        mine = jnp.sum(jnp.where(lane == expert, dense, 0.0), axis=1, keepdims=True)
        routed = jnp.broadcast_to(mine, (rows, LANES)) > 0.0
        rank = jnp.dot(lower, routed.astype(F32).astype(BF16), preferred_element_type=F32)
        pick = jnp.where(routed & (rank == lane.astype(F32)), 1.0, 0.0).T[:CAP, :].astype(BF16)
        here = pl.ds(s * CAP, CAP)
        inputs[here, :] = jnp.dot(
            pick, block[:, :features], preferred_element_type=F32
        ).astype(BF16)
        chosen = jnp.dot(pick, block[:, 2 * features :], preferred_element_type=F32)
        scale = jnp.sum(
            jnp.where((slot_lane == expert) | (slot_lane == expert + EXPERTS), chosen, 0.0),
            axis=1,
            keepdims=True,
        )
        cots[here, :] = (
            scale
            * jnp.dot(pick, block[:, features : 2 * features], preferred_element_type=F32)
        ).astype(BF16)

    @pl.when(step == 0)
    def _():
        for copy in copies():
            copy.wait()
        total[...] = jnp.zeros_like(total)

    projected = jnp.dot(inputs[...], weights[:, : 2 * hidden], preferred_element_type=F32)
    hidden_grad = jnp.dot(cots[...], weights[:, 2 * hidden :], preferred_element_type=F32)
    gate_part = projected[:, :hidden]
    up_part = projected[:, hidden:]
    sigmoid_gate = jax.nn.sigmoid(gate_part)
    grad_gate = hidden_grad * up_part * sigmoid_gate * (1.0 + gate_part * (1.0 - sigmoid_gate))
    grad_up = hidden_grad * gate_part * sigmoid_gate
    pre_grad = jnp.concatenate([grad_gate, grad_up], axis=1).astype(BF16)
    row_ref[...] = lax.dot_general(
        pre_grad, weights[:, : 2 * hidden], (((1,), (1,)), ((), ())), preferred_element_type=F32
    ).astype(BF16)
    total[...] += lax.dot_general(
        inputs[...], pre_grad, (((0,), (0,)), ((), ())), preferred_element_type=F32
    )

    @pl.when(step == pl.num_programs(0) - 1)
    def _():
        mine_ref[...] = total[pl.ds(pl.multiple_of(upper * half, half), half), :].astype(BF16)
        theirs_ref[...] = total[pl.ds(pl.multiple_of((1 - upper) * half, half), half), :].astype(BF16)


def piece_plan(pieces, shard):
    plan = []
    offsets = [0] + [o for j in range(1, RING // 2) for o in (-j, j)]
    for ref, offset in zip(pieces, offsets):
        plan += [(ref, offset, 0, 0), (ref, offset, 1, shard)]
    far_own, far_other = pieces[len(offsets) :]
    plan += [(far_own, -(RING // 2), 0, 0), (far_other, RING // 2, 1, 0)]
    return plan


def expert_work(gathered, pieces, features, hidden, my_expert, my_dp):
    rows = gathered.shape[0] // EXPERTS
    steps = EXPERTS // GROUP
    half = features // 2
    return pl.pallas_call(
        functools.partial(expert_kernel, my_expert, my_dp, features, hidden, len(pieces)),
        grid=(steps,),
        in_specs=[pl.BlockSpec((GROUP * rows, gathered.shape[1]), lambda i: (i, 0))]
        + [pl.BlockSpec(memory_space=pl.ANY)] * len(pieces),
        out_specs=(
            pl.BlockSpec((GROUP * CAP, features), lambda i: (i, 0)),
            pl.BlockSpec((half, 2 * hidden), lambda i: (0, 0)),
            pl.BlockSpec((half, 2 * hidden), lambda i: (0, 0)),
        ),
        out_shape=(
            jax.ShapeDtypeStruct((EXPERTS * CAP, features), BF16),
            jax.ShapeDtypeStruct((half, 2 * hidden), BF16),
            jax.ShapeDtypeStruct((half, 2 * hidden), BF16),
        ),
        scratch_shapes=[
            pltpu.VMEM((features, 3 * hidden), BF16),
            pltpu.VMEM((GROUP * CAP, features), BF16),
            pltpu.VMEM((GROUP * CAP, features), BF16),
            pltpu.VMEM((features, 2 * hidden), F32),
            pltpu.SemaphoreType.DMA((2 * RING,)),
        ],
        compiler_params=pltpu.CompilerParams(vmem_limit_bytes=48 * 1024 * 1024),
        cost_estimate=pl.CostEstimate(
            flops=8 * EXPERTS * CAP * features * 2 * hidden,
            bytes_accessed=16 * 1024 * 1024,
            transcendentals=EXPERTS * CAP * hidden,
        ),
        name="expert_work",
    )(gathered, *pieces)


def combine_kernel(rank_ref, back_ref, out_ref):
    slots = back_ref.shape[0]
    lanes = rank_ref.shape[1]
    column = iota((lanes, slots), 1) - CAP * iota((lanes, slots), 0)
    spread = ((column >= 0) & (column < CAP)).astype(F32).astype(BF16)
    rank = jnp.dot(rank_ref[...], spread, preferred_element_type=F32)
    slot = iota((1, slots), 1)
    slot = (slot - CAP * ((slot * 3277) >> 18)).astype(F32)
    pick = jnp.where(rank == slot, 1.0, 0.0).astype(BF16)
    out_ref[...] = jnp.dot(pick, back_ref[...], preferred_element_type=F32).astype(BF16)


def combine(rank, back):
    return pl.pallas_call(
        combine_kernel,
        out_shape=jax.ShapeDtypeStruct((rank.shape[0], back.shape[1]), BF16),
        compiler_params=pltpu.CompilerParams(vmem_limit_bytes=32 * 1024 * 1024),
        name="combine_rows",
    )(rank, back)


def swap_halves(x):
    return lax.ppermute(x, "dp", [(d, (d + RING) % (2 * RING)) for d in range(2 * RING)])


def shift_ring(x, by):
    pairs = [(d, d // RING * RING + (d + by) % RING) for d in range(2 * RING)]
    return lax.ppermute(x, "dp", pairs)


def shift_near(x, by):
    pairs = [(d, d // NEAR * NEAR + (d + by) % NEAR) for d in range(2 * RING)]
    return lax.ppermute(x, "dp", pairs)


def gather_weights(gate_up, down):
    own = jnp.concatenate([gate_up[0], down[0]], axis=1)
    shard = own.shape[0]
    both = jnp.concatenate([own, swap_halves(own)], axis=0)
    pieces = [both]
    ahead = behind = both
    for _ in range(1, RING // 2):
        ahead = shift_ring(ahead, 1)
        behind = shift_ring(behind, -1)
        pieces += [ahead, behind]
    return pieces + [shift_ring(ahead[:shard], 1), shift_ring(behind[shard:], -1)]


def scatter_sum(mine, theirs, scale):
    shard = mine.shape[0] // RING
    place = lax.axis_index("dp") % RING
    near, far = place % NEAR, place // NEAR
    part = (mine.astype(F32) + swap_halves(theirs).astype(F32)).astype(BF16)
    part = part.reshape(RING // NEAR, NEAR, shard, -1)

    def column(k):
        return lax.dynamic_index_in_dim(part, k % NEAR, axis=1, keepdims=False)

    total = column(near).astype(F32)
    for by in range(1, NEAR):
        total += shift_near(column(near + by), by).astype(F32)
    part2 = total.astype(BF16)

    def row(k):
        return lax.dynamic_index_in_dim(part2, k % (RING // NEAR), axis=0, keepdims=False)

    total = row(far).astype(F32)
    for by in range(1, RING // NEAR):
        total += shift_ring(row(far + by), by * NEAR).astype(F32)
    return (total * scale)[None]


def shards(tokens, cotangent, route_experts, route_weights, gate_up, down):
    rows, features = tokens.shape
    hidden = down.shape[2]
    packed, rank = pack(tokens, cotangent, route_experts, route_weights)
    gathered = lax.all_gather(packed, "expert", axis=0, tiled=True)
    pieces = gather_weights(gate_up, down)
    row_grads, mine, theirs = expert_work(
        gathered,
        pieces,
        features,
        hidden,
        lambda: lax.axis_index("expert"),
        lambda: lax.axis_index("dp"),
    )
    returned = lax.all_to_all(
        row_grads.reshape(EXPERTS, CAP, features), "expert", split_axis=0, concat_axis=0, tiled=True
    )
    grad_scale = 1.0 / math.sqrt(rows * lax.axis_size("dp") * lax.axis_size("expert"))
    grad_gate_up = scatter_sum(mine, theirs, grad_scale)
    token_grad = combine(rank, returned.reshape(EXPERTS * CAP, features))
    return (token_grad, grad_gate_up)


def solution(mesh):
    in_specs = (
        P(("dp", "expert"), None),
        P(("dp", "expert"), None),
        P(("dp", "expert"), None),
        P(("dp", "expert"), None),
        P("expert", "dp", None),
        P("expert", "dp", None),
    )
    out_specs = (P(("dp", "expert"), None), P("expert", "dp", None))
    return jax.shard_map(shards, mesh=mesh, in_specs=in_specs, out_specs=out_specs, check_vma=False)
```

time: 536 us -> 247 us (0.46)
  the two profiles are of different devices: /device:TPU:6 before, /device:TPU:1 now
where the time goes in v1:
time: 247 us; the launch traced here: 245 us
  starting transfers between devices  110 us (45%)
  waiting for transfers between devices  67.1 us (27%)
  Pallas kernels  26.8 us (11%)
  local copies, waits for them, and re-layouts  21.5 us (9%)
  between operations  14.6 us (6%)
  other arithmetic  4.77 us (2%)
    ppermute x19, starting transfers between devices, shift_ring(): return lax.ppermute(x, 'dp', pairs)  78.1 us
    ppermute x2, waiting for transfers between devices, swap_halves(): lax.ppermute(x, 'dp', [(d, (d + RING) % (2 * RING)) for d in range(2 * RI...  46 us
    pallas_call x1, Pallas kernels, expert_work(): pl.pallas_call(functools.partial(expert_kernel, my_expert, my_dp, feature...  23.5 us
    unnamed x58, local copies, waits for them, and re-layouts  20.8 us
    all_to_all x1, starting transfers between devices, shards(): lax.all_to_all(row_grads.reshape(EXPERTS, CAP, features), 'expert', split...  13.8 us
    ppermute x3, waiting for transfers between devices, shift_near(): return lax.ppermute(x, 'dp', pairs)  13.2 us
    ppermute x2, starting transfers between devices, swap_halves(): lax.ppermute(x, 'dp', [(d, (d + RING) % (2 * RING)) for d in range(2 * RI...  10.2 us
    ppermute x19, waiting for transfers between devices, shift_ring(): return lax.ppermute(x, 'dp', pairs)  7.92 us
  transfers between devices with their start and end apart: 26, of which 10 were waited for; matrix products, arithmetic and copies ran while one was open for 2% of the time, Pallas kernels for 0%

profile of v1, /device:TPU:1, one launch (start us, length us, event | category | flops | bytes accessed | tf_op | source)
XLA Modules:
  0.0 244.6 jit_solution(17686804487966382108)
XLA Ops:
  7.2 2.0 pack_rows.1
  10.1 5.6 %collective-permute-start = (bf16[32,1152]{1,0:T(8,128)(2,1)S(1)}, bf16[32,1152]{1,0:T(8,128)(2,1)S(1)}, u32[]{:S(2)}, u32[]{:S(2)}) collective-permute-start(bf16[32,1152]{1,0:T(8,128)(2,1)S(1)} %pad_maximum_fusion.1), channel_id=1, source_target_pairs={{0,256},{16,272},{32,288},{48,304},{64,320},{80,336},{96,352},{112... | collective-permute-start | bytes 221192 | tf_op jit(solution)/shard_map/ppermute | solution.py:213
  18.3 3.6 %collective-permute-start.1 = (bf16[64,1152]{1,0:T(8,128)(2,1)S(1)}, bf16[64,1152]{1,0:T(8,128)(2,1)S(1)}, u32[]{:S(2)}, u32[]{:S(2)}) collective-permute-start(bf16[64,1152]{1,0:T(8,128)(2,1)S(1)} %pad_maximum_fusion.refs_0_), channel_id=1, source_target_pairs={{0,16},{16,32},{32,48},{48,64},{64,80},{80,96},{96,112},{112,128},... | collective-permute-start | bytes 442376 | tf_op jit(solution)/shard_map/ppermute | solution.py:218
  21.9 9.5 %collective-permute-start.2 = (bf16[64,1152]{1,0:T(8,128)(2,1)S(1)}, bf16[64,1152]{1,0:T(8,128)(2,1)S(1)}, u32[]{:S(2)}, u32[]{:S(2)}) collective-permute-start(bf16[64,1152]{1,0:T(8,128)(2,1)S(1)} %pad_maximum_fusion.refs_0_), channel_id=1, source_target_pairs={{0,240},{16,0},{32,16},{48,32},{64,48},{80,64},{96,80},{112,96},{1... | collective-permute-start | bytes 442376 | tf_op jit(solution)/shard_map/ppermute | solution.py:218
  34.5 4.6 %collective-permute-start.4 = (bf16[64,1152]{1,0:T(8,128)(2,1)S(1)}, bf16[64,1152]{1,0:T(8,128)(2,1)S(1)}, u32[]{:S(2)}, u32[]{:S(2)}) collective-permute-start(bf16[64,1152]{1,0:T(8,128)(2,1)S(1)} %collective-permute-done.2.refs_2_), channel_id=1, source_target_pairs={{0,240},{16,0},{32,16},{48,32},{64,48},{80,64},{96,80},{112,96},{1... | collective-permute-start | bytes 442376 | tf_op jit(solution)/shard_map/ppermute | solution.py:218
  41.7 4.6 %collective-permute-start.6 = (bf16[64,1152]{1,0:T(8,128)(2,1)S(1)}, bf16[64,1152]{1,0:T(8,128)(2,1)S(1)}, u32[]{:S(2)}, u32[]{:S(2)}) collective-permute-start(bf16[64,1152]{1,0:T(8,128)(2,1)S(1)} %collective-permute-done.4.refs_4_), channel_id=1, source_target_pairs={{0,240},{16,0},{32,16},{48,32},{64,48},{80,64},{96,80},{112,96},{1... | collective-permute-start | bytes 442376 | tf_op jit(solution)/shard_map/ppermute | solution.py:218
  49.5 4.6 %collective-permute-start.8 = (bf16[64,1152]{1,0:T(8,128)(2,1)S(1)}, bf16[64,1152]{1,0:T(8,128)(2,1)S(1)}, u32[]{:S(2)}, u32[]{:S(2)}) collective-permute-start(bf16[64,1152]{1,0:T(8,128)(2,1)S(1)} %collective-permute-done.6.refs_6_), channel_id=1, source_target_pairs={{0,240},{16,0},{32,16},{48,32},{64,48},{80,64},{96,80},{112,96},{1... | collective-permute-start | bytes 442376 | tf_op jit(solution)/shard_map/ppermute | solution.py:218
  57.3 4.6 %collective-permute-start.10 = (bf16[64,1152]{1,0:T(8,128)(2,1)S(1)}, bf16[64,1152]{1,0:T(8,128)(2,1)S(1)}, u32[]{:S(2)}, u32[]{:S(2)}) collective-permute-start(bf16[64,1152]{1,0:T(8,128)(2,1)S(1)} %collective-permute-done.8.refs_8_), channel_id=1, source_target_pairs={{0,240},{16,0},{32,16},{48,32},{64,48},{80,64},{96,80},{112,96},{1... | collective-permute-start | bytes 442376 | tf_op jit(solution)/shard_map/ppermute | solution.py:218
  65.1 4.6 %collective-permute-start.12 = (bf16[64,1152]{1,0:T(8,128)(2,1)S(1)}, bf16[64,1152]{1,0:T(8,128)(2,1)S(1)}, u32[]{:S(2)}, u32[]{:S(2)}) collective-permute-start(bf16[64,1152]{1,0:T(8,128)(2,1)S(1)} %collective-permute-done.10.refs_10_), channel_id=1, source_target_pairs={{0,240},{16,0},{32,16},{48,32},{64,48},{80,64},{96,80},{112,96},{1... | collective-permute-start | bytes 442376 | tf_op jit(solution)/shard_map/ppermute | solution.py:218
  72.9 4.6 %collective-permute-start.14 = (bf16[64,1152]{1,0:T(8,128)(2,1)S(1)}, bf16[64,1152]{1,0:T(8,128)(2,1)S(1)}, u32[]{:S(2)}, u32[]{:S(2)}) collective-permute-start(bf16[64,1152]{1,0:T(8,128)(2,1)S(1)} %collective-permute-done.12.refs_12_), channel_id=1, source_target_pairs={{0,240},{16,0},{32,16},{48,32},{64,48},{80,64},{96,80},{112,96},{1... | collective-permute-start | bytes 442376 | tf_op jit(solution)/shard_map/ppermute | solution.py:218
  78.1 1.9 collective-permute-start.15
  80.1 4.6 %collective-permute-start.16 = (bf16[32,1152]{1,0:T(8,128)(2,1)S(1)}, bf16[32,1152]{1,0:T(8,128)(2,1)S(1)}, u32[]{:S(2)}, u32[]{:S(2)}) collective-permute-start(bf16[32,1152]{1,0:T(8,128)(2,1)S(1)} %slice.9), channel_id=1, source_target_pairs={{0,240},{16,0},{32,16},{48,32},{64,48},{80,64},{96,80},{112,96},{1... | collective-permute-start | bytes 221192 | tf_op jit(solution)/shard_map/ppermute | solution.py:218
  99.1 23.5 %expert_work.1 = (bf16[1280,1024]{1,0:T(8,128)(2,1)}, bf16[512,768]{1,0:T(8,128)(2,1)S(1)}, bf16[512,768]{1,0:T(8,128)(2,1)S(1)}) custom-call(bf16[2048,2176]{1,0:T(8,128)(2,1)} %all-gather.2.cloned.1.call-done.g_ref, bf16[64,1152]{1,0:T(8,128)(2,1)S(1)} %pad_maximum_fusion.refs_0_, bf16[64,1152]{1,0:T(8,128)(2,1)S(1)} %copy-done.3, ...), custom_call_target="tpu_custom_call" | custom-call | flops 8053063680 | bytes 16777216 | tf_op jit(solution)/shard_map/expert_work/pallas_call | solution.py:159
  123.5 13.8 %all-to-all-start = ((bf16[16,80,1024]{2,1,0:T(8,128)(2,1)}), bf16[16,80,1024]{2,1,0:T(8,128)(2,1)S(1)}, u32[]{:S(2)}, u32[]{:S(2)}) async-start(bf16[16,80,1024]{2,1,0:T(8,128)(2,1)} %bitcast.32), calls=%async_computation | async-start | bytes 5242880 | tf_op jit(solution)/shard_map/all_to_all | solution.py:277
  137.3 4.6 %collective-permute-start.17 = (bf16[512,768]{1,0:T(8,128)(2,1)}, bf16[512,768]{1,0:T(8,128)(2,1)}, u32[]{:S(2)}, u32[]{:S(2)}) collective-permute-start(bf16[512,768]{1,0:T(8,128)(2,1)} %copy-done.1), channel_id=1, source_target_pairs={{0,256},{16,272},{32,288},{48,304},{64,320},{80,336},{96,352},{112... | collective-permute-start | bytes 2359304 | tf_op jit(solution)/shard_map/ppermute | solution.py:213
  141.9 44.3 %collective-permute-done.17 = bf16[512,768]{1,0:T(8,128)(2,1)} collective-permute-done((bf16[512,768]{1,0:T(8,128)(2,1)}, bf16[512,768]{1,0:T(8,128)(2,1)}, u32[]{:S(2)}, u32[]{:S(2)}) %collective-permute-start.17) | collective-permute-done | bytes 786464 | tf_op jit(solution)/shard_map/ppermute | solution.py:213
  189.1 3.6 %collective-permute-start.20 = (bf16[4,32,768]{2,1,0:T(8,128)(2,1)}, bf16[4,32,768]{2,1,0:T(8,128)(2,1)S(1)}, u32[]{:S(2)}, u32[]{:S(2)}) collective-permute-start(bf16[4,32,768]{2,1,0:T(8,128)(2,1)} %get-tuple-element.13), channel_id=1, source_target_pairs={{0,48},{16,0},{32,16},{48,32},{64,112},{80,64},{96,80},{112,96},{1... | collective-permute-start | bytes 589832 | tf_op jit(solution)/shard_map/ppermute | solution.py:223
  192.7 1.9 collective-permute-start.19
  194.7 2.2 collective-permute-start.18
  197.1 13.0 %collective-permute-done.19 = bf16[4,32,768]{2,1,0:T(8,128)(2,1)S(1)} collective-permute-done((bf16[4,32,768]{2,1,0:T(8,128)(2,1)S(1)}, bf16[4,32,768]{2,1,0:T(8,128)(2,1)S(1)}, u32[]{:S(2)}, u32[]{:S(2)}) %collective-permute-start.19) | collective-permute-done | bytes 196640 | tf_op jit(solution)/shard_map/ppermute | solution.py:223
  211.3 6.4 %collective-permute-start.23 = (bf16[32,768]{1,0:T(8,128)(2,1)S(1)}, bf16[32,768]{1,0:T(8,128)(2,1)S(1)}, u32[]{:S(2)}, u32[]{:S(2)}) collective-permute-start(bf16[32,768]{1,0:T(8,128)(2,1)S(1)} %get-tuple-element.16), channel_id=1, source_target_pairs={{0,192},{16,208},{32,224},{48,240},{64,0},{80,16},{96,32},{112,48}... | collective-permute-start | bytes 147464 | tf_op jit(solution)/shard_map/ppermute | solution.py:218
  217.7 9.3 %collective-permute-start.22 = (bf16[32,768]{1,0:T(8,128)(2,1)S(1)}, bf16[32,768]{1,0:T(8,128)(2,1)S(1)}, u32[]{:S(2)}, u32[]{:S(2)}) collective-permute-start(bf16[32,768]{1,0:T(8,128)(2,1)S(1)} %get-tuple-element.17), channel_id=1, source_target_pairs={{0,128},{16,144},{32,160},{48,176},{64,192},{80,208},{96,224},{112... | collective-permute-start | bytes 147464 | tf_op jit(solution)/shard_map/ppermute | solution.py:218
  227.0 4.0 %collective-permute-start.21 = (bf16[32,768]{1,0:T(8,128)(2,1)S(1)}, bf16[32,768]{1,0:T(8,128)(2,1)S(1)}, u32[]{:S(2)}, u32[]{:S(2)}) collective-permute-start(bf16[32,768]{1,0:T(8,128)(2,1)S(1)} %get-tuple-element.15), channel_id=1, source_target_pairs={{0,64},{16,80},{32,96},{48,112},{64,128},{80,144},{96,160},{112,17... | collective-permute-start | bytes 147464 | tf_op jit(solution)/shard_map/ppermute | solution.py:218
  231.3 4.5 %collective-permute-done.21 = bf16[32,768]{1,0:T(8,128)(2,1)S(1)} collective-permute-done((bf16[32,768]{1,0:T(8,128)(2,1)S(1)}, bf16[32,768]{1,0:T(8,128)(2,1)S(1)}, u32[]{:S(2)}, u32[]{:S(2)}) %collective-permute-start.21) | collective-permute-done | bytes 49184 | tf_op jit(solution)/shard_map/ppermute | solution.py:218
  (99 shorter events, 44.4 us)
Async XLA Ops:
  7.2 80.1 %all-gather.2.cloned.1.call-start = ((), (), s32[]{:S(2)}) async-start(), calls=%async_computation.1 | async-start | bytes 9469952 | tf_op jit(solution)/shard_map/all_gather | solution.py:267
  10.1 7.4 %collective-permute-start = (bf16[32,1152]{1,0:T(8,128)(2,1)S(1)}, bf16[32,1152]{1,0:T(8,128)(2,1)S(1)}, u32[]{:S(2)}, u32[]{:S(2)}) collective-permute-start(bf16[32,1152]{1,0:T(8,128)(2,1)S(1)} %pad_maximum_fusion.1), channel_id=1, source_target_pairs={{0,256},{16,272},{32,288},{48,304},{64,320},{80,336},{96,352},{112... | collective-permute-start | bytes 221192 | tf_op jit(solution)/shard_map/ppermute | solution.py:213
  18.3 13.7 %collective-permute-start.1 = (bf16[64,1152]{1,0:T(8,128)(2,1)S(1)}, bf16[64,1152]{1,0:T(8,128)(2,1)S(1)}, u32[]{:S(2)}, u32[]{:S(2)}) collective-permute-start(bf16[64,1152]{1,0:T(8,128)(2,1)S(1)} %pad_maximum_fusion.refs_0_), channel_id=1, source_target_pairs={{0,16},{16,32},{32,48},{48,64},{64,80},{80,96},{96,112},{112,128},... | collective-permute-start | bytes 442376 | tf_op jit(solution)/shard_map/ppermute | solution.py:218
  21.9 12.7 %collective-permute-start.2 = (bf16[64,1152]{1,0:T(8,128)(2,1)S(1)}, bf16[64,1152]{1,0:T(8,128)(2,1)S(1)}, u32[]{:S(2)}, u32[]{:S(2)}) collective-permute-start(bf16[64,1152]{1,0:T(8,128)(2,1)S(1)} %pad_maximum_fusion.refs_0_), channel_id=1, source_target_pairs={{0,240},{16,0},{32,16},{48,32},{64,48},{80,64},{96,80},{112,96},{1... | collective-permute-start | bytes 442376 | tf_op jit(solution)/shard_map/ppermute | solution.py:218
  32.0 7.8 %collective-permute-start.3 = (bf16[64,1152]{1,0:T(8,128)(2,1)S(1)}, bf16[64,1152]{1,0:T(8,128)(2,1)S(1)}, u32[]{:S(2)}, u32[]{:S(2)}) collective-permute-start(bf16[64,1152]{1,0:T(8,128)(2,1)S(1)} %collective-permute-done.1.refs_1_), channel_id=1, source_target_pairs={{0,16},{16,32},{32,48},{48,64},{64,80},{80,96},{96,112},{112,128},... | collective-permute-start | bytes 442376 | tf_op jit(solution)/shard_map/ppermute | solution.py:218
  34.5 7.2 %collective-permute-start.4 = (bf16[64,1152]{1,0:T(8,128)(2,1)S(1)}, bf16[64,1152]{1,0:T(8,128)(2,1)S(1)}, u32[]{:S(2)}, u32[]{:S(2)}) collective-permute-start(bf16[64,1152]{1,0:T(8,128)(2,1)S(1)} %collective-permute-done.2.refs_2_), channel_id=1, source_target_pairs={{0,240},{16,0},{32,16},{48,32},{64,48},{80,64},{96,80},{112,96},{1... | collective-permute-start | bytes 442376 | tf_op jit(solution)/shard_map/ppermute | solution.py:218
  39.8 7.1 %collective-permute-start.5 = (bf16[64,1152]{1,0:T(8,128)(2,1)S(1)}, bf16[64,1152]{1,0:T(8,128)(2,1)S(1)}, u32[]{:S(2)}, u32[]{:S(2)}) collective-permute-start(bf16[64,1152]{1,0:T(8,128)(2,1)S(1)} %collective-permute-done.3.refs_3_), channel_id=1, source_target_pairs={{0,16},{16,32},{32,48},{48,64},{64,80},{80,96},{96,112},{112,128},... | collective-permute-start | bytes 442376 | tf_op jit(solution)/shard_map/ppermute | solution.py:218
  41.7 7.7 %collective-permute-start.6 = (bf16[64,1152]{1,0:T(8,128)(2,1)S(1)}, bf16[64,1152]{1,0:T(8,128)(2,1)S(1)}, u32[]{:S(2)}, u32[]{:S(2)}) collective-permute-start(bf16[64,1152]{1,0:T(8,128)(2,1)S(1)} %collective-permute-done.4.refs_4_), channel_id=1, source_target_pairs={{0,240},{16,0},{32,16},{48,32},{64,48},{80,64},{96,80},{112,96},{1... | collective-permute-start | bytes 442376 | tf_op jit(solution)/shard_map/ppermute | solution.py:218
  46.9 7.8 %collective-permute-start.7 = (bf16[64,1152]{1,0:T(8,128)(2,1)S(1)}, bf16[64,1152]{1,0:T(8,128)(2,1)S(1)}, u32[]{:S(2)}, u32[]{:S(2)}) collective-permute-start(bf16[64,1152]{1,0:T(8,128)(2,1)S(1)} %collective-permute-done.5.refs_5_), channel_id=1, source_target_pairs={{0,16},{16,32},{32,48},{48,64},{64,80},{80,96},{96,112},{112,128},... | collective-permute-start | bytes 442376 | tf_op jit(solution)/shard_map/ppermute | solution.py:218
  49.5 7.8 %collective-permute-start.8 = (bf16[64,1152]{1,0:T(8,128)(2,1)S(1)}, bf16[64,1152]{1,0:T(8,128)(2,1)S(1)}, u32[]{:S(2)}, u32[]{:S(2)}) collective-permute-start(bf16[64,1152]{1,0:T(8,128)(2,1)S(1)} %collective-permute-done.6.refs_6_), channel_id=1, source_target_pairs={{0,240},{16,0},{32,16},{48,32},{64,48},{80,64},{96,80},{112,96},{1... | collective-permute-start | bytes 442376 | tf_op jit(solution)/shard_map/ppermute | solution.py:218
  54.7 7.8 %collective-permute-start.9 = (bf16[64,1152]{1,0:T(8,128)(2,1)S(1)}, bf16[64,1152]{1,0:T(8,128)(2,1)S(1)}, u32[]{:S(2)}, u32[]{:S(2)}) collective-permute-start(bf16[64,1152]{1,0:T(8,128)(2,1)S(1)} %collective-permute-done.7.refs_7_), channel_id=1, source_target_pairs={{0,16},{16,32},{32,48},{48,64},{64,80},{80,96},{96,112},{112,128},... | collective-permute-start | bytes 442376 | tf_op jit(solution)/shard_map/ppermute | solution.py:218
  57.3 7.8 %collective-permute-start.10 = (bf16[64,1152]{1,0:T(8,128)(2,1)S(1)}, bf16[64,1152]{1,0:T(8,128)(2,1)S(1)}, u32[]{:S(2)}, u32[]{:S(2)}) collective-permute-start(bf16[64,1152]{1,0:T(8,128)(2,1)S(1)} %collective-permute-done.8.refs_8_), channel_id=1, source_target_pairs={{0,240},{16,0},{32,16},{48,32},{64,48},{80,64},{96,80},{112,96},{1... | collective-permute-start | bytes 442376 | tf_op jit(solution)/shard_map/ppermute | solution.py:218
  62.5 7.8 %collective-permute-start.11 = (bf16[64,1152]{1,0:T(8,128)(2,1)S(1)}, bf16[64,1152]{1,0:T(8,128)(2,1)S(1)}, u32[]{:S(2)}, u32[]{:S(2)}) collective-permute-start(bf16[64,1152]{1,0:T(8,128)(2,1)S(1)} %collective-permute-done.9.refs_9_), channel_id=1, source_target_pairs={{0,16},{16,32},{32,48},{48,64},{64,80},{80,96},{96,112},{112,128},... | collective-permute-start | bytes 442376 | tf_op jit(solution)/shard_map/ppermute | solution.py:218
  65.1 7.8 %collective-permute-start.12 = (bf16[64,1152]{1,0:T(8,128)(2,1)S(1)}, bf16[64,1152]{1,0:T(8,128)(2,1)S(1)}, u32[]{:S(2)}, u32[]{:S(2)}) collective-permute-start(bf16[64,1152]{1,0:T(8,128)(2,1)S(1)} %collective-permute-done.10.refs_10_), channel_id=1, source_target_pairs={{0,240},{16,0},{32,16},{48,32},{64,48},{80,64},{96,80},{112,96},{1... | collective-permute-start | bytes 442376 | tf_op jit(solution)/shard_map/ppermute | solution.py:218
  70.3 7.8 %collective-permute-start.13 = (bf16[64,1152]{1,0:T(8,128)(2,1)S(1)}, bf16[64,1152]{1,0:T(8,128)(2,1)S(1)}, u32[]{:S(2)}, u32[]{:S(2)}) collective-permute-start(bf16[64,1152]{1,0:T(8,128)(2,1)S(1)} %collective-permute-done.11.refs_11_), channel_id=1, source_target_pairs={{0,16},{16,32},{32,48},{48,64},{64,80},{80,96},{96,112},{112,128},... | collective-permute-start | bytes 442376 | tf_op jit(solution)/shard_map/ppermute | solution.py:218
  72.9 7.2 %collective-permute-start.14 = (bf16[64,1152]{1,0:T(8,128)(2,1)S(1)}, bf16[64,1152]{1,0:T(8,128)(2,1)S(1)}, u32[]{:S(2)}, u32[]{:S(2)}) collective-permute-start(bf16[64,1152]{1,0:T(8,128)(2,1)S(1)} %collective-permute-done.12.refs_12_), channel_id=1, source_target_pairs={{0,240},{16,0},{32,16},{48,32},{64,48},{80,64},{96,80},{112,96},{1... | collective-permute-start | bytes 442376 | tf_op jit(solution)/shard_map/ppermute | solution.py:218
  123.5 113.0 %all-to-all-start = ((bf16[16,80,1024]{2,1,0:T(8,128)(2,1)}), bf16[16,80,1024]{2,1,0:T(8,128)(2,1)S(1)}, u32[]{:S(2)}, u32[]{:S(2)}) async-start(bf16[16,80,1024]{2,1,0:T(8,128)(2,1)} %bitcast.32), calls=%async_computation | async-start | bytes 5242880 | tf_op jit(solution)/shard_map/all_to_all | solution.py:277
  137.3 48.9 %collective-permute-start.17 = (bf16[512,768]{1,0:T(8,128)(2,1)}, bf16[512,768]{1,0:T(8,128)(2,1)}, u32[]{:S(2)}, u32[]{:S(2)}) collective-permute-start(bf16[512,768]{1,0:T(8,128)(2,1)} %copy-done.1), channel_id=1, source_target_pairs={{0,256},{16,272},{32,288},{48,304},{64,320},{80,336},{96,352},{112... | collective-permute-start | bytes 2359304 | tf_op jit(solution)/shard_map/ppermute | solution.py:213
  189.1 8.0 %collective-permute-start.20 = (bf16[4,32,768]{2,1,0:T(8,128)(2,1)}, bf16[4,32,768]{2,1,0:T(8,128)(2,1)S(1)}, u32[]{:S(2)}, u32[]{:S(2)}) collective-permute-start(bf16[4,32,768]{2,1,0:T(8,128)(2,1)} %get-tuple-element.13), channel_id=1, source_target_pairs={{0,48},{16,0},{32,16},{48,32},{64,112},{80,64},{96,80},{112,96},{1... | collective-permute-start | bytes 589832 | tf_op jit(solution)/shard_map/ppermute | solution.py:223
  192.7 17.4 %collective-permute-start.19 = (bf16[4,32,768]{2,1,0:T(8,128)(2,1)S(1)}, bf16[4,32,768]{2,1,0:T(8,128)(2,1)S(1)}, u32[]{:S(2)}, u32[]{:S(2)}) collective-permute-start(bf16[4,32,768]{2,1,0:T(8,128)(2,1)S(1)} %get-tuple-element.14), channel_id=1, source_target_pairs={{0,32},{16,48},{32,0},{48,16},{64,96},{80,112},{96,64},{112,80},{1... | collective-permute-start | bytes 589832 | tf_op jit(solution)/shard_map/ppermute | solution.py:223
  194.7 15.5 %collective-permute-start.18 = (bf16[4,32,768]{2,1,0:T(8,128)(2,1)S(1)}, bf16[4,32,768]{2,1,0:T(8,128)(2,1)}, u32[]{:S(2)}, u32[]{:S(2)}) collective-permute-start(bf16[4,32,768]{2,1,0:T(8,128)(2,1)S(1)} %get-tuple-element.12), channel_id=1, source_target_pairs={{0,16},{16,32},{32,48},{48,0},{64,80},{80,96},{96,112},{112,64},{1... | collective-permute-start | bytes 589832 | tf_op jit(solution)/shard_map/ppermute | solution.py:223
  211.3 19.7 %collective-permute-start.23 = (bf16[32,768]{1,0:T(8,128)(2,1)S(1)}, bf16[32,768]{1,0:T(8,128)(2,1)S(1)}, u32[]{:S(2)}, u32[]{:S(2)}) collective-permute-start(bf16[32,768]{1,0:T(8,128)(2,1)S(1)} %get-tuple-element.16), channel_id=1, source_target_pairs={{0,192},{16,208},{32,224},{48,240},{64,0},{80,16},{96,32},{112,48}... | collective-permute-start | bytes 147464 | tf_op jit(solution)/shard_map/ppermute | solution.py:218
  217.7 13.6 %collective-permute-start.22 = (bf16[32,768]{1,0:T(8,128)(2,1)S(1)}, bf16[32,768]{1,0:T(8,128)(2,1)S(1)}, u32[]{:S(2)}, u32[]{:S(2)}) collective-permute-start(bf16[32,768]{1,0:T(8,128)(2,1)S(1)} %get-tuple-element.17), channel_id=1, source_target_pairs={{0,128},{16,144},{32,160},{48,176},{64,192},{80,208},{96,224},{112... | collective-permute-start | bytes 147464 | tf_op jit(solution)/shard_map/ppermute | solution.py:218
  227.0 8.8 %collective-permute-start.21 = (bf16[32,768]{1,0:T(8,128)(2,1)S(1)}, bf16[32,768]{1,0:T(8,128)(2,1)S(1)}, u32[]{:S(2)}, u32[]{:S(2)}) collective-permute-start(bf16[32,768]{1,0:T(8,128)(2,1)S(1)} %get-tuple-element.15), channel_id=1, source_target_pairs={{0,64},{16,80},{32,96},{48,112},{64,128},{80,144},{96,160},{112,17... | collective-permute-start | bytes 147464 | tf_op jit(solution)/shard_map/ppermute | solution.py:218
  (31 other events, 176.1 us)
Sparse Core Ops, SparseCore 0:
  10.1 67.9 all-gather.1

commit v2 on v0

v2 whole, which is shorter than its diff:
```python
import functools
import math

import jax
import jax.numpy as jnp
from jax import lax
from jax.experimental import pallas as pl
from jax.experimental.pallas import tpu as pltpu
from jax.sharding import PartitionSpec as P

EXPERTS = 16
CAP = 80
LANES = 128
RING = 16
NEAR = 4
PAIR = 2
BLOCKS = 4
UNROUTED = 200.0
BF16 = jnp.bfloat16
F32 = jnp.float32


def iota(shape, dim):
    return lax.broadcasted_iota(jnp.int32, shape, dim)


def as_bf16(mask):
    return jnp.where(mask, 1.0, 0.0).astype(BF16)


def pack_kernel(tok_ref, cot_ref, experts_ref, weights_ref, packed_ref, rank_ref):
    rows, features = tok_ref.shape
    packed_ref[:, :features] = tok_ref[...]
    packed_ref[:, features : 2 * features] = cot_ref[...]
    label = iota((EXPERTS, rows), 0)
    dense = jnp.zeros((EXPERTS, rows), F32)
    for k in range(experts_ref.shape[0]):
        dense += jnp.where(experts_ref[k : k + 1, :] == label, weights_ref[k : k + 1, :], 0.0)
    routed = dense > 0.0
    before = as_bf16(iota((rows, rows), 0) < iota((rows, rows), 1))
    rank = jnp.dot(as_bf16(routed), before, preferred_element_type=F32)
    rank = jnp.where(routed, rank, UNROUTED).astype(BF16)
    high = dense.astype(BF16)
    low = (dense - high.astype(F32)).astype(BF16)
    rest = jnp.zeros((rows - 3 * EXPERTS, rows), BF16)
    packed_ref[:, 2 * features :] = jnp.concatenate([high, low, rank, rest], axis=0)
    rank_ref[...] = rank


def pack(tokens, cotangent, route_experts, route_weights):
    rows, features = tokens.shape
    return pl.pallas_call(
        pack_kernel,
        out_shape=(
            jax.ShapeDtypeStruct((rows, 2 * features + rows), BF16),
            jax.ShapeDtypeStruct((EXPERTS, rows), BF16),
        ),
        name="pack_rows",
    )(tokens, cotangent, route_experts.T, route_weights.T)


def expert_kernel(my_expert, my_dp, plan, features, hidden, g_ref, *refs):
    piece_total = 5
    pieces = refs[:piece_total]
    pre_ref, gate_up_ref, plus_ref, minus_ref, keep_ref = refs[piece_total : piece_total + 5]
    blocks, weights, inputs, cots, total, block_sems, sems = refs[piece_total + 5 :]
    expert = my_expert()
    dp = my_dp()
    upper = dp // RING
    place = dp % RING
    half = features // 2
    shard = half // RING
    pair_total = blocks.shape[0]
    pair_rows = blocks.shape[1]
    rows = pair_rows // PAIR

    def block_copy(p):
        return pltpu.make_async_copy(
            g_ref.at[pl.ds(p * pair_rows, pair_rows), :], blocks.at[p], block_sems.at[p]
        )

    def first_row(owner, offset):
        return pl.multiple_of(owner * half + ((place + offset + RING) % RING) * shard, shard)

    weight_copies = []
    for array, source, offset in plan:
        for part, owner in ((0, upper), (1, 1 - upper)):
            weight_copies.append(
                pltpu.make_async_copy(
                    pieces[array].at[pl.ds(source + part * shard, shard), :],
                    weights.at[pl.ds(first_row(owner, offset), shard), :],
                    sems.at[len(weight_copies)],
                )
            )
    block_copies = [block_copy(p) for p in range(pair_total)]
    for copy in block_copies[:2] + weight_copies + block_copies[2:]:
        copy.start()

    slot = iota((PAIR * CAP, pair_rows), 0).astype(F32)
    label = iota((3 * EXPERTS, rows), 0)

    def compact(p):
        block_copies[p].wait()
        ranks, scales = [], []
        for s in range(PAIR):
            table = blocks[p, s * rows : s * rows + 3 * EXPERTS, 2 * features :].astype(F32)

            def line(k):
                return jnp.sum(
                    jnp.where(label == expert + k * EXPERTS, table, 0.0), axis=0, keepdims=True
                )

            scales.append(line(0) + line(1))
            ranks.append(line(2) + float(s * CAP))
        hit = slot == jnp.concatenate(ranks, axis=1)
        scale = jnp.sum(
            jnp.where(hit, jnp.concatenate(scales, axis=1), 0.0), axis=1, keepdims=True
        )
        pick = as_bf16(hit)
        here = pl.ds(p * PAIR * CAP, PAIR * CAP)
        inputs[here, :] = jnp.dot(
            pick, blocks[p, :, :features], preferred_element_type=F32
        ).astype(BF16)
        cots[here, :] = (
            scale
            * jnp.dot(pick, blocks[p, :, features : 2 * features], preferred_element_type=F32)
        ).astype(BF16)

    block_rows = inputs.shape[0] // BLOCKS
    for m in range(BLOCKS):
        for p in range(m * pair_total // BLOCKS, (m + 1) * pair_total // BLOCKS):
            compact(p)
        if m == 0:
            for copy in weight_copies:
                copy.wait()
            gate_up_ref[...] = weights[:, : 2 * hidden]
        here = pl.ds(m * block_rows, block_rows)
        projected = jnp.dot(inputs[here, :], weights[:, : 2 * hidden], preferred_element_type=F32)
        hidden_grad = jnp.dot(cots[here, :], weights[:, 2 * hidden :], preferred_element_type=F32)
        gate_part = projected[:, :hidden]
        up_part = projected[:, hidden:]
        sigmoid_gate = jax.nn.sigmoid(gate_part)
        grad_gate = hidden_grad * up_part * sigmoid_gate * (1.0 + gate_part * (1.0 - sigmoid_gate))
        grad_up = hidden_grad * gate_part * sigmoid_gate
        pre_ref[here, :hidden] = grad_gate.astype(BF16)
        pre_ref[here, hidden:] = grad_up.astype(BF16)

    strip = features // BLOCKS
    for c in range(BLOCKS):
        total[c * strip : (c + 1) * strip, :] = lax.dot_general(
            inputs[:, c * strip : (c + 1) * strip],
            pre_ref[...],
            (((0,), (0,)), ((), ())),
            preferred_element_type=F32,
        )

    def put(ref, index, offset):
        for owner in range(2):
            ref[index, owner * shard : (owner + 1) * shard, :] = total[
                pl.ds(first_row(owner, offset), shard), :
            ].astype(BF16)

    for j in range(RING // 4):
        put(plus_ref, j, 2 * j + 1)
        put(minus_ref, j, -(2 * j + 1))
    for j in range(RING // 2):
        put(keep_ref, j, 2 * j)


def expert_work(gathered, pieces, plan, features, hidden, my_expert, my_dp):
    rows = gathered.shape[0] // EXPERTS
    slots = EXPERTS * CAP
    shard = features // (2 * RING)
    hbm = pl.BlockSpec(memory_space=pltpu.HBM)
    return pl.pallas_call(
        functools.partial(expert_kernel, my_expert, my_dp, plan, features, hidden),
        in_specs=[hbm] * (1 + len(pieces)),
        out_shape=(
            jax.ShapeDtypeStruct((slots, 2 * hidden), BF16),
            jax.ShapeDtypeStruct((features, 2 * hidden), BF16),
            jax.ShapeDtypeStruct((RING // 4, 2 * shard, 2 * hidden), BF16),
            jax.ShapeDtypeStruct((RING // 4, 2 * shard, 2 * hidden), BF16),
            jax.ShapeDtypeStruct((RING // 2, 2 * shard, 2 * hidden), BF16),
        ),
        scratch_shapes=[
            pltpu.VMEM((EXPERTS // PAIR, PAIR * rows, gathered.shape[1]), BF16),
            pltpu.VMEM((features, 3 * hidden), BF16),
            pltpu.VMEM((slots, features), BF16),
            pltpu.VMEM((slots, features), BF16),
            pltpu.VMEM((features, 2 * hidden), F32),
            pltpu.SemaphoreType.DMA((EXPERTS // PAIR,)),
            pltpu.SemaphoreType.DMA((2 * RING,)),
        ],
        compiler_params=pltpu.CompilerParams(vmem_limit_bytes=48 * 1024 * 1024),
        cost_estimate=pl.CostEstimate(
            flops=5 * slots * features * 2 * hidden,
            bytes_accessed=16 * 1024 * 1024,
            transcendentals=slots * hidden,
        ),
        name="expert_work",
    )(gathered, *pieces)


def row_kernel(pre_ref, gate_up_ref, out_ref):
    out_ref[...] = lax.dot_general(
        pre_ref[...], gate_up_ref[...], (((1,), (1,)), ((), ())), preferred_element_type=F32
    ).astype(BF16)


def row_gradients(pre_grad, gate_up):
    slots, columns = pre_grad.shape
    features = gate_up.shape[0]
    block = slots // BLOCKS
    return pl.pallas_call(
        row_kernel,
        grid=(BLOCKS,),
        in_specs=[
            pl.BlockSpec((block, columns), lambda i: (i, 0)),
            pl.BlockSpec((features, columns), lambda i: (0, 0)),
        ],
        out_specs=pl.BlockSpec((block, features), lambda i: (i, 0)),
        out_shape=jax.ShapeDtypeStruct((slots, features), BF16),
        compiler_params=pltpu.CompilerParams(vmem_limit_bytes=32 * 1024 * 1024),
        cost_estimate=pl.CostEstimate(
            flops=2 * slots * features * columns,
            bytes_accessed=6 * 1024 * 1024,
            transcendentals=0,
        ),
        name="row_gradients",
    )(pre_grad, gate_up)


def combine_kernel(rank_ref, back_ref, out_ref):
    slots = back_ref.shape[0]
    column = iota((EXPERTS, slots), 1) - CAP * iota((EXPERTS, slots), 0)
    spread = as_bf16((column >= 0) & (column < CAP))
    rank = lax.dot_general(
        rank_ref[...], spread, (((0,), (0,)), ((), ())), preferred_element_type=F32
    )
    slot = iota((1, slots), 1)
    slot = (slot - CAP * ((slot * 3277) >> 18)).astype(F32)
    out_ref[...] = jnp.dot(
        as_bf16(rank == slot), back_ref[...], preferred_element_type=F32
    ).astype(BF16)


def combine(rank, back):
    return pl.pallas_call(
        combine_kernel,
        out_shape=jax.ShapeDtypeStruct((rank.shape[1], back.shape[1]), BF16),
        compiler_params=pltpu.CompilerParams(vmem_limit_bytes=32 * 1024 * 1024),
        name="combine_rows",
    )(rank, back)


def swap_halves(x):
    return lax.ppermute(x, "dp", [(d, (d + RING) % (2 * RING)) for d in range(2 * RING)])


def shift_ring(x, by):
    pairs = [(d, d // RING * RING + (d + by) % RING) for d in range(2 * RING)]
    return lax.ppermute(x, "dp", pairs)


def gather_weights(gate_up, down):
    own = jnp.concatenate([gate_up[0], down[0]], axis=1)
    both = jnp.concatenate([own, swap_halves(own)], axis=0)
    unit = both.shape[0]
    up4, down4, far = shift_ring(both, -4), shift_ring(both, 4), shift_ring(both, 8)
    ahead = jnp.concatenate([both, up4], axis=0)
    behind = jnp.concatenate([both, down4], axis=0)
    ahead = jnp.concatenate([ahead, shift_ring(ahead, -2)], axis=0)
    behind = jnp.concatenate([behind, shift_ring(behind, 2)], axis=0)
    odd_ahead, odd_behind = shift_ring(ahead, -1), shift_ring(behind, 1)
    pieces = [ahead, behind, far, odd_ahead, odd_behind]
    held = [[0, 4, 2, 6], [None, -4, -2, -6], [8], [1, 5, 3, 7], [-1, -5, -3, -7]]
    plan = [
        (array, unit * k, offset)
        for array, offsets in enumerate(held)
        for k, offset in enumerate(offsets)
        if offset is not None
    ]
    return pieces, plan


def first_sum_kernel(keep_ref, plus_ref, minus_ref, up_ref, down_ref, rest_ref):
    def part(k):
        value = keep_ref[k].astype(F32)
        if k < 4:
            value += plus_ref[k].astype(F32)
        if k % 8 == 0 or k > 4:
            value += minus_ref[(8 - k) % 8].astype(F32)
        return value.astype(BF16)

    up_ref[0], up_ref[1] = part(1), part(3)
    down_ref[0], down_ref[1] = part(7), part(5)
    for j in range(4):
        rest_ref[j] = part(2 * j)


def second_sum_kernel(my_dp, rest_ref, up_ref, down_ref, out_ref):
    shard = out_ref.shape[1]
    far = (my_dp() % RING) // NEAR
    groups = RING // NEAR
    for j in range(groups):
        value = rest_ref[j].astype(F32)
        if j < 2:
            value += up_ref[j].astype(F32)
        if j == 0 or j == 3:
            value += down_ref[(4 - j) % 4].astype(F32)
        value = value.astype(BF16)
        target = (far + j) % groups
        out_ref[target] = value[:shard]
        out_ref[groups + target] = value[shard:]


def scatter_sum(plus, minus, keep, scale, my_dp):
    unit, columns = keep.shape[1:]
    got_plus, got_minus = shift_ring(plus, 1), shift_ring(minus, -1)
    piece = jax.ShapeDtypeStruct((2, unit, columns), BF16)
    up, down, rest = pl.pallas_call(
        first_sum_kernel,
        out_shape=(piece, piece, jax.ShapeDtypeStruct((4, unit, columns), BF16)),
        name="first_sum",
    )(keep, got_plus, got_minus)
    got_up, got_down = shift_ring(up, 2), shift_ring(down, -2)
    parts = pl.pallas_call(
        functools.partial(second_sum_kernel, my_dp),
        out_shape=jax.ShapeDtypeStruct((2 * RING // NEAR, unit // 2, columns), BF16),
        name="second_sum",
    )(rest, got_up, got_down)
    groups = [
        [y * RING + far * NEAR + near for y in range(2) for far in range(RING // NEAR)]
        for near in range(NEAR)
    ]
    parts = lax.all_to_all(
        parts, "dp", split_axis=0, concat_axis=0, axis_index_groups=groups, tiled=True
    )
    return jnp.sum(parts.astype(F32), axis=0, keepdims=True) * scale


def shards(tokens, cotangent, route_experts, route_weights, gate_up, down):
    rows, features = tokens.shape
    hidden = down.shape[2]
    packed, rank = pack(tokens, cotangent, route_experts, route_weights)
    gathered = lax.all_gather(packed, "expert", axis=0, tiled=True)
    pieces, plan = gather_weights(gate_up, down)

    def my_dp():
        return lax.axis_index("dp")

    pre_grad, full_gate_up, plus, minus, keep = expert_work(
        gathered, pieces, plan, features, hidden, lambda: lax.axis_index("expert"), my_dp
    )
    row_grads = row_gradients(pre_grad, full_gate_up)
    returned = lax.all_to_all(
        row_grads.reshape(EXPERTS, CAP, features), "expert", split_axis=0, concat_axis=0, tiled=True
    )
    grad_scale = 1.0 / math.sqrt(rows * lax.axis_size("dp") * lax.axis_size("expert"))
    grad_gate_up = scatter_sum(plus, minus, keep, grad_scale, my_dp)
    token_grad = combine(rank, returned.reshape(EXPERTS * CAP, features))
    return (token_grad, grad_gate_up)


def solution(mesh):
    in_specs = (
        P(("dp", "expert"), None),
        P(("dp", "expert"), None),
        P(("dp", "expert"), None),
        P(("dp", "expert"), None),
        P("expert", "dp", None),
        P("expert", "dp", None),
    )
    out_specs = (P(("dp", "expert"), None), P("expert", "dp", None))
    return jax.shard_map(shards, mesh=mesh, in_specs=in_specs, out_specs=out_specs, check_vma=False)
```

time: 536 us -> 233 us (0.43)
  the two profiles are of different devices: /device:TPU:6 before, /device:TPU:1 now
where the time goes in v2:
time: 233 us; the launch traced here: 230 us
  waiting for transfers between devices  102 us (44%)
  starting transfers between devices  81.3 us (35%)
  Pallas kernels  25.6 us (11%)
  between operations  14.2 us (6%)
  local copies, waits for them, and re-layouts  4.36 us (2%)
  other arithmetic  2.68 us (1%)
    ppermute x11, waiting for transfers between devices, shift_ring(): return lax.ppermute(x, 'dp', pairs)  56.4 us
    ppermute x11, starting transfers between devices, shift_ring(): return lax.ppermute(x, 'dp', pairs)  52.6 us
    all_to_all x1, waiting for transfers between devices, shards(): lax.all_to_all(row_grads.reshape(EXPERTS, CAP, features), 'expert', split...  33.2 us
    all_to_all x1, starting transfers between devices, shards(): lax.all_to_all(row_grads.reshape(EXPERTS, CAP, features), 'expert', split...  16.2 us
    pallas_call x1, Pallas kernels, expert_work(): pl.pallas_call(functools.partial(expert_kernel, my_expert, my_dp, plan, f...  15 us
    all_to_all x1, waiting for transfers between devices, scatter_sum(): lax.all_to_all(parts, 'dp', split_axis=0, concat_axis=0, axis_index_group...  10.8 us
    all_to_all x1, starting transfers between devices, scatter_sum(): lax.all_to_all(parts, 'dp', split_axis=0, concat_axis=0, axis_index_group...  6.76 us
    ppermute x1, starting transfers between devices, swap_halves(): lax.ppermute(x, 'dp', [(d, (d + RING) % (2 * RING)) for d in range(2 * RI...  5.64 us
  transfers between devices with their start and end apart: 15, of which 12 were waited for; matrix products, arithmetic and copies ran while one was open for 1% of the time, Pallas kernels for 1%

profile of v2, /device:TPU:1, one launch (start us, length us, event | category | flops | bytes accessed | tf_op | source)
XLA Modules:
  0.0 230.3 jit_solution(4049130778122808049)
XLA Ops:
  7.2 2.0 pack_rows.1
  10.1 5.6 %collective-permute-start = (bf16[32,1152]{1,0:T(8,128)(2,1)S(1)}, bf16[32,1152]{1,0:T(8,128)(2,1)S(1)}, u32[]{:S(2)}, u32[]{:S(2)}) collective-permute-start(bf16[32,1152]{1,0:T(8,128)(2,1)S(1)} %pad_maximum_fusion.7), channel_id=1, source_target_pairs={{0,256},{16,272},{32,288},{48,304},{64,320},{80,336},{96,352},{112... | collective-permute-start | bytes 221192 | tf_op jit(solution)/shard_map/ppermute | solution.py:257
  17.5 8.9 %collective-permute-start.3 = (bf16[64,1152]{1,0:T(8,128)(2,1)S(1)}, bf16[64,1152]{1,0:T(8,128)(2,1)S(1)}, u32[]{:S(2)}, u32[]{:S(2)}) collective-permute-start(bf16[64,1152]{1,0:T(8,128)(2,1)S(1)} %pad_maximum_fusion.6), channel_id=1, source_target_pairs={{0,64},{16,80},{32,96},{48,112},{64,128},{80,144},{96,160},{112,17... | collective-permute-start | bytes 442376 | tf_op jit(solution)/shard_map/ppermute | solution.py:262
  26.3 5.6 %collective-permute-start.1 = (bf16[64,1152]{1,0:T(8,128)(2,1)S(1)}, bf16[64,1152]{1,0:T(8,128)(2,1)S(1)}, u32[]{:S(2)}, u32[]{:S(2)}) collective-permute-start(bf16[64,1152]{1,0:T(8,128)(2,1)S(1)} %pad_maximum_fusion.6), channel_id=1, source_target_pairs={{0,192},{16,208},{32,224},{48,240},{64,0},{80,16},{96,32},{112,48}... | collective-permute-start | bytes 442376 | tf_op jit(solution)/shard_map/ppermute | solution.py:262
  32.8 15.7 %collective-permute-done.1 = bf16[64,1152]{1,0:T(8,128)(2,1)S(1)} collective-permute-done((bf16[64,1152]{1,0:T(8,128)(2,1)S(1)}, bf16[64,1152]{1,0:T(8,128)(2,1)S(1)}, u32[]{:S(2)}, u32[]{:S(2)}) %collective-permute-start.1) | collective-permute-done | bytes 147488 | tf_op jit(solution)/shard_map/ppermute | solution.py:262
  50.4 5.5 %collective-permute-start.2 = (bf16[128,1152]{1,0:T(8,128)(2,1)S(1)}, bf16[128,1152]{1,0:T(8,128)(2,1)S(1)}, u32[]{:S(2)}, u32[]{:S(2)}) collective-permute-start(bf16[128,1152]{1,0:T(8,128)(2,1)S(1)} %get-tuple-element.25), channel_id=1, source_target_pairs={{0,224},{16,240},{32,0},{48,16},{64,32},{80,48},{96,64},{112,80},{... | collective-permute-start | bytes 884744 | tf_op jit(solution)/shard_map/ppermute | solution.py:262
  55.9 9.9 %collective-permute-done.4 = bf16[128,1152]{1,0:T(8,128)(2,1)S(1)} collective-permute-done((bf16[128,1152]{1,0:T(8,128)(2,1)S(1)}, bf16[128,1152]{1,0:T(8,128)(2,1)S(1)}, u32[]{:S(2)}, u32[]{:S(2)}) %collective-permute-start.4) | collective-permute-done | bytes 294944 | tf_op jit(solution)/shard_map/ppermute | solution.py:262
  65.8 3.8 %collective-permute-done.2 = bf16[128,1152]{1,0:T(8,128)(2,1)S(1)} collective-permute-done((bf16[128,1152]{1,0:T(8,128)(2,1)S(1)}, bf16[128,1152]{1,0:T(8,128)(2,1)S(1)}, u32[]{:S(2)}, u32[]{:S(2)}) %collective-permute-start.2) | collective-permute-done | bytes 294944 | tf_op jit(solution)/shard_map/ppermute | solution.py:262
  71.7 4.6 %collective-permute-start.6 = (bf16[256,1152]{1,0:T(8,128)(2,1)S(1)}, bf16[256,1152]{1,0:T(8,128)(2,1)S(1)}, u32[]{:S(2)}, u32[]{:S(2)}) collective-permute-start(bf16[256,1152]{1,0:T(8,128)(2,1)S(1)} %get-tuple-element.23.refs_0_), channel_id=1, source_target_pairs={{0,240},{16,0},{32,16},{48,32},{64,48},{80,64},{96,80},{112,96},{1... | collective-permute-start | bytes 1769480 | tf_op jit(solution)/shard_map/ppermute | solution.py:262
  76.3 6.2 %collective-permute-start.5 = (bf16[64,1152]{1,0:T(8,128)(2,1)S(1)}, bf16[64,1152]{1,0:T(8,128)(2,1)S(1)}, u32[]{:S(2)}, u32[]{:S(2)}) collective-permute-start(bf16[64,1152]{1,0:T(8,128)(2,1)S(1)} %pad_maximum_fusion.6), channel_id=1, source_target_pairs={{0,128},{16,144},{32,160},{48,176},{64,192},{80,208},{96,224},{112... | collective-permute-start | bytes 442376 | tf_op jit(solution)/shard_map/ppermute | solution.py:262
  82.4 14.1 %collective-permute-done.5.refs_2_ = bf16[64,1152]{1,0:T(8,128)(2,1)S(1)} collective-permute-done((bf16[64,1152]{1,0:T(8,128)(2,1)S(1)}, bf16[64,1152]{1,0:T(8,128)(2,1)S(1)}, u32[]{:S(2)}, u32[]{:S(2)}) %collective-permute-start.5) | collective-permute-done | bytes 147488 | tf_op jit(solution)/shard_map/ppermute | solution.py:262
  96.5 15.0 %expert_work.1 = (bf16[1280,768]{1,0:T(8,128)(2,1)}, bf16[1024,768]{1,0:T(8,128)(2,1)S(1)}, bf16[4,64,768]{2,1,0:T(8,128)(2,1)S(1)}, bf16[4,64,768]{2,1,0:T(8,128)(2,1)S(1)}, bf16[8,64,768]{2,1,0:T(8,128)(2,1)S(1)}) custom-call(bf16[2048,2176]{1,0:T(8,128)(2,1)} %all-gather.2.cloned.1.call-done.g_ref, bf16[256,1152]{1,0:T(8,128)(2,1)S(1)} %get-tuple-element.23.refs_0_, ...), custom_call_target="tpu_custom_call" | custom-call | flops 5033164800 | bytes 16777216 | tf_op jit(solution)/shard_map/expert_work/pallas_call | solution.py:175
  113.7 8.7 %collective-permute-start.8 = (bf16[4,64,768]{2,1,0:T(8,128)(2,1)S(1)}, bf16[4,64,768]{2,1,0:T(8,128)(2,1)S(1)}, u32[]{:S(2)}, u32[]{:S(2)}) collective-permute-start(bf16[4,64,768]{2,1,0:T(8,128)(2,1)S(1)} %get-tuple-element.17), channel_id=1, source_target_pairs={{0,16},{16,32},{32,48},{48,64},{64,80},{80,96},{96,112},{112,128},... | collective-permute-start | bytes 1179656 | tf_op jit(solution)/shard_map/ppermute | solution.py:262
  124.3 3.2 %collective-permute-done.8.plus_ref = bf16[4,64,768]{2,1,0:T(8,128)(2,1)S(1)} collective-permute-done((bf16[4,64,768]{2,1,0:T(8,128)(2,1)S(1)}, bf16[4,64,768]{2,1,0:T(8,128)(2,1)S(1)}, u32[]{:S(2)}, u32[]{:S(2)}) %collective-permute-start.8) | collective-permute-done | bytes 393248 | tf_op jit(solution)/shard_map/ppermute | solution.py:262
  127.5 3.8 %collective-permute-done.9.minus_ref = bf16[4,64,768]{2,1,0:T(8,128)(2,1)S(1)} collective-permute-done((bf16[4,64,768]{2,1,0:T(8,128)(2,1)S(1)}, bf16[4,64,768]{2,1,0:T(8,128)(2,1)S(1)}, u32[]{:S(2)}, u32[]{:S(2)}) %collective-permute-start.9) | collective-permute-done | bytes 393248 | tf_op jit(solution)/shard_map/ppermute | solution.py:262
  132.1 2.4 %first_sum.1 = (bf16[2,64,768]{2,1,0:T(8,128)(2,1)}, bf16[2,64,768]{2,1,0:T(8,128)(2,1)}, bf16[4,64,768]{2,1,0:T(8,128)(2,1)}) custom-call(bf16[8,64,768]{2,1,0:T(8,128)(2,1)} %copy-done.1, bf16[4,64,768]{2,1,0:T(8,128)(2,1)} %copy-done.8, bf16[4,64,768]{2,1,0:T(8,128)(2,1)} %copy-done.9), custom_call_target="tpu_custom_call" | custom-call | tf_op jit(solution)/shard_map/first_sum/pallas_call | solution.py:321
  134.5 2.0 collective-permute-start.10
  136.5 5.5 %collective-permute-start.11 = (bf16[2,64,768]{2,1,0:T(8,128)(2,1)}, bf16[2,64,768]{2,1,0:T(8,128)(2,1)}, u32[]{:S(2)}, u32[]{:S(2)}) collective-permute-start(bf16[2,64,768]{2,1,0:T(8,128)(2,1)} %get-tuple-element.21), channel_id=1, source_target_pairs={{0,224},{16,240},{32,0},{48,16},{64,32},{80,48},{96,64},{112,80},{... | collective-permute-start | bytes 589832 | tf_op jit(solution)/shard_map/ppermute | solution.py:262
  142.0 3.6 %collective-permute-done.10.up_ref = bf16[2,64,768]{2,1,0:T(8,128)(2,1)} collective-permute-done((bf16[2,64,768]{2,1,0:T(8,128)(2,1)}, bf16[2,64,768]{2,1,0:T(8,128)(2,1)}, u32[]{:S(2)}, u32[]{:S(2)}) %collective-permute-start.10) | collective-permute-done | bytes 196640 | tf_op jit(solution)/shard_map/ppermute | solution.py:262
  149.0 6.8 %all-to-all-start.1 = ((bf16[8,32,768]{2,1,0:T(8,128)(2,1)}), bf16[8,32,768]{2,1,0:T(8,128)(2,1)}, u32[]{:S(2)}, u32[]{:S(2)}) async-start(bf16[8,32,768]{2,1,0:T(8,128)(2,1)} %second_sum.1), calls=%async_computation.1 | async-start | bytes 786432 | tf_op jit(solution)/shard_map/all_to_all | solution.py:336
  155.8 2.9 %row_gradients.1 = bf16[1280,1024]{1,0:T(8,128)(2,1)S(1)} custom-call(bf16[1280,768]{1,0:T(8,128)(2,1)S(1)} %copy-done.3, bf16[1024,768]{1,0:T(8,128)(2,1)S(1)} %copy-done.5), custom_call_target="tpu_custom_call" | custom-call | flops 2013265920 | bytes 6291456 | tf_op jit(solution)/shard_map/row_gradients/pallas_call | solution.py:214
  160.2 10.8 %all-to-all-done.1 = bf16[8,32,768]{2,1,0:T(8,128)(2,1)} async-done(((bf16[8,32,768]{2,1,0:T(8,128)(2,1)}), bf16[8,32,768]{2,1,0:T(8,128)(2,1)}, u32[]{:S(2)}, u32[]{:S(2)}) %all-to-all-start.1) | async-done | bytes 393248 | tf_op jit(solution)/shard_map/all_to_all | solution.py:336
  171.0 16.2 %all-to-all-start = ((bf16[16,80,1024]{2,1,0:T(8,128)(2,1)}), bf16[16,80,1024]{2,1,0:T(8,128)(2,1)S(1)}, u32[]{:S(2)}, u32[]{:S(2)}) async-start(bf16[16,80,1024]{2,1,0:T(8,128)(2,1)} %bitcast.9), calls=%async_computation | async-start | bytes 5242880 | tf_op jit(solution)/shard_map/all_to_all | solution.py:356
  188.9 33.2 %all-to-all-done = bf16[16,80,1024]{2,1,0:T(8,128)(2,1)S(1)} async-done(((bf16[16,80,1024]{2,1,0:T(8,128)(2,1)}), bf16[16,80,1024]{2,1,0:T(8,128)(2,1)S(1)}, u32[]{:S(2)}, u32[]{:S(2)}) %all-to-all-start) | async-done | bytes 2621472 | tf_op jit(solution)/shard_map/all_to_all | solution.py:356
  (39 shorter events, 20.3 us)
Async XLA Ops:
  7.2 10.3 %copy-start.7 = (bf16[1,32,384]{2,1,0:T(8,128)(2,1)S(1)}, bf16[1,32,384]{2,1,0:T(8,128)(2,1)}, u32[]{:S(2)}) copy-start(bf16[1,32,384]{2,1,0:T(8,128)(2,1)} %param.11) | copy-start | bytes 73732
  7.2 10.3 %copy-start.6 = (bf16[1,32,768]{2,1,0:T(8,128)(2,1)S(1)}, bf16[1,32,768]{2,1,0:T(8,128)(2,1)}, u32[]{:S(2)}) copy-start(bf16[1,32,768]{2,1,0:T(8,128)(2,1)} %param.10) | copy-start | bytes 147460
  7.2 89.3 %all-gather.2.cloned.1.call-start = ((), (), s32[]{:S(2)}) async-start(), calls=%async_computation.2 | async-start | bytes 9469952 | tf_op jit(solution)/shard_map/all_gather | solution.py:346
  10.1 7.4 %collective-permute-start = (bf16[32,1152]{1,0:T(8,128)(2,1)S(1)}, bf16[32,1152]{1,0:T(8,128)(2,1)S(1)}, u32[]{:S(2)}, u32[]{:S(2)}) collective-permute-start(bf16[32,1152]{1,0:T(8,128)(2,1)S(1)} %pad_maximum_fusion.7), channel_id=1, source_target_pairs={{0,256},{16,272},{32,288},{48,304},{64,320},{80,336},{96,352},{112... | collective-permute-start | bytes 221192 | tf_op jit(solution)/shard_map/ppermute | solution.py:257
  17.5 15.3 %collective-permute-start.3 = (bf16[64,1152]{1,0:T(8,128)(2,1)S(1)}, bf16[64,1152]{1,0:T(8,128)(2,1)S(1)}, u32[]{:S(2)}, u32[]{:S(2)}) collective-permute-start(bf16[64,1152]{1,0:T(8,128)(2,1)S(1)} %pad_maximum_fusion.6), channel_id=1, source_target_pairs={{0,64},{16,80},{32,96},{48,112},{64,128},{80,144},{96,160},{112,17... | collective-permute-start | bytes 442376 | tf_op jit(solution)/shard_map/ppermute | solution.py:262
  26.3 22.1 %collective-permute-start.1 = (bf16[64,1152]{1,0:T(8,128)(2,1)S(1)}, bf16[64,1152]{1,0:T(8,128)(2,1)S(1)}, u32[]{:S(2)}, u32[]{:S(2)}) collective-permute-start(bf16[64,1152]{1,0:T(8,128)(2,1)S(1)} %pad_maximum_fusion.6), channel_id=1, source_target_pairs={{0,192},{16,208},{32,224},{48,240},{64,0},{80,16},{96,32},{112,48}... | collective-permute-start | bytes 442376 | tf_op jit(solution)/shard_map/ppermute | solution.py:262
  48.5 17.3 %collective-permute-start.4 = (bf16[128,1152]{1,0:T(8,128)(2,1)S(1)}, bf16[128,1152]{1,0:T(8,128)(2,1)S(1)}, u32[]{:S(2)}, u32[]{:S(2)}) collective-permute-start(bf16[128,1152]{1,0:T(8,128)(2,1)S(1)} %get-tuple-element.24), channel_id=1, source_target_pairs={{0,32},{16,48},{32,64},{48,80},{64,96},{80,112},{96,128},{112,144}... | collective-permute-start | bytes 884744 | tf_op jit(solution)/shard_map/ppermute | solution.py:262
  50.4 19.2 %collective-permute-start.2 = (bf16[128,1152]{1,0:T(8,128)(2,1)S(1)}, bf16[128,1152]{1,0:T(8,128)(2,1)S(1)}, u32[]{:S(2)}, u32[]{:S(2)}) collective-permute-start(bf16[128,1152]{1,0:T(8,128)(2,1)S(1)} %get-tuple-element.25), channel_id=1, source_target_pairs={{0,224},{16,240},{32,0},{48,16},{64,32},{80,48},{96,64},{112,80},{... | collective-permute-start | bytes 884744 | tf_op jit(solution)/shard_map/ppermute | solution.py:262
  69.7 26.8 %collective-permute-start.7 = (bf16[256,1152]{1,0:T(8,128)(2,1)S(1)}, bf16[256,1152]{1,0:T(8,128)(2,1)S(1)}, u32[]{:S(2)}, u32[]{:S(2)}) collective-permute-start(bf16[256,1152]{1,0:T(8,128)(2,1)S(1)} %get-tuple-element.22.refs_1_), channel_id=1, source_target_pairs={{0,16},{16,32},{32,48},{48,64},{64,80},{80,96},{96,112},{112,128},... | collective-permute-start | bytes 1769480 | tf_op jit(solution)/shard_map/ppermute | solution.py:262
  71.7 24.9 %collective-permute-start.6 = (bf16[256,1152]{1,0:T(8,128)(2,1)S(1)}, bf16[256,1152]{1,0:T(8,128)(2,1)S(1)}, u32[]{:S(2)}, u32[]{:S(2)}) collective-permute-start(bf16[256,1152]{1,0:T(8,128)(2,1)S(1)} %get-tuple-element.23.refs_0_), channel_id=1, source_target_pairs={{0,240},{16,0},{32,16},{48,32},{64,48},{80,64},{96,80},{112,96},{1... | collective-permute-start | bytes 1769480 | tf_op jit(solution)/shard_map/ppermute | solution.py:262
  76.3 20.3 %collective-permute-start.5 = (bf16[64,1152]{1,0:T(8,128)(2,1)S(1)}, bf16[64,1152]{1,0:T(8,128)(2,1)S(1)}, u32[]{:S(2)}, u32[]{:S(2)}) collective-permute-start(bf16[64,1152]{1,0:T(8,128)(2,1)S(1)} %pad_maximum_fusion.6), channel_id=1, source_target_pairs={{0,128},{16,144},{32,160},{48,176},{64,192},{80,208},{96,224},{112... | collective-permute-start | bytes 442376 | tf_op jit(solution)/shard_map/ppermute | solution.py:262
  111.6 0.9 copy-start.1
  112.5 1.2 copy-start.4
  113.7 13.8 %collective-permute-start.8 = (bf16[4,64,768]{2,1,0:T(8,128)(2,1)S(1)}, bf16[4,64,768]{2,1,0:T(8,128)(2,1)S(1)}, u32[]{:S(2)}, u32[]{:S(2)}) collective-permute-start(bf16[4,64,768]{2,1,0:T(8,128)(2,1)S(1)} %get-tuple-element.17), channel_id=1, source_target_pairs={{0,16},{16,32},{32,48},{48,64},{64,80},{80,96},{96,112},{112,128},... | collective-permute-start | bytes 1179656 | tf_op jit(solution)/shard_map/ppermute | solution.py:262
  122.4 8.9 %collective-permute-start.9 = (bf16[4,64,768]{2,1,0:T(8,128)(2,1)S(1)}, bf16[4,64,768]{2,1,0:T(8,128)(2,1)S(1)}, u32[]{:S(2)}, u32[]{:S(2)}) collective-permute-start(bf16[4,64,768]{2,1,0:T(8,128)(2,1)S(1)} %get-tuple-element.18), channel_id=1, source_target_pairs={{0,240},{16,0},{32,16},{48,32},{64,48},{80,64},{96,80},{112,96},{1... | collective-permute-start | bytes 1179656 | tf_op jit(solution)/shard_map/ppermute | solution.py:262
  127.5 3.8 %copy-start.8 = (bf16[4,64,768]{2,1,0:T(8,128)(2,1)}, bf16[4,64,768]{2,1,0:T(8,128)(2,1)S(1)}, u32[]{:S(2)}) copy-start(bf16[4,64,768]{2,1,0:T(8,128)(2,1)S(1)} %collective-permute-done.8.plus_ref) | copy-start | bytes 1179652
  132.1 23.7 %copy-start.5 = (bf16[1024,768]{1,0:T(8,128)(2,1)S(1)}, bf16[1024,768]{1,0:T(8,128)(2,1)}, u32[]{:S(2)}) copy-start(bf16[1024,768]{1,0:T(8,128)(2,1)} %copy-done.4) | copy-start | bytes 4718596
  134.5 21.3 %copy-start.3 = (bf16[1280,768]{1,0:T(8,128)(2,1)S(1)}, bf16[1280,768]{1,0:T(8,128)(2,1)}, u32[]{:S(2)}) copy-start(bf16[1280,768]{1,0:T(8,128)(2,1)} %get-tuple-element.14.pre_ref) | copy-start | bytes 5898244
  134.5 11.1 %collective-permute-start.10 = (bf16[2,64,768]{2,1,0:T(8,128)(2,1)}, bf16[2,64,768]{2,1,0:T(8,128)(2,1)}, u32[]{:S(2)}, u32[]{:S(2)}) collective-permute-start(bf16[2,64,768]{2,1,0:T(8,128)(2,1)} %get-tuple-element.20), channel_id=1, source_target_pairs={{0,32},{16,48},{32,64},{48,80},{64,96},{80,112},{96,128},{112,144}... | collective-permute-start | bytes 589832 | tf_op jit(solution)/shard_map/ppermute | solution.py:262
  136.5 10.5 %collective-permute-start.11 = (bf16[2,64,768]{2,1,0:T(8,128)(2,1)}, bf16[2,64,768]{2,1,0:T(8,128)(2,1)}, u32[]{:S(2)}, u32[]{:S(2)}) collective-permute-start(bf16[2,64,768]{2,1,0:T(8,128)(2,1)} %get-tuple-element.21), channel_id=1, source_target_pairs={{0,224},{16,240},{32,0},{48,16},{64,32},{80,48},{96,64},{112,80},{... | collective-permute-start | bytes 589832 | tf_op jit(solution)/shard_map/ppermute | solution.py:262
  149.0 22.0 %all-to-all-start.1 = ((bf16[8,32,768]{2,1,0:T(8,128)(2,1)}), bf16[8,32,768]{2,1,0:T(8,128)(2,1)}, u32[]{:S(2)}, u32[]{:S(2)}) async-start(bf16[8,32,768]{2,1,0:T(8,128)(2,1)} %second_sum.1), calls=%async_computation.1 | async-start | bytes 786432 | tf_op jit(solution)/shard_map/all_to_all | solution.py:336
  158.7 1.5 copy-start
  171.0 51.1 %copy-start.2 = (bf16[16,128]{1,0:T(8,128)(2,1)S(1)}, bf16[16,128]{1,0:T(8,128)(2,1)}, u32[]{:S(2)}) copy-start(bf16[16,128]{1,0:T(8,128)(2,1)} %get-tuple-element.12.rank_ref) | copy-start | bytes 12292
  171.0 51.0 %all-to-all-start = ((bf16[16,80,1024]{2,1,0:T(8,128)(2,1)}), bf16[16,80,1024]{2,1,0:T(8,128)(2,1)S(1)}, u32[]{:S(2)}, u32[]{:S(2)}) async-start(bf16[16,80,1024]{2,1,0:T(8,128)(2,1)} %bitcast.9), calls=%async_computation | async-start | bytes 5242880 | tf_op jit(solution)/shard_map/all_to_all | solution.py:356
  (1 other events, 0.7 us)
Sparse Core Ops, SparseCore 0:
  10.2 67.9 all-gather.1

commit v3 on v2

--- a/solution.py
+++ b/solution.py
@@ -60,7 +60,7 @@
 
 
 def expert_kernel(my_expert, my_dp, plan, features, hidden, g_ref, *refs):
-    piece_total = 5
+    piece_total = 1 + max(array for array, _, _, _ in plan)
     pieces = refs[:piece_total]
     pre_ref, gate_up_ref, plus_ref, minus_ref, keep_ref = refs[piece_total : piece_total + 5]
     blocks, weights, inputs, cots, total, block_sems, sems = refs[piece_total + 5 :]
@@ -83,15 +83,15 @@
         return pl.multiple_of(owner * half + ((place + offset + RING) % RING) * shard, shard)
 
     weight_copies = []
-    for array, source, offset in plan:
-        for part, owner in ((0, upper), (1, 1 - upper)):
-            weight_copies.append(
-                pltpu.make_async_copy(
-                    pieces[array].at[pl.ds(source + part * shard, shard), :],
-                    weights.at[pl.ds(first_row(owner, offset), shard), :],
-                    sems.at[len(weight_copies)],
-                )
+    for array, source, offset, part in plan:
+        owner = upper if part == 0 else 1 - upper
+        weight_copies.append(
+            pltpu.make_async_copy(
+                pieces[array].at[pl.ds(source, shard), :],
+                weights.at[pl.ds(first_row(owner, offset), shard), :],
+                sems.at[len(weight_copies)],
             )
+        )
     block_copies = [block_copy(p) for p in range(pair_total)]
     for copy in block_copies[:2] + weight_copies + block_copies[2:]:
         copy.start()
@@ -201,25 +201,38 @@
     )(gathered, *pieces)
 
 
-def row_kernel(pre_ref, gate_up_ref, out_ref):
-    out_ref[...] = lax.dot_general(
-        pre_ref[...], gate_up_ref[...], (((1,), (1,)), ((), ())), preferred_element_type=F32
-    ).astype(BF16)
+def row_kernel(pre_hbm, gate_up_hbm, out_ref, pre_ref, gate_up_ref, sems):
+    copies = [
+        pltpu.make_async_copy(gate_up_hbm, gate_up_ref, sems.at[0]),
+        pltpu.make_async_copy(pre_hbm, pre_ref, sems.at[1]),
+    ]
+    for copy in copies:
+        copy.start()
+    for copy in copies:
+        copy.wait()
+    block = pre_ref.shape[0] // BLOCKS
+    for m in range(BLOCKS):
+        here = pl.ds(m * block, block)
+        out_ref[here, :] = lax.dot_general(
+            pre_ref[here, :],
+            gate_up_ref[...],
+            (((1,), (1,)), ((), ())),
+            preferred_element_type=F32,
+        ).astype(BF16)
 
 
 def row_gradients(pre_grad, gate_up):
     slots, columns = pre_grad.shape
     features = gate_up.shape[0]
-    block = slots // BLOCKS
     return pl.pallas_call(
         row_kernel,
-        grid=(BLOCKS,),
-        in_specs=[
-            pl.BlockSpec((block, columns), lambda i: (i, 0)),
-            pl.BlockSpec((features, columns), lambda i: (0, 0)),
+        in_specs=[pl.BlockSpec(memory_space=pltpu.HBM)] * 2,
+        out_shape=jax.ShapeDtypeStruct((slots, features), BF16),
+        scratch_shapes=[
+            pltpu.VMEM((slots, columns), BF16),
+            pltpu.VMEM((features, columns), BF16),
+            pltpu.SemaphoreType.DMA((2,)),
         ],
-        out_specs=pl.BlockSpec((block, features), lambda i: (i, 0)),
-        out_shape=jax.ShapeDtypeStruct((slots, features), BF16),
         compiler_params=pltpu.CompilerParams(vmem_limit_bytes=32 * 1024 * 1024),
         cost_estimate=pl.CostEstimate(
             flops=2 * slots * features * columns,
@@ -264,22 +277,17 @@
 
 def gather_weights(gate_up, down):
     own = jnp.concatenate([gate_up[0], down[0]], axis=1)
-    both = jnp.concatenate([own, swap_halves(own)], axis=0)
-    unit = both.shape[0]
-    up4, down4, far = shift_ring(both, -4), shift_ring(both, 4), shift_ring(both, 8)
-    ahead = jnp.concatenate([both, up4], axis=0)
-    behind = jnp.concatenate([both, down4], axis=0)
-    ahead = jnp.concatenate([ahead, shift_ring(ahead, -2)], axis=0)
-    behind = jnp.concatenate([behind, shift_ring(behind, 2)], axis=0)
-    odd_ahead, odd_behind = shift_ring(ahead, -1), shift_ring(behind, 1)
-    pieces = [ahead, behind, far, odd_ahead, odd_behind]
-    held = [[0, 4, 2, 6], [None, -4, -2, -6], [8], [1, 5, 3, 7], [-1, -5, -3, -7]]
-    plan = [
-        (array, unit * k, offset)
-        for array, offsets in enumerate(held)
-        for k, offset in enumerate(offsets)
-        if offset is not None
-    ]
+    shard = own.shape[0]
+    ahead = behind = jnp.concatenate([own, swap_halves(own)], axis=0)
+    pieces = [ahead]
+    plan = [(0, 0, 0, 0), (0, shard, 0, 1)]
+    for j in range(1, RING // 2):
+        ahead, behind = shift_ring(ahead, 1), shift_ring(behind, -1)
+        for piece, offset in ((ahead, -j), (behind, j)):
+            plan += [(len(pieces), part * shard, offset, part) for part in range(2)]
+            pieces.append(piece)
+    plan += [(len(pieces), 0, RING // 2, 0), (len(pieces) + 1, 0, RING // 2, 1)]
+    pieces += [shift_ring(ahead[:shard], 1), shift_ring(behind[shard:], -1)]
     return pieces, plan
 
 
@@ -298,7 +306,8 @@
         rest_ref[j] = part(2 * j)
 
 
-def second_sum_kernel(my_dp, rest_ref, up_ref, down_ref, out_ref):
+def second_sum_kernel(my_dp, rest_ref, up_ref, down_ref, later_ref, out_ref):
+    del later_ref
     shard = out_ref.shape[1]
     far = (my_dp() % RING) // NEAR
     groups = RING // NEAR
@@ -314,7 +323,7 @@
         out_ref[groups + target] = value[shard:]
 
 
-def scatter_sum(plus, minus, keep, scale, my_dp):
+def scatter_sum(plus, minus, keep, later, scale, my_dp):
     unit, columns = keep.shape[1:]
     got_plus, got_minus = shift_ring(plus, 1), shift_ring(minus, -1)
     piece = jax.ShapeDtypeStruct((2, unit, columns), BF16)
@@ -327,8 +336,10 @@
     parts = pl.pallas_call(
         functools.partial(second_sum_kernel, my_dp),
         out_shape=jax.ShapeDtypeStruct((2 * RING // NEAR, unit // 2, columns), BF16),
+        in_specs=[pl.BlockSpec(memory_space=pltpu.VMEM)] * 3
+        + [pl.BlockSpec(memory_space=pltpu.HBM)],
         name="second_sum",
-    )(rest, got_up, got_down)
+    )(rest, got_up, got_down, later)
     groups = [
         [y * RING + far * NEAR + near for y in range(2) for far in range(RING // NEAR)]
         for near in range(NEAR)
@@ -357,7 +368,7 @@
         row_grads.reshape(EXPERTS, CAP, features), "expert", split_axis=0, concat_axis=0, tiled=True
     )
     grad_scale = 1.0 / math.sqrt(rows * lax.axis_size("dp") * lax.axis_size("expert"))
-    grad_gate_up = scatter_sum(plus, minus, keep, grad_scale, my_dp)
+    grad_gate_up = scatter_sum(plus, minus, keep, returned, grad_scale, my_dp)
     token_grad = combine(rank, returned.reshape(EXPERTS * CAP, features))
     return (token_grad, grad_gate_up)
 

time: 233 us -> 209 us (0.90)
  the two profiles are of different devices: /device:TPU:1 before, /device:TPU:32 now
where the time goes in v3:
time: 209 us; the launch traced here: 208 us
  starting transfers between devices  102 us (49%)
  waiting for transfers between devices  56.6 us (27%)
  Pallas kernels  25.4 us (12%)
  between operations  14.3 us (7%)
  local copies, waits for them, and re-layouts  7.45 us (4%)
  other arithmetic  2.36 us (1%)
    ppermute x20, starting transfers between devices, shift_ring(): return lax.ppermute(x, 'dp', pairs)  78.9 us
    ppermute x20, waiting for transfers between devices, shift_ring(): return lax.ppermute(x, 'dp', pairs)  29.9 us
    all_to_all x1, waiting for transfers between devices, scatter_sum(): lax.all_to_all(parts, 'dp', split_axis=0, concat_axis=0, axis_index_group...  24 us
    pallas_call x1, Pallas kernels, expert_work(): pl.pallas_call(functools.partial(expert_kernel, my_expert, my_dp, plan, f...  15.1 us
    all_to_all x1, starting transfers between devices, scatter_sum(): lax.all_to_all(parts, 'dp', split_axis=0, concat_axis=0, axis_index_group...  12.8 us
    unnamed x20, local copies, waits for them, and re-layouts  7.44 us
    all_to_all x1, starting transfers between devices, shards(): lax.all_to_all(row_grads.reshape(EXPERTS, CAP, features), 'expert', split...  5.42 us
    ppermute x1, starting transfers between devices, swap_halves(): lax.ppermute(x, 'dp', [(d, (d + RING) % (2 * RING)) for d in range(2 * RI...  5.09 us
  transfers between devices with their start and end apart: 24, of which 19 were waited for; matrix products, arithmetic and copies ran while one was open for 1% of the time, Pallas kernels for 2%

profile of v3, /device:TPU:32, one launch (start us, length us, event | category | flops | bytes accessed | tf_op | source)
XLA Modules:
  0.0 208.4 jit_solution(3655946875029383609)
XLA Ops:
  7.2 2.0 pack_rows.1
  10.0 5.1 %collective-permute-start = (bf16[32,1152]{1,0:T(8,128)(2,1)S(1)}, bf16[32,1152]{1,0:T(8,128)(2,1)S(1)}, u32[]{:S(2)}, u32[]{:S(2)}) collective-permute-start(bf16[32,1152]{1,0:T(8,128)(2,1)S(1)} %pad_maximum_fusion.1), channel_id=1, source_target_pairs={{0,256},{16,272},{32,288},{48,304},{64,320},{80,336},{96,352},{112... | collective-permute-start | bytes 221192 | tf_op jit(solution)/shard_map/ppermute | solution.py:270
  15.1 2.6 %collective-permute-done = bf16[32,1152]{1,0:T(8,128)(2,1)S(1)} collective-permute-done((bf16[32,1152]{1,0:T(8,128)(2,1)S(1)}, bf16[32,1152]{1,0:T(8,128)(2,1)S(1)}, u32[]{:S(2)}, u32[]{:S(2)}) %collective-permute-start) | collective-permute-done | bytes 73760 | tf_op jit(solution)/shard_map/ppermute | solution.py:270
  18.6 7.4 %collective-permute-start.2 = (bf16[64,1152]{1,0:T(8,128)(2,1)S(1)}, bf16[64,1152]{1,0:T(8,128)(2,1)S(1)}, u32[]{:S(2)}, u32[]{:S(2)}) collective-permute-start(bf16[64,1152]{1,0:T(8,128)(2,1)S(1)} %pad_maximum_fusion.refs_0_), channel_id=1, source_target_pairs={{0,240},{16,0},{32,16},{48,32},{64,48},{80,64},{96,80},{112,96},{1... | collective-permute-start | bytes 442376 | tf_op jit(solution)/shard_map/ppermute | solution.py:275
  28.7 6.0 %collective-permute-start.4 = (bf16[64,1152]{1,0:T(8,128)(2,1)S(1)}, bf16[64,1152]{1,0:T(8,128)(2,1)S(1)}, u32[]{:S(2)}, u32[]{:S(2)}) collective-permute-start(bf16[64,1152]{1,0:T(8,128)(2,1)S(1)} %collective-permute-done.2.refs_2_), channel_id=1, source_target_pairs={{0,240},{16,0},{32,16},{48,32},{64,48},{80,64},{96,80},{112,96},{1... | collective-permute-start | bytes 442376 | tf_op jit(solution)/shard_map/ppermute | solution.py:275
  37.3 5.6 %collective-permute-start.6 = (bf16[64,1152]{1,0:T(8,128)(2,1)S(1)}, bf16[64,1152]{1,0:T(8,128)(2,1)S(1)}, u32[]{:S(2)}, u32[]{:S(2)}) collective-permute-start(bf16[64,1152]{1,0:T(8,128)(2,1)S(1)} %collective-permute-done.4.refs_4_), channel_id=1, source_target_pairs={{0,240},{16,0},{32,16},{48,32},{64,48},{80,64},{96,80},{112,96},{1... | collective-permute-start | bytes 442376 | tf_op jit(solution)/shard_map/ppermute | solution.py:275
  45.6 5.6 %collective-permute-start.8 = (bf16[64,1152]{1,0:T(8,128)(2,1)S(1)}, bf16[64,1152]{1,0:T(8,128)(2,1)S(1)}, u32[]{:S(2)}, u32[]{:S(2)}) collective-permute-start(bf16[64,1152]{1,0:T(8,128)(2,1)S(1)} %collective-permute-done.6.refs_6_), channel_id=1, source_target_pairs={{0,240},{16,0},{32,16},{48,32},{64,48},{80,64},{96,80},{112,96},{1... | collective-permute-start | bytes 442376 | tf_op jit(solution)/shard_map/ppermute | solution.py:275
  53.8 5.7 %collective-permute-start.10 = (bf16[64,1152]{1,0:T(8,128)(2,1)S(1)}, bf16[64,1152]{1,0:T(8,128)(2,1)S(1)}, u32[]{:S(2)}, u32[]{:S(2)}) collective-permute-start(bf16[64,1152]{1,0:T(8,128)(2,1)S(1)} %collective-permute-done.8.refs_8_), channel_id=1, source_target_pairs={{0,240},{16,0},{32,16},{48,32},{64,48},{80,64},{96,80},{112,96},{1... | collective-permute-start | bytes 442376 | tf_op jit(solution)/shard_map/ppermute | solution.py:275
  63.3 5.8 %collective-permute-start.12 = (bf16[64,1152]{1,0:T(8,128)(2,1)S(1)}, bf16[64,1152]{1,0:T(8,128)(2,1)S(1)}, u32[]{:S(2)}, u32[]{:S(2)}) collective-permute-start(bf16[64,1152]{1,0:T(8,128)(2,1)S(1)} %collective-permute-done.10.refs_10_), channel_id=1, source_target_pairs={{0,240},{16,0},{32,16},{48,32},{64,48},{80,64},{96,80},{112,96},{1... | collective-permute-start | bytes 442376 | tf_op jit(solution)/shard_map/ppermute | solution.py:275
  72.7 5.3 %collective-permute-start.14 = (bf16[64,1152]{1,0:T(8,128)(2,1)S(1)}, bf16[64,1152]{1,0:T(8,128)(2,1)S(1)}, u32[]{:S(2)}, u32[]{:S(2)}) collective-permute-start(bf16[64,1152]{1,0:T(8,128)(2,1)S(1)} %collective-permute-done.12.refs_12_), channel_id=1, source_target_pairs={{0,240},{16,0},{32,16},{48,32},{64,48},{80,64},{96,80},{112,96},{1... | collective-permute-start | bytes 442376 | tf_op jit(solution)/shard_map/ppermute | solution.py:275
  81.2 5.1 %collective-permute-start.16 = (bf16[32,1152]{1,0:T(8,128)(2,1)S(1)}, bf16[32,1152]{1,0:T(8,128)(2,1)S(1)}, u32[]{:S(2)}, u32[]{:S(2)}) collective-permute-start(bf16[32,1152]{1,0:T(8,128)(2,1)S(1)} %slice.9), channel_id=1, source_target_pairs={{0,240},{16,0},{32,16},{48,32},{64,48},{80,64},{96,80},{112,96},{1... | collective-permute-start | bytes 221192 | tf_op jit(solution)/shard_map/ppermute | solution.py:275
  89.2 5.5 %collective-permute-done.15.refs_15_ = bf16[32,1152]{1,0:T(8,128)(2,1)S(1)} collective-permute-done((bf16[32,1152]{1,0:T(8,128)(2,1)S(1)}, bf16[32,1152]{1,0:T(8,128)(2,1)S(1)}, u32[]{:S(2)}, u32[]{:S(2)}) %collective-permute-start.15) | collective-permute-done | bytes 73760 | tf_op jit(solution)/shard_map/ppermute | solution.py:275
  94.7 15.1 %expert_work.1 = (bf16[1280,768]{1,0:T(8,128)(2,1)}, bf16[1024,768]{1,0:T(8,128)(2,1)S(1)}, bf16[4,64,768]{2,1,0:T(8,128)(2,1)S(1)}, bf16[4,64,768]{2,1,0:T(8,128)(2,1)S(1)}, bf16[8,64,768]{2,1,0:T(8,128)(2,1)S(1)}) custom-call(bf16[2048,2176]{1,0:T(8,128)(2,1)} %all-gather.2.cloned.1.call-done.g_ref, bf16[64,1152]{1,0:T(8,128)(2,1)S(1)} %pad_maximum_fusion.refs_0_, ...), custom_call_target="tpu_custom_call" | custom-call | flops 5033164800 | bytes 16777216 | tf_op jit(solution)/shard_map/expert_work/pallas_call | solution.py:175
  111.7 2.6 %row_gradients.1 = bf16[1280,1024]{1,0:T(8,128)(2,1)S(1)} custom-call(bf16[1280,768]{1,0:T(8,128)(2,1)S(1)} %copy-done.5, bf16[1024,768]{1,0:T(8,128)(2,1)S(1)} %get-tuple-element.15.gate_up_hbm), custom_call_target="tpu_custom_call" | custom-call | flops 2013265920 | bytes 6291456 | tf_op jit(solution)/shard_map/row_gradients/pallas_call | solution.py:227
  115.9 5.4 %all-to-all-start = ((bf16[16,80,1024]{2,1,0:T(8,128)(2,1)}), bf16[16,80,1024]{2,1,0:T(8,128)(2,1)S(1)}, u32[]{:S(2)}, u32[]{:S(2)}) async-start(bf16[16,80,1024]{2,1,0:T(8,128)(2,1)} %bitcast.9), calls=%async_computation | async-start | bytes 5242880 | tf_op jit(solution)/shard_map/all_to_all | solution.py:367
  123.2 5.1 %collective-permute-start.18 = (bf16[4,64,768]{2,1,0:T(8,128)(2,1)S(1)}, bf16[4,64,768]{2,1,0:T(8,128)(2,1)S(1)}, u32[]{:S(2)}, u32[]{:S(2)}) collective-permute-start(bf16[4,64,768]{2,1,0:T(8,128)(2,1)S(1)} %get-tuple-element.18), channel_id=1, source_target_pairs={{0,240},{16,0},{32,16},{48,32},{64,48},{80,64},{96,80},{112,96},{1... | collective-permute-start | bytes 1179656 | tf_op jit(solution)/shard_map/ppermute | solution.py:275
  128.3 7.7 %collective-permute-done.17.plus_ref = bf16[4,64,768]{2,1,0:T(8,128)(2,1)S(1)} collective-permute-done((bf16[4,64,768]{2,1,0:T(8,128)(2,1)S(1)}, bf16[4,64,768]{2,1,0:T(8,128)(2,1)S(1)}, u32[]{:S(2)}, u32[]{:S(2)}) %collective-permute-start.17) | collective-permute-done | bytes 393248 | tf_op jit(solution)/shard_map/ppermute | solution.py:275
  138.1 2.3 %first_sum.1 = (bf16[2,64,768]{2,1,0:T(8,128)(2,1)}, bf16[2,64,768]{2,1,0:T(8,128)(2,1)}, bf16[4,64,768]{2,1,0:T(8,128)(2,1)}) custom-call(bf16[8,64,768]{2,1,0:T(8,128)(2,1)} %copy-done.3, bf16[4,64,768]{2,1,0:T(8,128)(2,1)} %copy-done.6, bf16[4,64,768]{2,1,0:T(8,128)(2,1)} %copy-done.7), custom_call_target="tpu_custom_call" | custom-call | tf_op jit(solution)/shard_map/first_sum/pallas_call | solution.py:330
  140.3 2.1 %collective-permute-start.19 = (bf16[2,64,768]{2,1,0:T(8,128)(2,1)}, bf16[2,64,768]{2,1,0:T(8,128)(2,1)S(1)}, u32[]{:S(2)}, u32[]{:S(2)}) collective-permute-start(bf16[2,64,768]{2,1,0:T(8,128)(2,1)} %get-tuple-element.20), channel_id=1, source_target_pairs={{0,32},{16,48},{32,64},{48,80},{64,96},{80,112},{96,128},{112,144}... | collective-permute-start | bytes 589832 | tf_op jit(solution)/shard_map/ppermute | solution.py:275
  142.5 7.9 %collective-permute-start.20 = (bf16[2,64,768]{2,1,0:T(8,128)(2,1)}, bf16[2,64,768]{2,1,0:T(8,128)(2,1)S(1)}, u32[]{:S(2)}, u32[]{:S(2)}) collective-permute-start(bf16[2,64,768]{2,1,0:T(8,128)(2,1)} %get-tuple-element.21), channel_id=1, source_target_pairs={{0,224},{16,240},{32,0},{48,16},{64,32},{80,48},{96,64},{112,80},{... | collective-permute-start | bytes 589832 | tf_op jit(solution)/shard_map/ppermute | solution.py:275
  150.4 6.9 %collective-permute-done.19.up_ref = bf16[2,64,768]{2,1,0:T(8,128)(2,1)S(1)} collective-permute-done((bf16[2,64,768]{2,1,0:T(8,128)(2,1)}, bf16[2,64,768]{2,1,0:T(8,128)(2,1)S(1)}, u32[]{:S(2)}, u32[]{:S(2)}) %collective-permute-start.19) | collective-permute-done | bytes 196640 | tf_op jit(solution)/shard_map/ppermute | solution.py:275
  158.9 2.0 second_sum.1
  160.8 12.8 %all-to-all-start.1 = ((bf16[8,32,768]{2,1,0:T(8,128)(2,1)}), bf16[8,32,768]{2,1,0:T(8,128)(2,1)S(1)}, u32[]{:S(2)}, u32[]{:S(2)}) async-start(bf16[8,32,768]{2,1,0:T(8,128)(2,1)} %second_sum.1), calls=%async_computation.1 | async-start | bytes 786432 | tf_op jit(solution)/shard_map/all_to_all | solution.py:347
  176.8 24.0 %all-to-all-done.1 = bf16[8,32,768]{2,1,0:T(8,128)(2,1)S(1)} async-done(((bf16[8,32,768]{2,1,0:T(8,128)(2,1)}), bf16[8,32,768]{2,1,0:T(8,128)(2,1)S(1)}, u32[]{:S(2)}, u32[]{:S(2)}) %all-to-all-start.1) | async-done | bytes 393248 | tf_op jit(solution)/shard_map/all_to_all | solution.py:347
  (57 shorter events, 38.2 us)
Async XLA Ops:
  7.2 87.5 %all-gather.2.cloned.1.call-start = ((), (), s32[]{:S(2)}) async-start(), calls=%async_computation.2 | async-start | bytes 9469952 | tf_op jit(solution)/shard_map/all_gather | solution.py:357
  10.0 7.7 %collective-permute-start = (bf16[32,1152]{1,0:T(8,128)(2,1)S(1)}, bf16[32,1152]{1,0:T(8,128)(2,1)S(1)}, u32[]{:S(2)}, u32[]{:S(2)}) collective-permute-start(bf16[32,1152]{1,0:T(8,128)(2,1)S(1)} %pad_maximum_fusion.1), channel_id=1, source_target_pairs={{0,256},{16,272},{32,288},{48,304},{64,320},{80,336},{96,352},{112... | collective-permute-start | bytes 221192 | tf_op jit(solution)/shard_map/ppermute | solution.py:270
  18.6 10.1 %collective-permute-start.2 = (bf16[64,1152]{1,0:T(8,128)(2,1)S(1)}, bf16[64,1152]{1,0:T(8,128)(2,1)S(1)}, u32[]{:S(2)}, u32[]{:S(2)}) collective-permute-start(bf16[64,1152]{1,0:T(8,128)(2,1)S(1)} %pad_maximum_fusion.refs_0_), channel_id=1, source_target_pairs={{0,240},{16,0},{32,16},{48,32},{64,48},{80,64},{96,80},{112,96},{1... | collective-permute-start | bytes 442376 | tf_op jit(solution)/shard_map/ppermute | solution.py:275
  26.0 9.1 %collective-permute-start.1 = (bf16[64,1152]{1,0:T(8,128)(2,1)S(1)}, bf16[64,1152]{1,0:T(8,128)(2,1)S(1)}, u32[]{:S(2)}, u32[]{:S(2)}) collective-permute-start(bf16[64,1152]{1,0:T(8,128)(2,1)S(1)} %pad_maximum_fusion.refs_0_), channel_id=1, source_target_pairs={{0,16},{16,32},{32,48},{48,64},{64,80},{80,96},{96,112},{112,128},... | collective-permute-start | bytes 442376 | tf_op jit(solution)/shard_map/ppermute | solution.py:275
  28.7 8.7 %collective-permute-start.4 = (bf16[64,1152]{1,0:T(8,128)(2,1)S(1)}, bf16[64,1152]{1,0:T(8,128)(2,1)S(1)}, u32[]{:S(2)}, u32[]{:S(2)}) collective-permute-start(bf16[64,1152]{1,0:T(8,128)(2,1)S(1)} %collective-permute-done.2.refs_2_), channel_id=1, source_target_pairs={{0,240},{16,0},{32,16},{48,32},{64,48},{80,64},{96,80},{112,96},{1... | collective-permute-start | bytes 442376 | tf_op jit(solution)/shard_map/ppermute | solution.py:275
  35.2 8.2 %collective-permute-start.3 = (bf16[64,1152]{1,0:T(8,128)(2,1)S(1)}, bf16[64,1152]{1,0:T(8,128)(2,1)S(1)}, u32[]{:S(2)}, u32[]{:S(2)}) collective-permute-start(bf16[64,1152]{1,0:T(8,128)(2,1)S(1)} %collective-permute-done.1.refs_1_), channel_id=1, source_target_pairs={{0,16},{16,32},{32,48},{48,64},{64,80},{80,96},{96,112},{112,128},... | collective-permute-start | bytes 442376 | tf_op jit(solution)/shard_map/ppermute | solution.py:275
  37.3 8.2 %collective-permute-start.6 = (bf16[64,1152]{1,0:T(8,128)(2,1)S(1)}, bf16[64,1152]{1,0:T(8,128)(2,1)S(1)}, u32[]{:S(2)}, u32[]{:S(2)}) collective-permute-start(bf16[64,1152]{1,0:T(8,128)(2,1)S(1)} %collective-permute-done.4.refs_4_), channel_id=1, source_target_pairs={{0,240},{16,0},{32,16},{48,32},{64,48},{80,64},{96,80},{112,96},{1... | collective-permute-start | bytes 442376 | tf_op jit(solution)/shard_map/ppermute | solution.py:275
  43.4 8.2 %collective-permute-start.5 = (bf16[64,1152]{1,0:T(8,128)(2,1)S(1)}, bf16[64,1152]{1,0:T(8,128)(2,1)S(1)}, u32[]{:S(2)}, u32[]{:S(2)}) collective-permute-start(bf16[64,1152]{1,0:T(8,128)(2,1)S(1)} %collective-permute-done.3.refs_3_), channel_id=1, source_target_pairs={{0,16},{16,32},{32,48},{48,64},{64,80},{80,96},{96,112},{112,128},... | collective-permute-start | bytes 442376 | tf_op jit(solution)/shard_map/ppermute | solution.py:275
  45.6 8.2 %collective-permute-start.8 = (bf16[64,1152]{1,0:T(8,128)(2,1)S(1)}, bf16[64,1152]{1,0:T(8,128)(2,1)S(1)}, u32[]{:S(2)}, u32[]{:S(2)}) collective-permute-start(bf16[64,1152]{1,0:T(8,128)(2,1)S(1)} %collective-permute-done.6.refs_6_), channel_id=1, source_target_pairs={{0,240},{16,0},{32,16},{48,32},{64,48},{80,64},{96,80},{112,96},{1... | collective-permute-start | bytes 442376 | tf_op jit(solution)/shard_map/ppermute | solution.py:275
  51.6 8.4 %collective-permute-start.7 = (bf16[64,1152]{1,0:T(8,128)(2,1)S(1)}, bf16[64,1152]{1,0:T(8,128)(2,1)S(1)}, u32[]{:S(2)}, u32[]{:S(2)}) collective-permute-start(bf16[64,1152]{1,0:T(8,128)(2,1)S(1)} %collective-permute-done.5.refs_5_), channel_id=1, source_target_pairs={{0,16},{16,32},{32,48},{48,64},{64,80},{80,96},{96,112},{112,128},... | collective-permute-start | bytes 442376 | tf_op jit(solution)/shard_map/ppermute | solution.py:275
  53.8 9.5 %collective-permute-start.10 = (bf16[64,1152]{1,0:T(8,128)(2,1)S(1)}, bf16[64,1152]{1,0:T(8,128)(2,1)S(1)}, u32[]{:S(2)}, u32[]{:S(2)}) collective-permute-start(bf16[64,1152]{1,0:T(8,128)(2,1)S(1)} %collective-permute-done.8.refs_8_), channel_id=1, source_target_pairs={{0,240},{16,0},{32,16},{48,32},{64,48},{80,64},{96,80},{112,96},{1... | collective-permute-start | bytes 442376 | tf_op jit(solution)/shard_map/ppermute | solution.py:275
  60.0 9.9 %collective-permute-start.9 = (bf16[64,1152]{1,0:T(8,128)(2,1)S(1)}, bf16[64,1152]{1,0:T(8,128)(2,1)S(1)}, u32[]{:S(2)}, u32[]{:S(2)}) collective-permute-start(bf16[64,1152]{1,0:T(8,128)(2,1)S(1)} %collective-permute-done.7.refs_7_), channel_id=1, source_target_pairs={{0,16},{16,32},{32,48},{48,64},{64,80},{80,96},{96,112},{112,128},... | collective-permute-start | bytes 442376 | tf_op jit(solution)/shard_map/ppermute | solution.py:275
  63.3 9.4 %collective-permute-start.12 = (bf16[64,1152]{1,0:T(8,128)(2,1)S(1)}, bf16[64,1152]{1,0:T(8,128)(2,1)S(1)}, u32[]{:S(2)}, u32[]{:S(2)}) collective-permute-start(bf16[64,1152]{1,0:T(8,128)(2,1)S(1)} %collective-permute-done.10.refs_10_), channel_id=1, source_target_pairs={{0,240},{16,0},{32,16},{48,32},{64,48},{80,64},{96,80},{112,96},{1... | collective-permute-start | bytes 442376 | tf_op jit(solution)/shard_map/ppermute | solution.py:275
  70.0 9.3 %collective-permute-start.11 = (bf16[64,1152]{1,0:T(8,128)(2,1)S(1)}, bf16[64,1152]{1,0:T(8,128)(2,1)S(1)}, u32[]{:S(2)}, u32[]{:S(2)}) collective-permute-start(bf16[64,1152]{1,0:T(8,128)(2,1)S(1)} %collective-permute-done.9.refs_9_), channel_id=1, source_target_pairs={{0,16},{16,32},{32,48},{48,64},{64,80},{80,96},{96,112},{112,128},... | collective-permute-start | bytes 442376 | tf_op jit(solution)/shard_map/ppermute | solution.py:275
  72.7 8.5 %collective-permute-start.14 = (bf16[64,1152]{1,0:T(8,128)(2,1)S(1)}, bf16[64,1152]{1,0:T(8,128)(2,1)S(1)}, u32[]{:S(2)}, u32[]{:S(2)}) collective-permute-start(bf16[64,1152]{1,0:T(8,128)(2,1)S(1)} %collective-permute-done.12.refs_12_), channel_id=1, source_target_pairs={{0,240},{16,0},{32,16},{48,32},{64,48},{80,64},{96,80},{112,96},{1... | collective-permute-start | bytes 442376 | tf_op jit(solution)/shard_map/ppermute | solution.py:275
  79.3 8.0 %collective-permute-start.13 = (bf16[64,1152]{1,0:T(8,128)(2,1)S(1)}, bf16[64,1152]{1,0:T(8,128)(2,1)S(1)}, u32[]{:S(2)}, u32[]{:S(2)}) collective-permute-start(bf16[64,1152]{1,0:T(8,128)(2,1)S(1)} %collective-permute-done.11.refs_11_), channel_id=1, source_target_pairs={{0,16},{16,32},{32,48},{48,64},{64,80},{80,96},{96,112},{112,128},... | collective-permute-start | bytes 442376 | tf_op jit(solution)/shard_map/ppermute | solution.py:275
  81.2 7.9 %collective-permute-start.16 = (bf16[32,1152]{1,0:T(8,128)(2,1)S(1)}, bf16[32,1152]{1,0:T(8,128)(2,1)S(1)}, u32[]{:S(2)}, u32[]{:S(2)}) collective-permute-start(bf16[32,1152]{1,0:T(8,128)(2,1)S(1)} %slice.9), channel_id=1, source_target_pairs={{0,240},{16,0},{32,16},{48,32},{64,48},{80,64},{96,80},{112,96},{1... | collective-permute-start | bytes 221192 | tf_op jit(solution)/shard_map/ppermute | solution.py:275
  87.3 7.4 %collective-permute-start.15 = (bf16[32,1152]{1,0:T(8,128)(2,1)S(1)}, bf16[32,1152]{1,0:T(8,128)(2,1)S(1)}, u32[]{:S(2)}, u32[]{:S(2)}) collective-permute-start(bf16[32,1152]{1,0:T(8,128)(2,1)S(1)} %slice.8), channel_id=1, source_target_pairs={{0,16},{16,32},{32,48},{48,64},{64,80},{80,96},{96,112},{112,128},... | collective-permute-start | bytes 221192 | tf_op jit(solution)/shard_map/ppermute | solution.py:275
  115.9 41.4 %all-to-all-start = ((bf16[16,80,1024]{2,1,0:T(8,128)(2,1)}), bf16[16,80,1024]{2,1,0:T(8,128)(2,1)S(1)}, u32[]{:S(2)}, u32[]{:S(2)}) async-start(bf16[16,80,1024]{2,1,0:T(8,128)(2,1)} %bitcast.9), calls=%async_computation | async-start | bytes 5242880 | tf_op jit(solution)/shard_map/all_to_all | solution.py:367
  121.3 14.8 %collective-permute-start.17 = (bf16[4,64,768]{2,1,0:T(8,128)(2,1)S(1)}, bf16[4,64,768]{2,1,0:T(8,128)(2,1)S(1)}, u32[]{:S(2)}, u32[]{:S(2)}) collective-permute-start(bf16[4,64,768]{2,1,0:T(8,128)(2,1)S(1)} %get-tuple-element.17), channel_id=1, source_target_pairs={{0,16},{16,32},{32,48},{48,64},{64,80},{80,96},{96,112},{112,128},... | collective-permute-start | bytes 1179656 | tf_op jit(solution)/shard_map/ppermute | solution.py:275
  123.2 14.1 %collective-permute-start.18 = (bf16[4,64,768]{2,1,0:T(8,128)(2,1)S(1)}, bf16[4,64,768]{2,1,0:T(8,128)(2,1)S(1)}, u32[]{:S(2)}, u32[]{:S(2)}) collective-permute-start(bf16[4,64,768]{2,1,0:T(8,128)(2,1)S(1)} %get-tuple-element.18), channel_id=1, source_target_pairs={{0,240},{16,0},{32,16},{48,32},{64,48},{80,64},{96,80},{112,96},{1... | collective-permute-start | bytes 1179656 | tf_op jit(solution)/shard_map/ppermute | solution.py:275
  140.3 16.9 %collective-permute-start.19 = (bf16[2,64,768]{2,1,0:T(8,128)(2,1)}, bf16[2,64,768]{2,1,0:T(8,128)(2,1)S(1)}, u32[]{:S(2)}, u32[]{:S(2)}) collective-permute-start(bf16[2,64,768]{2,1,0:T(8,128)(2,1)} %get-tuple-element.20), channel_id=1, source_target_pairs={{0,32},{16,48},{32,64},{48,80},{64,96},{80,112},{96,128},{112,144}... | collective-permute-start | bytes 589832 | tf_op jit(solution)/shard_map/ppermute | solution.py:275
  142.5 14.8 %collective-permute-start.20 = (bf16[2,64,768]{2,1,0:T(8,128)(2,1)}, bf16[2,64,768]{2,1,0:T(8,128)(2,1)S(1)}, u32[]{:S(2)}, u32[]{:S(2)}) collective-permute-start(bf16[2,64,768]{2,1,0:T(8,128)(2,1)} %get-tuple-element.21), channel_id=1, source_target_pairs={{0,224},{16,240},{32,0},{48,16},{64,32},{80,48},{96,64},{112,80},{... | collective-permute-start | bytes 589832 | tf_op jit(solution)/shard_map/ppermute | solution.py:275
  160.8 40.0 %all-to-all-start.1 = ((bf16[8,32,768]{2,1,0:T(8,128)(2,1)}), bf16[8,32,768]{2,1,0:T(8,128)(2,1)S(1)}, u32[]{:S(2)}, u32[]{:S(2)}) async-start(bf16[8,32,768]{2,1,0:T(8,128)(2,1)} %second_sum.1), calls=%async_computation.1 | async-start | bytes 786432 | tf_op jit(solution)/shard_map/all_to_all | solution.py:347
  (10 other events, 47.9 us)
Sparse Core Ops, SparseCore 0:
  10.1 66.3 all-gather.1

commit v4 on v3

--- a/solution.py
+++ b/solution.py
@@ -55,6 +55,7 @@
             jax.ShapeDtypeStruct((rows, 2 * features + rows), BF16),
             jax.ShapeDtypeStruct((EXPERTS, rows), BF16),
         ),
+        compiler_params=pltpu.CompilerParams(vmem_limit_bytes=8 * 1024 * 1024),
         name="pack_rows",
     )(tokens, cotangent, route_experts.T, route_weights.T)
 
@@ -62,8 +63,9 @@
 def expert_kernel(my_expert, my_dp, plan, features, hidden, g_ref, *refs):
     piece_total = 1 + max(array for array, _, _, _ in plan)
     pieces = refs[:piece_total]
-    pre_ref, gate_up_ref, plus_ref, minus_ref, keep_ref = refs[piece_total : piece_total + 5]
-    blocks, weights, inputs, cots, total, block_sems, sems = refs[piece_total + 5 :]
+    row_ref, keep_ref, plus_ref, minus_ref, plus2_ref, minus2_ref = refs[piece_total : piece_total + 6]
+    blocks, weights, inputs, cots, pre_grad, row_grad, total = refs[piece_total + 6 : -3]
+    block_sems, sems, row_sems = refs[-3:]
     expert = my_expert()
     dp = my_dp()
     upper = dp // RING
@@ -127,13 +129,13 @@
         ).astype(BF16)
 
     block_rows = inputs.shape[0] // BLOCKS
+    row_copies = []
     for m in range(BLOCKS):
         for p in range(m * pair_total // BLOCKS, (m + 1) * pair_total // BLOCKS):
             compact(p)
         if m == 0:
             for copy in weight_copies:
                 copy.wait()
-            gate_up_ref[...] = weights[:, : 2 * hidden]
         here = pl.ds(m * block_rows, block_rows)
         projected = jnp.dot(inputs[here, :], weights[:, : 2 * hidden], preferred_element_type=F32)
         hidden_grad = jnp.dot(cots[here, :], weights[:, 2 * hidden :], preferred_element_type=F32)
@@ -142,29 +144,39 @@
         sigmoid_gate = jax.nn.sigmoid(gate_part)
         grad_gate = hidden_grad * up_part * sigmoid_gate * (1.0 + gate_part * (1.0 - sigmoid_gate))
         grad_up = hidden_grad * gate_part * sigmoid_gate
-        pre_ref[here, :hidden] = grad_gate.astype(BF16)
-        pre_ref[here, hidden:] = grad_up.astype(BF16)
+        pre_grad[here, :hidden] = grad_gate.astype(BF16)
+        pre_grad[here, hidden:] = grad_up.astype(BF16)
+        row_grad[here, :] = lax.dot_general(
+            pre_grad[here, :],
+            weights[:, : 2 * hidden],
+            (((1,), (1,)), ((), ())),
+            preferred_element_type=F32,
+        ).astype(BF16)
+        row_copies.append(
+            pltpu.make_async_copy(row_grad.at[here, :], row_ref.at[here, :], row_sems.at[m])
+        )
+        row_copies[m].start()
 
     strip = features // BLOCKS
     for c in range(BLOCKS):
         total[c * strip : (c + 1) * strip, :] = lax.dot_general(
             inputs[:, c * strip : (c + 1) * strip],
-            pre_ref[...],
+            pre_grad[...],
             (((0,), (0,)), ((), ())),
             preferred_element_type=F32,
         )
 
-    def put(ref, index, offset):
-        for owner in range(2):
-            ref[index, owner * shard : (owner + 1) * shard, :] = total[
-                pl.ds(first_row(owner, offset), shard), :
-            ].astype(BF16)
-
-    for j in range(RING // 4):
-        put(plus_ref, j, 2 * j + 1)
-        put(minus_ref, j, -(2 * j + 1))
-    for j in range(RING // 2):
-        put(keep_ref, j, 2 * j)
+    def part(owner, offset):
+        return total[pl.ds(first_row(owner, offset), shard), :].astype(BF16)
+
+    for j in range(RING // NEAR):
+        for ref, offset in ((keep_ref, 0), (plus_ref, 1), (minus_ref, -1)):
+            for owner in range(2):
+                ref[j, owner * shard : (owner + 1) * shard, :] = part(owner, NEAR * j + offset)
+        plus2_ref[j] = part(0, NEAR * j + 2)
+        minus2_ref[j] = part(1, NEAR * j + 2)
+    for copy in row_copies:
+        copy.wait()
 
 
 def expert_work(gathered, pieces, plan, features, hidden, my_expert, my_dp):
@@ -172,75 +184,40 @@
     slots = EXPERTS * CAP
     shard = features // (2 * RING)
     hbm = pl.BlockSpec(memory_space=pltpu.HBM)
+    whole = jax.ShapeDtypeStruct((RING // NEAR, 2 * shard, 2 * hidden), BF16)
+    half = jax.ShapeDtypeStruct((RING // NEAR, shard, 2 * hidden), BF16)
     return pl.pallas_call(
         functools.partial(expert_kernel, my_expert, my_dp, plan, features, hidden),
         in_specs=[hbm] * (1 + len(pieces)),
         out_shape=(
-            jax.ShapeDtypeStruct((slots, 2 * hidden), BF16),
-            jax.ShapeDtypeStruct((features, 2 * hidden), BF16),
-            jax.ShapeDtypeStruct((RING // 4, 2 * shard, 2 * hidden), BF16),
-            jax.ShapeDtypeStruct((RING // 4, 2 * shard, 2 * hidden), BF16),
-            jax.ShapeDtypeStruct((RING // 2, 2 * shard, 2 * hidden), BF16),
+            jax.ShapeDtypeStruct((slots, features), BF16),
+            whole,
+            whole,
+            whole,
+            half,
+            half,
         ),
+        out_specs=(hbm,) + (pl.BlockSpec(memory_space=pltpu.VMEM),) * 5,
         scratch_shapes=[
             pltpu.VMEM((EXPERTS // PAIR, PAIR * rows, gathered.shape[1]), BF16),
             pltpu.VMEM((features, 3 * hidden), BF16),
             pltpu.VMEM((slots, features), BF16),
             pltpu.VMEM((slots, features), BF16),
+            pltpu.VMEM((slots, 2 * hidden), BF16),
+            pltpu.VMEM((slots, features), BF16),
             pltpu.VMEM((features, 2 * hidden), F32),
             pltpu.SemaphoreType.DMA((EXPERTS // PAIR,)),
             pltpu.SemaphoreType.DMA((2 * RING,)),
+            pltpu.SemaphoreType.DMA((BLOCKS,)),
         ],
         compiler_params=pltpu.CompilerParams(vmem_limit_bytes=48 * 1024 * 1024),
         cost_estimate=pl.CostEstimate(
-            flops=5 * slots * features * 2 * hidden,
+            flops=7 * slots * features * 2 * hidden,
             bytes_accessed=16 * 1024 * 1024,
             transcendentals=slots * hidden,
         ),
         name="expert_work",
     )(gathered, *pieces)
-
-
-def row_kernel(pre_hbm, gate_up_hbm, out_ref, pre_ref, gate_up_ref, sems):
-    copies = [
-        pltpu.make_async_copy(gate_up_hbm, gate_up_ref, sems.at[0]),
-        pltpu.make_async_copy(pre_hbm, pre_ref, sems.at[1]),
-    ]
-    for copy in copies:
-        copy.start()
-    for copy in copies:
-        copy.wait()
-    block = pre_ref.shape[0] // BLOCKS
-    for m in range(BLOCKS):
-        here = pl.ds(m * block, block)
-        out_ref[here, :] = lax.dot_general(
-            pre_ref[here, :],
-            gate_up_ref[...],
-            (((1,), (1,)), ((), ())),
-            preferred_element_type=F32,
-        ).astype(BF16)
-
-
-def row_gradients(pre_grad, gate_up):
-    slots, columns = pre_grad.shape
-    features = gate_up.shape[0]
-    return pl.pallas_call(
-        row_kernel,
-        in_specs=[pl.BlockSpec(memory_space=pltpu.HBM)] * 2,
-        out_shape=jax.ShapeDtypeStruct((slots, features), BF16),
-        scratch_shapes=[
-            pltpu.VMEM((slots, columns), BF16),
-            pltpu.VMEM((features, columns), BF16),
-            pltpu.SemaphoreType.DMA((2,)),
-        ],
-        compiler_params=pltpu.CompilerParams(vmem_limit_bytes=32 * 1024 * 1024),
-        cost_estimate=pl.CostEstimate(
-            flops=2 * slots * features * columns,
-            bytes_accessed=6 * 1024 * 1024,
-            transcendentals=0,
-        ),
-        name="row_gradients",
-    )(pre_grad, gate_up)
 
 
 def combine_kernel(rank_ref, back_ref, out_ref):
@@ -261,7 +238,7 @@
     return pl.pallas_call(
         combine_kernel,
         out_shape=jax.ShapeDtypeStruct((rank.shape[1], back.shape[1]), BF16),
-        compiler_params=pltpu.CompilerParams(vmem_limit_bytes=32 * 1024 * 1024),
+        compiler_params=pltpu.CompilerParams(vmem_limit_bytes=16 * 1024 * 1024),
         name="combine_rows",
     )(rank, back)
 
@@ -275,71 +252,66 @@
     return lax.ppermute(x, "dp", pairs)
 
 
+def shift_across(x, by):
+    pairs = [(d, (d + RING) % (2 * RING) // RING * RING + (d + by) % RING) for d in range(2 * RING)]
+    return lax.ppermute(x, "dp", pairs)
+
+
 def gather_weights(gate_up, down):
     own = jnp.concatenate([gate_up[0], down[0]], axis=1)
     shard = own.shape[0]
-    ahead = behind = jnp.concatenate([own, swap_halves(own)], axis=0)
-    pieces = [ahead]
-    plan = [(0, 0, 0, 0), (0, shard, 0, 1)]
-    for j in range(1, RING // 2):
+    opposite = RING // 2
+    other = swap_halves(own)
+    far_own, far_other = shift_ring(own, opposite), shift_across(own, opposite)
+    both = jnp.concatenate([own, other], axis=0)
+    far = jnp.concatenate([far_own, far_other], axis=0)
+    ahead, behind = shift_ring(both, 1), shift_ring(both, -1)
+    pieces = [both, far, ahead, behind]
+    held = [[0], [opposite], [-1], [1]]
+    ahead, behind = jnp.concatenate([ahead, far], axis=0), jnp.concatenate([behind, far], axis=0)
+    for j in range(2, opposite // 2 + 1):
         ahead, behind = shift_ring(ahead, 1), shift_ring(behind, -1)
-        for piece, offset in ((ahead, -j), (behind, j)):
-            plan += [(len(pieces), part * shard, offset, part) for part in range(2)]
-            pieces.append(piece)
-    plan += [(len(pieces), 0, RING // 2, 0), (len(pieces) + 1, 0, RING // 2, 1)]
-    pieces += [shift_ring(ahead[:shard], 1), shift_ring(behind[shard:], -1)]
+        pieces += [ahead, behind]
+        held += [[-j, opposite + 1 - j], [j, j - 1 - opposite]]
+    plan = [
+        (array, (2 * k + part) * shard, offset, part)
+        for array, offsets in enumerate(held)
+        for k, offset in enumerate(offsets)
+        for part in range(2)
+    ]
     return pieces, plan
 
 
-def first_sum_kernel(keep_ref, plus_ref, minus_ref, up_ref, down_ref, rest_ref):
-    def part(k):
-        value = keep_ref[k].astype(F32)
-        if k < 4:
-            value += plus_ref[k].astype(F32)
-        if k % 8 == 0 or k > 4:
-            value += minus_ref[(8 - k) % 8].astype(F32)
-        return value.astype(BF16)
-
-    up_ref[0], up_ref[1] = part(1), part(3)
-    down_ref[0], down_ref[1] = part(7), part(5)
-    for j in range(4):
-        rest_ref[j] = part(2 * j)
-
-
-def second_sum_kernel(my_dp, rest_ref, up_ref, down_ref, later_ref, out_ref):
+def near_sum_kernel(my_dp, keep_ref, plus_ref, minus_ref, plus2_ref, minus2_ref, later_ref, out_ref):
     del later_ref
     shard = out_ref.shape[1]
     far = (my_dp() % RING) // NEAR
     groups = RING // NEAR
     for j in range(groups):
-        value = rest_ref[j].astype(F32)
-        if j < 2:
-            value += up_ref[j].astype(F32)
-        if j == 0 or j == 3:
-            value += down_ref[(4 - j) % 4].astype(F32)
-        value = value.astype(BF16)
+        value = keep_ref[j].astype(F32) + plus_ref[j].astype(F32) + minus_ref[j].astype(F32)
         target = (far + j) % groups
-        out_ref[target] = value[:shard]
-        out_ref[groups + target] = value[shard:]
-
-
-def scatter_sum(plus, minus, keep, later, scale, my_dp):
+        out_ref[target] = (value[:shard] + plus2_ref[j].astype(F32)).astype(BF16)
+        out_ref[groups + target] = (
+            value[shard:] + minus2_ref[(j - 1) % groups].astype(F32)
+        ).astype(BF16)
+
+
+def scatter_sum(keep, plus, minus, plus2, minus2, later, scale, my_dp):
     unit, columns = keep.shape[1:]
-    got_plus, got_minus = shift_ring(plus, 1), shift_ring(minus, -1)
-    piece = jax.ShapeDtypeStruct((2, unit, columns), BF16)
-    up, down, rest = pl.pallas_call(
-        first_sum_kernel,
-        out_shape=(piece, piece, jax.ShapeDtypeStruct((4, unit, columns), BF16)),
-        name="first_sum",
-    )(keep, got_plus, got_minus)
-    got_up, got_down = shift_ring(up, 2), shift_ring(down, -2)
     parts = pl.pallas_call(
-        functools.partial(second_sum_kernel, my_dp),
+        functools.partial(near_sum_kernel, my_dp),
         out_shape=jax.ShapeDtypeStruct((2 * RING // NEAR, unit // 2, columns), BF16),
-        in_specs=[pl.BlockSpec(memory_space=pltpu.VMEM)] * 3
-        + [pl.BlockSpec(memory_space=pltpu.HBM)],
-        name="second_sum",
-    )(rest, got_up, got_down, later)
+        in_specs=[pl.BlockSpec(memory_space=pltpu.VMEM)] * 5 + [pl.BlockSpec(memory_space=pl.ANY)],
+        compiler_params=pltpu.CompilerParams(vmem_limit_bytes=12 * 1024 * 1024),
+        name="near_sum",
+    )(
+        keep,
+        shift_ring(plus, 1),
+        shift_ring(minus, -1),
+        shift_ring(plus2, 2),
+        shift_ring(minus2, -2),
+        later,
+    )
     groups = [
         [y * RING + far * NEAR + near for y in range(2) for far in range(RING // NEAR)]
         for near in range(NEAR)
@@ -360,15 +332,14 @@
     def my_dp():
         return lax.axis_index("dp")
 
-    pre_grad, full_gate_up, plus, minus, keep = expert_work(
+    row_grads, *grad_parts = expert_work(
         gathered, pieces, plan, features, hidden, lambda: lax.axis_index("expert"), my_dp
     )
-    row_grads = row_gradients(pre_grad, full_gate_up)
     returned = lax.all_to_all(
         row_grads.reshape(EXPERTS, CAP, features), "expert", split_axis=0, concat_axis=0, tiled=True
     )
     grad_scale = 1.0 / math.sqrt(rows * lax.axis_size("dp") * lax.axis_size("expert"))
-    grad_gate_up = scatter_sum(plus, minus, keep, returned, grad_scale, my_dp)
+    grad_gate_up = scatter_sum(*grad_parts, returned, grad_scale, my_dp)
     token_grad = combine(rank, returned.reshape(EXPERTS * CAP, features))
     return (token_grad, grad_gate_up)
 

time: 209 us -> 208 us (level)
  the two profiles are of different devices: /device:TPU:32 before, /device:TPU:1 now
where the time goes in v4:
time: 208 us; the launch traced here: 207 us
  starting transfers between devices  89.5 us (43%)
  waiting for transfers between devices  67 us (32%)
  Pallas kernels  20.6 us (10%)
  between operations  14.2 us (7%)
  local copies, waits for them, and re-layouts  12.8 us (6%)
  other arithmetic  2.41 us (1%)
    ppermute x13, starting transfers between devices, shift_ring(): return lax.ppermute(x, 'dp', pairs)  51 us
    all_to_all x1, waiting for transfers between devices, scatter_sum(): lax.all_to_all(parts, 'dp', split_axis=0, concat_axis=0, axis_index_group...  23.5 us
    ppermute x13, waiting for transfers between devices, shift_ring(): return lax.ppermute(x, 'dp', pairs)  22.5 us
    pallas_call x1, Pallas kernels, expert_work(): pl.pallas_call(functools.partial(expert_kernel, my_expert, my_dp, plan, f...  17.3 us
    all_to_all x1, starting transfers between devices, shards(): lax.all_to_all(row_grads.reshape(EXPERTS, CAP, features), 'expert', split...  15.6 us
    unnamed x32, local copies, waits for them, and re-layouts  12.8 us
    all_to_all x1, waiting for transfers between devices, shards(): lax.all_to_all(row_grads.reshape(EXPERTS, CAP, features), 'expert', split...  10.2 us
    ppermute x1, waiting for transfers between devices, shift_across(): return lax.ppermute(x, 'dp', pairs)  9.06 us
  transfers between devices with their start and end apart: 18, of which 11 were waited for; matrix products, arithmetic and copies ran while one was open for 1% of the time, Pallas kernels for 1%

profile of v4, /device:TPU:1, one launch (start us, length us, event | category | flops | bytes accessed | tf_op | source)
XLA Modules:
  0.0 206.5 jit_solution(14521052356123072370)
XLA Ops:
  12.3 5.6 %collective-permute-start = (bf16[32,1152]{1,0:T(8,128)(2,1)S(1)}, bf16[32,1152]{1,0:T(8,128)(2,1)S(1)}, u32[]{:S(2)}, u32[]{:S(2)}) collective-permute-start(bf16[32,1152]{1,0:T(8,128)(2,1)S(1)} %pad_maximum_fusion.6), channel_id=1, source_target_pairs={{0,256},{16,272},{32,288},{48,304},{64,320},{80,336},{96,352},{112... | collective-permute-start | bytes 221192 | tf_op jit(solution)/shard_map/ppermute | solution.py:247
  20.5 11.2 %collective-permute-start.4 = (bf16[64,1152]{1,0:T(8,128)(2,1)S(1)}, bf16[64,1152]{1,0:T(8,128)(2,1)S(1)}, u32[]{:S(2)}, u32[]{:S(2)}) collective-permute-start(bf16[64,1152]{1,0:T(8,128)(2,1)S(1)} %pad_maximum_fusion.4.refs_0_), channel_id=1, source_target_pairs={{0,240},{16,0},{32,16},{48,32},{64,48},{80,64},{96,80},{112,96},{1... | collective-permute-start | bytes 442376 | tf_op jit(solution)/shard_map/ppermute | solution.py:252
  31.7 1.9 collective-permute-start.3
  33.6 7.7 %collective-permute-start.1 = (bf16[32,1152]{1,0:T(8,128)(2,1)S(1)}, bf16[32,1152]{1,0:T(8,128)(2,1)S(1)}, u32[]{:S(2)}, u32[]{:S(2)}) collective-permute-start(bf16[32,1152]{1,0:T(8,128)(2,1)S(1)} %pad_maximum_fusion.6), channel_id=1, source_target_pairs={{0,128},{16,144},{32,160},{48,176},{64,192},{80,208},{96,224},{112... | collective-permute-start | bytes 221192 | tf_op jit(solution)/shard_map/ppermute | solution.py:252
  41.3 8.9 %collective-permute-start.2 = (bf16[32,1152]{1,0:T(8,128)(2,1)S(1)}, bf16[32,1152]{1,0:T(8,128)(2,1)S(1)}, u32[]{:S(2)}, u32[]{:S(2)}) collective-permute-start(bf16[32,1152]{1,0:T(8,128)(2,1)S(1)} %pad_maximum_fusion.6), channel_id=1, source_target_pairs={{0,384},{16,400},{32,416},{48,432},{64,448},{80,464},{96,480},{112... | collective-permute-start | bytes 221192 | tf_op jit(solution)/shard_map/ppermute | solution.py:257
  50.2 9.1 %collective-permute-done.2 = bf16[32,1152]{1,0:T(8,128)(2,1)S(1)} collective-permute-done((bf16[32,1152]{1,0:T(8,128)(2,1)S(1)}, bf16[32,1152]{1,0:T(8,128)(2,1)S(1)}, u32[]{:S(2)}, u32[]{:S(2)}) %collective-permute-start.2) | collective-permute-done | bytes 73760 | tf_op jit(solution)/shard_map/ppermute | solution.py:257
  59.4 1.9 collective-permute-start.6
  61.3 3.4 %collective-permute-start.5 = (bf16[128,1152]{1,0:T(8,128)(2,1)S(1)}, bf16[128,1152]{1,0:T(8,128)(2,1)S(1)}, u32[]{:S(2)}, u32[]{:S(2)}) collective-permute-start(bf16[128,1152]{1,0:T(8,128)(2,1)S(1)} %get-tuple-element.19), channel_id=1, source_target_pairs={{0,16},{16,32},{32,48},{48,64},{64,80},{80,96},{96,112},{112,128},... | collective-permute-start | bytes 884744 | tf_op jit(solution)/shard_map/ppermute | solution.py:252
  64.7 2.6 %collective-permute-done.6.refs_5_ = bf16[128,1152]{1,0:T(8,128)(2,1)S(1)} collective-permute-done((bf16[128,1152]{1,0:T(8,128)(2,1)S(1)}, bf16[128,1152]{1,0:T(8,128)(2,1)S(1)}, u32[]{:S(2)}, u32[]{:S(2)}) %collective-permute-start.6) | collective-permute-done | bytes 294944 | tf_op jit(solution)/shard_map/ppermute | solution.py:252
  67.2 2.7 %collective-permute-start.8 = (bf16[128,1152]{1,0:T(8,128)(2,1)S(1)}, bf16[128,1152]{1,0:T(8,128)(2,1)S(1)}, u32[]{:S(2)}, u32[]{:S(2)}) collective-permute-start(bf16[128,1152]{1,0:T(8,128)(2,1)S(1)} %collective-permute-done.6.refs_5_), channel_id=1, source_target_pairs={{0,240},{16,0},{32,16},{48,32},{64,48},{80,64},{96,80},{112,96},{1... | collective-permute-start | bytes 884744 | tf_op jit(solution)/shard_map/ppermute | solution.py:252
  70.0 2.6 %collective-permute-start.7 = (bf16[128,1152]{1,0:T(8,128)(2,1)S(1)}, bf16[128,1152]{1,0:T(8,128)(2,1)S(1)}, u32[]{:S(2)}, u32[]{:S(2)}) collective-permute-start(bf16[128,1152]{1,0:T(8,128)(2,1)S(1)} %collective-permute-done.5.refs_4_), channel_id=1, source_target_pairs={{0,16},{16,32},{32,48},{48,64},{64,80},{80,96},{96,112},{112,128},... | collective-permute-start | bytes 884744 | tf_op jit(solution)/shard_map/ppermute | solution.py:252
  72.5 2.6 %collective-permute-done.8.refs_7_ = bf16[128,1152]{1,0:T(8,128)(2,1)S(1)} collective-permute-done((bf16[128,1152]{1,0:T(8,128)(2,1)S(1)}, bf16[128,1152]{1,0:T(8,128)(2,1)S(1)}, u32[]{:S(2)}, u32[]{:S(2)}) %collective-permute-start.8) | collective-permute-done | bytes 294944 | tf_op jit(solution)/shard_map/ppermute | solution.py:252
  75.1 3.9 %collective-permute-start.10 = (bf16[128,1152]{1,0:T(8,128)(2,1)S(1)}, bf16[128,1152]{1,0:T(8,128)(2,1)S(1)}, u32[]{:S(2)}, u32[]{:S(2)}) collective-permute-start(bf16[128,1152]{1,0:T(8,128)(2,1)S(1)} %collective-permute-done.8.refs_7_), channel_id=1, source_target_pairs={{0,240},{16,0},{32,16},{48,32},{64,48},{80,64},{96,80},{112,96},{1... | collective-permute-start | bytes 884744 | tf_op jit(solution)/shard_map/ppermute | solution.py:252
  81.2 2.9 %collective-permute-done.10.refs_9_ = bf16[128,1152]{1,0:T(8,128)(2,1)S(1)} collective-permute-done((bf16[128,1152]{1,0:T(8,128)(2,1)S(1)}, bf16[128,1152]{1,0:T(8,128)(2,1)S(1)}, u32[]{:S(2)}, u32[]{:S(2)}) %collective-permute-start.10) | collective-permute-done | bytes 294944 | tf_op jit(solution)/shard_map/ppermute | solution.py:252
  84.1 5.6 %collective-permute-done.9.refs_8_ = bf16[128,1152]{1,0:T(8,128)(2,1)S(1)} collective-permute-done((bf16[128,1152]{1,0:T(8,128)(2,1)S(1)}, bf16[128,1152]{1,0:T(8,128)(2,1)S(1)}, u32[]{:S(2)}, u32[]{:S(2)}) %collective-permute-start.9) | collective-permute-done | bytes 294944 | tf_op jit(solution)/shard_map/ppermute | solution.py:252
  91.3 17.3 %expert_work.1 = (bf16[1280,1024]{1,0:T(8,128)(2,1)}, bf16[4,64,768]{2,1,0:T(8,128)(2,1)S(1)}, bf16[4,64,768]{2,1,0:T(8,128)(2,1)S(1)}, bf16[4,64,768]{2,1,0:T(8...) custom-call(bf16[2048,2176]{1,0:T(8,128)(2,1)} %all-gather.2.cloned.1.call-done.g_ref, ...), custom_call_target="tpu_custom_call" | custom-call | flops 7046430720 | bytes 16777216 | tf_op jit(solution)/shard_map/expert_work/pallas_call | solution.py:189
  111.5 15.6 %all-to-all-start = ((bf16[16,80,1024]{2,1,0:T(8,128)(2,1)}), bf16[16,80,1024]{2,1,0:T(8,128)(2,1)S(1)}, u32[]{:S(2)}, u32[]{:S(2)}) async-start(bf16[16,80,1024]{2,1,0:T(8,128)(2,1)} %bitcast.11), calls=%async_computation | async-start | bytes 5242880 | tf_op jit(solution)/shard_map/all_to_all | solution.py:338
  129.0 4.6 %collective-permute-start.12 = (bf16[4,64,768]{2,1,0:T(8,128)(2,1)}, bf16[4,64,768]{2,1,0:T(8,128)(2,1)S(1)}, u32[]{:S(2)}, u32[]{:S(2)}) collective-permute-start(bf16[4,64,768]{2,1,0:T(8,128)(2,1)} %copy-done.10), channel_id=1, source_target_pairs={{0,240},{16,0},{32,16},{48,32},{64,48},{80,64},{96,80},{112,96},{1... | collective-permute-start | bytes 1179656 | tf_op jit(solution)/shard_map/ppermute | solution.py:252
  135.6 5.5 %collective-permute-start.14 = (bf16[4,32,768]{2,1,0:T(8,128)(2,1)}, bf16[4,32,768]{2,1,0:T(8,128)(2,1)S(1)}, u32[]{:S(2)}, u32[]{:S(2)}) collective-permute-start(bf16[4,32,768]{2,1,0:T(8,128)(2,1)} %copy-done.14), channel_id=1, source_target_pairs={{0,224},{16,240},{32,0},{48,16},{64,32},{80,48},{96,64},{112,80},{... | collective-permute-start | bytes 589832 | tf_op jit(solution)/shard_map/ppermute | solution.py:252
  141.0 6.5 %collective-permute-done.13.plus2_ref = bf16[4,32,768]{2,1,0:T(8,128)(2,1)S(1)} collective-permute-done((bf16[4,32,768]{2,1,0:T(8,128)(2,1)}, bf16[4,32,768]{2,1,0:T(8,128)(2,1)S(1)}, u32[]{:S(2)}, u32[]{:S(2)}) %collective-permute-start.13) | collective-permute-done | bytes 196640 | tf_op jit(solution)/shard_map/ppermute | solution.py:252
  148.2 2.2 %collective-permute-done.14.minus2_ref = bf16[4,32,768]{2,1,0:T(8,128)(2,1)S(1)} collective-permute-done((bf16[4,32,768]{2,1,0:T(8,128)(2,1)}, bf16[4,32,768]{2,1,0:T(8,128)(2,1)S(1)}, u32[]{:S(2)}, u32[]{:S(2)}) %collective-permute-start.14) | collective-permute-done | bytes 196640 | tf_op jit(solution)/shard_map/ppermute | solution.py:252
  151.8 10.2 %all-to-all-done.later_ref = bf16[16,80,1024]{2,1,0:T(8,128)(2,1)S(1)} async-done(((bf16[16,80,1024]{2,1,0:T(8,128)(2,1)}), bf16[16,80,1024]{2,1,0:T(8,128)(2,1)S(1)}, u32[]{:S(2)}, u32[]{:S(2)}) %all-to-all-start) | async-done | bytes 2621472 | tf_op jit(solution)/shard_map/all_to_all | solution.py:338
  165.8 8.3 %all-to-all-start.1 = ((bf16[8,32,768]{2,1,0:T(8,128)(2,1)}), bf16[8,32,768]{2,1,0:T(8,128)(2,1)S(1)}, u32[]{:S(2)}, u32[]{:S(2)}) async-start(bf16[8,32,768]{2,1,0:T(8,128)(2,1)} %near_sum.1), calls=%async_computation.1 | async-start | bytes 786432 | tf_op jit(solution)/shard_map/all_to_all | solution.py:319
  175.5 23.5 %all-to-all-done.1 = bf16[8,32,768]{2,1,0:T(8,128)(2,1)S(1)} async-done(((bf16[8,32,768]{2,1,0:T(8,128)(2,1)}), bf16[8,32,768]{2,1,0:T(8,128)(2,1)S(1)}, u32[]{:S(2)}, u32[]{:S(2)}) %all-to-all-start.1) | async-done | bytes 393248 | tf_op jit(solution)/shard_map/all_to_all | solution.py:319
  (55 shorter events, 26.3 us)
Async XLA Ops:
  7.2 83.2 %all-gather.2.cloned.1.call-start = ((), (), s32[]{:S(2)}) async-start(), calls=%async_computation.2 | async-start | bytes 9469952 | tf_op jit(solution)/shard_map/all_gather | solution.py:329
  7.2 1.0 copy-start.2
  8.2 0.9 copy-start.3
  12.3 7.4 %collective-permute-start = (bf16[32,1152]{1,0:T(8,128)(2,1)S(1)}, bf16[32,1152]{1,0:T(8,128)(2,1)S(1)}, u32[]{:S(2)}, u32[]{:S(2)}) collective-permute-start(bf16[32,1152]{1,0:T(8,128)(2,1)S(1)} %pad_maximum_fusion.6), channel_id=1, source_target_pairs={{0,256},{16,272},{32,288},{48,304},{64,320},{80,336},{96,352},{112... | collective-permute-start | bytes 221192 | tf_op jit(solution)/shard_map/ppermute | solution.py:247
  20.5 38.8 %collective-permute-start.4 = (bf16[64,1152]{1,0:T(8,128)(2,1)S(1)}, bf16[64,1152]{1,0:T(8,128)(2,1)S(1)}, u32[]{:S(2)}, u32[]{:S(2)}) collective-permute-start(bf16[64,1152]{1,0:T(8,128)(2,1)S(1)} %pad_maximum_fusion.4.refs_0_), channel_id=1, source_target_pairs={{0,240},{16,0},{32,16},{48,32},{64,48},{80,64},{96,80},{112,96},{1... | collective-permute-start | bytes 442376 | tf_op jit(solution)/shard_map/ppermute | solution.py:252
  31.7 27.6 %collective-permute-start.3 = (bf16[64,1152]{1,0:T(8,128)(2,1)S(1)}, bf16[64,1152]{1,0:T(8,128)(2,1)S(1)}, u32[]{:S(2)}, u32[]{:S(2)}) collective-permute-start(bf16[64,1152]{1,0:T(8,128)(2,1)S(1)} %pad_maximum_fusion.4.refs_0_), channel_id=1, source_target_pairs={{0,16},{16,32},{32,48},{48,64},{64,80},{80,96},{96,112},{112,128},... | collective-permute-start | bytes 442376 | tf_op jit(solution)/shard_map/ppermute | solution.py:252
  33.6 16.6 %collective-permute-start.1 = (bf16[32,1152]{1,0:T(8,128)(2,1)S(1)}, bf16[32,1152]{1,0:T(8,128)(2,1)S(1)}, u32[]{:S(2)}, u32[]{:S(2)}) collective-permute-start(bf16[32,1152]{1,0:T(8,128)(2,1)S(1)} %pad_maximum_fusion.6), channel_id=1, source_target_pairs={{0,128},{16,144},{32,160},{48,176},{64,192},{80,208},{96,224},{112... | collective-permute-start | bytes 221192 | tf_op jit(solution)/shard_map/ppermute | solution.py:252
  41.3 18.0 %collective-permute-start.2 = (bf16[32,1152]{1,0:T(8,128)(2,1)S(1)}, bf16[32,1152]{1,0:T(8,128)(2,1)S(1)}, u32[]{:S(2)}, u32[]{:S(2)}) collective-permute-start(bf16[32,1152]{1,0:T(8,128)(2,1)S(1)} %pad_maximum_fusion.6), channel_id=1, source_target_pairs={{0,384},{16,400},{32,416},{48,432},{64,448},{80,464},{96,480},{112... | collective-permute-start | bytes 221192 | tf_op jit(solution)/shard_map/ppermute | solution.py:257
  59.4 7.9 %collective-permute-start.6 = (bf16[128,1152]{1,0:T(8,128)(2,1)S(1)}, bf16[128,1152]{1,0:T(8,128)(2,1)S(1)}, u32[]{:S(2)}, u32[]{:S(2)}) collective-permute-start(bf16[128,1152]{1,0:T(8,128)(2,1)S(1)} %get-tuple-element.18), channel_id=1, source_target_pairs={{0,240},{16,0},{32,16},{48,32},{64,48},{80,64},{96,80},{112,96},{1... | collective-permute-start | bytes 884744 | tf_op jit(solution)/shard_map/ppermute | solution.py:252
  61.3 8.7 %collective-permute-start.5 = (bf16[128,1152]{1,0:T(8,128)(2,1)S(1)}, bf16[128,1152]{1,0:T(8,128)(2,1)S(1)}, u32[]{:S(2)}, u32[]{:S(2)}) collective-permute-start(bf16[128,1152]{1,0:T(8,128)(2,1)S(1)} %get-tuple-element.19), channel_id=1, source_target_pairs={{0,16},{16,32},{32,48},{48,64},{64,80},{80,96},{96,112},{112,128},... | collective-permute-start | bytes 884744 | tf_op jit(solution)/shard_map/ppermute | solution.py:252
  67.2 7.9 %collective-permute-start.8 = (bf16[128,1152]{1,0:T(8,128)(2,1)S(1)}, bf16[128,1152]{1,0:T(8,128)(2,1)S(1)}, u32[]{:S(2)}, u32[]{:S(2)}) collective-permute-start(bf16[128,1152]{1,0:T(8,128)(2,1)S(1)} %collective-permute-done.6.refs_5_), channel_id=1, source_target_pairs={{0,240},{16,0},{32,16},{48,32},{64,48},{80,64},{96,80},{112,96},{1... | collective-permute-start | bytes 884744 | tf_op jit(solution)/shard_map/ppermute | solution.py:252
  70.0 9.3 %collective-permute-start.7 = (bf16[128,1152]{1,0:T(8,128)(2,1)S(1)}, bf16[128,1152]{1,0:T(8,128)(2,1)S(1)}, u32[]{:S(2)}, u32[]{:S(2)}) collective-permute-start(bf16[128,1152]{1,0:T(8,128)(2,1)S(1)} %collective-permute-done.5.refs_4_), channel_id=1, source_target_pairs={{0,16},{16,32},{32,48},{48,64},{64,80},{80,96},{96,112},{112,128},... | collective-permute-start | bytes 884744 | tf_op jit(solution)/shard_map/ppermute | solution.py:252
  75.1 9.0 %collective-permute-start.10 = (bf16[128,1152]{1,0:T(8,128)(2,1)S(1)}, bf16[128,1152]{1,0:T(8,128)(2,1)S(1)}, u32[]{:S(2)}, u32[]{:S(2)}) collective-permute-start(bf16[128,1152]{1,0:T(8,128)(2,1)S(1)} %collective-permute-done.8.refs_7_), channel_id=1, source_target_pairs={{0,240},{16,0},{32,16},{48,32},{64,48},{80,64},{96,80},{112,96},{1... | collective-permute-start | bytes 884744 | tf_op jit(solution)/shard_map/ppermute | solution.py:252
  79.3 10.4 %collective-permute-start.9 = (bf16[128,1152]{1,0:T(8,128)(2,1)S(1)}, bf16[128,1152]{1,0:T(8,128)(2,1)S(1)}, u32[]{:S(2)}, u32[]{:S(2)}) collective-permute-start(bf16[128,1152]{1,0:T(8,128)(2,1)S(1)} %collective-permute-done.7.refs_6_), channel_id=1, source_target_pairs={{0,16},{16,32},{32,48},{48,64},{64,80},{80,96},{96,112},{112,128},... | collective-permute-start | bytes 884744 | tf_op jit(solution)/shard_map/ppermute | solution.py:252
  90.4 1.0 copy-start.13
  111.5 50.4 %all-to-all-start = ((bf16[16,80,1024]{2,1,0:T(8,128)(2,1)}), bf16[16,80,1024]{2,1,0:T(8,128)(2,1)S(1)}, u32[]{:S(2)}, u32[]{:S(2)}) async-start(bf16[16,80,1024]{2,1,0:T(8,128)(2,1)} %bitcast.11), calls=%async_computation | async-start | bytes 5242880 | tf_op jit(solution)/shard_map/all_to_all | solution.py:338
  127.1 23.9 %collective-permute-start.11 = (bf16[4,64,768]{2,1,0:T(8,128)(2,1)}, bf16[4,64,768]{2,1,0:T(8,128)(2,1)S(1)}, u32[]{:S(2)}, u32[]{:S(2)}) collective-permute-start(bf16[4,64,768]{2,1,0:T(8,128)(2,1)} %copy-done.11), channel_id=1, source_target_pairs={{0,16},{16,32},{32,48},{48,64},{64,80},{80,96},{96,112},{112,128},... | collective-permute-start | bytes 1179656 | tf_op jit(solution)/shard_map/ppermute | solution.py:252
  129.0 22.0 %collective-permute-start.12 = (bf16[4,64,768]{2,1,0:T(8,128)(2,1)}, bf16[4,64,768]{2,1,0:T(8,128)(2,1)S(1)}, u32[]{:S(2)}, u32[]{:S(2)}) collective-permute-start(bf16[4,64,768]{2,1,0:T(8,128)(2,1)} %copy-done.10), channel_id=1, source_target_pairs={{0,240},{16,0},{32,16},{48,32},{64,48},{80,64},{96,80},{112,96},{1... | collective-permute-start | bytes 1179656 | tf_op jit(solution)/shard_map/ppermute | solution.py:252
  133.6 13.9 %collective-permute-start.13 = (bf16[4,32,768]{2,1,0:T(8,128)(2,1)}, bf16[4,32,768]{2,1,0:T(8,128)(2,1)S(1)}, u32[]{:S(2)}, u32[]{:S(2)}) collective-permute-start(bf16[4,32,768]{2,1,0:T(8,128)(2,1)} %copy-done.15), channel_id=1, source_target_pairs={{0,32},{16,48},{32,64},{48,80},{64,96},{80,112},{96,128},{112,144}... | collective-permute-start | bytes 589832 | tf_op jit(solution)/shard_map/ppermute | solution.py:252
  135.6 14.8 %collective-permute-start.14 = (bf16[4,32,768]{2,1,0:T(8,128)(2,1)}, bf16[4,32,768]{2,1,0:T(8,128)(2,1)S(1)}, u32[]{:S(2)}, u32[]{:S(2)}) collective-permute-start(bf16[4,32,768]{2,1,0:T(8,128)(2,1)} %copy-done.14), channel_id=1, source_target_pairs={{0,224},{16,240},{32,0},{48,16},{64,32},{80,48},{96,64},{112,80},{... | collective-permute-start | bytes 589832 | tf_op jit(solution)/shard_map/ppermute | solution.py:252
  162.0 1.0 copy-start.1
  163.0 0.9 copy-start.5
  163.9 0.9 copy-start.7
  165.8 33.2 %all-to-all-start.1 = ((bf16[8,32,768]{2,1,0:T(8,128)(2,1)}), bf16[8,32,768]{2,1,0:T(8,128)(2,1)S(1)}, u32[]{:S(2)}, u32[]{:S(2)}) async-start(bf16[8,32,768]{2,1,0:T(8,128)(2,1)} %near_sum.1), calls=%async_computation.1 | async-start | bytes 786432 | tf_op jit(solution)/shard_map/all_to_all | solution.py:319
  (10 other events, 7.1 us)
Sparse Core Ops, SparseCore 0:
  11.6 69.5 all-gather.1

commit v5 on v4

v5 whole, which is shorter than its diff:
```python
import functools
import math

import jax
import jax.numpy as jnp
from jax import lax
from jax.experimental import pallas as pl
from jax.experimental.pallas import tpu as pltpu
from jax.sharding import PartitionSpec as P

EXPERTS = 16
CAP = 80
LANES = 128
RING = 16
NEAR = 4
PAIR = 2
BLOCKS = 4
UNROUTED = 200.0
MIB = 1024 * 1024
VMEM_BYTES = 60 * MIB
HBM = pl.BlockSpec(memory_space=pltpu.HBM)
VMEM = pl.BlockSpec(memory_space=pltpu.VMEM)
BF16 = jnp.bfloat16
F32 = jnp.float32


def iota(shape, dim):
    return lax.broadcasted_iota(jnp.int32, shape, dim)


def as_bf16(mask):
    return jnp.where(mask, 1.0, 0.0).astype(BF16)


def pack_kernel(tok_hbm, cot_hbm, experts_ref, weights_ref, packed_hbm, rank_ref, table_ref, sems):
    rows, features = tok_hbm.shape
    copies = [
        pltpu.make_async_copy(tok_hbm, packed_hbm.at[:, pl.ds(0, features)], sems.at[0]),
        pltpu.make_async_copy(cot_hbm, packed_hbm.at[:, pl.ds(features, features)], sems.at[1]),
        pltpu.make_async_copy(table_ref, packed_hbm.at[:, pl.ds(2 * features, rows)], sems.at[2]),
    ]
    copies[0].start()
    copies[1].start()
    label = iota((EXPERTS, rows), 0)
    dense = jnp.zeros((EXPERTS, rows), F32)
    for k in range(experts_ref.shape[0]):
        dense += jnp.where(experts_ref[k : k + 1, :] == label, weights_ref[k : k + 1, :], 0.0)
    routed = dense > 0.0
    before = as_bf16(iota((rows, rows), 0) < iota((rows, rows), 1))
    rank = jnp.dot(as_bf16(routed), before, preferred_element_type=F32)
    rank = jnp.where(routed, rank, UNROUTED).astype(BF16)
    high = dense.astype(BF16)
    low = (dense - high.astype(F32)).astype(BF16)
    rest = jnp.zeros((rows - 3 * EXPERTS, rows), BF16)
    table_ref[...] = jnp.concatenate([high, low, rank, rest], axis=0)
    copies[2].start()
    rank_ref[...] = rank
    for copy in copies:
        copy.wait()


def pack(tokens, cotangent, route_experts, route_weights):
    rows, features = tokens.shape
    return pl.pallas_call(
        pack_kernel,
        in_specs=[HBM, HBM, VMEM, VMEM],
        out_specs=(HBM, VMEM),
        out_shape=(
            jax.ShapeDtypeStruct((rows, 2 * features + rows), BF16),
            jax.ShapeDtypeStruct((EXPERTS, rows), BF16),
        ),
        scratch_shapes=[pltpu.VMEM((rows, rows), BF16), pltpu.SemaphoreType.DMA((3,))],
        compiler_params=pltpu.CompilerParams(vmem_limit_bytes=VMEM_BYTES),
        name="pack_rows",
    )(tokens, cotangent, route_experts.T, route_weights.T)


def compact_kernel(my_expert, features, g_hbm, inputs_hbm, cots_hbm, blocks, inputs, cots, *sems):
    expert = my_expert()
    pair_total, pair_rows = blocks.shape[:2]
    rows = pair_rows // PAIR
    slots = PAIR * CAP
    loads = [
        pltpu.make_async_copy(
            g_hbm.at[pl.ds(p * pair_rows, pair_rows), :], blocks.at[p], sems[0].at[p]
        )
        for p in range(pair_total)
    ]
    for copy in loads:
        copy.start()
    slot = iota((slots, pair_rows), 0).astype(F32)
    label = iota((3 * EXPERTS, rows), 0)
    stores = []
    for p in range(pair_total):
        loads[p].wait()
        ranks, scales = [], []
        for s in range(PAIR):
            table = blocks[p, s * rows : s * rows + 3 * EXPERTS, 2 * features :].astype(F32)

            def line(k):
                return jnp.sum(
                    jnp.where(label == expert + k * EXPERTS, table, 0.0), axis=0, keepdims=True
                )

            scales.append(line(0) + line(1))
            ranks.append(line(2) + float(s * CAP))
        hit = slot == jnp.concatenate(ranks, axis=1)
        scale = jnp.sum(
            jnp.where(hit, jnp.concatenate(scales, axis=1), 0.0), axis=1, keepdims=True
        )
        pick = as_bf16(hit)
        here = pl.ds(p * slots, slots)
        inputs[here, :] = jnp.dot(
            pick, blocks[p, :, :features], preferred_element_type=F32
        ).astype(BF16)
        cots[here, :] = (
            scale
            * jnp.dot(pick, blocks[p, :, features : 2 * features], preferred_element_type=F32)
        ).astype(BF16)
        stores += [
            pltpu.make_async_copy(inputs.at[here, :], inputs_hbm.at[here, :], sems[1].at[2 * p]),
            pltpu.make_async_copy(cots.at[here, :], cots_hbm.at[here, :], sems[1].at[2 * p + 1]),
        ]
        for copy in stores[-2:]:
            copy.start()
    for copy in stores:
        copy.wait()


def compact(gathered, features, my_expert):
    rows = gathered.shape[0] // EXPERTS
    rows_out = jax.ShapeDtypeStruct((EXPERTS * CAP, features), BF16)
    pairs = EXPERTS // PAIR
    return pl.pallas_call(
        functools.partial(compact_kernel, my_expert, features),
        in_specs=[HBM],
        out_specs=(HBM, HBM),
        out_shape=(rows_out, rows_out),
        scratch_shapes=[
            pltpu.VMEM((pairs, PAIR * rows, gathered.shape[1]), BF16),
            pltpu.VMEM((EXPERTS * CAP, features), BF16),
            pltpu.VMEM((EXPERTS * CAP, features), BF16),
            pltpu.SemaphoreType.DMA((pairs,)),
            pltpu.SemaphoreType.DMA((2 * pairs,)),
        ],
        compiler_params=pltpu.CompilerParams(vmem_limit_bytes=VMEM_BYTES),
        cost_estimate=pl.CostEstimate(
            flops=4 * EXPERTS * CAP * PAIR * rows * features,
            bytes_accessed=16 * MIB,
            transcendentals=0,
        ),
        name="compact_rows",
    )(gathered)


def expert_kernel(my_dp, plan, x_hbm, c_hbm, *refs):
    piece_total = 1 + max(array for array, _, _, _ in plan)
    pieces = refs[:piece_total]
    pre_hbm, gate_up_hbm, *parts_hbm = refs[piece_total : piece_total + 7]
    weights, gate_up, inputs, cots, pre_grad, total, *parts = refs[piece_total + 7 : -4]
    load_sems, weight_sems, pre_sems, out_sems = refs[-4:]
    features, hidden = inputs.shape[1], gate_up.shape[1] // 2
    dp = my_dp()
    upper = dp // RING
    place = dp % RING
    half = features // 2
    shard = half // RING
    block_rows = inputs.shape[0] // BLOCKS

    def rows_of(m):
        return pl.ds(m * block_rows, block_rows)

    def first_row(owner, offset):
        return pl.multiple_of(owner * half + ((place + offset + RING) % RING) * shard, shard)

    loads = []
    for m in range(BLOCKS):
        here = rows_of(m)
        loads += [
            pltpu.make_async_copy(x_hbm.at[here, :], inputs.at[here, :], load_sems.at[2 * m]),
            pltpu.make_async_copy(c_hbm.at[here, :], cots.at[here, :], load_sems.at[2 * m + 1]),
        ]
    weight_loads = []
    for array, source, offset, part in plan:
        owner = upper if part == 0 else 1 - upper
        weight_loads.append(
            pltpu.make_async_copy(
                pieces[array].at[pl.ds(source, shard), :],
                weights.at[pl.ds(first_row(owner, offset), shard), :],
                weight_sems.at[len(weight_loads)],
            )
        )
    for copy in loads[:2] + weight_loads + loads[2:]:
        copy.start()
    for copy in weight_loads:
        copy.wait()
    gate_up[...] = weights[:, : 2 * hidden]
    stores = [pltpu.make_async_copy(gate_up, gate_up_hbm, out_sems.at[0])]
    stores[0].start()
    for m in range(BLOCKS):
        here = rows_of(m)
        loads[2 * m].wait()
        loads[2 * m + 1].wait()
        projected = jnp.dot(inputs[here, :], gate_up[...], preferred_element_type=F32)
        hidden_grad = jnp.dot(cots[here, :], weights[:, 2 * hidden :], preferred_element_type=F32)
        gate_part = projected[:, :hidden]
        up_part = projected[:, hidden:]
        sigmoid_gate = jax.nn.sigmoid(gate_part)
        grad_gate = hidden_grad * up_part * sigmoid_gate * (1.0 + gate_part * (1.0 - sigmoid_gate))
        grad_up = hidden_grad * gate_part * sigmoid_gate
        pre_grad[here, :hidden] = grad_gate.astype(BF16)
        pre_grad[here, hidden:] = grad_up.astype(BF16)
        stores.append(
            pltpu.make_async_copy(pre_grad.at[here, :], pre_hbm.at[here, :], pre_sems.at[m])
        )
        stores[-1].start()

    strip = features // BLOCKS
    for c in range(BLOCKS):
        total[c * strip : (c + 1) * strip, :] = lax.dot_general(
            inputs[:, c * strip : (c + 1) * strip],
            pre_grad[...],
            (((0,), (0,)), ((), ())),
            preferred_element_type=F32,
        )

    def part(owner, offset):
        return total[pl.ds(first_row(owner, offset), shard), :].astype(BF16)

    keep, plus, minus, plus2, minus2 = parts
    for j in range(RING // NEAR):
        for ref, offset in ((keep, 0), (plus, 1), (minus, -1)):
            for owner in range(2):
                ref[j, owner * shard : (owner + 1) * shard, :] = part(owner, NEAR * j + offset)
        plus2[j] = part(0, NEAR * j + 2)
        minus2[j] = part(1, NEAR * j + 2)
    for k, (ref, hbm) in enumerate(zip(parts, parts_hbm)):
        stores.append(pltpu.make_async_copy(ref, hbm, out_sems.at[1 + k]))
        stores[-1].start()
    for copy in stores:
        copy.wait()


def expert_work(inputs, cots, pieces, plan, hidden, my_dp):
    slots, features = inputs.shape
    shard = features // (2 * RING)
    whole = (RING // NEAR, 2 * shard, 2 * hidden)
    half = (RING // NEAR, shard, 2 * hidden)
    parts = [whole, whole, whole, half, half]
    out_shapes = [(slots, 2 * hidden), (features, 2 * hidden)] + parts
    return pl.pallas_call(
        functools.partial(expert_kernel, my_dp, plan),
        in_specs=[HBM] * (2 + len(pieces)),
        out_specs=(HBM,) * len(out_shapes),
        out_shape=tuple(jax.ShapeDtypeStruct(shape, BF16) for shape in out_shapes),
        scratch_shapes=[
            pltpu.VMEM((features, 3 * hidden), BF16),
            pltpu.VMEM((features, 2 * hidden), BF16),
            pltpu.VMEM((slots, features), BF16),
            pltpu.VMEM((slots, features), BF16),
            pltpu.VMEM((slots, 2 * hidden), BF16),
            pltpu.VMEM((features, 2 * hidden), F32),
            *[pltpu.VMEM(shape, BF16) for shape in parts],
            pltpu.SemaphoreType.DMA((2 * BLOCKS,)),
            pltpu.SemaphoreType.DMA((2 * RING,)),
            pltpu.SemaphoreType.DMA((BLOCKS,)),
            pltpu.SemaphoreType.DMA((1 + len(parts),)),
        ],
        compiler_params=pltpu.CompilerParams(vmem_limit_bytes=52 * MIB),
        cost_estimate=pl.CostEstimate(
            flops=5 * slots * features * 2 * hidden,
            bytes_accessed=16 * MIB,
            transcendentals=slots * hidden,
        ),
        name="expert_work",
    )(inputs, cots, *pieces)


def row_kernel(pre_hbm, gate_up_hbm, row_hbm, pre_grad, gate_up, row_grad, sems):
    block = pre_grad.shape[0] // BLOCKS
    loads = [pltpu.make_async_copy(gate_up_hbm, gate_up, sems.at[0])]
    stores = []
    for m in range(BLOCKS):
        here = pl.ds(m * block, block)
        loads.append(
            pltpu.make_async_copy(pre_hbm.at[here, :], pre_grad.at[here, :], sems.at[1 + m])
        )
        stores.append(
            pltpu.make_async_copy(
                row_grad.at[here, :], row_hbm.at[here, :], sems.at[1 + BLOCKS + m]
            )
        )
    for copy in loads:
        copy.start()
    loads[0].wait()
    for m in range(BLOCKS):
        here = pl.ds(m * block, block)
        loads[1 + m].wait()
        row_grad[here, :] = lax.dot_general(
            pre_grad[here, :], gate_up[...], (((1,), (1,)), ((), ())), preferred_element_type=F32
        ).astype(BF16)
        stores[m].start()
    for copy in stores:
        copy.wait()


def row_gradients(pre_grad, gate_up):
    slots, columns = pre_grad.shape
    features = gate_up.shape[0]
    return pl.pallas_call(
        row_kernel,
        in_specs=[HBM, HBM],
        out_specs=HBM,
        out_shape=jax.ShapeDtypeStruct((slots, features), BF16),
        scratch_shapes=[
            pltpu.VMEM((slots, columns), BF16),
            pltpu.VMEM((features, columns), BF16),
            pltpu.VMEM((slots, features), BF16),
            pltpu.SemaphoreType.DMA((1 + 2 * BLOCKS,)),
        ],
        compiler_params=pltpu.CompilerParams(vmem_limit_bytes=VMEM_BYTES),
        cost_estimate=pl.CostEstimate(
            flops=2 * slots * features * columns, bytes_accessed=6 * MIB, transcendentals=0
        ),
        name="row_gradients",
    )(pre_grad, gate_up)


def combine_kernel(rank_ref, back_ref, out_ref):
    slots = back_ref.shape[0]
    column = iota((EXPERTS, slots), 1) - CAP * iota((EXPERTS, slots), 0)
    spread = as_bf16((column >= 0) & (column < CAP))
    rank = lax.dot_general(
        rank_ref[...], spread, (((0,), (0,)), ((), ())), preferred_element_type=F32
    )
    slot = iota((1, slots), 1)
    slot = (slot - CAP * ((slot * 3277) >> 18)).astype(F32)
    pick = as_bf16(rank == slot)
    out_ref[...] = jnp.dot(pick, back_ref[...], preferred_element_type=F32).astype(BF16)


def combine(rank, back):
    return pl.pallas_call(
        combine_kernel,
        out_shape=jax.ShapeDtypeStruct((rank.shape[1], back.shape[1]), BF16),
        compiler_params=pltpu.CompilerParams(vmem_limit_bytes=16 * MIB),
        name="combine_rows",
    )(rank, back)


def swap_halves(x):
    return lax.ppermute(x, "dp", [(d, (d + RING) % (2 * RING)) for d in range(2 * RING)])


def shift_ring(x, by):
    pairs = [(d, d // RING * RING + (d + by) % RING) for d in range(2 * RING)]
    return lax.ppermute(x, "dp", pairs)


def gather_weights(gate_up, down):
    own = jnp.concatenate([gate_up[0], down[0]], axis=1)
    shard = own.shape[0]
    far = [shift_ring(own, -by) for by in range(NEAR, RING, NEAR)]
    base = jnp.concatenate([own, *far], axis=0)
    other = swap_halves(base)
    both = jnp.concatenate([base, other], axis=0)
    pieces = [
        base,
        other,
        shift_ring(both, 1),
        shift_ring(both, -1),
        shift_ring(base, 2),
        shift_ring(other, -2),
    ]
    held = [(0, (0,)), (0, (1,)), (-1, (0, 1)), (1, (0, 1)), (-2, (0,)), (2, (1,))]
    plan = []
    for array, (offset, halves) in enumerate(held):
        for k, part in enumerate(halves):
            for j in range(RING // NEAR):
                row = (k * (RING // NEAR) + j) * shard
                plan.append((array, row, NEAR * j + offset, part))
    return pieces, plan


def near_sum_kernel(my_dp, keep, plus, minus, plus2, minus2, mine, theirs):
    groups, shard = plus2.shape[:2]
    upper = my_dp() // RING
    for j in range(groups):
        value = keep[j].astype(F32) + plus[j].astype(F32) + minus[j].astype(F32)
        low = (value[:shard] + plus2[j].astype(F32)).astype(BF16)
        high = (value[shard:] + minus2[(j - 1) % groups].astype(F32)).astype(BF16)
        mine[j] = jnp.where(upper == 0, low, high)
        theirs[j] = jnp.where(upper == 0, high, low)


def near_sum(my_dp, *parts):
    out = jax.ShapeDtypeStruct(parts[-1].shape, BF16)
    return pl.pallas_call(
        functools.partial(near_sum_kernel, my_dp),
        out_shape=(out, out),
        compiler_params=pltpu.CompilerParams(vmem_limit_bytes=12 * MIB),
        name="near_sum",
    )(*parts)


def scatter_sum(keep, plus, minus, plus2, minus2, scale, my_dp):
    mine, theirs = near_sum(
        my_dp,
        keep,
        shift_ring(plus, 1),
        shift_ring(minus, -1),
        shift_ring(plus2, 2),
        shift_ring(minus2, -2),
    )
    part = (mine.astype(F32) + swap_halves(theirs).astype(F32)).astype(BF16)
    total = part[0].astype(F32)
    for j in range(1, RING // NEAR):
        total += shift_ring(part[j], NEAR * j).astype(F32)
    return (total * scale)[None]


def shards(tokens, cotangent, route_experts, route_weights, gate_up, down):
    rows, features = tokens.shape
    hidden = down.shape[2]
    packed, rank = pack(tokens, cotangent, route_experts, route_weights)
    gathered = lax.all_gather(packed, "expert", axis=0, tiled=True)
    pieces, plan = gather_weights(gate_up, down)

    def my_dp():
        return lax.axis_index("dp")

    inputs, cots = compact(gathered, features, lambda: lax.axis_index("expert"))
    pre_grad, full_gate_up, *grad_parts = expert_work(inputs, cots, pieces, plan, hidden, my_dp)
    row_grads = row_gradients(pre_grad, full_gate_up)
    returned = lax.all_to_all(
        row_grads.reshape(EXPERTS, CAP, features), "expert", split_axis=0, concat_axis=0, tiled=True
    )
    grad_scale = 1.0 / math.sqrt(rows * lax.axis_size("dp") * lax.axis_size("expert"))
    grad_gate_up = scatter_sum(*grad_parts, grad_scale, my_dp)
    token_grad = combine(rank, returned.reshape(EXPERTS * CAP, features))
    return (token_grad, grad_gate_up)


def solution(mesh):
    in_specs = (
        P(("dp", "expert"), None),
        P(("dp", "expert"), None),
        P(("dp", "expert"), None),
        P(("dp", "expert"), None),
        P("expert", "dp", None),
        P("expert", "dp", None),
    )
    out_specs = (P(("dp", "expert"), None), P("expert", "dp", None))
    return jax.shard_map(shards, mesh=mesh, in_specs=in_specs, out_specs=out_specs, check_vma=False)
```

time: 208 us -> 207 us (level)
  Pallas kernels: 20.6 us -> 42.1 us
  local copies, waits for them, and re-layouts: 12.8 us -> 1.12 us
  waiting for transfers between devices: 67 us -> 56.4 us
    all_to_all x1 -> x0, waiting for transfers between devices: 23.5 us -> none  [scatter_sum(): lax.all_to_all(parts, 'dp', split_axis=0, concat_axis=0, axis_index_group...]
    pallas_call x3 -> x5, Pallas kernels: 19.2 us -> 40.7 us  [the longest x1 18.3 us: pack(): pl.pallas_call(pack_kernel, in_specs=[HBM, HBM, VMEM, VMEM], out_specs=(H...]
    ppermute x13 -> x14, starting transfers between devices: 51 us -> 71 us  [shift_ring(): return lax.ppermute(x, 'dp', pairs)]
    ppermute x1 -> x2, waiting for transfers between devices: 1.73 us -> 20.7 us  [swap_halves(): lax.ppermute(x, 'dp', [(d, (d + RING) % (2 * RING)) for d in range(2 * RI...]
    unnamed x32 -> x9, local copies, waits for them, and re-layouts: 12.8 us -> 1.08 us
    all_to_all x1, waiting for transfers between devices: 10.2 us -> 0.01 us  [shards(): lax.all_to_all(row_grads.reshape(EXPERTS, CAP, features), 'expert', split...]
    ppermute x1 -> x0, waiting for transfers between devices: 9.06 us -> none  [shift_across(): return lax.ppermute(x, 'dp', pairs)]
    ppermute x1 -> x0, starting transfers between devices: 8.94 us -> none  [shift_across(): return lax.ppermute(x, 'dp', pairs)]
  transfers between devices with their start and end apart: 18 -> 18, of which waited for: 11 -> 9; matrix products, arithmetic and copies ran while one was open for 1% -> 1% of each run, Pallas kernels for 1% -> 3%
where the time goes in v5:
time: 207 us; the launch traced here: 205 us
  starting transfers between devices  88.3 us (43%)
  waiting for transfers between devices  56.4 us (27%)
  Pallas kernels  42.1 us (20%)
  between operations  14.3 us (7%)
  other arithmetic  2.39 us (1%)
    ppermute x14, starting transfers between devices, shift_ring(): return lax.ppermute(x, 'dp', pairs)  71 us
    ppermute x14, waiting for transfers between devices, shift_ring(): return lax.ppermute(x, 'dp', pairs)  28.9 us
    ppermute x2, waiting for transfers between devices, swap_halves(): lax.ppermute(x, 'dp', [(d, (d + RING) % (2 * RING)) for d in range(2 * RI...  20.7 us
    pallas_call x1, Pallas kernels, pack(): pl.pallas_call(pack_kernel, in_specs=[HBM, HBM, VMEM, VMEM], out_specs=(H...  18.3 us
    pallas_call x1, Pallas kernels, expert_work(): pl.pallas_call(functools.partial(expert_kernel, my_dp, plan), in_specs=[H...  10.8 us
    ppermute x2, starting transfers between devices, swap_halves(): lax.ppermute(x, 'dp', [(d, (d + RING) % (2 * RING)) for d in range(2 * RI...  9.34 us
    all_to_all x1, starting transfers between devices, shards(): lax.all_to_all(row_grads.reshape(EXPERTS, CAP, features), 'expert', split...  7.94 us
    all_gather x1, waiting for transfers between devices, shards(): gathered = lax.all_gather(packed, 'expert', axis=0, tiled=True)  6.82 us
  transfers between devices with their start and end apart: 18, of which 9 were waited for; matrix products, arithmetic and copies ran while one was open for 1% of the time, Pallas kernels for 3%

profile of v5, /device:TPU:1, one launch (start us, length us, event | category | flops | bytes accessed | tf_op | source)
XLA Modules:
  0.0 204.6 jit_solution(9698293372289093617)
XLA Ops:
  7.2 18.3 %pack_rows.1 = (bf16[128,2176]{1,0:T(8,128)(2,1)}, bf16[16,128]{1,0:T(8,128)(2,1)}) custom-call(bf16[128,1024]{1,0:T(8,128)(2,1)} %tok_hbm.1, bf16[128,1024]{1,0:T(8,128)(2,1)} %cot_hbm.1, s32[8,128]{1,0:T(8,128)} %bitcast.25, f32[8,128]{1,0:T(8,128)} %bitcast.26), custom_call_target="tpu_custom_call" | custom-call | tf_op jit(solution)/shard_map/pack_rows/pallas_call | solution.py:64
  26.4 9.6 %collective-permute-start.2 = (bf16[32,1152]{1,0:T(8,128)(2,1)S(1)}, bf16[32,1152]{1,0:T(8,128)(2,1)S(1)}, u32[]{:S(2)}, u32[]{:S(2)}) collective-permute-start(bf16[32,1152]{1,0:T(8,128)(2,1)S(1)} %get-tuple-element.32), channel_id=1, source_target_pairs={{0,64},{16,80},{32,96},{48,112},{64,128},{80,144},{96,160},{112,17... | collective-permute-start | bytes 221192 | tf_op jit(solution)/shard_map/ppermute | solution.py:357
  36.0 10.6 %collective-permute-start.1 = (bf16[32,1152]{1,0:T(8,128)(2,1)S(1)}, bf16[32,1152]{1,0:T(8,128)(2,1)S(1)}, u32[]{:S(2)}, u32[]{:S(2)}) collective-permute-start(bf16[32,1152]{1,0:T(8,128)(2,1)S(1)} %get-tuple-element.32), channel_id=1, source_target_pairs={{0,128},{16,144},{32,160},{48,176},{64,192},{80,208},{96,224},{112... | collective-permute-start | bytes 221192 | tf_op jit(solution)/shard_map/ppermute | solution.py:357
  46.7 5.2 %collective-permute-start = (bf16[32,1152]{1,0:T(8,128)(2,1)S(1)}, bf16[32,1152]{1,0:T(8,128)(2,1)S(1)}, u32[]{:S(2)}, u32[]{:S(2)}) collective-permute-start(bf16[32,1152]{1,0:T(8,128)(2,1)S(1)} %get-tuple-element.32), channel_id=1, source_target_pairs={{0,192},{16,208},{32,224},{48,240},{64,0},{80,16},{96,32},{112,48}... | collective-permute-start | bytes 221192 | tf_op jit(solution)/shard_map/ppermute | solution.py:357
  54.8 6.4 %collective-permute-done = bf16[32,1152]{1,0:T(8,128)(2,1)S(1)} collective-permute-done((bf16[32,1152]{1,0:T(8,128)(2,1)S(1)}, bf16[32,1152]{1,0:T(8,128)(2,1)S(1)}, u32[]{:S(2)}, u32[]{:S(2)}) %collective-permute-start) | collective-permute-done | bytes 73760 | tf_op jit(solution)/shard_map/ppermute | solution.py:357
  62.0 4.8 %collective-permute-start.3 = (bf16[128,1152]{1,0:T(8,128)(2,1)S(1)}, bf16[128,1152]{1,0:T(8,128)(2,1)S(1)}, u32[]{:S(2)}, u32[]{:S(2)}) collective-permute-start(bf16[128,1152]{1,0:T(8,128)(2,1)S(1)} %pad_maximum_fusion.refs_0_), channel_id=1, source_target_pairs={{0,256},{16,272},{32,288},{48,304},{64,320},{80,336},{96,352},{112... | collective-permute-start | bytes 884744 | tf_op jit(solution)/shard_map/ppermute | solution.py:352
  66.9 13.5 %collective-permute-done.3.refs_1_ = bf16[128,1152]{1,0:T(8,128)(2,1)S(1)} collective-permute-done((bf16[128,1152]{1,0:T(8,128)(2,1)S(1)}, bf16[128,1152]{1,0:T(8,128)(2,1)S(1)}, u32[]{:S(2)}, u32[]{:S(2)}) %collective-permute-start.3) | collective-permute-done | bytes 294944 | tf_op jit(solution)/shard_map/ppermute | solution.py:352
  82.4 3.4 %collective-permute-start.4 = (bf16[256,1152]{1,0:T(8,128)(2,1)S(1)}, bf16[256,1152]{1,0:T(8,128)(2,1)S(1)}, u32[]{:S(2)}, u32[]{:S(2)}) collective-permute-start(bf16[256,1152]{1,0:T(8,128)(2,1)S(1)} %constant_dynamic-update-slice_fusion), channel_id=1, source_target_pairs={{0,16},{16,32},{32,48},{48,64},{64,80},{80,96},{96,112},{112,128},... | collective-permute-start | bytes 1769480 | tf_op jit(solution)/shard_map/ppermute | solution.py:357
  87.8 5.4 %collective-permute-start.7 = (bf16[128,1152]{1,0:T(8,128)(2,1)S(1)}, bf16[128,1152]{1,0:T(8,128)(2,1)S(1)}, u32[]{:S(2)}, u32[]{:S(2)}) collective-permute-start(bf16[128,1152]{1,0:T(8,128)(2,1)S(1)} %collective-permute-done.3.refs_1_), channel_id=1, source_target_pairs={{0,224},{16,240},{32,0},{48,16},{64,32},{80,48},{96,64},{112,80},{... | collective-permute-start | bytes 884744 | tf_op jit(solution)/shard_map/ppermute | solution.py:357
  93.2 6.8 %all-gather.2.cloned.1.call-done.g_hbm = bf16[2048,2176]{1,0:T(8,128)(2,1)} async-done(((bf16[128,2176]{1,0:T(8,128)(2,1)}), bf16[2048,2176]{1,0:T(8,128)(2,1)}) %all-gather.2.cloned.1.call-update) | async-done | bytes 8912912 | tf_op jit(solution)/shard_map/all_gather | solution.py:426
  100.0 6.1 %compact_rows.1 = (bf16[1280,1024]{1,0:T(8,128)(2,1)}, bf16[1280,1024]{1,0:T(8,128)(2,1)}) custom-call(bf16[2048,2176]{1,0:T(8,128)(2,1)} %all-gather.2.cloned.1.call-done.g_hbm), custom_call_target="tpu_custom_call" | custom-call | flops 1342177280 | bytes 16777216 | tf_op jit(solution)/shard_map/compact_rows/pallas_call | solution.py:134
  109.6 10.8 %expert_work.1 = (bf16[1280,768]{1,0:T(8,128)(2,1)}, bf16[1024,768]{1,0:T(8,128)(2,1)}, bf16[4,64,768]{2,1,0:T(8,128)(2,1)S(1)}, bf16[4,64,768]{2,1,0:T(8,128)(2...) custom-call(bf16[1280,1024]{1,0:T(8,128)(2,1)} %get-tuple-element.17.x_hbm, ...), custom_call_target="tpu_custom_call" | custom-call | flops 5033164800 | bytes 16777216 | tf_op jit(solution)/shard_map/expert_work/pallas_call | solution.py:251
  120.4 5.3 %row_gradients.1 = bf16[1280,1024]{1,0:T(8,128)(2,1)} custom-call(bf16[1280,768]{1,0:T(8,128)(2,1)} %get-tuple-element.19.pre_hbm, bf16[1024,768]{1,0:T(8,128)(2,1)} %get-tuple-element.20.gate_up_hbm), custom_call_target="tpu_custom_call" | custom-call | flops 2013265920 | bytes 6291456 | tf_op jit(solution)/shard_map/row_gradients/pallas_call | solution.py:310
  125.7 7.9 %all-to-all-start = ((bf16[16,80,1024]{2,1,0:T(8,128)(2,1)}), bf16[16,80,1024]{2,1,0:T(8,128)(2,1)S(1)}, u32[]{:S(2)}, u32[]{:S(2)}) async-start(bf16[16,80,1024]{2,1,0:T(8,128)(2,1)} %bitcast.20), calls=%async_computation | async-start | bytes 5242880 | tf_op jit(solution)/shard_map/all_to_all | solution.py:435
  133.7 5.7 %collective-permute-start.8 = (bf16[4,64,768]{2,1,0:T(8,128)(2,1)}, bf16[4,64,768]{2,1,0:T(8,128)(2,1)S(1)}, u32[]{:S(2)}, u32[]{:S(2)}) collective-permute-start(bf16[4,64,768]{2,1,0:T(8,128)(2,1)} %get-tuple-element.22), channel_id=1, source_target_pairs={{0,16},{16,32},{32,48},{48,64},{64,80},{80,96},{96,112},{112,128},... | collective-permute-start | bytes 1179656 | tf_op jit(solution)/shard_map/ppermute | solution.py:357
  139.3 3.5 %collective-permute-start.9 = (bf16[4,64,768]{2,1,0:T(8,128)(2,1)}, bf16[4,64,768]{2,1,0:T(8,128)(2,1)S(1)}, u32[]{:S(2)}, u32[]{:S(2)}) collective-permute-start(bf16[4,64,768]{2,1,0:T(8,128)(2,1)} %get-tuple-element.23), channel_id=1, source_target_pairs={{0,240},{16,0},{32,16},{48,32},{64,48},{80,64},{96,80},{112,96},{1... | collective-permute-start | bytes 1179656 | tf_op jit(solution)/shard_map/ppermute | solution.py:357
  144.7 5.5 %collective-permute-start.11 = (bf16[4,32,768]{2,1,0:T(8,128)(2,1)S(1)}, bf16[4,32,768]{2,1,0:T(8,128)(2,1)S(1)}, u32[]{:S(2)}, u32[]{:S(2)}) collective-permute-start(bf16[4,32,768]{2,1,0:T(8,128)(2,1)S(1)} %get-tuple-element.25), channel_id=1, source_target_pairs={{0,224},{16,240},{32,0},{48,16},{64,32},{80,48},{96,64},{112,80},{... | collective-permute-start | bytes 589832 | tf_op jit(solution)/shard_map/ppermute | solution.py:357
  150.2 9.7 %collective-permute-done.10.plus2 = bf16[4,32,768]{2,1,0:T(8,128)(2,1)S(1)} collective-permute-done((bf16[4,32,768]{2,1,0:T(8,128)(2,1)S(1)}, bf16[4,32,768]{2,1,0:T(8,128)(2,1)S(1)}, u32[]{:S(2)}, u32[]{:S(2)}) %collective-permute-start.10) | collective-permute-done | bytes 196640 | tf_op jit(solution)/shard_map/ppermute | solution.py:357
  160.5 4.5 %collective-permute-start.12 = (bf16[4,32,768]{2,1,0:T(8,128)(2,1)S(1)}, bf16[4,32,768]{2,1,0:T(8,128)(2,1)S(1)}, u32[]{:S(2)}, u32[]{:S(2)}) collective-permute-start(bf16[4,32,768]{2,1,0:T(8,128)(2,1)S(1)} %get-tuple-element.27), channel_id=1, source_target_pairs={{0,256},{16,272},{32,288},{48,304},{64,320},{80,336},{96,352},{112... | collective-permute-start | bytes 589832 | tf_op jit(solution)/shard_map/ppermute | solution.py:352
  165.1 7.2 %collective-permute-done.12 = bf16[4,32,768]{2,1,0:T(8,128)(2,1)S(1)} collective-permute-done((bf16[4,32,768]{2,1,0:T(8,128)(2,1)S(1)}, bf16[4,32,768]{2,1,0:T(8,128)(2,1)S(1)}, u32[]{:S(2)}, u32[]{:S(2)}) %collective-permute-start.12) | collective-permute-done | bytes 196640 | tf_op jit(solution)/shard_map/ppermute | solution.py:352
  172.3 4.3 %collective-permute-start.13 = (bf16[32,768]{1,0:T(8,128)(2,1)S(1)}, bf16[32,768]{1,0:T(8,128)(2,1)S(1)}, u32[]{:S(2)}, u32[]{:S(2)}) collective-permute-start(bf16[32,768]{1,0:T(8,128)(2,1)S(1)} %get-tuple-element.28), channel_id=1, source_target_pairs={{0,64},{16,80},{32,96},{48,112},{64,128},{80,144},{96,160},{112,17... | collective-permute-start | bytes 147464 | tf_op jit(solution)/shard_map/ppermute | solution.py:357
  176.6 4.9 %collective-permute-start.15 = (bf16[32,768]{1,0:T(8,128)(2,1)S(1)}, bf16[32,768]{1,0:T(8,128)(2,1)S(1)}, u32[]{:S(2)}, u32[]{:S(2)}) collective-permute-start(bf16[32,768]{1,0:T(8,128)(2,1)S(1)} %get-tuple-element.29), channel_id=1, source_target_pairs={{0,192},{16,208},{32,224},{48,240},{64,0},{80,16},{96,32},{112,48}... | collective-permute-start | bytes 147464 | tf_op jit(solution)/shard_map/ppermute | solution.py:357
  181.5 7.2 %collective-permute-start.14 = (bf16[32,768]{1,0:T(8,128)(2,1)S(1)}, bf16[32,768]{1,0:T(8,128)(2,1)S(1)}, u32[]{:S(2)}, u32[]{:S(2)}) collective-permute-start(bf16[32,768]{1,0:T(8,128)(2,1)S(1)} %get-tuple-element.30), channel_id=1, source_target_pairs={{0,128},{16,144},{32,160},{48,176},{64,192},{80,208},{96,224},{112... | collective-permute-start | bytes 147464 | tf_op jit(solution)/shard_map/ppermute | solution.py:357
  188.7 7.0 %collective-permute-done.14 = bf16[32,768]{1,0:T(8,128)(2,1)S(1)} collective-permute-done((bf16[32,768]{1,0:T(8,128)(2,1)S(1)}, bf16[32,768]{1,0:T(8,128)(2,1)S(1)}, u32[]{:S(2)}, u32[]{:S(2)}) %collective-permute-start.14) | collective-permute-done | bytes 49184 | tf_op jit(solution)/shard_map/ppermute | solution.py:357
  (34 shorter events, 16.8 us)
Async XLA Ops:
  7.2 92.8 %all-gather.2.cloned.1.call-start = ((), (), s32[]{:S(2)}) async-start(), calls=%async_computation.1 | async-start | bytes 9469952 | tf_op jit(solution)/shard_map/all_gather | solution.py:426
  26.4 25.5 %collective-permute-start.2 = (bf16[32,1152]{1,0:T(8,128)(2,1)S(1)}, bf16[32,1152]{1,0:T(8,128)(2,1)S(1)}, u32[]{:S(2)}, u32[]{:S(2)}) collective-permute-start(bf16[32,1152]{1,0:T(8,128)(2,1)S(1)} %get-tuple-element.32), channel_id=1, source_target_pairs={{0,64},{16,80},{32,96},{48,112},{64,128},{80,144},{96,160},{112,17... | collective-permute-start | bytes 221192 | tf_op jit(solution)/shard_map/ppermute | solution.py:357
  36.0 18.7 %collective-permute-start.1 = (bf16[32,1152]{1,0:T(8,128)(2,1)S(1)}, bf16[32,1152]{1,0:T(8,128)(2,1)S(1)}, u32[]{:S(2)}, u32[]{:S(2)}) collective-permute-start(bf16[32,1152]{1,0:T(8,128)(2,1)S(1)} %get-tuple-element.32), channel_id=1, source_target_pairs={{0,128},{16,144},{32,160},{48,176},{64,192},{80,208},{96,224},{112... | collective-permute-start | bytes 221192 | tf_op jit(solution)/shard_map/ppermute | solution.py:357
  46.7 14.5 %collective-permute-start = (bf16[32,1152]{1,0:T(8,128)(2,1)S(1)}, bf16[32,1152]{1,0:T(8,128)(2,1)S(1)}, u32[]{:S(2)}, u32[]{:S(2)}) collective-permute-start(bf16[32,1152]{1,0:T(8,128)(2,1)S(1)} %get-tuple-element.32), channel_id=1, source_target_pairs={{0,192},{16,208},{32,224},{48,240},{64,0},{80,16},{96,32},{112,48}... | collective-permute-start | bytes 221192 | tf_op jit(solution)/shard_map/ppermute | solution.py:357
  62.0 18.4 %collective-permute-start.3 = (bf16[128,1152]{1,0:T(8,128)(2,1)S(1)}, bf16[128,1152]{1,0:T(8,128)(2,1)S(1)}, u32[]{:S(2)}, u32[]{:S(2)}) collective-permute-start(bf16[128,1152]{1,0:T(8,128)(2,1)S(1)} %pad_maximum_fusion.refs_0_), channel_id=1, source_target_pairs={{0,256},{16,272},{32,288},{48,304},{64,320},{80,336},{96,352},{112... | collective-permute-start | bytes 884744 | tf_op jit(solution)/shard_map/ppermute | solution.py:352
  80.5 28.1 %collective-permute-start.5 = (bf16[256,1152]{1,0:T(8,128)(2,1)S(1)}, bf16[256,1152]{1,0:T(8,128)(2,1)S(1)}, u32[]{:S(2)}, u32[]{:S(2)}) collective-permute-start(bf16[256,1152]{1,0:T(8,128)(2,1)S(1)} %constant_dynamic-update-slice_fusion), channel_id=1, source_target_pairs={{0,240},{16,0},{32,16},{48,32},{64,48},{80,64},{96,80},{112,96},{1... | collective-permute-start | bytes 1769480 | tf_op jit(solution)/shard_map/ppermute | solution.py:357
  82.4 26.2 %collective-permute-start.4 = (bf16[256,1152]{1,0:T(8,128)(2,1)S(1)}, bf16[256,1152]{1,0:T(8,128)(2,1)S(1)}, u32[]{:S(2)}, u32[]{:S(2)}) collective-permute-start(bf16[256,1152]{1,0:T(8,128)(2,1)S(1)} %constant_dynamic-update-slice_fusion), channel_id=1, source_target_pairs={{0,16},{16,32},{32,48},{48,64},{64,80},{80,96},{96,112},{112,128},... | collective-permute-start | bytes 1769480 | tf_op jit(solution)/shard_map/ppermute | solution.py:357
  85.8 22.8 %collective-permute-start.6 = (bf16[128,1152]{1,0:T(8,128)(2,1)S(1)}, bf16[128,1152]{1,0:T(8,128)(2,1)S(1)}, u32[]{:S(2)}, u32[]{:S(2)}) collective-permute-start(bf16[128,1152]{1,0:T(8,128)(2,1)S(1)} %pad_maximum_fusion.refs_0_), channel_id=1, source_target_pairs={{0,32},{16,48},{32,64},{48,80},{64,96},{80,112},{96,128},{112,144}... | collective-permute-start | bytes 884744 | tf_op jit(solution)/shard_map/ppermute | solution.py:357
  87.8 20.8 %collective-permute-start.7 = (bf16[128,1152]{1,0:T(8,128)(2,1)S(1)}, bf16[128,1152]{1,0:T(8,128)(2,1)S(1)}, u32[]{:S(2)}, u32[]{:S(2)}) collective-permute-start(bf16[128,1152]{1,0:T(8,128)(2,1)S(1)} %collective-permute-done.3.refs_1_), channel_id=1, source_target_pairs={{0,224},{16,240},{32,0},{48,16},{64,32},{80,48},{96,64},{112,80},{... | collective-permute-start | bytes 884744 | tf_op jit(solution)/shard_map/ppermute | solution.py:357
  108.6 1.1 copy-start.1
  108.6 0.9 copy-start.2
  125.7 70.6 %all-to-all-start = ((bf16[16,80,1024]{2,1,0:T(8,128)(2,1)}), bf16[16,80,1024]{2,1,0:T(8,128)(2,1)S(1)}, u32[]{:S(2)}, u32[]{:S(2)}) async-start(bf16[16,80,1024]{2,1,0:T(8,128)(2,1)} %bitcast.20), calls=%async_computation | async-start | bytes 5242880 | tf_op jit(solution)/shard_map/all_to_all | solution.py:435
  133.7 62.7 %copy-start = (bf16[16,128]{1,0:T(8,128)(2,1)S(1)}, bf16[16,128]{1,0:T(8,128)(2,1)}, u32[]{:S(2)}) copy-start(bf16[16,128]{1,0:T(8,128)(2,1)} %get-tuple-element.15.rank_ref) | copy-start | bytes 12292
  133.7 26.6 %collective-permute-start.8 = (bf16[4,64,768]{2,1,0:T(8,128)(2,1)}, bf16[4,64,768]{2,1,0:T(8,128)(2,1)S(1)}, u32[]{:S(2)}, u32[]{:S(2)}) collective-permute-start(bf16[4,64,768]{2,1,0:T(8,128)(2,1)} %get-tuple-element.22), channel_id=1, source_target_pairs={{0,16},{16,32},{32,48},{48,64},{64,80},{80,96},{96,112},{112,128},... | collective-permute-start | bytes 1179656 | tf_op jit(solution)/shard_map/ppermute | solution.py:357
  139.3 21.0 %collective-permute-start.9 = (bf16[4,64,768]{2,1,0:T(8,128)(2,1)}, bf16[4,64,768]{2,1,0:T(8,128)(2,1)S(1)}, u32[]{:S(2)}, u32[]{:S(2)}) collective-permute-start(bf16[4,64,768]{2,1,0:T(8,128)(2,1)} %get-tuple-element.23), channel_id=1, source_target_pairs={{0,240},{16,0},{32,16},{48,32},{64,48},{80,64},{96,80},{112,96},{1... | collective-permute-start | bytes 1179656 | tf_op jit(solution)/shard_map/ppermute | solution.py:357
  142.8 17.1 %collective-permute-start.10 = (bf16[4,32,768]{2,1,0:T(8,128)(2,1)S(1)}, bf16[4,32,768]{2,1,0:T(8,128)(2,1)S(1)}, u32[]{:S(2)}, u32[]{:S(2)}) collective-permute-start(bf16[4,32,768]{2,1,0:T(8,128)(2,1)S(1)} %get-tuple-element.24), channel_id=1, source_target_pairs={{0,32},{16,48},{32,64},{48,80},{64,96},{80,112},{96,128},{112,144}... | collective-permute-start | bytes 589832 | tf_op jit(solution)/shard_map/ppermute | solution.py:357
  144.7 15.6 %collective-permute-start.11 = (bf16[4,32,768]{2,1,0:T(8,128)(2,1)S(1)}, bf16[4,32,768]{2,1,0:T(8,128)(2,1)S(1)}, u32[]{:S(2)}, u32[]{:S(2)}) collective-permute-start(bf16[4,32,768]{2,1,0:T(8,128)(2,1)S(1)} %get-tuple-element.25), channel_id=1, source_target_pairs={{0,224},{16,240},{32,0},{48,16},{64,32},{80,48},{96,64},{112,80},{... | collective-permute-start | bytes 589832 | tf_op jit(solution)/shard_map/ppermute | solution.py:357
  160.5 11.7 %collective-permute-start.12 = (bf16[4,32,768]{2,1,0:T(8,128)(2,1)S(1)}, bf16[4,32,768]{2,1,0:T(8,128)(2,1)S(1)}, u32[]{:S(2)}, u32[]{:S(2)}) collective-permute-start(bf16[4,32,768]{2,1,0:T(8,128)(2,1)S(1)} %get-tuple-element.27), channel_id=1, source_target_pairs={{0,256},{16,272},{32,288},{48,304},{64,320},{80,336},{96,352},{112... | collective-permute-start | bytes 589832 | tf_op jit(solution)/shard_map/ppermute | solution.py:352
  172.3 16.4 %collective-permute-start.13 = (bf16[32,768]{1,0:T(8,128)(2,1)S(1)}, bf16[32,768]{1,0:T(8,128)(2,1)S(1)}, u32[]{:S(2)}, u32[]{:S(2)}) collective-permute-start(bf16[32,768]{1,0:T(8,128)(2,1)S(1)} %get-tuple-element.28), channel_id=1, source_target_pairs={{0,64},{16,80},{32,96},{48,112},{64,128},{80,144},{96,160},{112,17... | collective-permute-start | bytes 147464 | tf_op jit(solution)/shard_map/ppermute | solution.py:357
  176.6 12.1 %collective-permute-start.15 = (bf16[32,768]{1,0:T(8,128)(2,1)S(1)}, bf16[32,768]{1,0:T(8,128)(2,1)S(1)}, u32[]{:S(2)}, u32[]{:S(2)}) collective-permute-start(bf16[32,768]{1,0:T(8,128)(2,1)S(1)} %get-tuple-element.29), channel_id=1, source_target_pairs={{0,192},{16,208},{32,224},{48,240},{64,0},{80,16},{96,32},{112,48}... | collective-permute-start | bytes 147464 | tf_op jit(solution)/shard_map/ppermute | solution.py:357
  181.5 14.2 %collective-permute-start.14 = (bf16[32,768]{1,0:T(8,128)(2,1)S(1)}, bf16[32,768]{1,0:T(8,128)(2,1)S(1)}, u32[]{:S(2)}, u32[]{:S(2)}) collective-permute-start(bf16[32,768]{1,0:T(8,128)(2,1)S(1)} %get-tuple-element.30), channel_id=1, source_target_pairs={{0,128},{16,144},{32,160},{48,176},{64,192},{80,208},{96,224},{112... | collective-permute-start | bytes 147464 | tf_op jit(solution)/shard_map/ppermute | solution.py:357
Sparse Core Ops, SparseCore 0:
  25.7 74.2 all-gather.1

commit v6 on v5

--- a/solution.py
+++ b/solution.py
@@ -32,15 +32,10 @@
     return jnp.where(mask, 1.0, 0.0).astype(BF16)
 
 
-def pack_kernel(tok_hbm, cot_hbm, experts_ref, weights_ref, packed_hbm, rank_ref, table_ref, sems):
-    rows, features = tok_hbm.shape
-    copies = [
-        pltpu.make_async_copy(tok_hbm, packed_hbm.at[:, pl.ds(0, features)], sems.at[0]),
-        pltpu.make_async_copy(cot_hbm, packed_hbm.at[:, pl.ds(features, features)], sems.at[1]),
-        pltpu.make_async_copy(table_ref, packed_hbm.at[:, pl.ds(2 * features, rows)], sems.at[2]),
-    ]
-    copies[0].start()
-    copies[1].start()
+def pack_kernel(tok_ref, cot_ref, experts_ref, weights_ref, packed_ref, rank_ref):
+    rows, features = tok_ref.shape
+    packed_ref[:, :features] = tok_ref[...]
+    packed_ref[:, features : 2 * features] = cot_ref[...]
     label = iota((EXPERTS, rows), 0)
     dense = jnp.zeros((EXPERTS, rows), F32)
     for k in range(experts_ref.shape[0]):
@@ -52,24 +47,18 @@
     high = dense.astype(BF16)
     low = (dense - high.astype(F32)).astype(BF16)
     rest = jnp.zeros((rows - 3 * EXPERTS, rows), BF16)
-    table_ref[...] = jnp.concatenate([high, low, rank, rest], axis=0)
-    copies[2].start()
+    packed_ref[:, 2 * features :] = jnp.concatenate([high, low, rank, rest], axis=0)
     rank_ref[...] = rank
-    for copy in copies:
-        copy.wait()
 
 
 def pack(tokens, cotangent, route_experts, route_weights):
     rows, features = tokens.shape
     return pl.pallas_call(
         pack_kernel,
-        in_specs=[HBM, HBM, VMEM, VMEM],
-        out_specs=(HBM, VMEM),
         out_shape=(
             jax.ShapeDtypeStruct((rows, 2 * features + rows), BF16),
             jax.ShapeDtypeStruct((EXPERTS, rows), BF16),
         ),
-        scratch_shapes=[pltpu.VMEM((rows, rows), BF16), pltpu.SemaphoreType.DMA((3,))],
         compiler_params=pltpu.CompilerParams(vmem_limit_bytes=VMEM_BYTES),
         name="pack_rows",
     )(tokens, cotangent, route_experts.T, route_weights.T)
@@ -154,7 +143,7 @@
 
 
 def expert_kernel(my_dp, plan, x_hbm, c_hbm, *refs):
-    piece_total = 1 + max(array for array, _, _, _ in plan)
+    piece_total = 1 + max(array for array, *_ in plan)
     pieces = refs[:piece_total]
     pre_hbm, gate_up_hbm, *parts_hbm = refs[piece_total : piece_total + 7]
     weights, gate_up, inputs, cots, pre_grad, total, *parts = refs[piece_total + 7 : -4]
@@ -170,8 +159,8 @@
     def rows_of(m):
         return pl.ds(m * block_rows, block_rows)
 
-    def first_row(owner, offset):
-        return pl.multiple_of(owner * half + ((place + offset + RING) % RING) * shard, shard)
+    def row_at(owner, spot):
+        return pl.multiple_of(owner * half + spot * shard, shard)
 
     loads = []
     for m in range(BLOCKS):
@@ -181,12 +170,13 @@
             pltpu.make_async_copy(c_hbm.at[here, :], cots.at[here, :], load_sems.at[2 * m + 1]),
         ]
     weight_loads = []
-    for array, source, offset, part in plan:
+    for array, source, step, far, part in plan:
         owner = upper if part == 0 else 1 - upper
+        spot = NEAR * far + (place + step + NEAR) % NEAR
         weight_loads.append(
             pltpu.make_async_copy(
                 pieces[array].at[pl.ds(source, shard), :],
-                weights.at[pl.ds(first_row(owner, offset), shard), :],
+                weights.at[pl.ds(row_at(owner, spot), shard), :],
                 weight_sems.at[len(weight_loads)],
             )
         )
@@ -225,7 +215,7 @@
         )
 
     def part(owner, offset):
-        return total[pl.ds(first_row(owner, offset), shard), :].astype(BF16)
+        return total[pl.ds(row_at(owner, (place + offset + RING) % RING), shard), :].astype(BF16)
 
     keep, plus, minus, plus2, minus2 = parts
     for j in range(RING // NEAR):
@@ -357,28 +347,36 @@
     return lax.ppermute(x, "dp", pairs)
 
 
+def far_groups():
+    return [
+        [y * RING + far * NEAR + near for far in range(RING // NEAR)]
+        for y in range(2)
+        for near in range(NEAR)
+    ]
+
+
 def gather_weights(gate_up, down):
     own = jnp.concatenate([gate_up[0], down[0]], axis=1)
     shard = own.shape[0]
-    far = [shift_ring(own, -by) for by in range(NEAR, RING, NEAR)]
-    base = jnp.concatenate([own, *far], axis=0)
-    other = swap_halves(base)
-    both = jnp.concatenate([base, other], axis=0)
+    both = jnp.concatenate([own, swap_halves(own)], axis=0)
+    held = lax.all_gather(both, "dp", axis=0, axis_index_groups=far_groups(), tiled=True)
+    middle = held.shape[0] // 2
     pieces = [
-        base,
-        other,
-        shift_ring(both, 1),
-        shift_ring(both, -1),
-        shift_ring(base, 2),
-        shift_ring(other, -2),
+        held,
+        shift_ring(held, 1),
+        shift_ring(held, -1),
+        shift_ring(held[:middle], 2),
+        shift_ring(held[middle:], -2),
     ]
-    held = [(0, (0,)), (0, (1,)), (-1, (0, 1)), (1, (0, 1)), (-2, (0,)), (2, (1,))]
-    plan = []
-    for array, (offset, halves) in enumerate(held):
-        for k, part in enumerate(halves):
-            for j in range(RING // NEAR):
-                row = (k * (RING // NEAR) + j) * shard
-                plan.append((array, row, NEAR * j + offset, part))
+    groups = RING // NEAR
+    everything, first, second = range(groups), range(groups // 2), range(groups // 2, groups)
+    steps = [(0, everything), (-1, everything), (1, everything), (2, first), (2, second)]
+    plan = [
+        (array, (2 * k + part) * shard, step, far, part)
+        for array, (step, fars) in enumerate(steps)
+        for k, far in enumerate(fars)
+        for part in range(2)
+    ]
     return pieces, plan
 
 
@@ -399,6 +397,9 @@
         functools.partial(near_sum_kernel, my_dp),
         out_shape=(out, out),
         compiler_params=pltpu.CompilerParams(vmem_limit_bytes=12 * MIB),
+        cost_estimate=pl.CostEstimate(
+            flops=100 * 1000**3, bytes_accessed=4 * MIB, transcendentals=0
+        ),
         name="near_sum",
     )(*parts)
 

time: 207 us -> 194 us (0.937)
  blocking collectives: 0 us -> 32.6 us
  starting transfers between devices: 88.3 us -> 65.8 us
  Pallas kernels: 42.1 us -> 26.9 us
  waiting for transfers between devices: 56.4 us -> 48.5 us
    all_gather x0 -> x1, blocking collectives: none -> 32.6 us  [gather_weights(): lax.all_gather(both, 'dp', axis=0, axis_index_groups=far_groups(), tiled=...]
    ppermute x14 -> x11, waiting for transfers between devices: 28.9 us -> 4.2 us  [shift_ring(): return lax.ppermute(x, 'dp', pairs)]
    ppermute x14 -> x11, starting transfers between devices: 71 us -> 49.8 us  [shift_ring(): return lax.ppermute(x, 'dp', pairs)]
    pallas_call x1, Pallas kernels: 18.3 us -> 1.98 us  [pack(): pl.pallas_call(pack_kernel, out_shape=(jax.ShapeDtypeStruct((rows, 2 * fe...]
    ppermute x2, waiting for transfers between devices: 20.7 us -> 31 us  [swap_halves(): lax.ppermute(x, 'dp', [(d, (d + RING) % (2 * RING)) for d in range(2 * RI...]
    all_gather x1, waiting for transfers between devices: 6.82 us -> 13.3 us  [shards(): gathered = lax.all_gather(packed, 'expert', axis=0, tiled=True)]
  transfers between devices with their start and end apart: 18 -> 15, of which waited for: 9 -> 5; matrix products, arithmetic and copies ran while one was open for 1% -> 1% of each run, Pallas kernels for 3% -> 7%
where the time goes in v6:
time: 194 us; the launch traced here: 193 us
  starting transfers between devices  65.8 us (34%)
  waiting for transfers between devices  48.5 us (25%)
  blocking collectives  32.6 us (17%)
  Pallas kernels  26.9 us (14%)
  between operations  14.3 us (7%)
  local copies, waits for them, and re-layouts  2.81 us (1%)
  other arithmetic  2.37 us (1%)
    ppermute x11, starting transfers between devices, shift_ring(): return lax.ppermute(x, 'dp', pairs)  49.8 us
    all_gather x1, blocking collectives, gather_weights(): lax.all_gather(both, 'dp', axis=0, axis_index_groups=far_groups(), tiled=...  32.6 us
    ppermute x2, waiting for transfers between devices, swap_halves(): lax.ppermute(x, 'dp', [(d, (d + RING) % (2 * RING)) for d in range(2 * RI...  31 us
    all_gather x1, waiting for transfers between devices, shards(): gathered = lax.all_gather(packed, 'expert', axis=0, tiled=True)  13.3 us
    pallas_call x1, Pallas kernels, expert_work(): pl.pallas_call(functools.partial(expert_kernel, my_dp, plan), in_specs=[H...  10.8 us
    ppermute x2, starting transfers between devices, swap_halves(): lax.ppermute(x, 'dp', [(d, (d + RING) % (2 * RING)) for d in range(2 * RI...  9.99 us
    pallas_call x1, Pallas kernels, compact(): pl.pallas_call(functools.partial(compact_kernel, my_expert, features), in...  6.09 us
    all_to_all x1, starting transfers between devices, shards(): lax.all_to_all(row_grads.reshape(EXPERTS, CAP, features), 'expert', split...  5.98 us
  transfers between devices with their start and end apart: 15, of which 5 were waited for; matrix products, arithmetic and copies ran while one was open for 1% of the time, Pallas kernels for 7%

profile of v6, /device:TPU:1, one launch (start us, length us, event | category | flops | bytes accessed | tf_op | source)
XLA Modules:
  0.0 193.3 jit_solution(11537634066499932006)
XLA Ops:
  7.2 2.0 %pack_rows.1 = (bf16[128,2176]{1,0:T(8,128)(2,1)}, bf16[16,128]{1,0:T(8,128)(2,1)}) custom-call(bf16[128,1024]{1,0:T(8,128)(2,1)} %tok_ref.1, bf16[128,1024]{1,0:T(8,128)(2,1)} %cot_ref.1, s32[8,128]{1,0:T(8,128)} %bitcast.25, f32[8,128]{1,0:T(8,128)} %bitcast.26), custom_call_target="tpu_custom_call" | custom-call | tf_op jit(solution)/shard_map/pack_rows/pallas_call | solution.py:56
  10.0 5.6 %collective-permute-start = (bf16[32,1152]{1,0:T(8,128)(2,1)S(1)}, bf16[32,1152]{1,0:T(8,128)(2,1)S(1)}, u32[]{:S(2)}, u32[]{:S(2)}) collective-permute-start(bf16[32,1152]{1,0:T(8,128)(2,1)S(1)} %pad_maximum_fusion.1), channel_id=1, source_target_pairs={{0,256},{16,272},{32,288},{48,304},{64,320},{80,336},{96,352},{112... | collective-permute-start | bytes 221192 | tf_op jit(solution)/shard_map/ppermute | solution.py:342
  15.7 1.7 collective-permute-done
  18.2 32.6 %all_gather.7.refs_0_ = bf16[256,1152]{1,0:T(8,128)(2,1)S(1)} all-gather(bf16[64,1152]{1,0:T(8,128)(2,1)S(1)} %pad_maximum_fusion), channel_id=1, replica_groups={{0,64,128,192},{16,80,144,208},{32,96,160,224},{48,112,176,240},{256,32..., dimensions={0}, use_global_device_ids=true | all-gather | bytes 737280 | tf_op jit(solution)/shard_map/all_gather | solution.py:362
  50.8 2.7 %collective-permute-start.1 = (bf16[256,1152]{1,0:T(8,128)(2,1)S(1)}, bf16[256,1152]{1,0:T(8,128)(2,1)S(1)}, u32[]{:S(2)}, u32[]{:S(2)}) collective-permute-start(bf16[256,1152]{1,0:T(8,128)(2,1)S(1)} %all_gather.7.refs_0_), channel_id=1, source_target_pairs={{0,16},{16,32},{32,48},{48,64},{64,80},{80,96},{96,112},{112,128},... | collective-permute-start | bytes 1769480 | tf_op jit(solution)/shard_map/ppermute | solution.py:347
  53.6 3.8 %collective-permute-start.2 = (bf16[256,1152]{1,0:T(8,128)(2,1)S(1)}, bf16[256,1152]{1,0:T(8,128)(2,1)S(1)}, u32[]{:S(2)}, u32[]{:S(2)}) collective-permute-start(bf16[256,1152]{1,0:T(8,128)(2,1)S(1)} %all_gather.7.refs_0_), channel_id=1, source_target_pairs={{0,240},{16,0},{32,16},{48,32},{64,48},{80,64},{96,80},{112,96},{1... | collective-permute-start | bytes 1769480 | tf_op jit(solution)/shard_map/ppermute | solution.py:347
  57.4 1.9 collective-permute-start.3
  59.3 5.5 %collective-permute-start.4 = (bf16[128,1152]{1,0:T(8,128)(2,1)S(1)}, bf16[128,1152]{1,0:T(8,128)(2,1)S(1)}, u32[]{:S(2)}, u32[]{:S(2)}) collective-permute-start(bf16[128,1152]{1,0:T(8,128)(2,1)S(1)} %get-tuple-element.28), channel_id=1, source_target_pairs={{0,224},{16,240},{32,0},{48,16},{64,32},{80,48},{96,64},{112,80},{... | collective-permute-start | bytes 884744 | tf_op jit(solution)/shard_map/ppermute | solution.py:347
  64.8 13.3 %all-gather.2.cloned.1.call-done.g_hbm = bf16[2048,2176]{1,0:T(8,128)(2,1)} async-done(((bf16[128,2176]{1,0:T(8,128)(2,1)}), bf16[2048,2176]{1,0:T(8,128)(2,1)}) %all-gather.2.cloned.1.call-update) | async-done | bytes 8912912 | tf_op jit(solution)/shard_map/all_gather | solution.py:427
  78.1 6.1 %compact_rows.1 = (bf16[1280,1024]{1,0:T(8,128)(2,1)}, bf16[1280,1024]{1,0:T(8,128)(2,1)}) custom-call(bf16[2048,2176]{1,0:T(8,128)(2,1)} %all-gather.2.cloned.1.call-done.g_hbm), custom_call_target="tpu_custom_call" | custom-call | flops 1342177280 | bytes 16777216 | tf_op jit(solution)/shard_map/compact_rows/pallas_call | solution.py:123
  85.3 10.8 %expert_work.1 = (bf16[1280,768]{1,0:T(8,128)(2,1)}, bf16[1024,768]{1,0:T(8,128)(2,1)}, bf16[4,64,768]{2,1,0:T(8,128)(2,1)S(1)}, bf16[4,64,768]{2,1,0:T(8,128)(2...) custom-call(bf16[1280,1024]{1,0:T(8,128)(2,1)} %get-tuple-element.17.x_hbm, ...), custom_call_target="tpu_custom_call" | custom-call | flops 5033164800 | bytes 16777216 | tf_op jit(solution)/shard_map/expert_work/pallas_call | solution.py:241
  96.9 3.2 %collective-permute-start.5 = (bf16[4,64,768]{2,1,0:T(8,128)(2,1)S(1)}, bf16[4,64,768]{2,1,0:T(8,128)(2,1)S(1)}, u32[]{:S(2)}, u32[]{:S(2)}) collective-permute-start(bf16[4,64,768]{2,1,0:T(8,128)(2,1)S(1)} %get-tuple-element.22), channel_id=1, source_target_pairs={{0,16},{16,32},{32,48},{48,64},{64,80},{80,96},{96,112},{112,128},... | collective-permute-start | bytes 1179656 | tf_op jit(solution)/shard_map/ppermute | solution.py:347
  100.1 4.4 %collective-permute-start.6 = (bf16[4,64,768]{2,1,0:T(8,128)(2,1)}, bf16[4,64,768]{2,1,0:T(8,128)(2,1)}, u32[]{:S(2)}, u32[]{:S(2)}) collective-permute-start(bf16[4,64,768]{2,1,0:T(8,128)(2,1)} %get-tuple-element.23), channel_id=1, source_target_pairs={{0,240},{16,0},{32,16},{48,32},{64,48},{80,64},{96,80},{112,96},{1... | collective-permute-start | bytes 1179656 | tf_op jit(solution)/shard_map/ppermute | solution.py:347
  104.5 1.9 collective-permute-start.7
  106.4 5.5 %collective-permute-start.8 = (bf16[4,32,768]{2,1,0:T(8,128)(2,1)}, bf16[4,32,768]{2,1,0:T(8,128)(2,1)}, u32[]{:S(2)}, u32[]{:S(2)}) collective-permute-start(bf16[4,32,768]{2,1,0:T(8,128)(2,1)} %get-tuple-element.25), channel_id=1, source_target_pairs={{0,224},{16,240},{32,0},{48,16},{64,32},{80,48},{96,64},{112,80},{... | collective-permute-start | bytes 589832 | tf_op jit(solution)/shard_map/ppermute | solution.py:347
  111.9 5.3 %row_gradients.1 = bf16[1280,1024]{1,0:T(8,128)(2,1)} custom-call(bf16[1280,768]{1,0:T(8,128)(2,1)} %get-tuple-element.19.pre_hbm, bf16[1024,768]{1,0:T(8,128)(2,1)} %get-tuple-element.20.gate_up_hbm), custom_call_target="tpu_custom_call" | custom-call | flops 2013265920 | bytes 6291456 | tf_op jit(solution)/shard_map/row_gradients/pallas_call | solution.py:300
  117.2 6.0 %all-to-all-start = ((bf16[16,80,1024]{2,1,0:T(8,128)(2,1)}), bf16[16,80,1024]{2,1,0:T(8,128)(2,1)S(1)}, u32[]{:S(2)}, u32[]{:S(2)}) async-start(bf16[16,80,1024]{2,1,0:T(8,128)(2,1)} %bitcast.20), calls=%async_computation | async-start | bytes 5242880 | tf_op jit(solution)/shard_map/all_to_all | solution.py:436
  125.6 4.4 %collective-permute-start.9 = (bf16[4,32,768]{2,1,0:T(8,128)(2,1)S(1)}, bf16[4,32,768]{2,1,0:T(8,128)(2,1)S(1)}, u32[]{:S(2)}, u32[]{:S(2)}) collective-permute-start(bf16[4,32,768]{2,1,0:T(8,128)(2,1)S(1)} %get-tuple-element.27), channel_id=1, source_target_pairs={{0,256},{16,272},{32,288},{48,304},{64,320},{80,336},{96,352},{112... | collective-permute-start | bytes 589832 | tf_op jit(solution)/shard_map/ppermute | solution.py:342
  129.9 29.2 %collective-permute-done.9 = bf16[4,32,768]{2,1,0:T(8,128)(2,1)S(1)} collective-permute-done((bf16[4,32,768]{2,1,0:T(8,128)(2,1)S(1)}, bf16[4,32,768]{2,1,0:T(8,128)(2,1)S(1)}, u32[]{:S(2)}, u32[]{:S(2)}) %collective-permute-start.9) | collective-permute-done | bytes 196640 | tf_op jit(solution)/shard_map/ppermute | solution.py:342
  159.2 7.3 %collective-permute-start.12 = (bf16[32,768]{1,0:T(8,128)(2,1)S(1)}, bf16[32,768]{1,0:T(8,128)(2,1)S(1)}, u32[]{:S(2)}, u32[]{:S(2)}) collective-permute-start(bf16[32,768]{1,0:T(8,128)(2,1)S(1)} %get-tuple-element.31), channel_id=1, source_target_pairs={{0,192},{16,208},{32,224},{48,240},{64,0},{80,16},{96,32},{112,48}... | collective-permute-start | bytes 147464 | tf_op jit(solution)/shard_map/ppermute | solution.py:347
  166.5 6.4 %collective-permute-start.11 = (bf16[32,768]{1,0:T(8,128)(2,1)S(1)}, bf16[32,768]{1,0:T(8,128)(2,1)S(1)}, u32[]{:S(2)}, u32[]{:S(2)}) collective-permute-start(bf16[32,768]{1,0:T(8,128)(2,1)S(1)} %get-tuple-element.32), channel_id=1, source_target_pairs={{0,128},{16,144},{32,160},{48,176},{64,192},{80,208},{96,224},{112... | collective-permute-start | bytes 147464 | tf_op jit(solution)/shard_map/ppermute | solution.py:347
  172.9 7.3 %collective-permute-start.10 = (bf16[32,768]{1,0:T(8,128)(2,1)S(1)}, bf16[32,768]{1,0:T(8,128)(2,1)S(1)}, u32[]{:S(2)}, u32[]{:S(2)}) collective-permute-start(bf16[32,768]{1,0:T(8,128)(2,1)S(1)} %get-tuple-element.30), channel_id=1, source_target_pairs={{0,64},{16,80},{32,96},{48,112},{64,128},{80,144},{96,160},{112,17... | collective-permute-start | bytes 147464 | tf_op jit(solution)/shard_map/ppermute | solution.py:347
  180.4 4.0 %collective-permute-done.10 = bf16[32,768]{1,0:T(8,128)(2,1)S(1)} collective-permute-done((bf16[32,768]{1,0:T(8,128)(2,1)S(1)}, bf16[32,768]{1,0:T(8,128)(2,1)S(1)}, u32[]{:S(2)}, u32[]{:S(2)}) %collective-permute-start.10) | collective-permute-done | bytes 49184 | tf_op jit(solution)/shard_map/ppermute | solution.py:347
  185.0 1.4 combine_rows.1
  (32 shorter events, 6.8 us)
Async XLA Ops:
  7.2 71.0 %all-gather.2.cloned.1.call-start = ((), (), s32[]{:S(2)}) async-start(), calls=%async_computation.1 | async-start | bytes 9469952 | tf_op jit(solution)/shard_map/all_gather | solution.py:427
  10.0 7.4 %collective-permute-start = (bf16[32,1152]{1,0:T(8,128)(2,1)S(1)}, bf16[32,1152]{1,0:T(8,128)(2,1)S(1)}, u32[]{:S(2)}, u32[]{:S(2)}) collective-permute-start(bf16[32,1152]{1,0:T(8,128)(2,1)S(1)} %pad_maximum_fusion.1), channel_id=1, source_target_pairs={{0,256},{16,272},{32,288},{48,304},{64,320},{80,336},{96,352},{112... | collective-permute-start | bytes 221192 | tf_op jit(solution)/shard_map/ppermute | solution.py:342
  50.8 33.4 %copy-start.3 = (bf16[256,1152]{1,0:T(8,128)(2,1)}, bf16[256,1152]{1,0:T(8,128)(2,1)S(1)}, u32[]{:S(2)}) copy-start(bf16[256,1152]{1,0:T(8,128)(2,1)S(1)} %all_gather.7.refs_0_) | copy-start | bytes 1769476
  50.8 33.4 %collective-permute-start.1 = (bf16[256,1152]{1,0:T(8,128)(2,1)S(1)}, bf16[256,1152]{1,0:T(8,128)(2,1)S(1)}, u32[]{:S(2)}, u32[]{:S(2)}) collective-permute-start(bf16[256,1152]{1,0:T(8,128)(2,1)S(1)} %all_gather.7.refs_0_), channel_id=1, source_target_pairs={{0,16},{16,32},{32,48},{48,64},{64,80},{80,96},{96,112},{112,128},... | collective-permute-start | bytes 1769480 | tf_op jit(solution)/shard_map/ppermute | solution.py:347
  53.6 30.7 %collective-permute-start.2 = (bf16[256,1152]{1,0:T(8,128)(2,1)S(1)}, bf16[256,1152]{1,0:T(8,128)(2,1)S(1)}, u32[]{:S(2)}, u32[]{:S(2)}) collective-permute-start(bf16[256,1152]{1,0:T(8,128)(2,1)S(1)} %all_gather.7.refs_0_), channel_id=1, source_target_pairs={{0,240},{16,0},{32,16},{48,32},{64,48},{80,64},{96,80},{112,96},{1... | collective-permute-start | bytes 1769480 | tf_op jit(solution)/shard_map/ppermute | solution.py:347
  57.4 26.9 %collective-permute-start.3 = (bf16[128,1152]{1,0:T(8,128)(2,1)S(1)}, bf16[128,1152]{1,0:T(8,128)(2,1)S(1)}, u32[]{:S(2)}, u32[]{:S(2)}) collective-permute-start(bf16[128,1152]{1,0:T(8,128)(2,1)S(1)} %get-tuple-element.29), channel_id=1, source_target_pairs={{0,32},{16,48},{32,64},{48,80},{64,96},{80,112},{96,128},{112,144}... | collective-permute-start | bytes 884744 | tf_op jit(solution)/shard_map/ppermute | solution.py:347
  59.3 24.9 %collective-permute-start.4 = (bf16[128,1152]{1,0:T(8,128)(2,1)S(1)}, bf16[128,1152]{1,0:T(8,128)(2,1)S(1)}, u32[]{:S(2)}, u32[]{:S(2)}) collective-permute-start(bf16[128,1152]{1,0:T(8,128)(2,1)S(1)} %get-tuple-element.28), channel_id=1, source_target_pairs={{0,224},{16,240},{32,0},{48,16},{64,32},{80,48},{96,64},{112,80},{... | collective-permute-start | bytes 884744 | tf_op jit(solution)/shard_map/ppermute | solution.py:347
  84.3 1.0 copy-start.4
  84.3 0.9 copy-start.5
  96.2 0.8 copy-start.1
  96.9 26.3 %collective-permute-start.5 = (bf16[4,64,768]{2,1,0:T(8,128)(2,1)S(1)}, bf16[4,64,768]{2,1,0:T(8,128)(2,1)S(1)}, u32[]{:S(2)}, u32[]{:S(2)}) collective-permute-start(bf16[4,64,768]{2,1,0:T(8,128)(2,1)S(1)} %get-tuple-element.22), channel_id=1, source_target_pairs={{0,16},{16,32},{32,48},{48,64},{64,80},{80,96},{96,112},{112,128},... | collective-permute-start | bytes 1179656 | tf_op jit(solution)/shard_map/ppermute | solution.py:347
  100.1 23.1 %collective-permute-start.6 = (bf16[4,64,768]{2,1,0:T(8,128)(2,1)}, bf16[4,64,768]{2,1,0:T(8,128)(2,1)}, u32[]{:S(2)}, u32[]{:S(2)}) collective-permute-start(bf16[4,64,768]{2,1,0:T(8,128)(2,1)} %get-tuple-element.23), channel_id=1, source_target_pairs={{0,240},{16,0},{32,16},{48,32},{64,48},{80,64},{96,80},{112,96},{1... | collective-permute-start | bytes 1179656 | tf_op jit(solution)/shard_map/ppermute | solution.py:347
  104.5 18.7 %collective-permute-start.7 = (bf16[4,32,768]{2,1,0:T(8,128)(2,1)}, bf16[4,32,768]{2,1,0:T(8,128)(2,1)}, u32[]{:S(2)}, u32[]{:S(2)}) collective-permute-start(bf16[4,32,768]{2,1,0:T(8,128)(2,1)} %get-tuple-element.24), channel_id=1, source_target_pairs={{0,32},{16,48},{32,64},{48,80},{64,96},{80,112},{96,128},{112,144}... | collective-permute-start | bytes 589832 | tf_op jit(solution)/shard_map/ppermute | solution.py:347
  106.4 16.7 %collective-permute-start.8 = (bf16[4,32,768]{2,1,0:T(8,128)(2,1)}, bf16[4,32,768]{2,1,0:T(8,128)(2,1)}, u32[]{:S(2)}, u32[]{:S(2)}) collective-permute-start(bf16[4,32,768]{2,1,0:T(8,128)(2,1)} %get-tuple-element.25), channel_id=1, source_target_pairs={{0,224},{16,240},{32,0},{48,16},{64,32},{80,48},{96,64},{112,80},{... | collective-permute-start | bytes 589832 | tf_op jit(solution)/shard_map/ppermute | solution.py:347
  117.2 67.8 %all-to-all-start = ((bf16[16,80,1024]{2,1,0:T(8,128)(2,1)}), bf16[16,80,1024]{2,1,0:T(8,128)(2,1)S(1)}, u32[]{:S(2)}, u32[]{:S(2)}) async-start(bf16[16,80,1024]{2,1,0:T(8,128)(2,1)} %bitcast.20), calls=%async_computation | async-start | bytes 5242880 | tf_op jit(solution)/shard_map/all_to_all | solution.py:436
  123.2 1.0 copy-start.2
  124.2 60.8 %copy-start = (bf16[16,128]{1,0:T(8,128)(2,1)S(1)}, bf16[16,128]{1,0:T(8,128)(2,1)}, u32[]{:S(2)}) copy-start(bf16[16,128]{1,0:T(8,128)(2,1)} %get-tuple-element.15.rank_ref) | copy-start | bytes 12292
  125.6 33.6 %collective-permute-start.9 = (bf16[4,32,768]{2,1,0:T(8,128)(2,1)S(1)}, bf16[4,32,768]{2,1,0:T(8,128)(2,1)S(1)}, u32[]{:S(2)}, u32[]{:S(2)}) collective-permute-start(bf16[4,32,768]{2,1,0:T(8,128)(2,1)S(1)} %get-tuple-element.27), channel_id=1, source_target_pairs={{0,256},{16,272},{32,288},{48,304},{64,320},{80,336},{96,352},{112... | collective-permute-start | bytes 589832 | tf_op jit(solution)/shard_map/ppermute | solution.py:342
  159.2 20.9 %collective-permute-start.12 = (bf16[32,768]{1,0:T(8,128)(2,1)S(1)}, bf16[32,768]{1,0:T(8,128)(2,1)S(1)}, u32[]{:S(2)}, u32[]{:S(2)}) collective-permute-start(bf16[32,768]{1,0:T(8,128)(2,1)S(1)} %get-tuple-element.31), channel_id=1, source_target_pairs={{0,192},{16,208},{32,224},{48,240},{64,0},{80,16},{96,32},{112,48}... | collective-permute-start | bytes 147464 | tf_op jit(solution)/shard_map/ppermute | solution.py:347
  166.5 13.9 %collective-permute-start.11 = (bf16[32,768]{1,0:T(8,128)(2,1)S(1)}, bf16[32,768]{1,0:T(8,128)(2,1)S(1)}, u32[]{:S(2)}, u32[]{:S(2)}) collective-permute-start(bf16[32,768]{1,0:T(8,128)(2,1)S(1)} %get-tuple-element.32), channel_id=1, source_target_pairs={{0,128},{16,144},{32,160},{48,176},{64,192},{80,208},{96,224},{112... | collective-permute-start | bytes 147464 | tf_op jit(solution)/shard_map/ppermute | solution.py:347
  172.9 11.5 %collective-permute-start.10 = (bf16[32,768]{1,0:T(8,128)(2,1)S(1)}, bf16[32,768]{1,0:T(8,128)(2,1)S(1)}, u32[]{:S(2)}, u32[]{:S(2)}) collective-permute-start(bf16[32,768]{1,0:T(8,128)(2,1)S(1)} %get-tuple-element.30), channel_id=1, source_target_pairs={{0,64},{16,80},{32,96},{48,112},{64,128},{80,144},{96,160},{112,17... | collective-permute-start | bytes 147464 | tf_op jit(solution)/shard_map/ppermute | solution.py:347
Sparse Core Ops, SparseCore 0:
  10.1 67.9 all-gather.1

commit v7 on v6

--- a/solution.py
+++ b/solution.py
@@ -64,90 +64,13 @@
     )(tokens, cotangent, route_experts.T, route_weights.T)
 
 
-def compact_kernel(my_expert, features, g_hbm, inputs_hbm, cots_hbm, blocks, inputs, cots, *sems):
-    expert = my_expert()
-    pair_total, pair_rows = blocks.shape[:2]
-    rows = pair_rows // PAIR
-    slots = PAIR * CAP
-    loads = [
-        pltpu.make_async_copy(
-            g_hbm.at[pl.ds(p * pair_rows, pair_rows), :], blocks.at[p], sems[0].at[p]
-        )
-        for p in range(pair_total)
-    ]
-    for copy in loads:
-        copy.start()
-    slot = iota((slots, pair_rows), 0).astype(F32)
-    label = iota((3 * EXPERTS, rows), 0)
-    stores = []
-    for p in range(pair_total):
-        loads[p].wait()
-        ranks, scales = [], []
-        for s in range(PAIR):
-            table = blocks[p, s * rows : s * rows + 3 * EXPERTS, 2 * features :].astype(F32)
-
-            def line(k):
-                return jnp.sum(
-                    jnp.where(label == expert + k * EXPERTS, table, 0.0), axis=0, keepdims=True
-                )
-
-            scales.append(line(0) + line(1))
-            ranks.append(line(2) + float(s * CAP))
-        hit = slot == jnp.concatenate(ranks, axis=1)
-        scale = jnp.sum(
-            jnp.where(hit, jnp.concatenate(scales, axis=1), 0.0), axis=1, keepdims=True
-        )
-        pick = as_bf16(hit)
-        here = pl.ds(p * slots, slots)
-        inputs[here, :] = jnp.dot(
-            pick, blocks[p, :, :features], preferred_element_type=F32
-        ).astype(BF16)
-        cots[here, :] = (
-            scale
-            * jnp.dot(pick, blocks[p, :, features : 2 * features], preferred_element_type=F32)
-        ).astype(BF16)
-        stores += [
-            pltpu.make_async_copy(inputs.at[here, :], inputs_hbm.at[here, :], sems[1].at[2 * p]),
-            pltpu.make_async_copy(cots.at[here, :], cots_hbm.at[here, :], sems[1].at[2 * p + 1]),
-        ]
-        for copy in stores[-2:]:
-            copy.start()
-    for copy in stores:
-        copy.wait()
-
-
-def compact(gathered, features, my_expert):
-    rows = gathered.shape[0] // EXPERTS
-    rows_out = jax.ShapeDtypeStruct((EXPERTS * CAP, features), BF16)
-    pairs = EXPERTS // PAIR
-    return pl.pallas_call(
-        functools.partial(compact_kernel, my_expert, features),
-        in_specs=[HBM],
-        out_specs=(HBM, HBM),
-        out_shape=(rows_out, rows_out),
-        scratch_shapes=[
-            pltpu.VMEM((pairs, PAIR * rows, gathered.shape[1]), BF16),
-            pltpu.VMEM((EXPERTS * CAP, features), BF16),
-            pltpu.VMEM((EXPERTS * CAP, features), BF16),
-            pltpu.SemaphoreType.DMA((pairs,)),
-            pltpu.SemaphoreType.DMA((2 * pairs,)),
-        ],
-        compiler_params=pltpu.CompilerParams(vmem_limit_bytes=VMEM_BYTES),
-        cost_estimate=pl.CostEstimate(
-            flops=4 * EXPERTS * CAP * PAIR * rows * features,
-            bytes_accessed=16 * MIB,
-            transcendentals=0,
-        ),
-        name="compact_rows",
-    )(gathered)
-
-
-def expert_kernel(my_dp, plan, x_hbm, c_hbm, *refs):
+def expert_kernel(my_expert, my_dp, plan, g_hbm, *refs):
     piece_total = 1 + max(array for array, *_ in plan)
     pieces = refs[:piece_total]
     pre_hbm, gate_up_hbm, *parts_hbm = refs[piece_total : piece_total + 7]
-    weights, gate_up, inputs, cots, pre_grad, total, *parts = refs[piece_total + 7 : -4]
+    blocks, weights, gate_up, inputs, cots, pre_grad, total, *parts = refs[piece_total + 7 : -4]
     load_sems, weight_sems, pre_sems, out_sems = refs[-4:]
+    expert = my_expert()
     features, hidden = inputs.shape[1], gate_up.shape[1] // 2
     dp = my_dp()
     upper = dp // RING
@@ -162,13 +85,14 @@
     def row_at(owner, spot):
         return pl.multiple_of(owner * half + spot * shard, shard)
 
-    loads = []
-    for m in range(BLOCKS):
-        here = rows_of(m)
-        loads += [
-            pltpu.make_async_copy(x_hbm.at[here, :], inputs.at[here, :], load_sems.at[2 * m]),
-            pltpu.make_async_copy(c_hbm.at[here, :], cots.at[here, :], load_sems.at[2 * m + 1]),
-        ]
+    pair_total, pair_rows = blocks.shape[:2]
+    rows = pair_rows // PAIR
+    loads = [
+        pltpu.make_async_copy(
+            g_hbm.at[pl.ds(p * pair_rows, pair_rows), :], blocks.at[p], load_sems.at[p]
+        )
+        for p in range(pair_total)
+    ]
     weight_loads = []
     for array, source, step, far, part in plan:
         owner = upper if part == 0 else 1 - upper
@@ -182,15 +106,47 @@
         )
     for copy in loads[:2] + weight_loads + loads[2:]:
         copy.start()
-    for copy in weight_loads:
-        copy.wait()
-    gate_up[...] = weights[:, : 2 * hidden]
-    stores = [pltpu.make_async_copy(gate_up, gate_up_hbm, out_sems.at[0])]
-    stores[0].start()
+    slot = iota((PAIR * CAP, pair_rows), 0).astype(F32)
+    label = iota((3 * EXPERTS, rows), 0)
+
+    def compact(p):
+        loads[p].wait()
+        ranks, scales = [], []
+        for s in range(PAIR):
+            table = blocks[p, s * rows : s * rows + 3 * EXPERTS, 2 * features :].astype(F32)
+
+            def line(k):
+                return jnp.sum(
+                    jnp.where(label == expert + k * EXPERTS, table, 0.0), axis=0, keepdims=True
+                )
+
+            scales.append(line(0) + line(1))
+            ranks.append(line(2) + float(s * CAP))
+        hit = slot == jnp.concatenate(ranks, axis=1)
+        scale = jnp.sum(
+            jnp.where(hit, jnp.concatenate(scales, axis=1), 0.0), axis=1, keepdims=True
+        )
+        pick = as_bf16(hit)
+        here = pl.ds(p * PAIR * CAP, PAIR * CAP)
+        inputs[here, :] = jnp.dot(
+            pick, blocks[p, :, :features], preferred_element_type=F32
+        ).astype(BF16)
+        cots[here, :] = (
+            scale
+            * jnp.dot(pick, blocks[p, :, features : 2 * features], preferred_element_type=F32)
+        ).astype(BF16)
+
+    stores = []
     for m in range(BLOCKS):
         here = rows_of(m)
-        loads[2 * m].wait()
-        loads[2 * m + 1].wait()
+        for p in range(m * pair_total // BLOCKS, (m + 1) * pair_total // BLOCKS):
+            compact(p)
+        if m == 0:
+            for copy in weight_loads:
+                copy.wait()
+            gate_up[...] = weights[:, : 2 * hidden]
+            stores.append(pltpu.make_async_copy(gate_up, gate_up_hbm, out_sems.at[0]))
+            stores[0].start()
         projected = jnp.dot(inputs[here, :], gate_up[...], preferred_element_type=F32)
         hidden_grad = jnp.dot(cots[here, :], weights[:, 2 * hidden :], preferred_element_type=F32)
         gate_part = projected[:, :hidden]
@@ -231,19 +187,21 @@
         copy.wait()
 
 
-def expert_work(inputs, cots, pieces, plan, hidden, my_dp):
-    slots, features = inputs.shape
+def expert_work(gathered, pieces, plan, features, hidden, my_expert, my_dp):
+    slots = EXPERTS * CAP
+    pair_rows = gathered.shape[0] // EXPERTS * PAIR
     shard = features // (2 * RING)
     whole = (RING // NEAR, 2 * shard, 2 * hidden)
     half = (RING // NEAR, shard, 2 * hidden)
     parts = [whole, whole, whole, half, half]
     out_shapes = [(slots, 2 * hidden), (features, 2 * hidden)] + parts
     return pl.pallas_call(
-        functools.partial(expert_kernel, my_dp, plan),
-        in_specs=[HBM] * (2 + len(pieces)),
+        functools.partial(expert_kernel, my_expert, my_dp, plan),
+        in_specs=[HBM] * (1 + len(pieces)),
         out_specs=(HBM,) * len(out_shapes),
         out_shape=tuple(jax.ShapeDtypeStruct(shape, BF16) for shape in out_shapes),
         scratch_shapes=[
+            pltpu.VMEM((EXPERTS // PAIR, pair_rows, gathered.shape[1]), BF16),
             pltpu.VMEM((features, 3 * hidden), BF16),
             pltpu.VMEM((features, 2 * hidden), BF16),
             pltpu.VMEM((slots, features), BF16),
@@ -251,19 +209,19 @@
             pltpu.VMEM((slots, 2 * hidden), BF16),
             pltpu.VMEM((features, 2 * hidden), F32),
             *[pltpu.VMEM(shape, BF16) for shape in parts],
-            pltpu.SemaphoreType.DMA((2 * BLOCKS,)),
+            pltpu.SemaphoreType.DMA((EXPERTS // PAIR,)),
             pltpu.SemaphoreType.DMA((2 * RING,)),
             pltpu.SemaphoreType.DMA((BLOCKS,)),
             pltpu.SemaphoreType.DMA((1 + len(parts),)),
         ],
-        compiler_params=pltpu.CompilerParams(vmem_limit_bytes=52 * MIB),
+        compiler_params=pltpu.CompilerParams(vmem_limit_bytes=VMEM_BYTES),
         cost_estimate=pl.CostEstimate(
             flops=5 * slots * features * 2 * hidden,
             bytes_accessed=16 * MIB,
             transcendentals=slots * hidden,
         ),
         name="expert_work",
-    )(inputs, cots, *pieces)
+    )(gathered, *pieces)
 
 
 def row_kernel(pre_hbm, gate_up_hbm, row_hbm, pre_grad, gate_up, row_grad, sems):
@@ -334,6 +292,9 @@
         combine_kernel,
         out_shape=jax.ShapeDtypeStruct((rank.shape[1], back.shape[1]), BF16),
         compiler_params=pltpu.CompilerParams(vmem_limit_bytes=16 * MIB),
+        cost_estimate=pl.CostEstimate(
+            flops=20 * 1000**3, bytes_accessed=4 * MIB, transcendentals=0
+        ),
         name="combine_rows",
     )(rank, back)
 
@@ -380,22 +341,18 @@
     return pieces, plan
 
 
-def near_sum_kernel(my_dp, keep, plus, minus, plus2, minus2, mine, theirs):
+def near_sum_kernel(keep, plus, minus, plus2, minus2, out):
     groups, shard = plus2.shape[:2]
-    upper = my_dp() // RING
     for j in range(groups):
         value = keep[j].astype(F32) + plus[j].astype(F32) + minus[j].astype(F32)
-        low = (value[:shard] + plus2[j].astype(F32)).astype(BF16)
-        high = (value[shard:] + minus2[(j - 1) % groups].astype(F32)).astype(BF16)
-        mine[j] = jnp.where(upper == 0, low, high)
-        theirs[j] = jnp.where(upper == 0, high, low)
-
-
-def near_sum(my_dp, *parts):
-    out = jax.ShapeDtypeStruct(parts[-1].shape, BF16)
-    return pl.pallas_call(
-        functools.partial(near_sum_kernel, my_dp),
-        out_shape=(out, out),
+        out[j, :shard] = (value[:shard] + plus2[j].astype(F32)).astype(BF16)
+        out[j, shard:] = (value[shard:] + minus2[(j - 1) % groups].astype(F32)).astype(BF16)
+
+
+def near_sum(*parts):
+    return pl.pallas_call(
+        near_sum_kernel,
+        out_shape=jax.ShapeDtypeStruct(parts[0].shape, BF16),
         compiler_params=pltpu.CompilerParams(vmem_limit_bytes=12 * MIB),
         cost_estimate=pl.CostEstimate(
             flops=100 * 1000**3, bytes_accessed=4 * MIB, transcendentals=0
@@ -404,20 +361,39 @@
     )(*parts)
 
 
+def far_sum_kernel(my_dp, one, two, three, four, mine, theirs):
+    shard = mine.shape[0]
+    total = one[...].astype(F32) + two[...].astype(F32) + three[...].astype(F32)
+    total += four[...].astype(F32)
+    first = my_dp() < RING
+    mine[...] = jnp.where(first, total[:shard], total[shard:])
+    theirs[...] = jnp.where(first, total[shard:], total[:shard]).astype(BF16)
+
+
+def far_sum(my_dp, *parts):
+    rows, columns = parts[0].shape
+    return pl.pallas_call(
+        functools.partial(far_sum_kernel, my_dp),
+        out_shape=(
+            jax.ShapeDtypeStruct((rows // 2, columns), F32),
+            jax.ShapeDtypeStruct((rows // 2, columns), BF16),
+        ),
+        compiler_params=pltpu.CompilerParams(vmem_limit_bytes=12 * MIB),
+        name="far_sum",
+    )(*parts)
+
+
 def scatter_sum(keep, plus, minus, plus2, minus2, scale, my_dp):
-    mine, theirs = near_sum(
-        my_dp,
+    part = near_sum(
         keep,
         shift_ring(plus, 1),
         shift_ring(minus, -1),
         shift_ring(plus2, 2),
         shift_ring(minus2, -2),
     )
-    part = (mine.astype(F32) + swap_halves(theirs).astype(F32)).astype(BF16)
-    total = part[0].astype(F32)
-    for j in range(1, RING // NEAR):
-        total += shift_ring(part[j], NEAR * j).astype(F32)
-    return (total * scale)[None]
+    parts = [part[0]] + [shift_ring(part[j], NEAR * j) for j in range(1, RING // NEAR)]
+    mine, theirs = far_sum(my_dp, *parts)
+    return ((mine + swap_halves(theirs).astype(F32)) * scale)[None]
 
 
 def shards(tokens, cotangent, route_experts, route_weights, gate_up, down):
@@ -430,8 +406,9 @@
     def my_dp():
         return lax.axis_index("dp")
 
-    inputs, cots = compact(gathered, features, lambda: lax.axis_index("expert"))
-    pre_grad, full_gate_up, *grad_parts = expert_work(inputs, cots, pieces, plan, hidden, my_dp)
+    pre_grad, full_gate_up, *grad_parts = expert_work(
+        gathered, pieces, plan, features, hidden, lambda: lax.axis_index("expert"), my_dp
+    )
     row_grads = row_gradients(pre_grad, full_gate_up)
     returned = lax.all_to_all(
         row_grads.reshape(EXPERTS, CAP, features), "expert", split_axis=0, concat_axis=0, tiled=True

time: 194 us -> 176 us (0.907)
  waiting for transfers between devices: 48.5 us -> 33 us
  Pallas kernels: 26.9 us -> 24.4 us
    ppermute x2, waiting for transfers between devices: 31 us -> 3.53 us  [swap_halves(): lax.ppermute(x, 'dp', [(d, (d + RING) % (2 * RING)) for d in range(2 * RI...]
    ppermute x11, waiting for transfers between devices: 4.2 us -> 28.9 us  [shift_ring(): return lax.ppermute(x, 'dp', pairs)]
    all_gather x1, waiting for transfers between devices: 13.3 us -> 0.61 us  [shards(): gathered = lax.all_gather(packed, 'expert', axis=0, tiled=True)]
    ppermute x11, starting transfers between devices: 49.8 us -> 42.5 us  [shift_ring(): return lax.ppermute(x, 'dp', pairs)]
    all_to_all x1, starting transfers between devices: 5.98 us -> 12.9 us  [shards(): lax.all_to_all(row_grads.reshape(EXPERTS, CAP, features), 'expert', split...]
    pallas_call x3, Pallas kernels: 18.3 us -> 15.8 us  [the longest x1 14.6 us: expert_work(): pl.pallas_call(functools.partial(expert_kernel, my_expert, my_dp, plan),...]
  transfers between devices with their start and end apart: 15 -> 15, of which waited for: 5 -> 8; matrix products, arithmetic and copies ran while one was open for 1% -> 1% of each run, Pallas kernels for 7% -> 4%
where the time goes in v7:
time: 176 us; the launch traced here: 174 us
  starting transfers between devices  65.6 us (37%)
  waiting for transfers between devices  33 us (19%)
  blocking collectives  32.6 us (19%)
  Pallas kernels  24.4 us (14%)
  between operations  14.2 us (8%)
  other arithmetic  2.31 us (1%)
    ppermute x11, starting transfers between devices, shift_ring(): return lax.ppermute(x, 'dp', pairs)  42.5 us
    all_gather x1, blocking collectives, gather_weights(): lax.all_gather(both, 'dp', axis=0, axis_index_groups=far_groups(), tiled=...  32.6 us
    ppermute x11, waiting for transfers between devices, shift_ring(): return lax.ppermute(x, 'dp', pairs)  28.9 us
    pallas_call x1, Pallas kernels, expert_work(): pl.pallas_call(functools.partial(expert_kernel, my_expert, my_dp, plan),...  14.6 us
    all_to_all x1, starting transfers between devices, shards(): lax.all_to_all(row_grads.reshape(EXPERTS, CAP, features), 'expert', split...  12.9 us
    ppermute x2, starting transfers between devices, swap_halves(): lax.ppermute(x, 'dp', [(d, (d + RING) % (2 * RING)) for d in range(2 * RI...  10.2 us
    pallas_call x1, Pallas kernels, row_gradients(): pl.pallas_call(row_kernel, in_specs=[HBM, HBM], out_specs=HBM, out_shape=...  5.26 us
    ppermute x2, waiting for transfers between devices, swap_halves(): lax.ppermute(x, 'dp', [(d, (d + RING) % (2 * RING)) for d in range(2 * RI...  3.53 us
  transfers between devices with their start and end apart: 15, of which 8 were waited for; matrix products, arithmetic and copies ran while one was open for 1% of the time, Pallas kernels for 4%

profile of v7, /device:TPU:1, one launch (start us, length us, event | category | flops | bytes accessed | tf_op | source)
XLA Modules:
  0.0 173.8 jit_solution(16211702974409462633)
XLA Ops:
  7.2 2.0 %pack_rows.1 = (bf16[128,2176]{1,0:T(8,128)(2,1)}, bf16[16,128]{1,0:T(8,128)(2,1)}) custom-call(bf16[128,1024]{1,0:T(8,128)(2,1)} %tok_ref.1, bf16[128,1024]{1,0:T(8,128)(2,1)} %cot_ref.1, s32[8,128]{1,0:T(8,128)} %bitcast.22, f32[8,128]{1,0:T(8,128)} %bitcast.23), custom_call_target="tpu_custom_call" | custom-call | tf_op jit(solution)/shard_map/pack_rows/pallas_call | solution.py:56
  10.0 5.6 %collective-permute-start = (bf16[32,1152]{1,0:T(8,128)(2,1)S(1)}, bf16[32,1152]{1,0:T(8,128)(2,1)S(1)}, u32[]{:S(2)}, u32[]{:S(2)}) collective-permute-start(bf16[32,1152]{1,0:T(8,128)(2,1)S(1)} %pad_maximum_fusion.1), channel_id=1, source_target_pairs={{0,256},{16,272},{32,288},{48,304},{64,320},{80,336},{96,352},{112... | collective-permute-start | bytes 221192 | tf_op jit(solution)/shard_map/ppermute | solution.py:303
  15.7 1.7 collective-permute-done
  18.2 32.6 %all_gather.7.refs_0_ = bf16[256,1152]{1,0:T(8,128)(2,1)S(1)} all-gather(bf16[64,1152]{1,0:T(8,128)(2,1)S(1)} %pad_maximum_fusion), channel_id=1, replica_groups={{0,64,128,192},{16,80,144,208},{32,96,160,224},{48,112,176,240},{256,32..., dimensions={0}, use_global_device_ids=true | all-gather | bytes 737280 | tf_op jit(solution)/shard_map/all_gather | solution.py:323
  50.8 3.8 %collective-permute-start.2 = (bf16[256,1152]{1,0:T(8,128)(2,1)S(1)}, bf16[256,1152]{1,0:T(8,128)(2,1)S(1)}, u32[]{:S(2)}, u32[]{:S(2)}) collective-permute-start(bf16[256,1152]{1,0:T(8,128)(2,1)S(1)} %all_gather.7.refs_0_), channel_id=1, source_target_pairs={{0,240},{16,0},{32,16},{48,32},{64,48},{80,64},{96,80},{112,96},{1... | collective-permute-start | bytes 1769480 | tf_op jit(solution)/shard_map/ppermute | solution.py:308
  54.6 1.9 %collective-permute-start.1 = (bf16[256,1152]{1,0:T(8,128)(2,1)S(1)}, bf16[256,1152]{1,0:T(8,128)(2,1)S(1)}, u32[]{:S(2)}, u32[]{:S(2)}) collective-permute-start(bf16[256,1152]{1,0:T(8,128)(2,1)S(1)} %all_gather.7.refs_0_), channel_id=1, source_target_pairs={{0,16},{16,32},{32,48},{48,64},{64,80},{80,96},{96,112},{112,128},... | collective-permute-start | bytes 1769480 | tf_op jit(solution)/shard_map/ppermute | solution.py:308
  56.6 3.1 %collective-permute-start.4 = (bf16[128,1152]{1,0:T(8,128)(2,1)S(1)}, bf16[128,1152]{1,0:T(8,128)(2,1)S(1)}, u32[]{:S(2)}, u32[]{:S(2)}) collective-permute-start(bf16[128,1152]{1,0:T(8,128)(2,1)S(1)} %get-tuple-element.24), channel_id=1, source_target_pairs={{0,224},{16,240},{32,0},{48,16},{64,32},{80,48},{96,64},{112,80},{... | collective-permute-start | bytes 884744 | tf_op jit(solution)/shard_map/ppermute | solution.py:308
  59.7 3.1 %collective-permute-start.3 = (bf16[128,1152]{1,0:T(8,128)(2,1)S(1)}, bf16[128,1152]{1,0:T(8,128)(2,1)S(1)}, u32[]{:S(2)}, u32[]{:S(2)}) collective-permute-start(bf16[128,1152]{1,0:T(8,128)(2,1)S(1)} %get-tuple-element.25), channel_id=1, source_target_pairs={{0,32},{16,48},{32,64},{48,80},{64,96},{80,112},{96,128},{112,144}... | collective-permute-start | bytes 884744 | tf_op jit(solution)/shard_map/ppermute | solution.py:308
  62.8 14.2 %collective-permute-done.4.refs_4_ = bf16[128,1152]{1,0:T(8,128)(2,1)S(1)} collective-permute-done((bf16[128,1152]{1,0:T(8,128)(2,1)S(1)}, bf16[128,1152]{1,0:T(8,128)(2,1)S(1)}, u32[]{:S(2)}, u32[]{:S(2)}) %collective-permute-start.4) | collective-permute-done | bytes 294944 | tf_op jit(solution)/shard_map/ppermute | solution.py:308
  78.6 14.6 %expert_work.1 = (bf16[1280,768]{1,0:T(8,128)(2,1)}, bf16[1024,768]{1,0:T(8,128)(2,1)}, bf16[4,64,768]{2,1,0:T(8,128)(2,1)}, bf16[4,64,768]{2,1,0:T(8,128)(2,1)}...) custom-call(bf16[2048,2176]{1,0:T(8,128)(2,1)} %all-gather.2.cloned.1.call-done.g_hbm, ...), custom_call_target="tpu_custom_call" | custom-call | flops 5033164800 | bytes 16777216 | tf_op jit(solution)/shard_map/expert_work/pallas_call | solution.py:198
  93.2 4.7 %collective-permute-start.5 = (bf16[4,64,768]{2,1,0:T(8,128)(2,1)}, bf16[4,64,768]{2,1,0:T(8,128)(2,1)S(1)}, u32[]{:S(2)}, u32[]{:S(2)}) collective-permute-start(bf16[4,64,768]{2,1,0:T(8,128)(2,1)} %get-tuple-element.18), channel_id=1, source_target_pairs={{0,16},{16,32},{32,48},{48,64},{64,80},{80,96},{96,112},{112,128},... | collective-permute-start | bytes 1179656 | tf_op jit(solution)/shard_map/ppermute | solution.py:308
  97.9 2.5 %collective-permute-start.6 = (bf16[4,64,768]{2,1,0:T(8,128)(2,1)}, bf16[4,64,768]{2,1,0:T(8,128)(2,1)S(1)}, u32[]{:S(2)}, u32[]{:S(2)}) collective-permute-start(bf16[4,64,768]{2,1,0:T(8,128)(2,1)} %get-tuple-element.19), channel_id=1, source_target_pairs={{0,240},{16,0},{32,16},{48,32},{64,48},{80,64},{96,80},{112,96},{1... | collective-permute-start | bytes 1179656 | tf_op jit(solution)/shard_map/ppermute | solution.py:308
  100.4 2.5 %collective-permute-start.7 = (bf16[4,32,768]{2,1,0:T(8,128)(2,1)}, bf16[4,32,768]{2,1,0:T(8,128)(2,1)}, u32[]{:S(2)}, u32[]{:S(2)}) collective-permute-start(bf16[4,32,768]{2,1,0:T(8,128)(2,1)} %get-tuple-element.20), channel_id=1, source_target_pairs={{0,32},{16,48},{32,64},{48,80},{64,96},{80,112},{96,128},{112,144}... | collective-permute-start | bytes 589832 | tf_op jit(solution)/shard_map/ppermute | solution.py:308
  102.9 4.9 %collective-permute-start.8 = (bf16[4,32,768]{2,1,0:T(8,128)(2,1)}, bf16[4,32,768]{2,1,0:T(8,128)(2,1)}, u32[]{:S(2)}, u32[]{:S(2)}) collective-permute-start(bf16[4,32,768]{2,1,0:T(8,128)(2,1)} %get-tuple-element.21), channel_id=1, source_target_pairs={{0,224},{16,240},{32,0},{48,16},{64,32},{80,48},{96,64},{112,80},{... | collective-permute-start | bytes 589832 | tf_op jit(solution)/shard_map/ppermute | solution.py:308
  107.8 5.3 %row_gradients.1 = bf16[1280,1024]{1,0:T(8,128)(2,1)} custom-call(bf16[1280,768]{1,0:T(8,128)(2,1)} %get-tuple-element.15.pre_hbm, bf16[1024,768]{1,0:T(8,128)(2,1)} %get-tuple-element.16.gate_up_hbm), custom_call_target="tpu_custom_call" | custom-call | flops 2013265920 | bytes 6291456 | tf_op jit(solution)/shard_map/row_gradients/pallas_call | solution.py:258
  113.0 12.9 %all-to-all-start = ((bf16[16,80,1024]{2,1,0:T(8,128)(2,1)}), bf16[16,80,1024]{2,1,0:T(8,128)(2,1)S(1)}, u32[]{:S(2)}, u32[]{:S(2)}) async-start(bf16[16,80,1024]{2,1,0:T(8,128)(2,1)} %bitcast.17), calls=%async_computation | async-start | bytes 5242880 | tf_op jit(solution)/shard_map/all_to_all | solution.py:413
  128.2 4.2 %collective-permute-start.11 = (bf16[64,768]{1,0:T(8,128)(2,1)S(1)}, bf16[64,768]{1,0:T(8,128)(2,1)S(1)}, u32[]{:S(2)}, u32[]{:S(2)}) collective-permute-start(bf16[64,768]{1,0:T(8,128)(2,1)S(1)} %get-tuple-element.26), channel_id=1, source_target_pairs={{0,192},{16,208},{32,224},{48,240},{64,0},{80,16},{96,32},{112,48}... | collective-permute-start | bytes 294920 | tf_op jit(solution)/shard_map/ppermute | solution.py:308
  132.5 6.9 %collective-permute-start.10 = (bf16[64,768]{1,0:T(8,128)(2,1)S(1)}, bf16[64,768]{1,0:T(8,128)(2,1)S(1)}, u32[]{:S(2)}, u32[]{:S(2)}) collective-permute-start(bf16[64,768]{1,0:T(8,128)(2,1)S(1)} %get-tuple-element.27), channel_id=1, source_target_pairs={{0,128},{16,144},{32,160},{48,176},{64,192},{80,208},{96,224},{112... | collective-permute-start | bytes 294920 | tf_op jit(solution)/shard_map/ppermute | solution.py:308
  139.4 4.9 %collective-permute-start.9 = (bf16[64,768]{1,0:T(8,128)(2,1)S(1)}, bf16[64,768]{1,0:T(8,128)(2,1)S(1)}, u32[]{:S(2)}, u32[]{:S(2)}) collective-permute-start(bf16[64,768]{1,0:T(8,128)(2,1)S(1)} %get-tuple-element.28), channel_id=1, source_target_pairs={{0,64},{16,80},{32,96},{48,112},{64,128},{80,144},{96,160},{112,17... | collective-permute-start | bytes 294920 | tf_op jit(solution)/shard_map/ppermute | solution.py:308
  144.6 12.5 %collective-permute-done.10.three = bf16[64,768]{1,0:T(8,128)(2,1)S(1)} collective-permute-done((bf16[64,768]{1,0:T(8,128)(2,1)S(1)}, bf16[64,768]{1,0:T(8,128)(2,1)S(1)}, u32[]{:S(2)}, u32[]{:S(2)}) %collective-permute-start.10) | collective-permute-done | bytes 98336 | tf_op jit(solution)/shard_map/ppermute | solution.py:308
  157.1 1.4 collective-permute-done.9.two
  158.6 4.5 %collective-permute-start.12 = (bf16[32,768]{1,0:T(8,128)(2,1)S(1)}, bf16[32,768]{1,0:T(8,128)(2,1)S(1)}, u32[]{:S(2)}, u32[]{:S(2)}) collective-permute-start(bf16[32,768]{1,0:T(8,128)(2,1)S(1)} %get-tuple-element.23), channel_id=1, source_target_pairs={{0,256},{16,272},{32,288},{48,304},{64,320},{80,336},{96,352},{112... | collective-permute-start | bytes 147464 | tf_op jit(solution)/shard_map/ppermute | solution.py:303
  163.1 1.8 %collective-permute-done.12 = bf16[32,768]{1,0:T(8,128)(2,1)S(1)} collective-permute-done((bf16[32,768]{1,0:T(8,128)(2,1)S(1)}, bf16[32,768]{1,0:T(8,128)(2,1)S(1)}, u32[]{:S(2)}, u32[]{:S(2)}) %collective-permute-start.12) | collective-permute-done | bytes 49184 | tf_op jit(solution)/shard_map/ppermute | solution.py:303
  165.6 1.4 combine_rows.1
  (33 shorter events, 6.6 us)
Async XLA Ops:
  7.2 71.0 %all-gather.2.cloned.1.call-start = ((), (), s32[]{:S(2)}) async-start(), calls=%async_computation.1 | async-start | bytes 9469952 | tf_op jit(solution)/shard_map/all_gather | solution.py:403
  10.0 7.4 %collective-permute-start = (bf16[32,1152]{1,0:T(8,128)(2,1)S(1)}, bf16[32,1152]{1,0:T(8,128)(2,1)S(1)}, u32[]{:S(2)}, u32[]{:S(2)}) collective-permute-start(bf16[32,1152]{1,0:T(8,128)(2,1)S(1)} %pad_maximum_fusion.1), channel_id=1, source_target_pairs={{0,256},{16,272},{32,288},{48,304},{64,320},{80,336},{96,352},{112... | collective-permute-start | bytes 221192 | tf_op jit(solution)/shard_map/ppermute | solution.py:303
  50.8 27.3 %copy-start.2 = (bf16[256,1152]{1,0:T(8,128)(2,1)}, bf16[256,1152]{1,0:T(8,128)(2,1)S(1)}, u32[]{:S(2)}) copy-start(bf16[256,1152]{1,0:T(8,128)(2,1)S(1)} %all_gather.7.refs_0_) | copy-start | bytes 1769476
  50.8 26.7 %collective-permute-start.2 = (bf16[256,1152]{1,0:T(8,128)(2,1)S(1)}, bf16[256,1152]{1,0:T(8,128)(2,1)S(1)}, u32[]{:S(2)}, u32[]{:S(2)}) collective-permute-start(bf16[256,1152]{1,0:T(8,128)(2,1)S(1)} %all_gather.7.refs_0_), channel_id=1, source_target_pairs={{0,240},{16,0},{32,16},{48,32},{64,48},{80,64},{96,80},{112,96},{1... | collective-permute-start | bytes 1769480 | tf_op jit(solution)/shard_map/ppermute | solution.py:308
  54.6 22.9 %collective-permute-start.1 = (bf16[256,1152]{1,0:T(8,128)(2,1)S(1)}, bf16[256,1152]{1,0:T(8,128)(2,1)S(1)}, u32[]{:S(2)}, u32[]{:S(2)}) collective-permute-start(bf16[256,1152]{1,0:T(8,128)(2,1)S(1)} %all_gather.7.refs_0_), channel_id=1, source_target_pairs={{0,16},{16,32},{32,48},{48,64},{64,80},{80,96},{96,112},{112,128},... | collective-permute-start | bytes 1769480 | tf_op jit(solution)/shard_map/ppermute | solution.py:308
  56.6 20.4 %collective-permute-start.4 = (bf16[128,1152]{1,0:T(8,128)(2,1)S(1)}, bf16[128,1152]{1,0:T(8,128)(2,1)S(1)}, u32[]{:S(2)}, u32[]{:S(2)}) collective-permute-start(bf16[128,1152]{1,0:T(8,128)(2,1)S(1)} %get-tuple-element.24), channel_id=1, source_target_pairs={{0,224},{16,240},{32,0},{48,16},{64,32},{80,48},{96,64},{112,80},{... | collective-permute-start | bytes 884744 | tf_op jit(solution)/shard_map/ppermute | solution.py:308
  59.7 17.8 %collective-permute-start.3 = (bf16[128,1152]{1,0:T(8,128)(2,1)S(1)}, bf16[128,1152]{1,0:T(8,128)(2,1)S(1)}, u32[]{:S(2)}, u32[]{:S(2)}) collective-permute-start(bf16[128,1152]{1,0:T(8,128)(2,1)S(1)} %get-tuple-element.25), channel_id=1, source_target_pairs={{0,32},{16,48},{32,64},{48,80},{64,96},{80,112},{96,128},{112,144}... | collective-permute-start | bytes 884744 | tf_op jit(solution)/shard_map/ppermute | solution.py:308
  77.0 1.2 copy-start.5
  77.5 0.7 copy-start.6
  77.5 0.9 copy-start.3
  77.5 1.1 copy-start.4
  93.2 32.8 %collective-permute-start.5 = (bf16[4,64,768]{2,1,0:T(8,128)(2,1)}, bf16[4,64,768]{2,1,0:T(8,128)(2,1)S(1)}, u32[]{:S(2)}, u32[]{:S(2)}) collective-permute-start(bf16[4,64,768]{2,1,0:T(8,128)(2,1)} %get-tuple-element.18), channel_id=1, source_target_pairs={{0,16},{16,32},{32,48},{48,64},{64,80},{80,96},{96,112},{112,128},... | collective-permute-start | bytes 1179656 | tf_op jit(solution)/shard_map/ppermute | solution.py:308
  97.9 28.1 %collective-permute-start.6 = (bf16[4,64,768]{2,1,0:T(8,128)(2,1)}, bf16[4,64,768]{2,1,0:T(8,128)(2,1)S(1)}, u32[]{:S(2)}, u32[]{:S(2)}) collective-permute-start(bf16[4,64,768]{2,1,0:T(8,128)(2,1)} %get-tuple-element.19), channel_id=1, source_target_pairs={{0,240},{16,0},{32,16},{48,32},{64,48},{80,64},{96,80},{112,96},{1... | collective-permute-start | bytes 1179656 | tf_op jit(solution)/shard_map/ppermute | solution.py:308
  100.4 25.6 %collective-permute-start.7 = (bf16[4,32,768]{2,1,0:T(8,128)(2,1)}, bf16[4,32,768]{2,1,0:T(8,128)(2,1)}, u32[]{:S(2)}, u32[]{:S(2)}) collective-permute-start(bf16[4,32,768]{2,1,0:T(8,128)(2,1)} %get-tuple-element.20), channel_id=1, source_target_pairs={{0,32},{16,48},{32,64},{48,80},{64,96},{80,112},{96,128},{112,144}... | collective-permute-start | bytes 589832 | tf_op jit(solution)/shard_map/ppermute | solution.py:308
  102.9 23.1 %collective-permute-start.8 = (bf16[4,32,768]{2,1,0:T(8,128)(2,1)}, bf16[4,32,768]{2,1,0:T(8,128)(2,1)}, u32[]{:S(2)}, u32[]{:S(2)}) collective-permute-start(bf16[4,32,768]{2,1,0:T(8,128)(2,1)} %get-tuple-element.21), channel_id=1, source_target_pairs={{0,224},{16,240},{32,0},{48,16},{64,32},{80,48},{96,64},{112,80},{... | collective-permute-start | bytes 589832 | tf_op jit(solution)/shard_map/ppermute | solution.py:308
  113.0 52.6 %all-to-all-start = ((bf16[16,80,1024]{2,1,0:T(8,128)(2,1)}), bf16[16,80,1024]{2,1,0:T(8,128)(2,1)S(1)}, u32[]{:S(2)}, u32[]{:S(2)}) async-start(bf16[16,80,1024]{2,1,0:T(8,128)(2,1)} %bitcast.17), calls=%async_computation | async-start | bytes 5242880 | tf_op jit(solution)/shard_map/all_to_all | solution.py:413
  126.0 1.0 copy-start.1
  127.0 38.6 %copy-start = (bf16[16,128]{1,0:T(8,128)(2,1)S(1)}, bf16[16,128]{1,0:T(8,128)(2,1)}, u32[]{:S(2)}) copy-start(bf16[16,128]{1,0:T(8,128)(2,1)} %get-tuple-element.13.rank_ref) | copy-start | bytes 12292
  128.2 16.4 %collective-permute-start.11 = (bf16[64,768]{1,0:T(8,128)(2,1)S(1)}, bf16[64,768]{1,0:T(8,128)(2,1)S(1)}, u32[]{:S(2)}, u32[]{:S(2)}) collective-permute-start(bf16[64,768]{1,0:T(8,128)(2,1)S(1)} %get-tuple-element.26), channel_id=1, source_target_pairs={{0,192},{16,208},{32,224},{48,240},{64,0},{80,16},{96,32},{112,48}... | collective-permute-start | bytes 294920 | tf_op jit(solution)/shard_map/ppermute | solution.py:308
  132.5 24.7 %collective-permute-start.10 = (bf16[64,768]{1,0:T(8,128)(2,1)S(1)}, bf16[64,768]{1,0:T(8,128)(2,1)S(1)}, u32[]{:S(2)}, u32[]{:S(2)}) collective-permute-start(bf16[64,768]{1,0:T(8,128)(2,1)S(1)} %get-tuple-element.27), channel_id=1, source_target_pairs={{0,128},{16,144},{32,160},{48,176},{64,192},{80,208},{96,224},{112... | collective-permute-start | bytes 294920 | tf_op jit(solution)/shard_map/ppermute | solution.py:308
  139.4 19.1 %collective-permute-start.9 = (bf16[64,768]{1,0:T(8,128)(2,1)S(1)}, bf16[64,768]{1,0:T(8,128)(2,1)S(1)}, u32[]{:S(2)}, u32[]{:S(2)}) collective-permute-start(bf16[64,768]{1,0:T(8,128)(2,1)S(1)} %get-tuple-element.28), channel_id=1, source_target_pairs={{0,64},{16,80},{32,96},{48,112},{64,128},{80,144},{96,160},{112,17... | collective-permute-start | bytes 294920 | tf_op jit(solution)/shard_map/ppermute | solution.py:308
  158.6 6.3 %collective-permute-start.12 = (bf16[32,768]{1,0:T(8,128)(2,1)S(1)}, bf16[32,768]{1,0:T(8,128)(2,1)S(1)}, u32[]{:S(2)}, u32[]{:S(2)}) collective-permute-start(bf16[32,768]{1,0:T(8,128)(2,1)S(1)} %get-tuple-element.23), channel_id=1, source_target_pairs={{0,256},{16,272},{32,288},{48,304},{64,320},{80,336},{96,352},{112... | collective-permute-start | bytes 147464 | tf_op jit(solution)/shard_map/ppermute | solution.py:303
Sparse Core Ops, SparseCore 0:
  10.1 67.9 all-gather.1

commit v8 on v7

--- a/solution.py
+++ b/solution.py
@@ -274,7 +274,8 @@
     )(pre_grad, gate_up)
 
 
-def combine_kernel(rank_ref, back_ref, out_ref):
+def combine_kernel(rank_ref, back_ref, out_ref, done_ref):
+    done_ref[...] = jnp.zeros_like(done_ref)
     slots = back_ref.shape[0]
     column = iota((EXPERTS, slots), 1) - CAP * iota((EXPERTS, slots), 0)
     spread = as_bf16((column >= 0) & (column < CAP))
@@ -290,7 +291,10 @@
 def combine(rank, back):
     return pl.pallas_call(
         combine_kernel,
-        out_shape=jax.ShapeDtypeStruct((rank.shape[1], back.shape[1]), BF16),
+        out_shape=(
+            jax.ShapeDtypeStruct((rank.shape[1], back.shape[1]), BF16),
+            jax.ShapeDtypeStruct((8, LANES), F32),
+        ),
         compiler_params=pltpu.CompilerParams(vmem_limit_bytes=16 * MIB),
         cost_estimate=pl.CostEstimate(
             flops=20 * 1000**3, bytes_accessed=4 * MIB, transcendentals=0
@@ -341,18 +345,31 @@
     return pieces, plan
 
 
-def near_sum_kernel(keep, plus, minus, plus2, minus2, out):
+def near_sum_kernel(keep, plus, minus, plus2, minus2, here, ahead, behind, far_low, far_high):
     groups, shard = plus2.shape[:2]
-    for j in range(groups):
-        value = keep[j].astype(F32) + plus[j].astype(F32) + minus[j].astype(F32)
-        out[j, :shard] = (value[:shard] + plus2[j].astype(F32)).astype(BF16)
-        out[j, shard:] = (value[shard:] + minus2[(j - 1) % groups].astype(F32)).astype(BF16)
+
+    def low(j):
+        value = keep[j, :shard].astype(F32) + plus[j, :shard].astype(F32)
+        return (value + minus[j, :shard].astype(F32) + plus2[j].astype(F32)).astype(BF16)
+
+    def high(j):
+        value = keep[j, shard:].astype(F32) + plus[j, shard:].astype(F32)
+        value += minus[j, shard:].astype(F32) + minus2[(j - 1) % groups].astype(F32)
+        return value.astype(BF16)
+
+    for j, out in ((0, here), (1, ahead), (3, behind)):
+        out[:shard] = low(j)
+        out[shard:] = high(j)
+    far_low[...], far_high[...] = low(2), high(2)
 
 
 def near_sum(*parts):
+    _, rows, columns = parts[0].shape
+    whole = jax.ShapeDtypeStruct((rows, columns), BF16)
+    half = jax.ShapeDtypeStruct((rows // 2, columns), BF16)
     return pl.pallas_call(
         near_sum_kernel,
-        out_shape=jax.ShapeDtypeStruct(parts[0].shape, BF16),
+        out_shape=(whole, whole, whole, half, half),
         compiler_params=pltpu.CompilerParams(vmem_limit_bytes=12 * MIB),
         cost_estimate=pl.CostEstimate(
             flops=100 * 1000**3, bytes_accessed=4 * MIB, transcendentals=0
@@ -361,10 +378,27 @@
     )(*parts)
 
 
-def far_sum_kernel(my_dp, one, two, three, four, mine, theirs):
+def relay_sum_kernel(ahead, behind, got_low, got_high, ahead_out, behind_out):
+    shard = got_low.shape[0]
+    ahead_out[:shard] = (ahead[:shard].astype(F32) + got_low[...].astype(F32)).astype(BF16)
+    ahead_out[shard:] = ahead[shard:]
+    behind_out[:shard] = behind[:shard]
+    behind_out[shard:] = (behind[shard:].astype(F32) + got_high[...].astype(F32)).astype(BF16)
+
+
+def relay_sum(ahead, *parts):
+    whole = jax.ShapeDtypeStruct(ahead.shape, BF16)
+    return pl.pallas_call(
+        relay_sum_kernel,
+        out_shape=(whole, whole),
+        compiler_params=pltpu.CompilerParams(vmem_limit_bytes=12 * MIB),
+        name="relay_sum",
+    )(ahead, *parts)
+
+
+def far_sum_kernel(my_dp, here, got_ahead, got_behind, mine, theirs):
     shard = mine.shape[0]
-    total = one[...].astype(F32) + two[...].astype(F32) + three[...].astype(F32)
-    total += four[...].astype(F32)
+    total = here[...].astype(F32) + got_ahead[...].astype(F32) + got_behind[...].astype(F32)
     first = my_dp() < RING
     mine[...] = jnp.where(first, total[:shard], total[shard:])
     theirs[...] = jnp.where(first, total[shard:], total[:shard]).astype(BF16)
@@ -383,17 +417,34 @@
     )(*parts)
 
 
-def scatter_sum(keep, plus, minus, plus2, minus2, scale, my_dp):
-    part = near_sum(
+def last_sum_kernel(scale, mine, got, earlier, out):
+    del earlier
+    out[0] = (mine[...] + got[...].astype(F32)) * scale
+
+
+def last_sum(scale, mine, got, earlier):
+    return pl.pallas_call(
+        functools.partial(last_sum_kernel, scale),
+        in_specs=[VMEM, VMEM, pl.BlockSpec(memory_space=pl.ANY)],
+        out_shape=jax.ShapeDtypeStruct((1, *mine.shape), F32),
+        compiler_params=pltpu.CompilerParams(vmem_limit_bytes=8 * MIB),
+        name="last_sum",
+    )(mine, got, earlier)
+
+
+def scatter_sum(keep, plus, minus, plus2, minus2, my_dp):
+    here, ahead, behind, far_low, far_high = near_sum(
         keep,
         shift_ring(plus, 1),
         shift_ring(minus, -1),
         shift_ring(plus2, 2),
         shift_ring(minus2, -2),
     )
-    parts = [part[0]] + [shift_ring(part[j], NEAR * j) for j in range(1, RING // NEAR)]
-    mine, theirs = far_sum(my_dp, *parts)
-    return ((mine + swap_halves(theirs).astype(F32)) * scale)[None]
+    ahead, behind = relay_sum(
+        ahead, behind, shift_ring(far_low, NEAR), shift_ring(far_high, -NEAR)
+    )
+    mine, theirs = far_sum(my_dp, here, shift_ring(ahead, NEAR), shift_ring(behind, -NEAR))
+    return mine, swap_halves(theirs)
 
 
 def shards(tokens, cotangent, route_experts, route_weights, gate_up, down):
@@ -414,8 +465,9 @@
         row_grads.reshape(EXPERTS, CAP, features), "expert", split_axis=0, concat_axis=0, tiled=True
     )
     grad_scale = 1.0 / math.sqrt(rows * lax.axis_size("dp") * lax.axis_size("expert"))
-    grad_gate_up = scatter_sum(*grad_parts, grad_scale, my_dp)
-    token_grad = combine(rank, returned.reshape(EXPERTS * CAP, features))
+    mine, got = scatter_sum(*grad_parts, my_dp)
+    token_grad, done = combine(rank, returned.reshape(EXPERTS * CAP, features))
+    grad_gate_up = last_sum(grad_scale, mine, got, done)
     return (token_grad, grad_gate_up)
 
 

time: 176 us -> 178 us (1.011)
  starting transfers between devices: 65.6 us -> 67.7 us
    ppermute x11 -> x12, waiting for transfers between devices: 28.9 us -> 31.3 us  [shift_ring(): return lax.ppermute(x, 'dp', pairs)]
    ppermute x11 -> x12, starting transfers between devices: 42.5 us -> 44.8 us  [shift_ring(): return lax.ppermute(x, 'dp', pairs)]
  transfers between devices with their start and end apart: 15 -> 16, of which waited for: 8 -> 9; matrix products, arithmetic and copies ran while one was open for 1% -> 1% of each run, Pallas kernels for 4% -> 4%
where the time goes in v8:
time: 178 us; the launch traced here: 177 us
  starting transfers between devices  67.7 us (38%)
  waiting for transfers between devices  34.3 us (19%)
  blocking collectives  32.6 us (18%)
  Pallas kernels  25.1 us (14%)
  between operations  14.2 us (8%)
    ppermute x12, starting transfers between devices, shift_ring(): return lax.ppermute(x, 'dp', pairs)  44.8 us
    all_gather x1, blocking collectives, gather_weights(): lax.all_gather(both, 'dp', axis=0, axis_index_groups=far_groups(), tiled=...  32.6 us
    ppermute x12, waiting for transfers between devices, shift_ring(): return lax.ppermute(x, 'dp', pairs)  31.3 us
    pallas_call x1, Pallas kernels, expert_work(): pl.pallas_call(functools.partial(expert_kernel, my_expert, my_dp, plan),...  14.6 us
    all_to_all x1, starting transfers between devices, shards(): lax.all_to_all(row_grads.reshape(EXPERTS, CAP, features), 'expert', split...  12.9 us
    ppermute x2, starting transfers between devices, swap_halves(): lax.ppermute(x, 'dp', [(d, (d + RING) % (2 * RING)) for d in range(2 * RI...  9.95 us
    pallas_call x1, Pallas kernels, row_gradients(): pl.pallas_call(row_kernel, in_specs=[HBM, HBM], out_specs=HBM, out_shape=...  5.26 us
  transfers between devices with their start and end apart: 16, of which 9 were waited for; matrix products, arithmetic and copies ran while one was open for 1% of the time, Pallas kernels for 4%

profile of v8, /device:TPU:1, one launch (start us, length us, event | category | flops | bytes accessed | tf_op | source)
XLA Modules:
  0.0 177.2 jit_solution(12057681570474400014)
XLA Ops:
  7.2 2.0 %pack_rows.1 = (bf16[128,2176]{1,0:T(8,128)(2,1)}, bf16[16,128]{1,0:T(8,128)(2,1)}) custom-call(bf16[128,1024]{1,0:T(8,128)(2,1)} %tok_ref.1, bf16[128,1024]{1,0:T(8,128)(2,1)} %cot_ref.1, s32[8,128]{1,0:T(8,128)} %bitcast.12, f32[8,128]{1,0:T(8,128)} %bitcast.13), custom_call_target="tpu_custom_call" | custom-call | tf_op jit(solution)/shard_map/pack_rows/pallas_call | solution.py:56
  10.0 5.6 %collective-permute-start = (bf16[32,1152]{1,0:T(8,128)(2,1)S(1)}, bf16[32,1152]{1,0:T(8,128)(2,1)S(1)}, u32[]{:S(2)}, u32[]{:S(2)}) collective-permute-start(bf16[32,1152]{1,0:T(8,128)(2,1)S(1)} %pad_maximum_fusion.1), channel_id=1, source_target_pairs={{0,256},{16,272},{32,288},{48,304},{64,320},{80,336},{96,352},{112... | collective-permute-start | bytes 221192 | tf_op jit(solution)/shard_map/ppermute | solution.py:307
  18.2 32.6 %all_gather.7.refs_0_ = bf16[256,1152]{1,0:T(8,128)(2,1)S(1)} all-gather(bf16[64,1152]{1,0:T(8,128)(2,1)S(1)} %pad_maximum_fusion), channel_id=1, replica_groups={{0,64,128,192},{16,80,144,208},{32,96,160,224},{48,112,176,240},{256,32..., dimensions={0}, use_global_device_ids=true | all-gather | bytes 737280 | tf_op jit(solution)/shard_map/all_gather | solution.py:327
  50.8 3.8 %collective-permute-start.2 = (bf16[256,1152]{1,0:T(8,128)(2,1)S(1)}, bf16[256,1152]{1,0:T(8,128)(2,1)S(1)}, u32[]{:S(2)}, u32[]{:S(2)}) collective-permute-start(bf16[256,1152]{1,0:T(8,128)(2,1)S(1)} %all_gather.7.refs_0_), channel_id=1, source_target_pairs={{0,240},{16,0},{32,16},{48,32},{64,48},{80,64},{96,80},{112,96},{1... | collective-permute-start | bytes 1769480 | tf_op jit(solution)/shard_map/ppermute | solution.py:312
  54.6 1.9 %collective-permute-start.1 = (bf16[256,1152]{1,0:T(8,128)(2,1)S(1)}, bf16[256,1152]{1,0:T(8,128)(2,1)S(1)}, u32[]{:S(2)}, u32[]{:S(2)}) collective-permute-start(bf16[256,1152]{1,0:T(8,128)(2,1)S(1)} %all_gather.7.refs_0_), channel_id=1, source_target_pairs={{0,16},{16,32},{32,48},{48,64},{64,80},{80,96},{96,112},{112,128},... | collective-permute-start | bytes 1769480 | tf_op jit(solution)/shard_map/ppermute | solution.py:312
  56.6 3.1 %collective-permute-start.4 = (bf16[128,1152]{1,0:T(8,128)(2,1)S(1)}, bf16[128,1152]{1,0:T(8,128)(2,1)S(1)}, u32[]{:S(2)}, u32[]{:S(2)}) collective-permute-start(bf16[128,1152]{1,0:T(8,128)(2,1)S(1)} %get-tuple-element.42), channel_id=1, source_target_pairs={{0,224},{16,240},{32,0},{48,16},{64,32},{80,48},{96,64},{112,80},{... | collective-permute-start | bytes 884744 | tf_op jit(solution)/shard_map/ppermute | solution.py:312
  59.7 3.1 %collective-permute-start.3 = (bf16[128,1152]{1,0:T(8,128)(2,1)S(1)}, bf16[128,1152]{1,0:T(8,128)(2,1)S(1)}, u32[]{:S(2)}, u32[]{:S(2)}) collective-permute-start(bf16[128,1152]{1,0:T(8,128)(2,1)S(1)} %get-tuple-element.43), channel_id=1, source_target_pairs={{0,32},{16,48},{32,64},{48,80},{64,96},{80,112},{96,128},{112,144}... | collective-permute-start | bytes 884744 | tf_op jit(solution)/shard_map/ppermute | solution.py:312
  62.8 14.2 %collective-permute-done.4.refs_4_ = bf16[128,1152]{1,0:T(8,128)(2,1)S(1)} collective-permute-done((bf16[128,1152]{1,0:T(8,128)(2,1)S(1)}, bf16[128,1152]{1,0:T(8,128)(2,1)S(1)}, u32[]{:S(2)}, u32[]{:S(2)}) %collective-permute-start.4) | collective-permute-done | bytes 294944 | tf_op jit(solution)/shard_map/ppermute | solution.py:312
  78.6 14.6 %expert_work.1 = (bf16[1280,768]{1,0:T(8,128)(2,1)}, bf16[1024,768]{1,0:T(8,128)(2,1)}, bf16[4,64,768]{2,1,0:T(8,128)(2,1)}, bf16[4,64,768]{2,1,0:T(8,128)(2,1)}...) custom-call(bf16[2048,2176]{1,0:T(8,128)(2,1)} %all-gather.2.cloned.1.call-done.g_hbm, ...), custom_call_target="tpu_custom_call" | custom-call | flops 5033164800 | bytes 16777216 | tf_op jit(solution)/shard_map/expert_work/pallas_call | solution.py:198
  93.2 4.7 %collective-permute-start.5 = (bf16[4,64,768]{2,1,0:T(8,128)(2,1)}, bf16[4,64,768]{2,1,0:T(8,128)(2,1)S(1)}, u32[]{:S(2)}, u32[]{:S(2)}) collective-permute-start(bf16[4,64,768]{2,1,0:T(8,128)(2,1)} %get-tuple-element.28), channel_id=1, source_target_pairs={{0,16},{16,32},{32,48},{48,64},{64,80},{80,96},{96,112},{112,128},... | collective-permute-start | bytes 1179656 | tf_op jit(solution)/shard_map/ppermute | solution.py:312
  97.9 2.5 %collective-permute-start.6 = (bf16[4,64,768]{2,1,0:T(8,128)(2,1)}, bf16[4,64,768]{2,1,0:T(8,128)(2,1)S(1)}, u32[]{:S(2)}, u32[]{:S(2)}) collective-permute-start(bf16[4,64,768]{2,1,0:T(8,128)(2,1)} %get-tuple-element.29), channel_id=1, source_target_pairs={{0,240},{16,0},{32,16},{48,32},{64,48},{80,64},{96,80},{112,96},{1... | collective-permute-start | bytes 1179656 | tf_op jit(solution)/shard_map/ppermute | solution.py:312
  100.4 2.6 %collective-permute-start.7 = (bf16[4,32,768]{2,1,0:T(8,128)(2,1)}, bf16[4,32,768]{2,1,0:T(8,128)(2,1)}, u32[]{:S(2)}, u32[]{:S(2)}) collective-permute-start(bf16[4,32,768]{2,1,0:T(8,128)(2,1)} %get-tuple-element.30), channel_id=1, source_target_pairs={{0,32},{16,48},{32,64},{48,80},{64,96},{80,112},{96,128},{112,144}... | collective-permute-start | bytes 589832 | tf_op jit(solution)/shard_map/ppermute | solution.py:312
  102.9 4.8 %collective-permute-start.8 = (bf16[4,32,768]{2,1,0:T(8,128)(2,1)}, bf16[4,32,768]{2,1,0:T(8,128)(2,1)}, u32[]{:S(2)}, u32[]{:S(2)}) collective-permute-start(bf16[4,32,768]{2,1,0:T(8,128)(2,1)} %get-tuple-element.31), channel_id=1, source_target_pairs={{0,224},{16,240},{32,0},{48,16},{64,32},{80,48},{96,64},{112,80},{... | collective-permute-start | bytes 589832 | tf_op jit(solution)/shard_map/ppermute | solution.py:312
  107.8 5.3 %row_gradients.1 = bf16[1280,1024]{1,0:T(8,128)(2,1)} custom-call(bf16[1280,768]{1,0:T(8,128)(2,1)} %get-tuple-element.24.pre_hbm, bf16[1024,768]{1,0:T(8,128)(2,1)} %get-tuple-element.25.gate_up_hbm), custom_call_target="tpu_custom_call" | custom-call | flops 2013265920 | bytes 6291456 | tf_op jit(solution)/shard_map/row_gradients/pallas_call | solution.py:258
  113.1 12.9 %all-to-all-start = ((bf16[16,80,1024]{2,1,0:T(8,128)(2,1)}), bf16[16,80,1024]{2,1,0:T(8,128)(2,1)S(1)}, u32[]{:S(2)}, u32[]{:S(2)}) async-start(bf16[16,80,1024]{2,1,0:T(8,128)(2,1)} %bitcast.7), calls=%async_computation | async-start | bytes 5242880 | tf_op jit(solution)/shard_map/all_to_all | solution.py:464
  128.3 4.2 %collective-permute-start.9 = (bf16[32,768]{1,0:T(8,128)(2,1)S(1)}, bf16[32,768]{1,0:T(8,128)(2,1)S(1)}, u32[]{:S(2)}, u32[]{:S(2)}) collective-permute-start(bf16[32,768]{1,0:T(8,128)(2,1)S(1)} %get-tuple-element.35), channel_id=1, source_target_pairs={{0,64},{16,80},{32,96},{48,112},{64,128},{80,144},{96,160},{112,17... | collective-permute-start | bytes 147464 | tf_op jit(solution)/shard_map/ppermute | solution.py:312
  132.4 5.1 %collective-permute-start.10 = (bf16[32,768]{1,0:T(8,128)(2,1)S(1)}, bf16[32,768]{1,0:T(8,128)(2,1)S(1)}, u32[]{:S(2)}, u32[]{:S(2)}) collective-permute-start(bf16[32,768]{1,0:T(8,128)(2,1)S(1)} %get-tuple-element.36), channel_id=1, source_target_pairs={{0,192},{16,208},{32,224},{48,240},{64,0},{80,16},{96,32},{112,48}... | collective-permute-start | bytes 147464 | tf_op jit(solution)/shard_map/ppermute | solution.py:312
  137.5 2.2 %collective-permute-done.9.got_low = bf16[32,768]{1,0:T(8,128)(2,1)S(1)} collective-permute-done((bf16[32,768]{1,0:T(8,128)(2,1)S(1)}, bf16[32,768]{1,0:T(8,128)(2,1)S(1)}, u32[]{:S(2)}, u32[]{:S(2)}) %collective-permute-start.9) | collective-permute-done | bytes 49184 | tf_op jit(solution)/shard_map/ppermute | solution.py:312
  139.7 5.0 %collective-permute-done.10.got_high = bf16[32,768]{1,0:T(8,128)(2,1)S(1)} collective-permute-done((bf16[32,768]{1,0:T(8,128)(2,1)S(1)}, bf16[32,768]{1,0:T(8,128)(2,1)S(1)}, u32[]{:S(2)}, u32[]{:S(2)}) %collective-permute-start.10) | collective-permute-done | bytes 49184 | tf_op jit(solution)/shard_map/ppermute | solution.py:312
  144.7 4.7 %collective-permute-start.11 = (bf16[64,768]{1,0:T(8,128)(2,1)S(1)}, bf16[64,768]{1,0:T(8,128)(2,1)S(1)}, u32[]{:S(2)}, u32[]{:S(2)}) collective-permute-start(bf16[64,768]{1,0:T(8,128)(2,1)S(1)} %get-tuple-element.37), channel_id=1, source_target_pairs={{0,64},{16,80},{32,96},{48,112},{64,128},{80,144},{96,160},{112,17... | collective-permute-start | bytes 294920 | tf_op jit(solution)/shard_map/ppermute | solution.py:312
  149.5 4.4 %collective-permute-start.12 = (bf16[64,768]{1,0:T(8,128)(2,1)S(1)}, bf16[64,768]{1,0:T(8,128)(2,1)S(1)}, u32[]{:S(2)}, u32[]{:S(2)}) collective-permute-start(bf16[64,768]{1,0:T(8,128)(2,1)S(1)} %get-tuple-element.38), channel_id=1, source_target_pairs={{0,192},{16,208},{32,224},{48,240},{64,0},{80,16},{96,32},{112,48}... | collective-permute-start | bytes 294920 | tf_op jit(solution)/shard_map/ppermute | solution.py:312
  153.9 1.8 collective-permute-done.11.got_ahead
  155.7 7.6 %collective-permute-done.12.got_behind = bf16[64,768]{1,0:T(8,128)(2,1)S(1)} collective-permute-done((bf16[64,768]{1,0:T(8,128)(2,1)S(1)}, bf16[64,768]{1,0:T(8,128)(2,1)S(1)}, u32[]{:S(2)}, u32[]{:S(2)}) %collective-permute-start.12) | collective-permute-done | bytes 98336 | tf_op jit(solution)/shard_map/ppermute | solution.py:312
  163.3 4.3 %collective-permute-start.13 = (bf16[32,768]{1,0:T(8,128)(2,1)S(1)}, bf16[32,768]{1,0:T(8,128)(2,1)S(1)}, u32[]{:S(2)}, u32[]{:S(2)}) collective-permute-start(bf16[32,768]{1,0:T(8,128)(2,1)S(1)} %get-tuple-element.40), channel_id=1, source_target_pairs={{0,256},{16,272},{32,288},{48,304},{64,320},{80,336},{96,352},{112... | collective-permute-start | bytes 147464 | tf_op jit(solution)/shard_map/ppermute | solution.py:307
  (35 shorter events, 10.1 us)
Async XLA Ops:
  7.2 71.0 %all-gather.2.cloned.1.call-start = ((), (), s32[]{:S(2)}) async-start(), calls=%async_computation.1 | async-start | bytes 9469952 | tf_op jit(solution)/shard_map/all_gather | solution.py:454
  10.0 7.4 %collective-permute-start = (bf16[32,1152]{1,0:T(8,128)(2,1)S(1)}, bf16[32,1152]{1,0:T(8,128)(2,1)S(1)}, u32[]{:S(2)}, u32[]{:S(2)}) collective-permute-start(bf16[32,1152]{1,0:T(8,128)(2,1)S(1)} %pad_maximum_fusion.1), channel_id=1, source_target_pairs={{0,256},{16,272},{32,288},{48,304},{64,320},{80,336},{96,352},{112... | collective-permute-start | bytes 221192 | tf_op jit(solution)/shard_map/ppermute | solution.py:307
  50.8 27.3 %copy-start.2 = (bf16[256,1152]{1,0:T(8,128)(2,1)}, bf16[256,1152]{1,0:T(8,128)(2,1)S(1)}, u32[]{:S(2)}) copy-start(bf16[256,1152]{1,0:T(8,128)(2,1)S(1)} %all_gather.7.refs_0_) | copy-start | bytes 1769476
  50.8 26.7 %collective-permute-start.2 = (bf16[256,1152]{1,0:T(8,128)(2,1)S(1)}, bf16[256,1152]{1,0:T(8,128)(2,1)S(1)}, u32[]{:S(2)}, u32[]{:S(2)}) collective-permute-start(bf16[256,1152]{1,0:T(8,128)(2,1)S(1)} %all_gather.7.refs_0_), channel_id=1, source_target_pairs={{0,240},{16,0},{32,16},{48,32},{64,48},{80,64},{96,80},{112,96},{1... | collective-permute-start | bytes 1769480 | tf_op jit(solution)/shard_map/ppermute | solution.py:312
  54.6 22.9 %collective-permute-start.1 = (bf16[256,1152]{1,0:T(8,128)(2,1)S(1)}, bf16[256,1152]{1,0:T(8,128)(2,1)S(1)}, u32[]{:S(2)}, u32[]{:S(2)}) collective-permute-start(bf16[256,1152]{1,0:T(8,128)(2,1)S(1)} %all_gather.7.refs_0_), channel_id=1, source_target_pairs={{0,16},{16,32},{32,48},{48,64},{64,80},{80,96},{96,112},{112,128},... | collective-permute-start | bytes 1769480 | tf_op jit(solution)/shard_map/ppermute | solution.py:312
  56.6 20.4 %collective-permute-start.4 = (bf16[128,1152]{1,0:T(8,128)(2,1)S(1)}, bf16[128,1152]{1,0:T(8,128)(2,1)S(1)}, u32[]{:S(2)}, u32[]{:S(2)}) collective-permute-start(bf16[128,1152]{1,0:T(8,128)(2,1)S(1)} %get-tuple-element.42), channel_id=1, source_target_pairs={{0,224},{16,240},{32,0},{48,16},{64,32},{80,48},{96,64},{112,80},{... | collective-permute-start | bytes 884744 | tf_op jit(solution)/shard_map/ppermute | solution.py:312
  59.7 17.8 %collective-permute-start.3 = (bf16[128,1152]{1,0:T(8,128)(2,1)S(1)}, bf16[128,1152]{1,0:T(8,128)(2,1)S(1)}, u32[]{:S(2)}, u32[]{:S(2)}) collective-permute-start(bf16[128,1152]{1,0:T(8,128)(2,1)S(1)} %get-tuple-element.43), channel_id=1, source_target_pairs={{0,32},{16,48},{32,64},{48,80},{64,96},{80,112},{96,128},{112,144}... | collective-permute-start | bytes 884744 | tf_op jit(solution)/shard_map/ppermute | solution.py:312
  77.0 1.2 copy-start.5
  77.5 0.7 copy-start.6
  77.5 0.9 copy-start.3
  77.5 1.1 copy-start.4
  93.2 32.8 %collective-permute-start.5 = (bf16[4,64,768]{2,1,0:T(8,128)(2,1)}, bf16[4,64,768]{2,1,0:T(8,128)(2,1)S(1)}, u32[]{:S(2)}, u32[]{:S(2)}) collective-permute-start(bf16[4,64,768]{2,1,0:T(8,128)(2,1)} %get-tuple-element.28), channel_id=1, source_target_pairs={{0,16},{16,32},{32,48},{48,64},{64,80},{80,96},{96,112},{112,128},... | collective-permute-start | bytes 1179656 | tf_op jit(solution)/shard_map/ppermute | solution.py:312
  97.9 28.1 %collective-permute-start.6 = (bf16[4,64,768]{2,1,0:T(8,128)(2,1)}, bf16[4,64,768]{2,1,0:T(8,128)(2,1)S(1)}, u32[]{:S(2)}, u32[]{:S(2)}) collective-permute-start(bf16[4,64,768]{2,1,0:T(8,128)(2,1)} %get-tuple-element.29), channel_id=1, source_target_pairs={{0,240},{16,0},{32,16},{48,32},{64,48},{80,64},{96,80},{112,96},{1... | collective-permute-start | bytes 1179656 | tf_op jit(solution)/shard_map/ppermute | solution.py:312
  100.4 25.6 %collective-permute-start.7 = (bf16[4,32,768]{2,1,0:T(8,128)(2,1)}, bf16[4,32,768]{2,1,0:T(8,128)(2,1)}, u32[]{:S(2)}, u32[]{:S(2)}) collective-permute-start(bf16[4,32,768]{2,1,0:T(8,128)(2,1)} %get-tuple-element.30), channel_id=1, source_target_pairs={{0,32},{16,48},{32,64},{48,80},{64,96},{80,112},{96,128},{112,144}... | collective-permute-start | bytes 589832 | tf_op jit(solution)/shard_map/ppermute | solution.py:312
  102.9 23.1 %collective-permute-start.8 = (bf16[4,32,768]{2,1,0:T(8,128)(2,1)}, bf16[4,32,768]{2,1,0:T(8,128)(2,1)}, u32[]{:S(2)}, u32[]{:S(2)}) collective-permute-start(bf16[4,32,768]{2,1,0:T(8,128)(2,1)} %get-tuple-element.31), channel_id=1, source_target_pairs={{0,224},{16,240},{32,0},{48,16},{64,32},{80,48},{96,64},{112,80},{... | collective-permute-start | bytes 589832 | tf_op jit(solution)/shard_map/ppermute | solution.py:312
  113.1 54.6 %all-to-all-start = ((bf16[16,80,1024]{2,1,0:T(8,128)(2,1)}), bf16[16,80,1024]{2,1,0:T(8,128)(2,1)S(1)}, u32[]{:S(2)}, u32[]{:S(2)}) async-start(bf16[16,80,1024]{2,1,0:T(8,128)(2,1)} %bitcast.7), calls=%async_computation | async-start | bytes 5242880 | tf_op jit(solution)/shard_map/all_to_all | solution.py:464
  126.0 1.0 copy-start.1
  127.0 40.6 %copy-start = (bf16[16,128]{1,0:T(8,128)(2,1)S(1)}, bf16[16,128]{1,0:T(8,128)(2,1)}, u32[]{:S(2)}) copy-start(bf16[16,128]{1,0:T(8,128)(2,1)} %get-tuple-element.22.rank_ref) | copy-start | bytes 12292
  128.3 11.4 %collective-permute-start.9 = (bf16[32,768]{1,0:T(8,128)(2,1)S(1)}, bf16[32,768]{1,0:T(8,128)(2,1)S(1)}, u32[]{:S(2)}, u32[]{:S(2)}) collective-permute-start(bf16[32,768]{1,0:T(8,128)(2,1)S(1)} %get-tuple-element.35), channel_id=1, source_target_pairs={{0,64},{16,80},{32,96},{48,112},{64,128},{80,144},{96,160},{112,17... | collective-permute-start | bytes 147464 | tf_op jit(solution)/shard_map/ppermute | solution.py:312
  132.4 12.3 %collective-permute-start.10 = (bf16[32,768]{1,0:T(8,128)(2,1)S(1)}, bf16[32,768]{1,0:T(8,128)(2,1)S(1)}, u32[]{:S(2)}, u32[]{:S(2)}) collective-permute-start(bf16[32,768]{1,0:T(8,128)(2,1)S(1)} %get-tuple-element.36), channel_id=1, source_target_pairs={{0,192},{16,208},{32,224},{48,240},{64,0},{80,16},{96,32},{112,48}... | collective-permute-start | bytes 147464 | tf_op jit(solution)/shard_map/ppermute | solution.py:312
  144.7 11.0 %collective-permute-start.11 = (bf16[64,768]{1,0:T(8,128)(2,1)S(1)}, bf16[64,768]{1,0:T(8,128)(2,1)S(1)}, u32[]{:S(2)}, u32[]{:S(2)}) collective-permute-start(bf16[64,768]{1,0:T(8,128)(2,1)S(1)} %get-tuple-element.37), channel_id=1, source_target_pairs={{0,64},{16,80},{32,96},{48,112},{64,128},{80,144},{96,160},{112,17... | collective-permute-start | bytes 294920 | tf_op jit(solution)/shard_map/ppermute | solution.py:312
  149.5 13.8 %collective-permute-start.12 = (bf16[64,768]{1,0:T(8,128)(2,1)S(1)}, bf16[64,768]{1,0:T(8,128)(2,1)S(1)}, u32[]{:S(2)}, u32[]{:S(2)}) collective-permute-start(bf16[64,768]{1,0:T(8,128)(2,1)S(1)} %get-tuple-element.38), channel_id=1, source_target_pairs={{0,192},{16,208},{32,224},{48,240},{64,0},{80,16},{96,32},{112,48}... | collective-permute-start | bytes 294920 | tf_op jit(solution)/shard_map/ppermute | solution.py:312
  163.3 6.3 %collective-permute-start.13 = (bf16[32,768]{1,0:T(8,128)(2,1)S(1)}, bf16[32,768]{1,0:T(8,128)(2,1)S(1)}, u32[]{:S(2)}, u32[]{:S(2)}) collective-permute-start(bf16[32,768]{1,0:T(8,128)(2,1)S(1)} %get-tuple-element.40), channel_id=1, source_target_pairs={{0,256},{16,272},{32,288},{48,304},{64,320},{80,336},{96,352},{112... | collective-permute-start | bytes 147464 | tf_op jit(solution)/shard_map/ppermute | solution.py:307
Sparse Core Ops, SparseCore 0:
  10.1 67.9 all-gather.1

commit v9 on v7

--- a/solution.py
+++ b/solution.py
@@ -14,7 +14,9 @@
 RING = 16
 NEAR = 4
 PAIR = 2
-BLOCKS = 4
+BLOCKS = 1
+ROW_BLOCKS = 2
+STRIPS = 1
 UNROUTED = 200.0
 MIB = 1024 * 1024
 VMEM_BYTES = 60 * MIB
@@ -68,10 +70,10 @@
     piece_total = 1 + max(array for array, *_ in plan)
     pieces = refs[:piece_total]
     pre_hbm, gate_up_hbm, *parts_hbm = refs[piece_total : piece_total + 7]
-    blocks, weights, gate_up, inputs, cots, pre_grad, total, *parts = refs[piece_total + 7 : -4]
+    blocks, weights, inputs, cots, pre_grad, parts = refs[piece_total + 7 : -4]
     load_sems, weight_sems, pre_sems, out_sems = refs[-4:]
     expert = my_expert()
-    features, hidden = inputs.shape[1], gate_up.shape[1] // 2
+    features, hidden = inputs.shape[1], pre_grad.shape[1] // 2
     dp = my_dp()
     upper = dp // RING
     place = dp % RING
@@ -144,10 +146,15 @@
         if m == 0:
             for copy in weight_loads:
                 copy.wait()
-            gate_up[...] = weights[:, : 2 * hidden]
-            stores.append(pltpu.make_async_copy(gate_up, gate_up_hbm, out_sems.at[0]))
+            stores.append(
+                pltpu.make_async_copy(
+                    weights.at[:, pl.ds(0, 2 * hidden)], gate_up_hbm, out_sems.at[0]
+                )
+            )
             stores[0].start()
-        projected = jnp.dot(inputs[here, :], gate_up[...], preferred_element_type=F32)
+        projected = jnp.dot(
+            inputs[here, :], weights[:, : 2 * hidden], preferred_element_type=F32
+        )
         hidden_grad = jnp.dot(cots[here, :], weights[:, 2 * hidden :], preferred_element_type=F32)
         gate_part = projected[:, :hidden]
         up_part = projected[:, hidden:]
@@ -161,26 +168,24 @@
         )
         stores[-1].start()
 
-    strip = features // BLOCKS
-    for c in range(BLOCKS):
-        total[c * strip : (c + 1) * strip, :] = lax.dot_general(
+    strip = features // STRIPS
+    for c in range(STRIPS):
+        grad = lax.dot_general(
             inputs[:, c * strip : (c + 1) * strip],
             pre_grad[...],
             (((0,), (0,)), ((), ())),
             preferred_element_type=F32,
-        )
-
-    def part(owner, offset):
-        return total[pl.ds(row_at(owner, (place + offset + RING) % RING), shard), :].astype(BF16)
-
-    keep, plus, minus, plus2, minus2 = parts
-    for j in range(RING // NEAR):
-        for ref, offset in ((keep, 0), (plus, 1), (minus, -1)):
-            for owner in range(2):
-                ref[j, owner * shard : (owner + 1) * shard, :] = part(owner, NEAR * j + offset)
-        plus2[j] = part(0, NEAR * j + 2)
-        minus2[j] = part(1, NEAR * j + 2)
-    for k, (ref, hbm) in enumerate(zip(parts, parts_hbm)):
+        ).astype(BF16)
+        for k in range(strip // shard):
+            owner, spot = divmod(c * strip // shard + k, RING)
+            offset = (spot - place + RING) % RING
+            kind = offset % NEAR
+            kind = jnp.where(kind == 2, 3, jnp.where(kind == 3, 2, kind))
+            far = jnp.where(kind == 2, (offset + 1) // NEAR, offset // NEAR) % (RING // NEAR)
+            parts[kind, far, owner] = grad[k * shard : (k + 1) * shard]
+
+    sources = [parts.at[k] for k in range(3)] + [parts.at[3, :, half] for half in range(2)]
+    for k, (ref, hbm) in enumerate(zip(sources, parts_hbm)):
         stores.append(pltpu.make_async_copy(ref, hbm, out_sems.at[1 + k]))
         stores[-1].start()
     for copy in stores:
@@ -191,7 +196,7 @@
     slots = EXPERTS * CAP
     pair_rows = gathered.shape[0] // EXPERTS * PAIR
     shard = features // (2 * RING)
-    whole = (RING // NEAR, 2 * shard, 2 * hidden)
+    whole = (RING // NEAR, 2, shard, 2 * hidden)
     half = (RING // NEAR, shard, 2 * hidden)
     parts = [whole, whole, whole, half, half]
     out_shapes = [(slots, 2 * hidden), (features, 2 * hidden)] + parts
@@ -203,12 +208,10 @@
         scratch_shapes=[
             pltpu.VMEM((EXPERTS // PAIR, pair_rows, gathered.shape[1]), BF16),
             pltpu.VMEM((features, 3 * hidden), BF16),
-            pltpu.VMEM((features, 2 * hidden), BF16),
             pltpu.VMEM((slots, features), BF16),
             pltpu.VMEM((slots, features), BF16),
             pltpu.VMEM((slots, 2 * hidden), BF16),
-            pltpu.VMEM((features, 2 * hidden), F32),
-            *[pltpu.VMEM(shape, BF16) for shape in parts],
+            pltpu.VMEM((NEAR, *whole), BF16),
             pltpu.SemaphoreType.DMA((EXPERTS // PAIR,)),
             pltpu.SemaphoreType.DMA((2 * RING,)),
             pltpu.SemaphoreType.DMA((BLOCKS,)),
@@ -225,23 +228,23 @@
 
 
 def row_kernel(pre_hbm, gate_up_hbm, row_hbm, pre_grad, gate_up, row_grad, sems):
-    block = pre_grad.shape[0] // BLOCKS
+    block = pre_grad.shape[0] // ROW_BLOCKS
     loads = [pltpu.make_async_copy(gate_up_hbm, gate_up, sems.at[0])]
     stores = []
-    for m in range(BLOCKS):
+    for m in range(ROW_BLOCKS):
         here = pl.ds(m * block, block)
         loads.append(
             pltpu.make_async_copy(pre_hbm.at[here, :], pre_grad.at[here, :], sems.at[1 + m])
         )
         stores.append(
             pltpu.make_async_copy(
-                row_grad.at[here, :], row_hbm.at[here, :], sems.at[1 + BLOCKS + m]
+                row_grad.at[here, :], row_hbm.at[here, :], sems.at[1 + ROW_BLOCKS + m]
             )
         )
     for copy in loads:
         copy.start()
     loads[0].wait()
-    for m in range(BLOCKS):
+    for m in range(ROW_BLOCKS):
         here = pl.ds(m * block, block)
         loads[1 + m].wait()
         row_grad[here, :] = lax.dot_general(
@@ -264,7 +267,7 @@
             pltpu.VMEM((slots, columns), BF16),
             pltpu.VMEM((features, columns), BF16),
             pltpu.VMEM((slots, features), BF16),
-            pltpu.SemaphoreType.DMA((1 + 2 * BLOCKS,)),
+            pltpu.SemaphoreType.DMA((1 + 2 * ROW_BLOCKS,)),
         ],
         compiler_params=pltpu.CompilerParams(vmem_limit_bytes=VMEM_BYTES),
         cost_estimate=pl.CostEstimate(
@@ -274,7 +277,8 @@
     )(pre_grad, gate_up)
 
 
-def combine_kernel(rank_ref, back_ref, out_ref):
+def combine_kernel(rank_ref, back_ref, out_ref, done_ref):
+    done_ref[...] = jnp.zeros_like(done_ref)
     slots = back_ref.shape[0]
     column = iota((EXPERTS, slots), 1) - CAP * iota((EXPERTS, slots), 0)
     spread = as_bf16((column >= 0) & (column < CAP))
@@ -290,7 +294,10 @@
 def combine(rank, back):
     return pl.pallas_call(
         combine_kernel,
-        out_shape=jax.ShapeDtypeStruct((rank.shape[1], back.shape[1]), BF16),
+        out_shape=(
+            jax.ShapeDtypeStruct((rank.shape[1], back.shape[1]), BF16),
+            jax.ShapeDtypeStruct((8, LANES), F32),
+        ),
         compiler_params=pltpu.CompilerParams(vmem_limit_bytes=16 * MIB),
         cost_estimate=pl.CostEstimate(
             flops=20 * 1000**3, bytes_accessed=4 * MIB, transcendentals=0
@@ -341,18 +348,19 @@
     return pieces, plan
 
 
-def near_sum_kernel(keep, plus, minus, plus2, minus2, out):
+def near_sum_kernel(keep, plus, minus, plus2, minus2, *out):
     groups, shard = plus2.shape[:2]
     for j in range(groups):
         value = keep[j].astype(F32) + plus[j].astype(F32) + minus[j].astype(F32)
-        out[j, :shard] = (value[:shard] + plus2[j].astype(F32)).astype(BF16)
-        out[j, shard:] = (value[shard:] + minus2[(j - 1) % groups].astype(F32)).astype(BF16)
+        out[j][:shard] = (value[:shard] + plus2[j].astype(F32)).astype(BF16)
+        out[j][shard:] = (value[shard:] + minus2[(j - 1) % groups].astype(F32)).astype(BF16)
 
 
 def near_sum(*parts):
+    groups, rows, columns = parts[0].shape
     return pl.pallas_call(
         near_sum_kernel,
-        out_shape=jax.ShapeDtypeStruct(parts[0].shape, BF16),
+        out_shape=(jax.ShapeDtypeStruct((rows, columns), BF16),) * groups,
         compiler_params=pltpu.CompilerParams(vmem_limit_bytes=12 * MIB),
         cost_estimate=pl.CostEstimate(
             flops=100 * 1000**3, bytes_accessed=4 * MIB, transcendentals=0
@@ -383,17 +391,35 @@
     )(*parts)
 
 
-def scatter_sum(keep, plus, minus, plus2, minus2, scale, my_dp):
-    part = near_sum(
+def last_sum_kernel(scale, mine, got, earlier, out):
+    del earlier
+    out[0] = (mine[...] + got[...].astype(F32)) * scale
+
+
+def last_sum(scale, mine, got, earlier):
+    return pl.pallas_call(
+        functools.partial(last_sum_kernel, scale),
+        in_specs=[VMEM, VMEM, pl.BlockSpec(memory_space=pl.ANY)],
+        out_shape=jax.ShapeDtypeStruct((1, *mine.shape), F32),
+        compiler_params=pltpu.CompilerParams(vmem_limit_bytes=8 * MIB),
+        name="last_sum",
+    )(mine, got, earlier)
+
+
+def scatter_sum(keep, plus, minus, plus2, minus2, my_dp):
+    groups, halves, shard, columns = keep.shape
+    keep, plus, minus = (x.reshape(groups, halves * shard, columns) for x in (keep, plus, minus))
+    parts = near_sum(
         keep,
         shift_ring(plus, 1),
         shift_ring(minus, -1),
         shift_ring(plus2, 2),
         shift_ring(minus2, -2),
     )
-    parts = [part[0]] + [shift_ring(part[j], NEAR * j) for j in range(1, RING // NEAR)]
-    mine, theirs = far_sum(my_dp, *parts)
-    return ((mine + swap_halves(theirs).astype(F32)) * scale)[None]
+    mine, theirs = far_sum(
+        my_dp, parts[0], *[shift_ring(parts[j], NEAR * j) for j in range(1, RING // NEAR)]
+    )
+    return mine, swap_halves(theirs)
 
 
 def shards(tokens, cotangent, route_experts, route_weights, gate_up, down):
@@ -414,8 +440,9 @@
         row_grads.reshape(EXPERTS, CAP, features), "expert", split_axis=0, concat_axis=0, tiled=True
     )
     grad_scale = 1.0 / math.sqrt(rows * lax.axis_size("dp") * lax.axis_size("expert"))
-    grad_gate_up = scatter_sum(*grad_parts, grad_scale, my_dp)
-    token_grad = combine(rank, returned.reshape(EXPERTS * CAP, features))
+    mine, got = scatter_sum(*grad_parts, my_dp)
+    token_grad, done = combine(rank, returned.reshape(EXPERTS * CAP, features))
+    grad_gate_up = last_sum(grad_scale, mine, got, done)
     return (token_grad, grad_gate_up)
 
 

time: 176 us -> 173 us (0.983)
    pallas_call x1, Pallas kernels: 14.6 us -> 12.3 us  [expert_work(): pl.pallas_call(functools.partial(expert_kernel, my_expert, my_dp, plan),...]
    ppermute x11, waiting for transfers between devices: 28.9 us -> 30.7 us  [shift_ring(): return lax.ppermute(x, 'dp', pairs)]
  transfers between devices with their start and end apart: 15 -> 15, of which waited for: 8 -> 7; matrix products, arithmetic and copies ran while one was open for 1% -> 1% of each run, Pallas kernels for 4% -> 5%
where the time goes in v9:
time: 173 us; the launch traced here: 172 us
  starting transfers between devices  65.8 us (38%)
  waiting for transfers between devices  33.3 us (19%)
  blocking collectives  32.6 us (19%)
  Pallas kernels  22.9 us (13%)
  between operations  14.2 us (8%)
    ppermute x11, starting transfers between devices, shift_ring(): return lax.ppermute(x, 'dp', pairs)  42.5 us
    all_gather x1, blocking collectives, gather_weights(): lax.all_gather(both, 'dp', axis=0, axis_index_groups=far_groups(), tiled=...  32.6 us
    ppermute x11, waiting for transfers between devices, shift_ring(): return lax.ppermute(x, 'dp', pairs)  30.7 us
    all_to_all x1, starting transfers between devices, shards(): lax.all_to_all(row_grads.reshape(EXPERTS, CAP, features), 'expert', split...  12.9 us
    pallas_call x1, Pallas kernels, expert_work(): pl.pallas_call(functools.partial(expert_kernel, my_expert, my_dp, plan),...  12.3 us
    ppermute x2, starting transfers between devices, swap_halves(): lax.ppermute(x, 'dp', [(d, (d + RING) % (2 * RING)) for d in range(2 * RI...  10.4 us
    pallas_call x1, Pallas kernels, row_gradients(): pl.pallas_call(row_kernel, in_specs=[HBM, HBM], out_specs=HBM, out_shape=...  5.22 us
  transfers between devices with their start and end apart: 15, of which 7 were waited for; matrix products, arithmetic and copies ran while one was open for 1% of the time, Pallas kernels for 5%

profile of v9, /device:TPU:1, one launch (start us, length us, event | category | flops | bytes accessed | tf_op | source)
XLA Modules:
  0.0 172.0 jit_solution(3259546755292375976)
XLA Ops:
  7.2 2.0 %pack_rows.1 = (bf16[128,2176]{1,0:T(8,128)(2,1)}, bf16[16,128]{1,0:T(8,128)(2,1)}) custom-call(bf16[128,1024]{1,0:T(8,128)(2,1)} %tok_ref.1, bf16[128,1024]{1,0:T(8,128)(2,1)} %cot_ref.1, s32[8,128]{1,0:T(8,128)} %bitcast.16, f32[8,128]{1,0:T(8,128)} %bitcast.17), custom_call_target="tpu_custom_call" | custom-call | tf_op jit(solution)/shard_map/pack_rows/pallas_call | solution.py:58
  10.0 5.6 %collective-permute-start = (bf16[32,1152]{1,0:T(8,128)(2,1)S(1)}, bf16[32,1152]{1,0:T(8,128)(2,1)S(1)}, u32[]{:S(2)}, u32[]{:S(2)}) collective-permute-start(bf16[32,1152]{1,0:T(8,128)(2,1)S(1)} %pad_maximum_fusion.1), channel_id=1, source_target_pairs={{0,256},{16,272},{32,288},{48,304},{64,320},{80,336},{96,352},{112... | collective-permute-start | bytes 221192 | tf_op jit(solution)/shard_map/ppermute | solution.py:310
  15.7 1.7 %collective-permute-done = bf16[32,1152]{1,0:T(8,128)(2,1)S(1)} collective-permute-done((bf16[32,1152]{1,0:T(8,128)(2,1)S(1)}, bf16[32,1152]{1,0:T(8,128)(2,1)S(1)}, u32[]{:S(2)}, u32[]{:S(2)}) %collective-permute-start) | collective-permute-done | bytes 73760 | tf_op jit(solution)/shard_map/ppermute | solution.py:310
  18.3 32.6 %all_gather.7.refs_0_ = bf16[256,1152]{1,0:T(8,128)(2,1)S(1)} all-gather(bf16[64,1152]{1,0:T(8,128)(2,1)S(1)} %pad_maximum_fusion), channel_id=1, replica_groups={{0,64,128,192},{16,80,144,208},{32,96,160,224},{48,112,176,240},{256,32..., dimensions={0}, use_global_device_ids=true | all-gather | bytes 737280 | tf_op jit(solution)/shard_map/all_gather | solution.py:330
  50.9 3.8 %collective-permute-start.2 = (bf16[256,1152]{1,0:T(8,128)(2,1)S(1)}, bf16[256,1152]{1,0:T(8,128)(2,1)S(1)}, u32[]{:S(2)}, u32[]{:S(2)}) collective-permute-start(bf16[256,1152]{1,0:T(8,128)(2,1)S(1)} %all_gather.7.refs_0_), channel_id=1, source_target_pairs={{0,240},{16,0},{32,16},{48,32},{64,48},{80,64},{96,80},{112,96},{1... | collective-permute-start | bytes 1769480 | tf_op jit(solution)/shard_map/ppermute | solution.py:315
  54.6 1.9 %collective-permute-start.1 = (bf16[256,1152]{1,0:T(8,128)(2,1)S(1)}, bf16[256,1152]{1,0:T(8,128)(2,1)S(1)}, u32[]{:S(2)}, u32[]{:S(2)}) collective-permute-start(bf16[256,1152]{1,0:T(8,128)(2,1)S(1)} %all_gather.7.refs_0_), channel_id=1, source_target_pairs={{0,16},{16,32},{32,48},{48,64},{64,80},{80,96},{96,112},{112,128},... | collective-permute-start | bytes 1769480 | tf_op jit(solution)/shard_map/ppermute | solution.py:315
  56.6 3.1 %collective-permute-start.4 = (bf16[128,1152]{1,0:T(8,128)(2,1)S(1)}, bf16[128,1152]{1,0:T(8,128)(2,1)S(1)}, u32[]{:S(2)}, u32[]{:S(2)}) collective-permute-start(bf16[128,1152]{1,0:T(8,128)(2,1)S(1)} %get-tuple-element.36), channel_id=1, source_target_pairs={{0,224},{16,240},{32,0},{48,16},{64,32},{80,48},{96,64},{112,80},{... | collective-permute-start | bytes 884744 | tf_op jit(solution)/shard_map/ppermute | solution.py:315
  59.7 3.1 %collective-permute-start.3 = (bf16[128,1152]{1,0:T(8,128)(2,1)S(1)}, bf16[128,1152]{1,0:T(8,128)(2,1)S(1)}, u32[]{:S(2)}, u32[]{:S(2)}) collective-permute-start(bf16[128,1152]{1,0:T(8,128)(2,1)S(1)} %get-tuple-element.37), channel_id=1, source_target_pairs={{0,32},{16,48},{32,64},{48,80},{64,96},{80,112},{96,128},{112,144}... | collective-permute-start | bytes 884744 | tf_op jit(solution)/shard_map/ppermute | solution.py:315
  62.8 14.2 %collective-permute-done.4.refs_4_ = bf16[128,1152]{1,0:T(8,128)(2,1)S(1)} collective-permute-done((bf16[128,1152]{1,0:T(8,128)(2,1)S(1)}, bf16[128,1152]{1,0:T(8,128)(2,1)S(1)}, u32[]{:S(2)}, u32[]{:S(2)}) %collective-permute-start.4) | collective-permute-done | bytes 294944 | tf_op jit(solution)/shard_map/ppermute | solution.py:315
  78.6 12.3 %expert_work.1 = (bf16[1280,768]{1,0:T(8,128)(2,1)}, bf16[1024,768]{1,0:T(8,128)(2,1)}, bf16[4,2,32,768]{3,2,1,0:T(8,128)(2,1)}, bf16[4,2,32,768]{3,2,1,0:T(8,12...) custom-call(bf16[2048,2176]{1,0:T(8,128)(2,1)} %all-gather.2.cloned.1.call-done.g, ...), custom_call_target="tpu_custom_call" | custom-call | flops 5033164800 | bytes 16777216 | tf_op jit(solution)/shard_map/expert_work/pallas_call | solution.py:203
  91.0 4.7 %collective-permute-start.5 = (bf16[4,64,768]{2,1,0:T(8,128)(2,1)}, bf16[4,64,768]{2,1,0:T(8,128)(2,1)S(1)}, u32[]{:S(2)}, u32[]{:S(2)}) collective-permute-start(bf16[4,64,768]{2,1,0:T(8,128)(2,1)} %bitcast.19), channel_id=1, source_target_pairs={{0,16},{16,32},{32,48},{48,64},{64,80},{80,96},{96,112},{112,128},... | collective-permute-start | bytes 1179656 | tf_op jit(solution)/shard_map/ppermute | solution.py:315
  95.7 2.5 %collective-permute-start.6 = (bf16[4,64,768]{2,1,0:T(8,128)(2,1)}, bf16[4,64,768]{2,1,0:T(8,128)(2,1)S(1)}, u32[]{:S(2)}, u32[]{:S(2)}) collective-permute-start(bf16[4,64,768]{2,1,0:T(8,128)(2,1)} %bitcast.18), channel_id=1, source_target_pairs={{0,240},{16,0},{32,16},{48,32},{64,48},{80,64},{96,80},{112,96},{1... | collective-permute-start | bytes 1179656 | tf_op jit(solution)/shard_map/ppermute | solution.py:315
  98.1 2.5 %collective-permute-start.7 = (bf16[4,32,768]{2,1,0:T(8,128)(2,1)}, bf16[4,32,768]{2,1,0:T(8,128)(2,1)}, u32[]{:S(2)}, u32[]{:S(2)}) collective-permute-start(bf16[4,32,768]{2,1,0:T(8,128)(2,1)} %get-tuple-element.27), channel_id=1, source_target_pairs={{0,32},{16,48},{32,64},{48,80},{64,96},{80,112},{96,128},{112,144}... | collective-permute-start | bytes 589832 | tf_op jit(solution)/shard_map/ppermute | solution.py:315
  100.7 4.9 %collective-permute-start.8 = (bf16[4,32,768]{2,1,0:T(8,128)(2,1)}, bf16[4,32,768]{2,1,0:T(8,128)(2,1)}, u32[]{:S(2)}, u32[]{:S(2)}) collective-permute-start(bf16[4,32,768]{2,1,0:T(8,128)(2,1)} %get-tuple-element.28), channel_id=1, source_target_pairs={{0,224},{16,240},{32,0},{48,16},{64,32},{80,48},{96,64},{112,80},{... | collective-permute-start | bytes 589832 | tf_op jit(solution)/shard_map/ppermute | solution.py:315
  105.5 5.2 %row_gradients.1 = bf16[1280,1024]{1,0:T(8,128)(2,1)} custom-call(bf16[1280,768]{1,0:T(8,128)(2,1)} %get-tuple-element.21.pre_hbm, bf16[1024,768]{1,0:T(8,128)(2,1)} %get-tuple-element.22.gate_up_hbm), custom_call_target="tpu_custom_call" | custom-call | flops 2013265920 | bytes 6291456 | tf_op jit(solution)/shard_map/row_gradients/pallas_call | solution.py:261
  110.8 12.9 %all-to-all-start = ((bf16[16,80,1024]{2,1,0:T(8,128)(2,1)}), bf16[16,80,1024]{2,1,0:T(8,128)(2,1)S(1)}, u32[]{:S(2)}, u32[]{:S(2)}) async-start(bf16[16,80,1024]{2,1,0:T(8,128)(2,1)} %bitcast.11), calls=%async_computation | async-start | bytes 5242880 | tf_op jit(solution)/shard_map/all_to_all | solution.py:439
  124.7 1.2 near_sum.1
  126.0 4.2 %collective-permute-start.9 = (bf16[64,768]{1,0:T(8,128)(2,1)S(1)}, bf16[64,768]{1,0:T(8,128)(2,1)S(1)}, u32[]{:S(2)}, u32[]{:S(2)}) collective-permute-start(bf16[64,768]{1,0:T(8,128)(2,1)S(1)} %get-tuple-element.30), channel_id=1, source_target_pairs={{0,64},{16,80},{32,96},{48,112},{64,128},{80,144},{96,160},{112,17... | collective-permute-start | bytes 294920 | tf_op jit(solution)/shard_map/ppermute | solution.py:315
  130.1 7.1 %collective-permute-start.10 = (bf16[64,768]{1,0:T(8,128)(2,1)S(1)}, bf16[64,768]{1,0:T(8,128)(2,1)S(1)}, u32[]{:S(2)}, u32[]{:S(2)}) collective-permute-start(bf16[64,768]{1,0:T(8,128)(2,1)S(1)} %get-tuple-element.31), channel_id=1, source_target_pairs={{0,128},{16,144},{32,160},{48,176},{64,192},{80,208},{96,224},{112... | collective-permute-start | bytes 294920 | tf_op jit(solution)/shard_map/ppermute | solution.py:315
  137.2 4.9 %collective-permute-start.11 = (bf16[64,768]{1,0:T(8,128)(2,1)S(1)}, bf16[64,768]{1,0:T(8,128)(2,1)S(1)}, u32[]{:S(2)}, u32[]{:S(2)}) collective-permute-start(bf16[64,768]{1,0:T(8,128)(2,1)S(1)} %get-tuple-element.32), channel_id=1, source_target_pairs={{0,192},{16,208},{32,224},{48,240},{64,0},{80,16},{96,32},{112,48}... | collective-permute-start | bytes 294920 | tf_op jit(solution)/shard_map/ppermute | solution.py:315
  142.1 2.8 %collective-permute-done.10.three = bf16[64,768]{1,0:T(8,128)(2,1)S(1)} collective-permute-done((bf16[64,768]{1,0:T(8,128)(2,1)S(1)}, bf16[64,768]{1,0:T(8,128)(2,1)S(1)}, u32[]{:S(2)}, u32[]{:S(2)}) %collective-permute-start.10) | collective-permute-done | bytes 98336 | tf_op jit(solution)/shard_map/ppermute | solution.py:315
  144.9 13.2 %collective-permute-done.11.four = bf16[64,768]{1,0:T(8,128)(2,1)S(1)} collective-permute-done((bf16[64,768]{1,0:T(8,128)(2,1)S(1)}, bf16[64,768]{1,0:T(8,128)(2,1)S(1)}, u32[]{:S(2)}, u32[]{:S(2)}) %collective-permute-start.11) | collective-permute-done | bytes 98336 | tf_op jit(solution)/shard_map/ppermute | solution.py:315
  158.2 4.7 %collective-permute-start.12 = (bf16[32,768]{1,0:T(8,128)(2,1)S(1)}, bf16[32,768]{1,0:T(8,128)(2,1)S(1)}, u32[]{:S(2)}, u32[]{:S(2)}) collective-permute-start(bf16[32,768]{1,0:T(8,128)(2,1)S(1)} %get-tuple-element.34), channel_id=1, source_target_pairs={{0,256},{16,272},{32,288},{48,304},{64,320},{80,336},{96,352},{112... | collective-permute-start | bytes 147464 | tf_op jit(solution)/shard_map/ppermute | solution.py:310
  162.9 1.4 combine_rows.1
  (32 shorter events, 5.3 us)
Async XLA Ops:
  7.2 71.0 %all-gather.2.cloned.1.call-start = ((), (), s32[]{:S(2)}) async-start(), calls=%async_computation.1 | async-start | bytes 9469952 | tf_op jit(solution)/shard_map/all_gather | solution.py:429
  10.0 7.4 %collective-permute-start = (bf16[32,1152]{1,0:T(8,128)(2,1)S(1)}, bf16[32,1152]{1,0:T(8,128)(2,1)S(1)}, u32[]{:S(2)}, u32[]{:S(2)}) collective-permute-start(bf16[32,1152]{1,0:T(8,128)(2,1)S(1)} %pad_maximum_fusion.1), channel_id=1, source_target_pairs={{0,256},{16,272},{32,288},{48,304},{64,320},{80,336},{96,352},{112... | collective-permute-start | bytes 221192 | tf_op jit(solution)/shard_map/ppermute | solution.py:310
  50.9 27.3 %copy-start.2 = (bf16[256,1152]{1,0:T(8,128)(2,1)}, bf16[256,1152]{1,0:T(8,128)(2,1)S(1)}, u32[]{:S(2)}) copy-start(bf16[256,1152]{1,0:T(8,128)(2,1)S(1)} %all_gather.7.refs_0_) | copy-start | bytes 1769476
  50.9 26.7 %collective-permute-start.2 = (bf16[256,1152]{1,0:T(8,128)(2,1)S(1)}, bf16[256,1152]{1,0:T(8,128)(2,1)S(1)}, u32[]{:S(2)}, u32[]{:S(2)}) collective-permute-start(bf16[256,1152]{1,0:T(8,128)(2,1)S(1)} %all_gather.7.refs_0_), channel_id=1, source_target_pairs={{0,240},{16,0},{32,16},{48,32},{64,48},{80,64},{96,80},{112,96},{1... | collective-permute-start | bytes 1769480 | tf_op jit(solution)/shard_map/ppermute | solution.py:315
  54.6 22.9 %collective-permute-start.1 = (bf16[256,1152]{1,0:T(8,128)(2,1)S(1)}, bf16[256,1152]{1,0:T(8,128)(2,1)S(1)}, u32[]{:S(2)}, u32[]{:S(2)}) collective-permute-start(bf16[256,1152]{1,0:T(8,128)(2,1)S(1)} %all_gather.7.refs_0_), channel_id=1, source_target_pairs={{0,16},{16,32},{32,48},{48,64},{64,80},{80,96},{96,112},{112,128},... | collective-permute-start | bytes 1769480 | tf_op jit(solution)/shard_map/ppermute | solution.py:315
  56.6 20.4 %collective-permute-start.4 = (bf16[128,1152]{1,0:T(8,128)(2,1)S(1)}, bf16[128,1152]{1,0:T(8,128)(2,1)S(1)}, u32[]{:S(2)}, u32[]{:S(2)}) collective-permute-start(bf16[128,1152]{1,0:T(8,128)(2,1)S(1)} %get-tuple-element.36), channel_id=1, source_target_pairs={{0,224},{16,240},{32,0},{48,16},{64,32},{80,48},{96,64},{112,80},{... | collective-permute-start | bytes 884744 | tf_op jit(solution)/shard_map/ppermute | solution.py:315
  59.7 17.8 %collective-permute-start.3 = (bf16[128,1152]{1,0:T(8,128)(2,1)S(1)}, bf16[128,1152]{1,0:T(8,128)(2,1)S(1)}, u32[]{:S(2)}, u32[]{:S(2)}) collective-permute-start(bf16[128,1152]{1,0:T(8,128)(2,1)S(1)} %get-tuple-element.37), channel_id=1, source_target_pairs={{0,32},{16,48},{32,64},{48,80},{64,96},{80,112},{96,128},{112,144}... | collective-permute-start | bytes 884744 | tf_op jit(solution)/shard_map/ppermute | solution.py:315
  77.0 1.2 copy-start.5
  77.5 0.7 copy-start.6
  77.5 0.9 copy-start.3
  77.5 1.1 copy-start.4
  91.0 32.7 %collective-permute-start.5 = (bf16[4,64,768]{2,1,0:T(8,128)(2,1)}, bf16[4,64,768]{2,1,0:T(8,128)(2,1)S(1)}, u32[]{:S(2)}, u32[]{:S(2)}) collective-permute-start(bf16[4,64,768]{2,1,0:T(8,128)(2,1)} %bitcast.19), channel_id=1, source_target_pairs={{0,16},{16,32},{32,48},{48,64},{64,80},{80,96},{96,112},{112,128},... | collective-permute-start | bytes 1179656 | tf_op jit(solution)/shard_map/ppermute | solution.py:315
  95.7 28.1 %collective-permute-start.6 = (bf16[4,64,768]{2,1,0:T(8,128)(2,1)}, bf16[4,64,768]{2,1,0:T(8,128)(2,1)S(1)}, u32[]{:S(2)}, u32[]{:S(2)}) collective-permute-start(bf16[4,64,768]{2,1,0:T(8,128)(2,1)} %bitcast.18), channel_id=1, source_target_pairs={{0,240},{16,0},{32,16},{48,32},{64,48},{80,64},{96,80},{112,96},{1... | collective-permute-start | bytes 1179656 | tf_op jit(solution)/shard_map/ppermute | solution.py:315
  98.1 25.6 %collective-permute-start.7 = (bf16[4,32,768]{2,1,0:T(8,128)(2,1)}, bf16[4,32,768]{2,1,0:T(8,128)(2,1)}, u32[]{:S(2)}, u32[]{:S(2)}) collective-permute-start(bf16[4,32,768]{2,1,0:T(8,128)(2,1)} %get-tuple-element.27), channel_id=1, source_target_pairs={{0,32},{16,48},{32,64},{48,80},{64,96},{80,112},{96,128},{112,144}... | collective-permute-start | bytes 589832 | tf_op jit(solution)/shard_map/ppermute | solution.py:315
  100.7 23.0 %collective-permute-start.8 = (bf16[4,32,768]{2,1,0:T(8,128)(2,1)}, bf16[4,32,768]{2,1,0:T(8,128)(2,1)}, u32[]{:S(2)}, u32[]{:S(2)}) collective-permute-start(bf16[4,32,768]{2,1,0:T(8,128)(2,1)} %get-tuple-element.28), channel_id=1, source_target_pairs={{0,224},{16,240},{32,0},{48,16},{64,32},{80,48},{96,64},{112,80},{... | collective-permute-start | bytes 589832 | tf_op jit(solution)/shard_map/ppermute | solution.py:315
  110.8 52.1 %all-to-all-start = ((bf16[16,80,1024]{2,1,0:T(8,128)(2,1)}), bf16[16,80,1024]{2,1,0:T(8,128)(2,1)S(1)}, u32[]{:S(2)}, u32[]{:S(2)}) async-start(bf16[16,80,1024]{2,1,0:T(8,128)(2,1)} %bitcast.11), calls=%async_computation | async-start | bytes 5242880 | tf_op jit(solution)/shard_map/all_to_all | solution.py:439
  123.7 1.0 copy-start.1
  124.7 38.2 %copy-start = (bf16[16,128]{1,0:T(8,128)(2,1)S(1)}, bf16[16,128]{1,0:T(8,128)(2,1)}, u32[]{:S(2)}) copy-start(bf16[16,128]{1,0:T(8,128)(2,1)} %get-tuple-element.19.rank_ref) | copy-start | bytes 12292
  126.0 16.1 %collective-permute-start.9 = (bf16[64,768]{1,0:T(8,128)(2,1)S(1)}, bf16[64,768]{1,0:T(8,128)(2,1)S(1)}, u32[]{:S(2)}, u32[]{:S(2)}) collective-permute-start(bf16[64,768]{1,0:T(8,128)(2,1)S(1)} %get-tuple-element.30), channel_id=1, source_target_pairs={{0,64},{16,80},{32,96},{48,112},{64,128},{80,144},{96,160},{112,17... | collective-permute-start | bytes 294920 | tf_op jit(solution)/shard_map/ppermute | solution.py:315
  130.1 14.8 %collective-permute-start.10 = (bf16[64,768]{1,0:T(8,128)(2,1)S(1)}, bf16[64,768]{1,0:T(8,128)(2,1)S(1)}, u32[]{:S(2)}, u32[]{:S(2)}) collective-permute-start(bf16[64,768]{1,0:T(8,128)(2,1)S(1)} %get-tuple-element.31), channel_id=1, source_target_pairs={{0,128},{16,144},{32,160},{48,176},{64,192},{80,208},{96,224},{112... | collective-permute-start | bytes 294920 | tf_op jit(solution)/shard_map/ppermute | solution.py:315
  137.2 20.9 %collective-permute-start.11 = (bf16[64,768]{1,0:T(8,128)(2,1)S(1)}, bf16[64,768]{1,0:T(8,128)(2,1)S(1)}, u32[]{:S(2)}, u32[]{:S(2)}) collective-permute-start(bf16[64,768]{1,0:T(8,128)(2,1)S(1)} %get-tuple-element.32), channel_id=1, source_target_pairs={{0,192},{16,208},{32,224},{48,240},{64,0},{80,16},{96,32},{112,48}... | collective-permute-start | bytes 294920 | tf_op jit(solution)/shard_map/ppermute | solution.py:315
  158.2 6.3 %collective-permute-start.12 = (bf16[32,768]{1,0:T(8,128)(2,1)S(1)}, bf16[32,768]{1,0:T(8,128)(2,1)S(1)}, u32[]{:S(2)}, u32[]{:S(2)}) collective-permute-start(bf16[32,768]{1,0:T(8,128)(2,1)S(1)} %get-tuple-element.34), channel_id=1, source_target_pairs={{0,256},{16,272},{32,288},{48,304},{64,320},{80,336},{96,352},{112... | collective-permute-start | bytes 147464 | tf_op jit(solution)/shard_map/ppermute | solution.py:310
Sparse Core Ops, SparseCore 0:
  10.1 67.9 all-gather.1

commit v10 on v9

--- a/solution.py
+++ b/solution.py
@@ -34,8 +34,12 @@
     return jnp.where(mask, 1.0, 0.0).astype(BF16)
 
 
-def pack_kernel(tok_ref, cot_ref, experts_ref, weights_ref, packed_ref, rank_ref):
+def pack_kernel(
+    tok_ref, cot_ref, experts_ref, weights_ref, gate_up_ref, down_ref, packed_ref, rank_ref, own_ref
+):
     rows, features = tok_ref.shape
+    own_ref[:, : gate_up_ref.shape[2]] = gate_up_ref[0]
+    own_ref[:, gate_up_ref.shape[2] :] = down_ref[0]
     packed_ref[:, :features] = tok_ref[...]
     packed_ref[:, features : 2 * features] = cot_ref[...]
     label = iota((EXPERTS, rows), 0)
@@ -53,17 +57,18 @@
     rank_ref[...] = rank
 
 
-def pack(tokens, cotangent, route_experts, route_weights):
+def pack(tokens, cotangent, route_experts, route_weights, gate_up, down):
     rows, features = tokens.shape
     return pl.pallas_call(
         pack_kernel,
         out_shape=(
             jax.ShapeDtypeStruct((rows, 2 * features + rows), BF16),
             jax.ShapeDtypeStruct((EXPERTS, rows), BF16),
+            jax.ShapeDtypeStruct((gate_up.shape[1], gate_up.shape[2] + down.shape[2]), BF16),
         ),
         compiler_params=pltpu.CompilerParams(vmem_limit_bytes=VMEM_BYTES),
         name="pack_rows",
-    )(tokens, cotangent, route_experts.T, route_weights.T)
+    )(tokens, cotangent, route_experts.T, route_weights.T, gate_up, down)
 
 
 def expert_kernel(my_expert, my_dp, plan, g_hbm, *refs):
@@ -323,8 +328,7 @@
     ]
 
 
-def gather_weights(gate_up, down):
-    own = jnp.concatenate([gate_up[0], down[0]], axis=1)
+def gather_weights(own):
     shard = own.shape[0]
     both = jnp.concatenate([own, swap_halves(own)], axis=0)
     held = lax.all_gather(both, "dp", axis=0, axis_index_groups=far_groups(), tiled=True)
@@ -416,18 +420,18 @@
         shift_ring(plus2, 2),
         shift_ring(minus2, -2),
     )
-    mine, theirs = far_sum(
-        my_dp, parts[0], *[shift_ring(parts[j], NEAR * j) for j in range(1, RING // NEAR)]
-    )
+    mine, theirs = far_sum(my_dp, parts[0], *[shift_ring(parts[j], NEAR * j) for j in (2, 1, 3)])
     return mine, swap_halves(theirs)
 
 
 def shards(tokens, cotangent, route_experts, route_weights, gate_up, down):
     rows, features = tokens.shape
     hidden = down.shape[2]
-    packed, rank = pack(tokens, cotangent, route_experts, route_weights)
+    packed, rank, own = pack(
+        tokens, cotangent, route_experts, route_weights, gate_up, down
+    )
     gathered = lax.all_gather(packed, "expert", axis=0, tiled=True)
-    pieces, plan = gather_weights(gate_up, down)
+    pieces, plan = gather_weights(own)
 
     def my_dp():
         return lax.axis_index("dp")

time: 173 us -> 168 us (0.971)
  waiting for transfers between devices: 33.3 us -> 29.7 us
    ppermute x11, waiting for transfers between devices: 30.7 us -> 24.4 us  [shift_ring(): return lax.ppermute(x, 'dp', pairs)]
    all_to_all x1, waiting for transfers between devices: 0.01 us -> 2.16 us  [shards(): lax.all_to_all(row_grads.reshape(EXPERTS, CAP, features), 'expert', split...]
where the time goes in v10:
time: 168 us; the launch traced here: 167 us
  starting transfers between devices  65.6 us (39%)
  blocking collectives  32.6 us (19%)
  waiting for transfers between devices  29.7 us (18%)
  Pallas kernels  22.9 us (14%)
  between operations  14.2 us (8%)
    ppermute x11, starting transfers between devices, shift_ring(): return lax.ppermute(x, 'dp', pairs)  43 us
    all_gather x1, blocking collectives, gather_weights(): lax.all_gather(both, 'dp', axis=0, axis_index_groups=far_groups(), tiled=...  32.6 us
    ppermute x11, waiting for transfers between devices, shift_ring(): return lax.ppermute(x, 'dp', pairs)  24.4 us
    all_to_all x1, starting transfers between devices, shards(): lax.all_to_all(row_grads.reshape(EXPERTS, CAP, features), 'expert', split...  12.4 us
    pallas_call x1, Pallas kernels, expert_work(): pl.pallas_call(functools.partial(expert_kernel, my_expert, my_dp, plan),...  12.4 us
    ppermute x2, starting transfers between devices, swap_halves(): lax.ppermute(x, 'dp', [(d, (d + RING) % (2 * RING)) for d in range(2 * RI...  10.2 us
    pallas_call x1, Pallas kernels, row_gradients(): pl.pallas_call(row_kernel, in_specs=[HBM, HBM], out_specs=HBM, out_shape=...  5.22 us
  transfers between devices with their start and end apart: 15, of which 7 were waited for; matrix products, arithmetic and copies ran while one was open for 1% of the time, Pallas kernels for 5%

profile of v10, /device:TPU:1, one launch (start us, length us, event | category | flops | bytes accessed | tf_op | source)
XLA Modules:
  0.0 166.9 jit_solution(17750598466139913949)
XLA Ops:
  7.2 2.0 %pack_rows.1 = (bf16[128,2176]{1,0:T(8,128)(2,1)}, bf16[16,128]{1,0:T(8,128)(2,1)}, bf16[32,1152]{1,0:T(8,128)(2,1)}) custom-call(bf16[128,1024]{1,0:T(8,128)(2,1)} %tok_ref.1, bf16[128,1024]{1,0:T(8,128)(2,1)} %cot_ref.1, s32[8,128]{1,0:T(8,128)} %bitcast.10, f32[8,128]{1,0:T(8,128)} %bitcast.11, bf16[1,32,768]{2,1,0:T(8,128)(2,1)} %gate_up_ref.1, ...), custom_call_target="tpu_custom_call" | custom-call | tf_op jit(solution)/shard_map/pack_rows/pallas_call | solution.py:62
  9.2 5.7 %collective-permute-start = (bf16[32,1152]{1,0:T(8,128)(2,1)}, bf16[32,1152]{1,0:T(8,128)(2,1)S(1)}, u32[]{:S(2)}, u32[]{:S(2)}) collective-permute-start(bf16[32,1152]{1,0:T(8,128)(2,1)} %get-tuple-element.22), channel_id=1, source_target_pairs={{0,256},{16,272},{32,288},{48,304},{64,320},{80,336},{96,352},{112... | collective-permute-start | bytes 221192 | tf_op jit(solution)/shard_map/ppermute | solution.py:315
  14.9 1.9 %collective-permute-done = bf16[32,1152]{1,0:T(8,128)(2,1)S(1)} collective-permute-done((bf16[32,1152]{1,0:T(8,128)(2,1)}, bf16[32,1152]{1,0:T(8,128)(2,1)S(1)}, u32[]{:S(2)}, u32[]{:S(2)}) %collective-permute-start) | collective-permute-done | bytes 73760 | tf_op jit(solution)/shard_map/ppermute | solution.py:315
  17.7 32.6 %all_gather.7.refs_0_ = bf16[256,1152]{1,0:T(8,128)(2,1)S(1)} all-gather(bf16[64,1152]{1,0:T(8,128)(2,1)S(1)} %pad_maximum_fusion), channel_id=1, replica_groups={{0,64,128,192},{16,80,144,208},{32,96,160,224},{48,112,176,240},{256,32..., dimensions={0}, use_global_device_ids=true | all-gather | bytes 737280 | tf_op jit(solution)/shard_map/all_gather | solution.py:334
  50.3 3.8 %collective-permute-start.2 = (bf16[256,1152]{1,0:T(8,128)(2,1)S(1)}, bf16[256,1152]{1,0:T(8,128)(2,1)S(1)}, u32[]{:S(2)}, u32[]{:S(2)}) collective-permute-start(bf16[256,1152]{1,0:T(8,128)(2,1)S(1)} %all_gather.7.refs_0_), channel_id=1, source_target_pairs={{0,240},{16,0},{32,16},{48,32},{64,48},{80,64},{96,80},{112,96},{1... | collective-permute-start | bytes 1769480 | tf_op jit(solution)/shard_map/ppermute | solution.py:320
  54.1 1.9 %collective-permute-start.1 = (bf16[256,1152]{1,0:T(8,128)(2,1)S(1)}, bf16[256,1152]{1,0:T(8,128)(2,1)S(1)}, u32[]{:S(2)}, u32[]{:S(2)}) collective-permute-start(bf16[256,1152]{1,0:T(8,128)(2,1)S(1)} %all_gather.7.refs_0_), channel_id=1, source_target_pairs={{0,16},{16,32},{32,48},{48,64},{64,80},{80,96},{96,112},{112,128},... | collective-permute-start | bytes 1769480 | tf_op jit(solution)/shard_map/ppermute | solution.py:320
  56.1 3.1 %collective-permute-start.4 = (bf16[128,1152]{1,0:T(8,128)(2,1)S(1)}, bf16[128,1152]{1,0:T(8,128)(2,1)S(1)}, u32[]{:S(2)}, u32[]{:S(2)}) collective-permute-start(bf16[128,1152]{1,0:T(8,128)(2,1)S(1)} %get-tuple-element.38), channel_id=1, source_target_pairs={{0,224},{16,240},{32,0},{48,16},{64,32},{80,48},{96,64},{112,80},{... | collective-permute-start | bytes 884744 | tf_op jit(solution)/shard_map/ppermute | solution.py:320
  59.2 3.1 %collective-permute-start.3 = (bf16[128,1152]{1,0:T(8,128)(2,1)S(1)}, bf16[128,1152]{1,0:T(8,128)(2,1)S(1)}, u32[]{:S(2)}, u32[]{:S(2)}) collective-permute-start(bf16[128,1152]{1,0:T(8,128)(2,1)S(1)} %get-tuple-element.39), channel_id=1, source_target_pairs={{0,32},{16,48},{32,64},{48,80},{64,96},{80,112},{96,128},{112,144}... | collective-permute-start | bytes 884744 | tf_op jit(solution)/shard_map/ppermute | solution.py:320
  62.3 14.2 %collective-permute-done.4.refs_4_ = bf16[128,1152]{1,0:T(8,128)(2,1)S(1)} collective-permute-done((bf16[128,1152]{1,0:T(8,128)(2,1)S(1)}, bf16[128,1152]{1,0:T(8,128)(2,1)S(1)}, u32[]{:S(2)}, u32[]{:S(2)}) %collective-permute-start.4) | collective-permute-done | bytes 294944 | tf_op jit(solution)/shard_map/ppermute | solution.py:320
  78.2 12.4 %expert_work.1 = (bf16[1280,768]{1,0:T(8,128)(2,1)}, bf16[1024,768]{1,0:T(8,128)(2,1)}, bf16[4,2,32,768]{3,2,1,0:T(8,128)(2,1)}, bf16[4,2,32,768]{3,2,1,0:T(8,12...) custom-call(bf16[2048,2176]{1,0:T(8,128)(2,1)} %all-gather.2.cloned.1.call-done.g, ...), custom_call_target="tpu_custom_call" | custom-call | flops 5033164800 | bytes 16777216 | tf_op jit(solution)/shard_map/expert_work/pallas_call | solution.py:208
  90.5 4.6 %collective-permute-start.5 = (bf16[4,64,768]{2,1,0:T(8,128)(2,1)}, bf16[4,64,768]{2,1,0:T(8,128)(2,1)S(1)}, u32[]{:S(2)}, u32[]{:S(2)}) collective-permute-start(bf16[4,64,768]{2,1,0:T(8,128)(2,1)} %bitcast.13), channel_id=1, source_target_pairs={{0,16},{16,32},{32,48},{48,64},{64,80},{80,96},{96,112},{112,128},... | collective-permute-start | bytes 1179656 | tf_op jit(solution)/shard_map/ppermute | solution.py:320
  95.2 3.0 %collective-permute-start.6 = (bf16[4,64,768]{2,1,0:T(8,128)(2,1)}, bf16[4,64,768]{2,1,0:T(8,128)(2,1)S(1)}, u32[]{:S(2)}, u32[]{:S(2)}) collective-permute-start(bf16[4,64,768]{2,1,0:T(8,128)(2,1)} %bitcast.12), channel_id=1, source_target_pairs={{0,240},{16,0},{32,16},{48,32},{64,48},{80,64},{96,80},{112,96},{1... | collective-permute-start | bytes 1179656 | tf_op jit(solution)/shard_map/ppermute | solution.py:320
  98.1 2.0 %collective-permute-start.7 = (bf16[4,32,768]{2,1,0:T(8,128)(2,1)}, bf16[4,32,768]{2,1,0:T(8,128)(2,1)}, u32[]{:S(2)}, u32[]{:S(2)}) collective-permute-start(bf16[4,32,768]{2,1,0:T(8,128)(2,1)} %get-tuple-element.29), channel_id=1, source_target_pairs={{0,32},{16,48},{32,64},{48,80},{64,96},{80,112},{96,128},{112,144}... | collective-permute-start | bytes 589832 | tf_op jit(solution)/shard_map/ppermute | solution.py:320
  100.2 5.4 %collective-permute-start.8 = (bf16[4,32,768]{2,1,0:T(8,128)(2,1)}, bf16[4,32,768]{2,1,0:T(8,128)(2,1)}, u32[]{:S(2)}, u32[]{:S(2)}) collective-permute-start(bf16[4,32,768]{2,1,0:T(8,128)(2,1)} %get-tuple-element.30), channel_id=1, source_target_pairs={{0,224},{16,240},{32,0},{48,16},{64,32},{80,48},{96,64},{112,80},{... | collective-permute-start | bytes 589832 | tf_op jit(solution)/shard_map/ppermute | solution.py:320
  105.6 5.2 %row_gradients.1 = bf16[1280,1024]{1,0:T(8,128)(2,1)} custom-call(bf16[1280,768]{1,0:T(8,128)(2,1)} %get-tuple-element.23.pre_hbm, bf16[1024,768]{1,0:T(8,128)(2,1)} %get-tuple-element.24.gate_up_hbm), custom_call_target="tpu_custom_call" | custom-call | flops 2013265920 | bytes 6291456 | tf_op jit(solution)/shard_map/row_gradients/pallas_call | solution.py:266
  110.8 12.4 %all-to-all-start = ((bf16[16,80,1024]{2,1,0:T(8,128)(2,1)}), bf16[16,80,1024]{2,1,0:T(8,128)(2,1)S(1)}, u32[]{:S(2)}, u32[]{:S(2)}) async-start(bf16[16,80,1024]{2,1,0:T(8,128)(2,1)} %bitcast.9), calls=%async_computation | async-start | bytes 5242880 | tf_op jit(solution)/shard_map/all_to_all | solution.py:443
  124.2 1.2 near_sum.1
  125.4 6.9 %collective-permute-start.9 = (bf16[64,768]{1,0:T(8,128)(2,1)S(1)}, bf16[64,768]{1,0:T(8,128)(2,1)S(1)}, u32[]{:S(2)}, u32[]{:S(2)}) collective-permute-start(bf16[64,768]{1,0:T(8,128)(2,1)S(1)} %get-tuple-element.32), channel_id=1, source_target_pairs={{0,128},{16,144},{32,160},{48,176},{64,192},{80,208},{96,224},{112... | collective-permute-start | bytes 294920 | tf_op jit(solution)/shard_map/ppermute | solution.py:320
  132.4 4.3 %collective-permute-start.10 = (bf16[64,768]{1,0:T(8,128)(2,1)S(1)}, bf16[64,768]{1,0:T(8,128)(2,1)S(1)}, u32[]{:S(2)}, u32[]{:S(2)}) collective-permute-start(bf16[64,768]{1,0:T(8,128)(2,1)S(1)} %get-tuple-element.33), channel_id=1, source_target_pairs={{0,64},{16,80},{32,96},{48,112},{64,128},{80,144},{96,160},{112,17... | collective-permute-start | bytes 294920 | tf_op jit(solution)/shard_map/ppermute | solution.py:320
  136.7 4.9 %collective-permute-start.11 = (bf16[64,768]{1,0:T(8,128)(2,1)S(1)}, bf16[64,768]{1,0:T(8,128)(2,1)S(1)}, u32[]{:S(2)}, u32[]{:S(2)}) collective-permute-start(bf16[64,768]{1,0:T(8,128)(2,1)S(1)} %get-tuple-element.34), channel_id=1, source_target_pairs={{0,192},{16,208},{32,224},{48,240},{64,0},{80,16},{96,32},{112,48}... | collective-permute-start | bytes 294920 | tf_op jit(solution)/shard_map/ppermute | solution.py:320
  141.6 8.9 %collective-permute-done.9.two = bf16[64,768]{1,0:T(8,128)(2,1)S(1)} collective-permute-done((bf16[64,768]{1,0:T(8,128)(2,1)S(1)}, bf16[64,768]{1,0:T(8,128)(2,1)S(1)}, u32[]{:S(2)}, u32[]{:S(2)}) %collective-permute-start.9) | collective-permute-done | bytes 98336 | tf_op jit(solution)/shard_map/ppermute | solution.py:320
  151.3 4.5 %collective-permute-start.12 = (bf16[32,768]{1,0:T(8,128)(2,1)S(1)}, bf16[32,768]{1,0:T(8,128)(2,1)S(1)}, u32[]{:S(2)}, u32[]{:S(2)}) collective-permute-start(bf16[32,768]{1,0:T(8,128)(2,1)S(1)} %get-tuple-element.36), channel_id=1, source_target_pairs={{0,256},{16,272},{32,288},{48,304},{64,320},{80,336},{96,352},{112... | collective-permute-start | bytes 147464 | tf_op jit(solution)/shard_map/ppermute | solution.py:315
  155.9 2.2 %all-to-all-done = bf16[16,80,1024]{2,1,0:T(8,128)(2,1)S(1)} async-done(((bf16[16,80,1024]{2,1,0:T(8,128)(2,1)}), bf16[16,80,1024]{2,1,0:T(8,128)(2,1)S(1)}, u32[]{:S(2)}, u32[]{:S(2)}) %all-to-all-start) | async-done | bytes 2621472 | tf_op jit(solution)/shard_map/all_to_all | solution.py:443
  158.1 1.4 combine_rows.1
  (31 shorter events, 5.2 us)
Async XLA Ops:
  7.2 71.0 %all-gather.2.cloned.1.call-start = ((), (), s32[]{:S(2)}) async-start(), calls=%async_computation.1 | async-start | bytes 9469952 | tf_op jit(solution)/shard_map/all_gather | solution.py:433
  9.2 7.6 %collective-permute-start = (bf16[32,1152]{1,0:T(8,128)(2,1)}, bf16[32,1152]{1,0:T(8,128)(2,1)S(1)}, u32[]{:S(2)}, u32[]{:S(2)}) collective-permute-start(bf16[32,1152]{1,0:T(8,128)(2,1)} %get-tuple-element.22), channel_id=1, source_target_pairs={{0,256},{16,272},{32,288},{48,304},{64,320},{80,336},{96,352},{112... | collective-permute-start | bytes 221192 | tf_op jit(solution)/shard_map/ppermute | solution.py:315
  50.3 27.8 %copy-start.2 = (bf16[256,1152]{1,0:T(8,128)(2,1)}, bf16[256,1152]{1,0:T(8,128)(2,1)S(1)}, u32[]{:S(2)}) copy-start(bf16[256,1152]{1,0:T(8,128)(2,1)S(1)} %all_gather.7.refs_0_) | copy-start | bytes 1769476
  50.3 26.7 %collective-permute-start.2 = (bf16[256,1152]{1,0:T(8,128)(2,1)S(1)}, bf16[256,1152]{1,0:T(8,128)(2,1)S(1)}, u32[]{:S(2)}, u32[]{:S(2)}) collective-permute-start(bf16[256,1152]{1,0:T(8,128)(2,1)S(1)} %all_gather.7.refs_0_), channel_id=1, source_target_pairs={{0,240},{16,0},{32,16},{48,32},{64,48},{80,64},{96,80},{112,96},{1... | collective-permute-start | bytes 1769480 | tf_op jit(solution)/shard_map/ppermute | solution.py:320
  54.1 22.9 %collective-permute-start.1 = (bf16[256,1152]{1,0:T(8,128)(2,1)S(1)}, bf16[256,1152]{1,0:T(8,128)(2,1)S(1)}, u32[]{:S(2)}, u32[]{:S(2)}) collective-permute-start(bf16[256,1152]{1,0:T(8,128)(2,1)S(1)} %all_gather.7.refs_0_), channel_id=1, source_target_pairs={{0,16},{16,32},{32,48},{48,64},{64,80},{80,96},{96,112},{112,128},... | collective-permute-start | bytes 1769480 | tf_op jit(solution)/shard_map/ppermute | solution.py:320
  56.1 20.4 %collective-permute-start.4 = (bf16[128,1152]{1,0:T(8,128)(2,1)S(1)}, bf16[128,1152]{1,0:T(8,128)(2,1)S(1)}, u32[]{:S(2)}, u32[]{:S(2)}) collective-permute-start(bf16[128,1152]{1,0:T(8,128)(2,1)S(1)} %get-tuple-element.38), channel_id=1, source_target_pairs={{0,224},{16,240},{32,0},{48,16},{64,32},{80,48},{96,64},{112,80},{... | collective-permute-start | bytes 884744 | tf_op jit(solution)/shard_map/ppermute | solution.py:320
  59.2 17.8 %collective-permute-start.3 = (bf16[128,1152]{1,0:T(8,128)(2,1)S(1)}, bf16[128,1152]{1,0:T(8,128)(2,1)S(1)}, u32[]{:S(2)}, u32[]{:S(2)}) collective-permute-start(bf16[128,1152]{1,0:T(8,128)(2,1)S(1)} %get-tuple-element.39), channel_id=1, source_target_pairs={{0,32},{16,48},{32,64},{48,80},{64,96},{80,112},{96,128},{112,144}... | collective-permute-start | bytes 884744 | tf_op jit(solution)/shard_map/ppermute | solution.py:320
  76.5 1.7 %copy-start.5 = (bf16[128,1152]{1,0:T(8,128)(2,1)}, bf16[128,1152]{1,0:T(8,128)(2,1)S(1)}, u32[]{:S(2)}) copy-start(bf16[128,1152]{1,0:T(8,128)(2,1)S(1)} %collective-permute-done.4.refs_4_) | copy-start | bytes 884740
  77.0 1.1 copy-start.6
  77.0 1.1 copy-start.3
  77.0 1.1 copy-start.4
  90.5 32.7 %collective-permute-start.5 = (bf16[4,64,768]{2,1,0:T(8,128)(2,1)}, bf16[4,64,768]{2,1,0:T(8,128)(2,1)S(1)}, u32[]{:S(2)}, u32[]{:S(2)}) collective-permute-start(bf16[4,64,768]{2,1,0:T(8,128)(2,1)} %bitcast.13), channel_id=1, source_target_pairs={{0,16},{16,32},{32,48},{48,64},{64,80},{80,96},{96,112},{112,128},... | collective-permute-start | bytes 1179656 | tf_op jit(solution)/shard_map/ppermute | solution.py:320
  95.2 28.1 %collective-permute-start.6 = (bf16[4,64,768]{2,1,0:T(8,128)(2,1)}, bf16[4,64,768]{2,1,0:T(8,128)(2,1)S(1)}, u32[]{:S(2)}, u32[]{:S(2)}) collective-permute-start(bf16[4,64,768]{2,1,0:T(8,128)(2,1)} %bitcast.12), channel_id=1, source_target_pairs={{0,240},{16,0},{32,16},{48,32},{64,48},{80,64},{96,80},{112,96},{1... | collective-permute-start | bytes 1179656 | tf_op jit(solution)/shard_map/ppermute | solution.py:320
  98.1 25.0 %collective-permute-start.7 = (bf16[4,32,768]{2,1,0:T(8,128)(2,1)}, bf16[4,32,768]{2,1,0:T(8,128)(2,1)}, u32[]{:S(2)}, u32[]{:S(2)}) collective-permute-start(bf16[4,32,768]{2,1,0:T(8,128)(2,1)} %get-tuple-element.29), channel_id=1, source_target_pairs={{0,32},{16,48},{32,64},{48,80},{64,96},{80,112},{96,128},{112,144}... | collective-permute-start | bytes 589832 | tf_op jit(solution)/shard_map/ppermute | solution.py:320
  100.2 23.0 %collective-permute-start.8 = (bf16[4,32,768]{2,1,0:T(8,128)(2,1)}, bf16[4,32,768]{2,1,0:T(8,128)(2,1)}, u32[]{:S(2)}, u32[]{:S(2)}) collective-permute-start(bf16[4,32,768]{2,1,0:T(8,128)(2,1)} %get-tuple-element.30), channel_id=1, source_target_pairs={{0,224},{16,240},{32,0},{48,16},{64,32},{80,48},{96,64},{112,80},{... | collective-permute-start | bytes 589832 | tf_op jit(solution)/shard_map/ppermute | solution.py:320
  110.8 47.3 %all-to-all-start = ((bf16[16,80,1024]{2,1,0:T(8,128)(2,1)}), bf16[16,80,1024]{2,1,0:T(8,128)(2,1)S(1)}, u32[]{:S(2)}, u32[]{:S(2)}) async-start(bf16[16,80,1024]{2,1,0:T(8,128)(2,1)} %bitcast.9), calls=%async_computation | async-start | bytes 5242880 | tf_op jit(solution)/shard_map/all_to_all | solution.py:443
  123.2 1.0 copy-start.1
  124.2 33.8 %copy-start = (bf16[16,128]{1,0:T(8,128)(2,1)S(1)}, bf16[16,128]{1,0:T(8,128)(2,1)}, u32[]{:S(2)}) copy-start(bf16[16,128]{1,0:T(8,128)(2,1)} %get-tuple-element.20.rank_ref) | copy-start | bytes 12292
  125.4 25.0 %collective-permute-start.9 = (bf16[64,768]{1,0:T(8,128)(2,1)S(1)}, bf16[64,768]{1,0:T(8,128)(2,1)S(1)}, u32[]{:S(2)}, u32[]{:S(2)}) collective-permute-start(bf16[64,768]{1,0:T(8,128)(2,1)S(1)} %get-tuple-element.32), channel_id=1, source_target_pairs={{0,128},{16,144},{32,160},{48,176},{64,192},{80,208},{96,224},{112... | collective-permute-start | bytes 294920 | tf_op jit(solution)/shard_map/ppermute | solution.py:320
  132.4 18.1 %collective-permute-start.10 = (bf16[64,768]{1,0:T(8,128)(2,1)S(1)}, bf16[64,768]{1,0:T(8,128)(2,1)S(1)}, u32[]{:S(2)}, u32[]{:S(2)}) collective-permute-start(bf16[64,768]{1,0:T(8,128)(2,1)S(1)} %get-tuple-element.33), channel_id=1, source_target_pairs={{0,64},{16,80},{32,96},{48,112},{64,128},{80,144},{96,160},{112,17... | collective-permute-start | bytes 294920 | tf_op jit(solution)/shard_map/ppermute | solution.py:320
  136.7 14.6 %collective-permute-start.11 = (bf16[64,768]{1,0:T(8,128)(2,1)S(1)}, bf16[64,768]{1,0:T(8,128)(2,1)S(1)}, u32[]{:S(2)}, u32[]{:S(2)}) collective-permute-start(bf16[64,768]{1,0:T(8,128)(2,1)S(1)} %get-tuple-element.34), channel_id=1, source_target_pairs={{0,192},{16,208},{32,224},{48,240},{64,0},{80,16},{96,32},{112,48}... | collective-permute-start | bytes 294920 | tf_op jit(solution)/shard_map/ppermute | solution.py:320
  151.3 8.1 %collective-permute-start.12 = (bf16[32,768]{1,0:T(8,128)(2,1)S(1)}, bf16[32,768]{1,0:T(8,128)(2,1)S(1)}, u32[]{:S(2)}, u32[]{:S(2)}) collective-permute-start(bf16[32,768]{1,0:T(8,128)(2,1)S(1)} %get-tuple-element.36), channel_id=1, source_target_pairs={{0,256},{16,272},{32,288},{48,304},{64,320},{80,336},{96,352},{112... | collective-permute-start | bytes 147464 | tf_op jit(solution)/shard_map/ppermute | solution.py:315
Sparse Core Ops, SparseCore 0:
  10.1 67.9 all-gather.1

commit v11 on v10

--- a/solution.py
+++ b/solution.py
@@ -15,7 +15,6 @@
 NEAR = 4
 PAIR = 2
 BLOCKS = 1
-ROW_BLOCKS = 2
 STRIPS = 1
 UNROUTED = 200.0
 MIB = 1024 * 1024
@@ -74,8 +73,8 @@
 def expert_kernel(my_expert, my_dp, plan, g_hbm, *refs):
     piece_total = 1 + max(array for array, *_ in plan)
     pieces = refs[:piece_total]
-    pre_hbm, gate_up_hbm, *parts_hbm = refs[piece_total : piece_total + 7]
-    blocks, weights, inputs, cots, pre_grad, parts = refs[piece_total + 7 : -4]
+    row_hbm, *parts_hbm = refs[piece_total : piece_total + 6]
+    blocks, weights, inputs, cots, pre_grad, row_grad, parts = refs[piece_total + 6 : -4]
     load_sems, weight_sems, pre_sems, out_sems = refs[-4:]
     expert = my_expert()
     features, hidden = inputs.shape[1], pre_grad.shape[1] // 2
@@ -151,12 +150,6 @@
         if m == 0:
             for copy in weight_loads:
                 copy.wait()
-            stores.append(
-                pltpu.make_async_copy(
-                    weights.at[:, pl.ds(0, 2 * hidden)], gate_up_hbm, out_sems.at[0]
-                )
-            )
-            stores[0].start()
         projected = jnp.dot(
             inputs[here, :], weights[:, : 2 * hidden], preferred_element_type=F32
         )
@@ -168,8 +161,14 @@
         grad_up = hidden_grad * gate_part * sigmoid_gate
         pre_grad[here, :hidden] = grad_gate.astype(BF16)
         pre_grad[here, hidden:] = grad_up.astype(BF16)
+        row_grad[here, :] = lax.dot_general(
+            pre_grad[here, :],
+            weights[:, : 2 * hidden],
+            (((1,), (1,)), ((), ())),
+            preferred_element_type=F32,
+        ).astype(BF16)
         stores.append(
-            pltpu.make_async_copy(pre_grad.at[here, :], pre_hbm.at[here, :], pre_sems.at[m])
+            pltpu.make_async_copy(row_grad.at[here, :], row_hbm.at[here, :], pre_sems.at[m])
         )
         stores[-1].start()
 
@@ -204,7 +203,7 @@
     whole = (RING // NEAR, 2, shard, 2 * hidden)
     half = (RING // NEAR, shard, 2 * hidden)
     parts = [whole, whole, whole, half, half]
-    out_shapes = [(slots, 2 * hidden), (features, 2 * hidden)] + parts
+    out_shapes = [(slots, features)] + parts
     return pl.pallas_call(
         functools.partial(expert_kernel, my_expert, my_dp, plan),
         in_specs=[HBM] * (1 + len(pieces)),
@@ -216,6 +215,7 @@
             pltpu.VMEM((slots, features), BF16),
             pltpu.VMEM((slots, features), BF16),
             pltpu.VMEM((slots, 2 * hidden), BF16),
+            pltpu.VMEM((slots, features), BF16),
             pltpu.VMEM((NEAR, *whole), BF16),
             pltpu.SemaphoreType.DMA((EXPERTS // PAIR,)),
             pltpu.SemaphoreType.DMA((2 * RING,)),
@@ -224,62 +224,12 @@
         ],
         compiler_params=pltpu.CompilerParams(vmem_limit_bytes=VMEM_BYTES),
         cost_estimate=pl.CostEstimate(
-            flops=5 * slots * features * 2 * hidden,
+            flops=7 * slots * features * 2 * hidden,
             bytes_accessed=16 * MIB,
             transcendentals=slots * hidden,
         ),
         name="expert_work",
     )(gathered, *pieces)
-
-
-def row_kernel(pre_hbm, gate_up_hbm, row_hbm, pre_grad, gate_up, row_grad, sems):
-    block = pre_grad.shape[0] // ROW_BLOCKS
-    loads = [pltpu.make_async_copy(gate_up_hbm, gate_up, sems.at[0])]
-    stores = []
-    for m in range(ROW_BLOCKS):
-        here = pl.ds(m * block, block)
-        loads.append(
-            pltpu.make_async_copy(pre_hbm.at[here, :], pre_grad.at[here, :], sems.at[1 + m])
-        )
-        stores.append(
-            pltpu.make_async_copy(
-                row_grad.at[here, :], row_hbm.at[here, :], sems.at[1 + ROW_BLOCKS + m]
-            )
-        )
-    for copy in loads:
-        copy.start()
-    loads[0].wait()
-    for m in range(ROW_BLOCKS):
-        here = pl.ds(m * block, block)
-        loads[1 + m].wait()
-        row_grad[here, :] = lax.dot_general(
-            pre_grad[here, :], gate_up[...], (((1,), (1,)), ((), ())), preferred_element_type=F32
-        ).astype(BF16)
-        stores[m].start()
-    for copy in stores:
-        copy.wait()
-
-
-def row_gradients(pre_grad, gate_up):
-    slots, columns = pre_grad.shape
-    features = gate_up.shape[0]
-    return pl.pallas_call(
-        row_kernel,
-        in_specs=[HBM, HBM],
-        out_specs=HBM,
-        out_shape=jax.ShapeDtypeStruct((slots, features), BF16),
-        scratch_shapes=[
-            pltpu.VMEM((slots, columns), BF16),
-            pltpu.VMEM((features, columns), BF16),
-            pltpu.VMEM((slots, features), BF16),
-            pltpu.SemaphoreType.DMA((1 + 2 * ROW_BLOCKS,)),
-        ],
-        compiler_params=pltpu.CompilerParams(vmem_limit_bytes=VMEM_BYTES),
-        cost_estimate=pl.CostEstimate(
-            flops=2 * slots * features * columns, bytes_accessed=6 * MIB, transcendentals=0
-        ),
-        name="row_gradients",
-    )(pre_grad, gate_up)
 
 
 def combine_kernel(rank_ref, back_ref, out_ref, done_ref):
@@ -436,10 +386,9 @@
     def my_dp():
         return lax.axis_index("dp")
 
-    pre_grad, full_gate_up, *grad_parts = expert_work(
+    row_grads, *grad_parts = expert_work(
         gathered, pieces, plan, features, hidden, lambda: lax.axis_index("expert"), my_dp
     )
-    row_grads = row_gradients(pre_grad, full_gate_up)
     returned = lax.all_to_all(
         row_grads.reshape(EXPERTS, CAP, features), "expert", split_axis=0, concat_axis=0, tiled=True
     )

time: 168 us -> 166 us (0.988)
  Pallas kernels: 22.9 us -> 19.9 us
    pallas_call x1 -> x0, Pallas kernels: 5.22 us -> none  [row_gradients(): pl.pallas_call(row_kernel, in_specs=[HBM, HBM], out_specs=HBM, out_shape=...]
    all_to_all x1, waiting for transfers between devices: 2.16 us -> 4.6 us  [shards(): lax.all_to_all(row_grads.reshape(EXPERTS, CAP, features), 'expert', split...]
    ppermute x11, waiting for transfers between devices: 24.4 us -> 22.1 us  [shift_ring(): return lax.ppermute(x, 'dp', pairs)]
    pallas_call x1, Pallas kernels: 12.4 us -> 14.5 us  [expert_work(): pl.pallas_call(functools.partial(expert_kernel, my_expert, my_dp, plan),...]
  transfers between devices with their start and end apart: 15 -> 15, of which waited for: 7 -> 7; matrix products, arithmetic and copies ran while one was open for 1% -> 1% of each run, Pallas kernels for 5% -> 2%
where the time goes in v11:
time: 166 us; the launch traced here: 164 us
  starting transfers between devices  65.6 us (40%)
  blocking collectives  32.6 us (20%)
  waiting for transfers between devices  29.7 us (18%)
  Pallas kernels  19.9 us (12%)
  between operations  14.2 us (9%)
    ppermute x11, starting transfers between devices, shift_ring(): return lax.ppermute(x, 'dp', pairs)  42.9 us
    all_gather x1, blocking collectives, gather_weights(): lax.all_gather(both, 'dp', axis=0, axis_index_groups=far_groups(), tiled=...  32.6 us
    ppermute x11, waiting for transfers between devices, shift_ring(): return lax.ppermute(x, 'dp', pairs)  22.1 us
    pallas_call x1, Pallas kernels, expert_work(): pl.pallas_call(functools.partial(expert_kernel, my_expert, my_dp, plan),...  14.5 us
    all_to_all x1, starting transfers between devices, shards(): lax.all_to_all(row_grads.reshape(EXPERTS, CAP, features), 'expert', split...  12.5 us
    ppermute x2, starting transfers between devices, swap_halves(): lax.ppermute(x, 'dp', [(d, (d + RING) % (2 * RING)) for d in range(2 * RI...  10.1 us
    all_to_all x1, waiting for transfers between devices, shards(): lax.all_to_all(row_grads.reshape(EXPERTS, CAP, features), 'expert', split...  4.6 us
  transfers between devices with their start and end apart: 15, of which 7 were waited for; matrix products, arithmetic and copies ran while one was open for 1% of the time, Pallas kernels for 2%

profile of v11, /device:TPU:1, one launch (start us, length us, event | category | flops | bytes accessed | tf_op | source)
XLA Modules:
  0.0 164.0 jit_solution(15648165518593904191)
XLA Ops:
  7.2 2.0 %pack_rows.1 = (bf16[128,2176]{1,0:T(8,128)(2,1)}, bf16[16,128]{1,0:T(8,128)(2,1)}, bf16[32,1152]{1,0:T(8,128)(2,1)}) custom-call(bf16[128,1024]{1,0:T(8,128)(2,1)} %tok_ref.1, bf16[128,1024]{1,0:T(8,128)(2,1)} %cot_ref.1, s32[8,128]{1,0:T(8,128)} %bitcast.10, f32[8,128]{1,0:T(8,128)} %bitcast.11, bf16[1,32,768]{2,1,0:T(8,128)(2,1)} %gate_up_ref.1, ...), custom_call_target="tpu_custom_call" | custom-call | tf_op jit(solution)/shard_map/pack_rows/pallas_call | solution.py:61
  9.2 5.7 %collective-permute-start = (bf16[32,1152]{1,0:T(8,128)(2,1)}, bf16[32,1152]{1,0:T(8,128)(2,1)S(1)}, u32[]{:S(2)}, u32[]{:S(2)}) collective-permute-start(bf16[32,1152]{1,0:T(8,128)(2,1)} %get-tuple-element.21), channel_id=1, source_target_pairs={{0,256},{16,272},{32,288},{48,304},{64,320},{80,336},{96,352},{112... | collective-permute-start | bytes 221192 | tf_op jit(solution)/shard_map/ppermute | solution.py:265
  14.9 1.9 %collective-permute-done = bf16[32,1152]{1,0:T(8,128)(2,1)S(1)} collective-permute-done((bf16[32,1152]{1,0:T(8,128)(2,1)}, bf16[32,1152]{1,0:T(8,128)(2,1)S(1)}, u32[]{:S(2)}, u32[]{:S(2)}) %collective-permute-start) | collective-permute-done | bytes 73760 | tf_op jit(solution)/shard_map/ppermute | solution.py:265
  17.7 32.6 %all_gather.7.refs_0_ = bf16[256,1152]{1,0:T(8,128)(2,1)S(1)} all-gather(bf16[64,1152]{1,0:T(8,128)(2,1)S(1)} %pad_maximum_fusion), channel_id=1, replica_groups={{0,64,128,192},{16,80,144,208},{32,96,160,224},{48,112,176,240},{256,32..., dimensions={0}, use_global_device_ids=true | all-gather | bytes 737280 | tf_op jit(solution)/shard_map/all_gather | solution.py:284
  50.3 3.8 %collective-permute-start.2 = (bf16[256,1152]{1,0:T(8,128)(2,1)S(1)}, bf16[256,1152]{1,0:T(8,128)(2,1)S(1)}, u32[]{:S(2)}, u32[]{:S(2)}) collective-permute-start(bf16[256,1152]{1,0:T(8,128)(2,1)S(1)} %all_gather.7.refs_0_), channel_id=1, source_target_pairs={{0,240},{16,0},{32,16},{48,32},{64,48},{80,64},{96,80},{112,96},{1... | collective-permute-start | bytes 1769480 | tf_op jit(solution)/shard_map/ppermute | solution.py:270
  54.1 1.9 %collective-permute-start.1 = (bf16[256,1152]{1,0:T(8,128)(2,1)S(1)}, bf16[256,1152]{1,0:T(8,128)(2,1)S(1)}, u32[]{:S(2)}, u32[]{:S(2)}) collective-permute-start(bf16[256,1152]{1,0:T(8,128)(2,1)S(1)} %all_gather.7.refs_0_), channel_id=1, source_target_pairs={{0,16},{16,32},{32,48},{48,64},{64,80},{80,96},{96,112},{112,128},... | collective-permute-start | bytes 1769480 | tf_op jit(solution)/shard_map/ppermute | solution.py:270
  56.1 3.1 %collective-permute-start.4 = (bf16[128,1152]{1,0:T(8,128)(2,1)S(1)}, bf16[128,1152]{1,0:T(8,128)(2,1)S(1)}, u32[]{:S(2)}, u32[]{:S(2)}) collective-permute-start(bf16[128,1152]{1,0:T(8,128)(2,1)S(1)} %get-tuple-element.36), channel_id=1, source_target_pairs={{0,224},{16,240},{32,0},{48,16},{64,32},{80,48},{96,64},{112,80},{... | collective-permute-start | bytes 884744 | tf_op jit(solution)/shard_map/ppermute | solution.py:270
  59.2 3.1 %collective-permute-start.3 = (bf16[128,1152]{1,0:T(8,128)(2,1)S(1)}, bf16[128,1152]{1,0:T(8,128)(2,1)S(1)}, u32[]{:S(2)}, u32[]{:S(2)}) collective-permute-start(bf16[128,1152]{1,0:T(8,128)(2,1)S(1)} %get-tuple-element.37), channel_id=1, source_target_pairs={{0,32},{16,48},{32,64},{48,80},{64,96},{80,112},{96,128},{112,144}... | collective-permute-start | bytes 884744 | tf_op jit(solution)/shard_map/ppermute | solution.py:270
  62.3 14.2 %collective-permute-done.4.refs_4_ = bf16[128,1152]{1,0:T(8,128)(2,1)S(1)} collective-permute-done((bf16[128,1152]{1,0:T(8,128)(2,1)S(1)}, bf16[128,1152]{1,0:T(8,128)(2,1)S(1)}, u32[]{:S(2)}, u32[]{:S(2)}) %collective-permute-start.4) | collective-permute-done | bytes 294944 | tf_op jit(solution)/shard_map/ppermute | solution.py:270
  78.2 14.5 %expert_work.1 = (bf16[1280,1024]{1,0:T(8,128)(2,1)}, bf16[4,2,32,768]{3,2,1,0:T(8,128)(2,1)}, bf16[4,2,32,768]{3,2,1,0:T(8,128)(2,1)}, bf16[4,2,32,768]{3,2,1,0...) custom-call(bf16[2048,2176]{1,0:T(8,128)(2,1)} %all-gather.2.cloned.1.call-done.g_hbm, ...), custom_call_target="tpu_custom_call" | custom-call | flops 7046430720 | bytes 16777216 | tf_op jit(solution)/shard_map/expert_work/pallas_call | solution.py:207
  92.7 4.7 %collective-permute-start.5 = (bf16[4,64,768]{2,1,0:T(8,128)(2,1)}, bf16[4,64,768]{2,1,0:T(8,128)(2,1)S(1)}, u32[]{:S(2)}, u32[]{:S(2)}) collective-permute-start(bf16[4,64,768]{2,1,0:T(8,128)(2,1)} %bitcast.13), channel_id=1, source_target_pairs={{0,16},{16,32},{32,48},{48,64},{64,80},{80,96},{96,112},{112,128},... | collective-permute-start | bytes 1179656 | tf_op jit(solution)/shard_map/ppermute | solution.py:270
  97.4 2.9 %collective-permute-start.6 = (bf16[4,64,768]{2,1,0:T(8,128)(2,1)}, bf16[4,64,768]{2,1,0:T(8,128)(2,1)S(1)}, u32[]{:S(2)}, u32[]{:S(2)}) collective-permute-start(bf16[4,64,768]{2,1,0:T(8,128)(2,1)} %bitcast.12), channel_id=1, source_target_pairs={{0,240},{16,0},{32,16},{48,32},{64,48},{80,64},{96,80},{112,96},{1... | collective-permute-start | bytes 1179656 | tf_op jit(solution)/shard_map/ppermute | solution.py:270
  100.3 2.1 %collective-permute-start.7 = (bf16[4,32,768]{2,1,0:T(8,128)(2,1)}, bf16[4,32,768]{2,1,0:T(8,128)(2,1)}, u32[]{:S(2)}, u32[]{:S(2)}) collective-permute-start(bf16[4,32,768]{2,1,0:T(8,128)(2,1)} %get-tuple-element.27), channel_id=1, source_target_pairs={{0,32},{16,48},{32,64},{48,80},{64,96},{80,112},{96,128},{112,144}... | collective-permute-start | bytes 589832 | tf_op jit(solution)/shard_map/ppermute | solution.py:270
  102.5 5.3 %collective-permute-start.8 = (bf16[4,32,768]{2,1,0:T(8,128)(2,1)}, bf16[4,32,768]{2,1,0:T(8,128)(2,1)}, u32[]{:S(2)}, u32[]{:S(2)}) collective-permute-start(bf16[4,32,768]{2,1,0:T(8,128)(2,1)} %get-tuple-element.28), channel_id=1, source_target_pairs={{0,224},{16,240},{32,0},{48,16},{64,32},{80,48},{96,64},{112,80},{... | collective-permute-start | bytes 589832 | tf_op jit(solution)/shard_map/ppermute | solution.py:270
  107.7 12.5 %all-to-all-start = ((bf16[16,80,1024]{2,1,0:T(8,128)(2,1)}), bf16[16,80,1024]{2,1,0:T(8,128)(2,1)S(1)}, u32[]{:S(2)}, u32[]{:S(2)}) async-start(bf16[16,80,1024]{2,1,0:T(8,128)(2,1)} %bitcast.9), calls=%async_computation | async-start | bytes 5242880 | tf_op jit(solution)/shard_map/all_to_all | solution.py:392
  121.3 1.2 near_sum.1
  122.5 6.9 %collective-permute-start.9 = (bf16[64,768]{1,0:T(8,128)(2,1)S(1)}, bf16[64,768]{1,0:T(8,128)(2,1)S(1)}, u32[]{:S(2)}, u32[]{:S(2)}) collective-permute-start(bf16[64,768]{1,0:T(8,128)(2,1)S(1)} %get-tuple-element.30), channel_id=1, source_target_pairs={{0,128},{16,144},{32,160},{48,176},{64,192},{80,208},{96,224},{112... | collective-permute-start | bytes 294920 | tf_op jit(solution)/shard_map/ppermute | solution.py:270
  129.4 4.3 %collective-permute-start.10 = (bf16[64,768]{1,0:T(8,128)(2,1)S(1)}, bf16[64,768]{1,0:T(8,128)(2,1)S(1)}, u32[]{:S(2)}, u32[]{:S(2)}) collective-permute-start(bf16[64,768]{1,0:T(8,128)(2,1)S(1)} %get-tuple-element.31), channel_id=1, source_target_pairs={{0,64},{16,80},{32,96},{48,112},{64,128},{80,144},{96,160},{112,17... | collective-permute-start | bytes 294920 | tf_op jit(solution)/shard_map/ppermute | solution.py:270
  133.7 4.9 %collective-permute-start.11 = (bf16[64,768]{1,0:T(8,128)(2,1)S(1)}, bf16[64,768]{1,0:T(8,128)(2,1)S(1)}, u32[]{:S(2)}, u32[]{:S(2)}) collective-permute-start(bf16[64,768]{1,0:T(8,128)(2,1)S(1)} %get-tuple-element.32), channel_id=1, source_target_pairs={{0,192},{16,208},{32,224},{48,240},{64,0},{80,16},{96,32},{112,48}... | collective-permute-start | bytes 294920 | tf_op jit(solution)/shard_map/ppermute | solution.py:270
  138.6 4.2 %collective-permute-done.10.three = bf16[64,768]{1,0:T(8,128)(2,1)S(1)} collective-permute-done((bf16[64,768]{1,0:T(8,128)(2,1)S(1)}, bf16[64,768]{1,0:T(8,128)(2,1)S(1)}, u32[]{:S(2)}, u32[]{:S(2)}) %collective-permute-start.10) | collective-permute-done | bytes 98336 | tf_op jit(solution)/shard_map/ppermute | solution.py:270
  142.8 3.1 %collective-permute-done.11.four = bf16[64,768]{1,0:T(8,128)(2,1)S(1)} collective-permute-done((bf16[64,768]{1,0:T(8,128)(2,1)S(1)}, bf16[64,768]{1,0:T(8,128)(2,1)S(1)}, u32[]{:S(2)}, u32[]{:S(2)}) %collective-permute-start.11) | collective-permute-done | bytes 98336 | tf_op jit(solution)/shard_map/ppermute | solution.py:270
  146.0 4.5 %collective-permute-start.12 = (bf16[32,768]{1,0:T(8,128)(2,1)S(1)}, bf16[32,768]{1,0:T(8,128)(2,1)S(1)}, u32[]{:S(2)}, u32[]{:S(2)}) collective-permute-start(bf16[32,768]{1,0:T(8,128)(2,1)S(1)} %get-tuple-element.34), channel_id=1, source_target_pairs={{0,256},{16,272},{32,288},{48,304},{64,320},{80,336},{96,352},{112... | collective-permute-start | bytes 147464 | tf_op jit(solution)/shard_map/ppermute | solution.py:265
  150.5 4.6 %all-to-all-done = bf16[16,80,1024]{2,1,0:T(8,128)(2,1)S(1)} async-done(((bf16[16,80,1024]{2,1,0:T(8,128)(2,1)}), bf16[16,80,1024]{2,1,0:T(8,128)(2,1)S(1)}, u32[]{:S(2)}, u32[]{:S(2)}) %all-to-all-start) | async-done | bytes 2621472 | tf_op jit(solution)/shard_map/all_to_all | solution.py:392
  155.1 1.4 combine_rows.1
  (30 shorter events, 4.4 us)
Async XLA Ops:
  7.2 71.0 %all-gather.2.cloned.1.call-start = ((), (), s32[]{:S(2)}) async-start(), calls=%async_computation.1 | async-start | bytes 9469952 | tf_op jit(solution)/shard_map/all_gather | solution.py:383
  9.2 7.6 %collective-permute-start = (bf16[32,1152]{1,0:T(8,128)(2,1)}, bf16[32,1152]{1,0:T(8,128)(2,1)S(1)}, u32[]{:S(2)}, u32[]{:S(2)}) collective-permute-start(bf16[32,1152]{1,0:T(8,128)(2,1)} %get-tuple-element.21), channel_id=1, source_target_pairs={{0,256},{16,272},{32,288},{48,304},{64,320},{80,336},{96,352},{112... | collective-permute-start | bytes 221192 | tf_op jit(solution)/shard_map/ppermute | solution.py:265
  50.3 27.8 %copy-start.2 = (bf16[256,1152]{1,0:T(8,128)(2,1)}, bf16[256,1152]{1,0:T(8,128)(2,1)S(1)}, u32[]{:S(2)}) copy-start(bf16[256,1152]{1,0:T(8,128)(2,1)S(1)} %all_gather.7.refs_0_) | copy-start | bytes 1769476
  50.3 26.7 %collective-permute-start.2 = (bf16[256,1152]{1,0:T(8,128)(2,1)S(1)}, bf16[256,1152]{1,0:T(8,128)(2,1)S(1)}, u32[]{:S(2)}, u32[]{:S(2)}) collective-permute-start(bf16[256,1152]{1,0:T(8,128)(2,1)S(1)} %all_gather.7.refs_0_), channel_id=1, source_target_pairs={{0,240},{16,0},{32,16},{48,32},{64,48},{80,64},{96,80},{112,96},{1... | collective-permute-start | bytes 1769480 | tf_op jit(solution)/shard_map/ppermute | solution.py:270
  54.1 22.9 %collective-permute-start.1 = (bf16[256,1152]{1,0:T(8,128)(2,1)S(1)}, bf16[256,1152]{1,0:T(8,128)(2,1)S(1)}, u32[]{:S(2)}, u32[]{:S(2)}) collective-permute-start(bf16[256,1152]{1,0:T(8,128)(2,1)S(1)} %all_gather.7.refs_0_), channel_id=1, source_target_pairs={{0,16},{16,32},{32,48},{48,64},{64,80},{80,96},{96,112},{112,128},... | collective-permute-start | bytes 1769480 | tf_op jit(solution)/shard_map/ppermute | solution.py:270
  56.1 20.4 %collective-permute-start.4 = (bf16[128,1152]{1,0:T(8,128)(2,1)S(1)}, bf16[128,1152]{1,0:T(8,128)(2,1)S(1)}, u32[]{:S(2)}, u32[]{:S(2)}) collective-permute-start(bf16[128,1152]{1,0:T(8,128)(2,1)S(1)} %get-tuple-element.36), channel_id=1, source_target_pairs={{0,224},{16,240},{32,0},{48,16},{64,32},{80,48},{96,64},{112,80},{... | collective-permute-start | bytes 884744 | tf_op jit(solution)/shard_map/ppermute | solution.py:270
  59.2 17.8 %collective-permute-start.3 = (bf16[128,1152]{1,0:T(8,128)(2,1)S(1)}, bf16[128,1152]{1,0:T(8,128)(2,1)S(1)}, u32[]{:S(2)}, u32[]{:S(2)}) collective-permute-start(bf16[128,1152]{1,0:T(8,128)(2,1)S(1)} %get-tuple-element.37), channel_id=1, source_target_pairs={{0,32},{16,48},{32,64},{48,80},{64,96},{80,112},{96,128},{112,144}... | collective-permute-start | bytes 884744 | tf_op jit(solution)/shard_map/ppermute | solution.py:270
  76.5 1.7 %copy-start.5 = (bf16[128,1152]{1,0:T(8,128)(2,1)}, bf16[128,1152]{1,0:T(8,128)(2,1)S(1)}, u32[]{:S(2)}) copy-start(bf16[128,1152]{1,0:T(8,128)(2,1)S(1)} %collective-permute-done.4.refs_4_) | copy-start | bytes 884740
  77.0 1.1 copy-start.6
  77.0 1.1 copy-start.3
  77.0 1.2 copy-start.4
  92.7 27.5 %collective-permute-start.5 = (bf16[4,64,768]{2,1,0:T(8,128)(2,1)}, bf16[4,64,768]{2,1,0:T(8,128)(2,1)S(1)}, u32[]{:S(2)}, u32[]{:S(2)}) collective-permute-start(bf16[4,64,768]{2,1,0:T(8,128)(2,1)} %bitcast.13), channel_id=1, source_target_pairs={{0,16},{16,32},{32,48},{48,64},{64,80},{80,96},{96,112},{112,128},... | collective-permute-start | bytes 1179656 | tf_op jit(solution)/shard_map/ppermute | solution.py:270
  97.4 22.8 %collective-permute-start.6 = (bf16[4,64,768]{2,1,0:T(8,128)(2,1)}, bf16[4,64,768]{2,1,0:T(8,128)(2,1)S(1)}, u32[]{:S(2)}, u32[]{:S(2)}) collective-permute-start(bf16[4,64,768]{2,1,0:T(8,128)(2,1)} %bitcast.12), channel_id=1, source_target_pairs={{0,240},{16,0},{32,16},{48,32},{64,48},{80,64},{96,80},{112,96},{1... | collective-permute-start | bytes 1179656 | tf_op jit(solution)/shard_map/ppermute | solution.py:270
  100.3 19.9 %collective-permute-start.7 = (bf16[4,32,768]{2,1,0:T(8,128)(2,1)}, bf16[4,32,768]{2,1,0:T(8,128)(2,1)}, u32[]{:S(2)}, u32[]{:S(2)}) collective-permute-start(bf16[4,32,768]{2,1,0:T(8,128)(2,1)} %get-tuple-element.27), channel_id=1, source_target_pairs={{0,32},{16,48},{32,64},{48,80},{64,96},{80,112},{96,128},{112,144}... | collective-permute-start | bytes 589832 | tf_op jit(solution)/shard_map/ppermute | solution.py:270
  102.5 17.8 %collective-permute-start.8 = (bf16[4,32,768]{2,1,0:T(8,128)(2,1)}, bf16[4,32,768]{2,1,0:T(8,128)(2,1)}, u32[]{:S(2)}, u32[]{:S(2)}) collective-permute-start(bf16[4,32,768]{2,1,0:T(8,128)(2,1)} %get-tuple-element.28), channel_id=1, source_target_pairs={{0,224},{16,240},{32,0},{48,16},{64,32},{80,48},{96,64},{112,80},{... | collective-permute-start | bytes 589832 | tf_op jit(solution)/shard_map/ppermute | solution.py:270
  107.7 47.4 %all-to-all-start = ((bf16[16,80,1024]{2,1,0:T(8,128)(2,1)}), bf16[16,80,1024]{2,1,0:T(8,128)(2,1)S(1)}, u32[]{:S(2)}, u32[]{:S(2)}) async-start(bf16[16,80,1024]{2,1,0:T(8,128)(2,1)} %bitcast.9), calls=%async_computation | async-start | bytes 5242880 | tf_op jit(solution)/shard_map/all_to_all | solution.py:392
  120.3 1.0 copy-start.1
  121.3 33.8 %copy-start = (bf16[16,128]{1,0:T(8,128)(2,1)S(1)}, bf16[16,128]{1,0:T(8,128)(2,1)}, u32[]{:S(2)}) copy-start(bf16[16,128]{1,0:T(8,128)(2,1)} %get-tuple-element.19.rank_ref) | copy-start | bytes 12292
  122.5 16.1 %collective-permute-start.9 = (bf16[64,768]{1,0:T(8,128)(2,1)S(1)}, bf16[64,768]{1,0:T(8,128)(2,1)S(1)}, u32[]{:S(2)}, u32[]{:S(2)}) collective-permute-start(bf16[64,768]{1,0:T(8,128)(2,1)S(1)} %get-tuple-element.30), channel_id=1, source_target_pairs={{0,128},{16,144},{32,160},{48,176},{64,192},{80,208},{96,224},{112... | collective-permute-start | bytes 294920 | tf_op jit(solution)/shard_map/ppermute | solution.py:270
  129.4 13.4 %collective-permute-start.10 = (bf16[64,768]{1,0:T(8,128)(2,1)S(1)}, bf16[64,768]{1,0:T(8,128)(2,1)S(1)}, u32[]{:S(2)}, u32[]{:S(2)}) collective-permute-start(bf16[64,768]{1,0:T(8,128)(2,1)S(1)} %get-tuple-element.31), channel_id=1, source_target_pairs={{0,64},{16,80},{32,96},{48,112},{64,128},{80,144},{96,160},{112,17... | collective-permute-start | bytes 294920 | tf_op jit(solution)/shard_map/ppermute | solution.py:270
  133.7 12.2 %collective-permute-start.11 = (bf16[64,768]{1,0:T(8,128)(2,1)S(1)}, bf16[64,768]{1,0:T(8,128)(2,1)S(1)}, u32[]{:S(2)}, u32[]{:S(2)}) collective-permute-start(bf16[64,768]{1,0:T(8,128)(2,1)S(1)} %get-tuple-element.32), channel_id=1, source_target_pairs={{0,192},{16,208},{32,224},{48,240},{64,0},{80,16},{96,32},{112,48}... | collective-permute-start | bytes 294920 | tf_op jit(solution)/shard_map/ppermute | solution.py:270
  146.0 10.5 %collective-permute-start.12 = (bf16[32,768]{1,0:T(8,128)(2,1)S(1)}, bf16[32,768]{1,0:T(8,128)(2,1)S(1)}, u32[]{:S(2)}, u32[]{:S(2)}) collective-permute-start(bf16[32,768]{1,0:T(8,128)(2,1)S(1)} %get-tuple-element.34), channel_id=1, source_target_pairs={{0,256},{16,272},{32,288},{48,304},{64,320},{80,336},{96,352},{112... | collective-permute-start | bytes 147464 | tf_op jit(solution)/shard_map/ppermute | solution.py:265
Sparse Core Ops, SparseCore 0:
  10.1 67.9 all-gather.1
